TPU v7x, 512 devices: a whole 4x8x8 slice. The times are simulated.
512 devices in a mesh: row: 16 (over y_lo, x, core), col: 32 (over y_hi, z).
Axes of the slice: x: 4, y: 8 (y_hi: 4, y_lo: 2; y = y_hi * 2 + y_lo), z: 8, core: 2. Of those that a mesh axis runs over, the one named last changes fastest.
Arguments:
- inputs: bfloat16 [2048, 4096], P('row', 'col'), may hold values from -6 to 6
- out_grad: bfloat16 [2048, 4096], P('row', 'col'), may hold values from -2 to 2
- codes: bfloat16 [3, 4096, 8192], P(None, 'row', 'col'), may hold values from -0.09375 to 0.09375
- scales: bfloat16 [3, 16, 8192], P(None, 'row', 'col'), may hold values from 0.5 to 2
Outputs:
- input_grad: bfloat16 [2048, 4096], P('row', 'col')
- weight_grad: float32 [3, 4096, 8192], P(None, 'row', 'col')
All inputs are finite; a program needn't handle non-finite values.
Results may differ from a plain program's by a relative error of at most 0.022.
Values may be sent and summed in bfloat16 or wider, within the bound.
No kernel may reach another device: no remote copies, remote signals or barrier semaphores. Data moves between devices by JAX's collectives and lax.ppermute only.
A program may use at most 128 MiB of HBM per device.

v0:
```python
import jax
import jax.numpy as jnp
from jax import lax
from jax.sharding import PartitionSpec as P

QB = 256


def dequantize(codes, scales):
    depth, rows, width = codes.shape
    blocked = codes.reshape(depth, rows // QB, QB, width).astype(jnp.float32)
    full = blocked * scales.astype(jnp.float32)[:, :, None, :]
    return full.reshape(depth, rows, width).astype(jnp.bfloat16)


def pack_one(partial_value, groups):
    rows, width = partial_value.shape
    blocked = partial_value.reshape(rows // QB, QB, width)
    block_scale = (jnp.max(jnp.abs(blocked), axis=1) + 1e-06).astype(jnp.bfloat16)
    packed = (blocked / block_scale.astype(jnp.float32)[:, None, :]).astype(jnp.bfloat16)
    block_scale = block_scale.reshape(groups, rows // QB // groups, width)
    return (packed, block_scale)


def unpack_one(packed, block_scale):
    groups, rows, width = packed.shape
    blocked = packed.reshape(groups, rows // QB, QB, width).astype(jnp.float32)
    restored = blocked * block_scale.astype(jnp.float32)[:, :, None, :]
    return jnp.sum(restored, axis=0).reshape(rows, width)


def local(inputs, out_grad, codes, scales):
    groups = lax.axis_size("row")
    tokens_in, grads_in = (
        lax.all_gather(inputs, "col", axis=1, tiled=True),
        lax.all_gather(out_grad, "col", axis=1, tiled=True),
    )
    all_codes, all_scales = (
        lax.all_gather(codes, "row", axis=1, tiled=True),
        lax.all_gather(scales, "row", axis=1, tiled=True),
    )
    weights = dequantize(all_codes, all_scales)
    gate = jnp.dot(tokens_in, weights[0], preferred_element_type=jnp.float32)
    up = jnp.dot(tokens_in, weights[1], preferred_element_type=jnp.float32)
    hidden_grad = jnp.dot(grads_in, weights[2], preferred_element_type=jnp.float32)
    sig = jax.nn.sigmoid(gate)
    act = gate * sig
    hidden = (act * up).astype(jnp.bfloat16)
    down_part = jnp.einsum("td,tf->df", grads_in, hidden, preferred_element_type=jnp.float32)
    packed_down, scale_down = pack_one(down_part, groups)
    up_grad = (hidden_grad * act).astype(jnp.bfloat16)
    gate_grad = (hidden_grad * up * sig * (1.0 + gate * (1.0 - sig))).astype(jnp.bfloat16)
    partial_input = jnp.einsum(
        "tf,df->td", gate_grad, weights[0], preferred_element_type=jnp.float32
    )
    partial_input = partial_input + jnp.einsum(
        "tf,df->td", up_grad, weights[1], preferred_element_type=jnp.float32
    )
    input_grad = lax.psum_scatter(
        partial_input.astype(jnp.bfloat16), "col", scatter_dimension=1, tiled=True
    )
    gate_part = jnp.einsum("td,tf->df", tokens_in, gate_grad, preferred_element_type=jnp.float32)
    packed_gate, scale_gate = pack_one(gate_part, groups)
    up_part = jnp.einsum("td,tf->df", tokens_in, up_grad, preferred_element_type=jnp.float32)
    packed_up, scale_up = pack_one(up_part, groups)
    got_gate, got_gate_scale, got_up, got_up_scale, got_down, got_down_scale = (
        lax.all_to_all(packed_gate, "row", split_axis=0, concat_axis=0, tiled=True),
        lax.all_to_all(scale_gate, "row", split_axis=0, concat_axis=0, tiled=True),
        lax.all_to_all(packed_up, "row", split_axis=0, concat_axis=0, tiled=True),
        lax.all_to_all(scale_up, "row", split_axis=0, concat_axis=0, tiled=True),
        lax.all_to_all(packed_down, "row", split_axis=0, concat_axis=0, tiled=True),
        lax.all_to_all(scale_down, "row", split_axis=0, concat_axis=0, tiled=True),
    )
    weight_grad = jnp.stack(
        [
            unpack_one(got_gate, got_gate_scale),
            unpack_one(got_up, got_up_scale),
            unpack_one(got_down, got_down_scale),
        ]
    )
    return (input_grad, weight_grad)


def solution(mesh):
    return jax.shard_map(
        local,
        mesh=mesh,
        in_specs=(P("row", "col"), P("row", "col"), P(None, "row", "col"), P(None, "row", "col")),
        out_specs=(P("row", "col"), P(None, "row", "col")),
        check_vma=False,
    )
```

profile of v0, /device:TPU:2, one launch (start us, length us, event | category | flops | bytes accessed | tf_op | source)
XLA Modules:
  0.0 583.2 jit_solution(11493349313670669315)
XLA Ops:
  7.2 0.0 all-gather.4.cloned.1.call-start
  7.2 0.7 all-gather.4.cloned.1.call-update
  7.9 0.0 all-gather.8.cloned.1.call-start
  7.9 0.7 all-gather.8.cloned.1.call-update
  8.6 0.0 all-gather.6.cloned.1.call-start
  8.7 0.7 all-gather.6.cloned.1.call-update
  9.4 22.1 %all_gather.13 = bf16[3,16,256]{2,0,1:T(4,128)(2,1)S(1)} all-gather(bf16[3,1,256]{2,0,1:T(4,128)(2,1)} %param.7), channel_id=1, replica_groups=mesh['row'=16,'col'=32] {'row'}, dimensions={1}, use_global_device_ids=true | all-gather | bytes 26112 | tf_op jit(solution)/shard_map/all_gather | solution.py:40
  31.5 30.8 %all-gather.4.cloned.1.call-done = bf16[3,4096,256]{2,1,0:T(8,128)(2,1)} async-done(((bf16[3,256,256]{2,1,0:T(8,128)(2,1)}), bf16[3,4096,256]{2,1,0:T(8,128)(2,1)}) %all-gather.4.cloned.1.call-update) | async-done | bytes 6291472 | tf_op jit(solution)/shard_map/all_gather | solution.py:39
  62.3 6.6 %fusion = bf16[3,4096,256]{2,1,0:T(8,128)(2,1)} fusion(bf16[3,4096,256]{2,1,0:T(8,128)(2,1)} %all-gather.4.cloned.1.call-done, f32[3,16,256]{2,1,0:T(8,128)S(1)} %copy_convert_fusion), kind=kLoop, calls=%fused_computation.1 | loop fusion | flops 9437184 | bytes 12632064 | tf_op jit(solution)/shard_map/convert_element_type | solution.py:13
  68.8 76.2 %all-gather.8.cloned.1.call-done = bf16[128,4096]{1,0:T(8,128)(2,1)} async-done(((bf16[128,128]{1,0:T(8,128)(2,1)}), bf16[128,4096]{1,0:T(8,128)(2,1)}) %all-gather.8.cloned.1.call-update) | async-done | bytes 1048592 | tf_op jit(solution)/shard_map/all_gather | solution.py:35
  145.0 2.6 fusion.9
  147.6 2.6 fusion.10
  150.2 73.8 %all-gather.6.cloned.1.call-done = bf16[128,4096]{1,0:T(8,128)(2,1)} async-done(((bf16[128,128]{1,0:T(8,128)(2,1)}), bf16[128,4096]{1,0:T(8,128)(2,1)}) %all-gather.6.cloned.1.call-update) | async-done | bytes 1048592 | tf_op jit(solution)/shard_map/all_gather | solution.py:36
  224.1 1.9 fusion.13
  226.0 0.0 copy-start
  226.0 1.8 copy.70
  227.8 0.4 copy-done
  228.2 0.8 abs_reduce_fusion
  228.9 0.1 copy.52
  229.0 0.5 broadcast.74
  229.5 0.6 reduce.8
  230.2 0.6 reshape.100
  230.8 4.8 all-to-all-start.5
  235.6 2.3 multiply_convert_fusion.1
  238.0 0.7 fusion.23
  238.7 1.8 copy.69
  240.5 0.4 copy-done.2
  240.9 0.8 abs_reduce_fusion.1
  241.6 0.1 copy.48
  241.7 0.7 fusion.22
  242.4 1.8 copy.68
  244.2 0.4 copy-done.1
  244.6 0.8 abs_reduce_fusion.2
  245.4 0.6 reduce.7
  246.0 0.6 reshape.102
  246.6 0.1 copy.44
  246.7 0.0 all-to-all-done.5
  246.7 5.7 all-to-all-start.3
  252.4 0.6 reduce.6
  253.1 0.6 reshape.104
  253.7 3.4 all-to-all-done.3
  257.0 4.7 all-to-all-start.1
  261.8 3.6 fusion.2
  265.4 1.1 all-to-all-done.1
  266.5 5.0 all-to-all-start.4
  271.4 3.6 fusion.3
  275.0 23.8 %all-to-all-done.4 = bf16[16,256,256]{1,2,0:T(8,128)(2,1)S(1)} async-done(((bf16[16,256,256]{1,2,0:T(8,128)(2,1)}), bf16[16,256,256]{1,2,0:T(8,128)(2,1)S(1)}, u32[]{:S(2)}, u32[]{:S(2)}) %all-to-all-start.4) | async-done | bytes 2097184 | tf_op jit(solution)/shard_map/all_to_all | solution.py:71
  298.8 6.8 %all-to-all-start.2 = ((bf16[16,256,256]{1,2,0:T(8,128)(2,1)}), bf16[16,256,256]{1,2,0:T(8,128)(2,1)}, u32[]{:S(2)}, u32[]{:S(2)}) async-start(bf16[16,256,256]{1,2,0:T(8,128)(2,1)} %fusion.3), calls=%async_computation.2 | async-start | bytes 4194304 | tf_op jit(solution)/shard_map/all_to_all | solution.py:69
  305.5 3.6 fusion.4
  309.1 24.0 %all-to-all-done.2 = bf16[16,256,256]{1,2,0:T(8,128)(2,1)} async-done(((bf16[16,256,256]{1,2,0:T(8,128)(2,1)}), bf16[16,256,256]{1,2,0:T(8,128)(2,1)}, u32[]{:S(2)}, u32[]{:S(2)}) %all-to-all-start.2) | async-done | bytes 2097184 | tf_op jit(solution)/shard_map/all_to_all | solution.py:69
  333.1 6.9 %all-to-all-start = ((bf16[16,256,256]{1,2,0:T(8,128)(2,1)}), bf16[16,256,256]{1,2,0:T(8,128)(2,1)}, u32[]{:S(2)}, u32[]{:S(2)}) async-start(bf16[16,256,256]{1,2,0:T(8,128)(2,1)} %fusion.4), calls=%async_computation | async-start | bytes 4194304 | tf_op jit(solution)/shard_map/all_to_all | solution.py:67
  339.9 0.3 reduce-scatter.4.cloned.1.call-start
  340.2 2.4 fusion.7
  342.6 2.4 fusion.1
  345.1 1.4 copy.57
  346.4 0.0 reduce-scatter.4.cloned.1.call-update
  346.5 222.8 %reduce-scatter.4.cloned.1.call-done = bf16[128,128]{1,0:T(8,128)(2,1)} async-done(((bf16[4096,128]{1,0:T(8,128)(2,1)}), bf16[128,128]{1,0:T(8,128)(2,1)}) %reduce-scatter.4.cloned.1.call-update) | async-done | bytes 32784
  569.3 1.5 copy.58
  570.8 0.7 multiply_reduce_fusion
  571.5 2.0 multiply_reduce_fusion.1
  573.5 0.0 all-to-all-done
  573.5 2.0 multiply_reduce_fusion.2
  575.4 0.1 pad_maximum_fusion
  575.5 1.1 copy.56
  (16 shorter events, 0.1 us)
Async XLA Ops:
  7.2 55.1 %all-gather.4.cloned.1.call-start = ((), (), s32[]{:S(2)}) async-start(), calls=%async_computation.7 | async-start | bytes 6684672 | tf_op jit(solution)/shard_map/all_gather | solution.py:39
  7.9 137.1 %all-gather.8.cloned.1.call-start = ((), (), s32[]{:S(2)}) async-start(), calls=%async_computation.9 | async-start | bytes 1081344 | tf_op jit(solution)/shard_map/all_gather | solution.py:35
  8.6 215.4 %all-gather.6.cloned.1.call-start = ((), (), s32[]{:S(2)}) async-start(), calls=%async_computation.8 | async-start | bytes 1081344 | tf_op jit(solution)/shard_map/all_gather | solution.py:36
  226.0 2.2 copy-start
  228.2 7.5 %copy-start.4 = (bf16[128,4096]{1,0:T(8,128)(2,1)S(1)}, bf16[128,4096]{1,0:T(8,128)(2,1)}, u32[]{:S(2)}) copy-start(bf16[128,4096]{1,0:T(8,128)(2,1)} %all-gather.6.cloned.1.call-done) | copy-start | bytes 3145732
  228.2 9.8 %copy-start.3 = (bf16[128,4096]{1,0:T(8,128)(2,1)S(1)}, bf16[128,4096]{1,0:T(8,128)(2,1)}, u32[]{:S(2)}) copy-start(bf16[128,4096]{1,0:T(8,128)(2,1)} %all-gather.8.cloned.1.call-done) | copy-start | bytes 3145732
  230.8 15.9 %all-to-all-start.5 = ((bf16[16,2,128]{2,1,0:T(2,128)(2,1)}), bf16[16,2,128]{2,1,0:T(2,128)(2,1)S(1)}, u32[]{:S(2)}, u32[]{:S(2)}) async-start(bf16[16,2,128]{2,1,0:T(2,128)(2,1)} %reshape.100), calls=%async_computation.5 | async-start | bytes 16384 | tf_op jit(solution)/shard_map/all_to_all | solution.py:72
  238.7 2.2 copy-start.2
  242.4 2.2 copy-start.1
  246.7 10.4 %all-to-all-start.3 = ((bf16[16,2,128]{2,1,0:T(2,128)(2,1)}), bf16[16,2,128]{2,1,0:T(2,128)(2,1)S(1)}, u32[]{:S(2)}, u32[]{:S(2)}) async-start(bf16[16,2,128]{2,1,0:T(2,128)(2,1)} %reshape.102), calls=%async_computation.3 | async-start | bytes 16384 | tf_op jit(solution)/shard_map/all_to_all | solution.py:70
  257.0 9.4 %all-to-all-start.1 = ((bf16[16,2,128]{2,1,0:T(2,128)(2,1)}), bf16[16,2,128]{2,1,0:T(2,128)(2,1)S(1)}, u32[]{:S(2)}, u32[]{:S(2)}) async-start(bf16[16,2,128]{2,1,0:T(2,128)(2,1)} %reshape.104), calls=%async_computation.1 | async-start | bytes 16384 | tf_op jit(solution)/shard_map/all_to_all | solution.py:68
  266.5 32.3 %all-to-all-start.4 = ((bf16[16,256,256]{1,2,0:T(8,128)(2,1)}), bf16[16,256,256]{1,2,0:T(8,128)(2,1)S(1)}, u32[]{:S(2)}, u32[]{:S(2)}) async-start(bf16[16,256,256]{1,2,0:T(8,128)(2,1)} %fusion.2), calls=%async_computation.4 | async-start | bytes 4194304 | tf_op jit(solution)/shard_map/all_to_all | solution.py:71
  298.8 34.3 %all-to-all-start.2 = ((bf16[16,256,256]{1,2,0:T(8,128)(2,1)}), bf16[16,256,256]{1,2,0:T(8,128)(2,1)}, u32[]{:S(2)}, u32[]{:S(2)}) async-start(bf16[16,256,256]{1,2,0:T(8,128)(2,1)} %fusion.3), calls=%async_computation.2 | async-start | bytes 4194304 | tf_op jit(solution)/shard_map/all_to_all | solution.py:69
  333.1 240.4 %all-to-all-start = ((bf16[16,256,256]{1,2,0:T(8,128)(2,1)}), bf16[16,256,256]{1,2,0:T(8,128)(2,1)}, u32[]{:S(2)}, u32[]{:S(2)}) async-start(bf16[16,256,256]{1,2,0:T(8,128)(2,1)} %fusion.4), calls=%async_computation | async-start | bytes 4194304 | tf_op jit(solution)/shard_map/all_to_all | solution.py:67
  339.9 229.4 %reduce-scatter.4.cloned.1.call-start = ((), (), s32[]{:S(2)}) async-start(), calls=%async_computation.10 | async-start | bytes 1081344
Sparse Core Ops, SparseCore 0:
  10.1 52.1 all-gather.3
  65.3 79.6 all-gather.7
  148.1 75.9 all-gather.5
  346.6 222.6 reduce-scatter.3
where the time goes:
time: 584 us; the launch traced here: 583 us
  waiting for transfers between devices  458 us (78%)
  starting transfers between devices  34.3 us (6%)
  other arithmetic  26.2 us (4%)
  blocking collectives  22.1 us (4%)
  matrix products  15.7 us (3%)
  between operations  14 us (2%)
  local copies, waits for them, and re-layouts  13.1 us (2%)
    unnamed x5, waiting for transfers between devices  225 us
    all_gather x1, waiting for transfers between devices, local(): lax.all_gather(inputs, 'col', axis=1, tiled=True)  76.2 us
    all_gather x1, waiting for transfers between devices, local(): lax.all_gather(out_grad, 'col', axis=1, tiled=True)  73.8 us
    all_gather x1, waiting for transfers between devices, local(): lax.all_gather(codes, 'row', axis=1, tiled=True)  30.8 us
    all_to_all x1, waiting for transfers between devices, local(): lax.all_to_all(packed_up, 'row', split_axis=0, concat_axis=0, tiled=True)  24 us
    all_to_all x1, waiting for transfers between devices, local(): lax.all_to_all(packed_down, 'row', split_axis=0, concat_axis=0, tiled=True)  23.8 us
    all_gather x1, blocking collectives, local(): lax.all_gather(scales, 'row', axis=1, tiled=True)  22.1 us
    unnamed x25, local copies, waits for them, and re-layouts  12.4 us
  transfers between devices with their start and end apart: 10, of which 8 were waited for; matrix products, arithmetic and copies ran while one was open for 8% of the time, Pallas kernels for 0%

commit v1 on v0

v1 whole, which is shorter than its diff:
```python
import functools

import jax
import jax.numpy as jnp
from jax import lax
from jax.experimental import pallas as pl
from jax.experimental.pallas import tpu as pltpu
from jax.sharding import Mesh, PartitionSpec as P

F32 = jnp.float32
BF16 = jnp.bfloat16
ROW = ("yl", "x", "core")
COL = ("yh", "z")
YL, X, CORE, YH, Z = 2, 4, 2, 4, 8
N_ROW = YL * X * CORE
TOK = 128
VMEM_LIMIT = 56 * 1024 * 1024


def dot(a, b, dims):
    return lax.dot_general(a, b, (dims, ((), ())), preferred_element_type=F32)


def gather_by_swap(block, axis, size):
    copies = jnp.broadcast_to(block[None], (size,) + block.shape)
    return lax.all_to_all(copies, axis, split_axis=0, concat_axis=0, tiled=True)


def features(acts_ref, which, r):
    y, z = r // 4, (r % 4) * 2
    return jnp.concatenate([acts_ref[z, y, which], acts_ref[z + 1, y, which]], axis=1)


def forward_kernel(acts_ref, w_ref, grads_ref, dx_ref):
    gate = jnp.zeros((TOK, 256), F32)
    up = jnp.zeros((TOK, 256), F32)
    hidden_grad = jnp.zeros((TOK, 256), F32)
    for r in range(N_ROW):
        tokens = features(acts_ref, 0, r)
        gate += dot(tokens, w_ref[r, 0], ((1,), (0,)))
        up += dot(tokens, w_ref[r, 1], ((1,), (0,)))
        hidden_grad += dot(features(acts_ref, 1, r), w_ref[r, 2], ((1,), (0,)))
    sig = 1.0 / (1.0 + jnp.exp(-gate))
    act = gate * sig
    gate_grad = (hidden_grad * up * sig * (1.0 + gate * (1.0 - sig))).astype(BF16)
    up_grad = (hidden_grad * act).astype(BF16)
    grads_ref[0] = gate_grad
    grads_ref[1] = up_grad
    grads_ref[2] = (act * up).astype(BF16)
    for r in range(N_ROW):
        dx = dot(gate_grad, w_ref[r, 0], ((1,), (1,))) + dot(up_grad, w_ref[r, 1], ((1,), (1,)))
        dx = dx.astype(BF16)
        y, z = r // 4, (r % 4) * 2
        dx_ref[y, z] = dx[:, :128]
        dx_ref[y, z + 1] = dx[:, 128:]


def forward(acts, weights):
    whole = pl.BlockSpec(memory_space=pltpu.VMEM)
    return pl.pallas_call(
        forward_kernel,
        out_shape=(
            jax.ShapeDtypeStruct((3, TOK, 256), BF16),
            jax.ShapeDtypeStruct((YH, Z, TOK, 128), BF16),
        ),
        in_specs=[whole, whole],
        out_specs=(whole, whole),
        compiler_params=pltpu.CompilerParams(vmem_limit_bytes=VMEM_LIMIT),
        cost_estimate=pl.CostEstimate(flops=1400000000, bytes_accessed=10000000, transcendentals=32768),
        name="forward",
    )(acts, weights)


def weight_kernel(core_ref, acts_ref, other_acts_ref, grads_ref, other_grads_ref, out_ref):
    k = core_ref[0]
    for q in range(N_ROW // 2):
        y, j = q // 2, q % 2
        z = 4 * j + 2 * k
        feats = []
        for which in range(2):
            own = jnp.concatenate([acts_ref[z, y, which], acts_ref[z + 1, y, which]], axis=1)
            other = jnp.concatenate(
                [other_acts_ref[j, 0, y, which], other_acts_ref[j, 1, y, which]], axis=1
            )
            feats.append(jnp.concatenate([own, other], axis=0))
        for p in range(3):
            grads = jnp.concatenate([grads_ref[p], other_grads_ref[p]], axis=0)
            out_ref[q, p] = dot(feats[p // 2], grads, ((0,), (0,))).astype(BF16)


def weight_terms(core, acts, other_acts, grads, other_grads):
    whole = pl.BlockSpec(memory_space=pltpu.VMEM)
    return pl.pallas_call(
        weight_kernel,
        out_shape=jax.ShapeDtypeStruct((N_ROW // 2, 3, 256, 256), BF16),
        in_specs=[pl.BlockSpec(memory_space=pltpu.SMEM)] + [whole] * 4,
        out_specs=whole,
        compiler_params=pltpu.CompilerParams(vmem_limit_bytes=VMEM_LIMIT),
        cost_estimate=pl.CostEstimate(flops=800000000, bytes_accessed=6000000, transcendentals=0),
        name="weight_terms",
    )(core, acts, other_acts, grads, other_grads)


def local(inputs, out_grad, codes, scales):
    core = lax.axis_index("core")
    swap = [(0, 1), (1, 0)]
    weights = (codes.astype(F32) * scales.astype(F32)).astype(BF16)
    weights = lax.all_gather(weights, ROW, axis=0, tiled=False)

    acts = gather_by_swap(jnp.stack([inputs, out_grad]), "yh", YH)
    acts = gather_by_swap(acts, "z", Z)

    halves = acts.reshape(2, 2, 2, YH, 2, TOK, 128)
    other_half = lax.dynamic_index_in_dim(halves, 1 - core, axis=1, keepdims=False)
    other_acts = lax.ppermute(other_half, "core", swap)

    grads, dx = forward(acts, weights)
    other_grads = lax.ppermute(grads, "core", swap)
    dx = lax.all_to_all(dx.reshape(YH * Z, TOK, 128), COL, split_axis=0, concat_axis=0, tiled=True)
    input_grad = jnp.sum(dx.astype(F32), axis=0).astype(BF16)

    terms = weight_terms(core.reshape(1), acts, other_acts, grads, other_grads)
    terms = lax.all_to_all(terms, ("yl", "x"), split_axis=0, concat_axis=0, tiled=True)
    weight_grad = jnp.sum(terms.astype(F32), axis=0)
    return input_grad, weight_grad


def solution(mesh):
    fine = Mesh(mesh.devices.reshape(YL, X, CORE, YH, Z), ROW + COL)
    return jax.shard_map(
        local,
        mesh=fine,
        in_specs=(P(ROW, COL), P(ROW, COL), P(None, ROW, COL), P(None, ROW, COL)),
        out_specs=(P(ROW, COL), P(None, ROW, COL)),
        check_vma=False,
    )
```

time: 584 us -> 184 us (0.32)
  the two profiles are of different devices: /device:TPU:2 before, /device:TPU:56 now
where the time goes in v1:
time: 184 us
  blocking collectives  72.4 us (39%)
  waiting for transfers between devices  57.7 us (31%)
  starting transfers between devices  18.7 us (10%)
  between operations  14.1 us (8%)
  Pallas kernels  12.1 us (7%)
  other arithmetic  6.58 us (4%)
  local copies, waits for them, and re-layouts  2.31 us (1%)
    all_to_all x2, blocking collectives, gather_by_swap(): return lax.all_to_all(copies, axis, split_axis=0, concat_axis=0, tiled=True)  72.4 us
    all_to_all x1, waiting for transfers between devices, local(): lax.all_to_all(terms, ('yl', 'x'), split_axis=0, concat_axis=0, tiled=True)  32.9 us
    all_to_all x1, waiting for transfers between devices, local(): lax.all_to_all(dx.reshape(YH * Z, TOK, 128), COL, split_axis=0, concat_ax...  23.7 us
    all_to_all x1, starting transfers between devices, local(): lax.all_to_all(dx.reshape(YH * Z, TOK, 128), COL, split_axis=0, concat_ax...  8.56 us
    pallas_call x1, Pallas kernels, forward(): pl.pallas_call(forward_kernel, out_shape=(jax.ShapeDtypeStruct((3, TOK, 2...  7.5 us
    all_to_all x1, starting transfers between devices, local(): lax.all_to_all(terms, ('yl', 'x'), split_axis=0, concat_axis=0, tiled=True)  5.72 us
    pallas_call x1, Pallas kernels, weight_terms(): pl.pallas_call(weight_kernel, out_shape=jax.ShapeDtypeStruct((N_ROW // 2,...  4.58 us
  transfers between devices with their start and end apart: 5, of which 4 were waited for; matrix products, arithmetic and copies ran while one was open for 2% of the time, Pallas kernels for 2%

profile of v1, /device:TPU:56, one launch (start us, length us, event | category | flops | bytes accessed | tf_op | source)
XLA Modules:
  0.0 183.8 jit_solution(767594622968909489)
XLA Ops:
  7.2 0.0 all-gather.3.cloned.1.call-start
  7.2 0.7 bitcast_convert_fusion
  7.9 1.8 multiply_convert_fusion
  9.7 0.0 all-gather.3.cloned.1.call-update
  9.7 0.8 pad_maximum_fusion
  10.6 15.2 %all_to_all.20 = bf16[4,2,128,128]{3,2,1,0:T(8,128)(2,1)S(1)} all-to-all(bf16[4,2,128,128]{3,2,1,0:T(8,128)(2,1)S(1)} %broadcast_in_dim.4), channel_id=1, replica_groups=mesh['yl'=2,'x'=4,'core'=2,'yh'=4,'z'=8] {'yh'}, dimensions={0} | all-to-all | bytes 524288 | tf_op jit(solution)/shard_map/all_to_all | solution.py:26
  25.7 0.5 broadcast_in_dim.5
  26.2 57.2 %all_to_all.21.acts_ref = bf16[8,4,2,128,128]{4,3,2,1,0:T(8,128)(2,1)} all-to-all(bf16[8,4,2,128,128]{4,3,2,1,0:T(8,128)(2,1)S(1)} %broadcast_in_dim.5), channel_id=1, replica_groups=mesh['yl'=2,'x'=4,'core'=2,'yh'=4,'z'=8] {'z'}, dimensions={0} | all-to-all | bytes 4194304 | tf_op jit(solution)/shard_map/all_to_all | solution.py:26
  83.4 0.0 all-gather.3.cloned.1.call-done
  83.4 0.0 copy-start
  83.4 7.5 %forward.1 = (bf16[3,128,256]{2,1,0:T(8,128)(2,1)}, bf16[4,8,128,128]{3,2,1,0:T(8,128)(2,1)}) custom-call(bf16[8,4,2,128,128]{4,3,2,1,0:T(8,128)(2,1)} %all_to_all.21.acts_ref, bf16[16,3,256,256]{3,2,1,0:T(8,128)(2,1)} %bitcast.14), custom_call_target="tpu_custom_call" | custom-call | flops 1400000000 | bytes 10000000 | tf_op jit(solution)/shard_map/forward/pallas_call | solution.py:60
  90.9 0.0 copy-start.3
  90.9 8.6 %all-to-all-start.2 = ((bf16[32,128,128]{2,1,0:T(8,128)(2,1)}), bf16[32,128,128]{2,1,0:T(8,128)(2,1)S(1)}, u32[]{:S(2)}, u32[]{:S(2)}) async-start(bf16[32,128,128]{2,1,0:T(8,128)(2,1)} %bitcast.15), calls=%async_computation.2 | async-start | bytes 2097152 | tf_op jit(solution)/shard_map/all_to_all | solution.py:119
  99.5 0.0 copy-done
  99.5 0.1 dynamic-slice_bitcast_fusion
  99.6 1.9 %collective-permute-start = (bf16[2,2,4,2,128,128]{5,4,3,2,1,0:T(8,128)(2,1)S(1)}, bf16[2,2,4,2,128,128]{5,4,3,2,1,0:T(8,128)(2,1)S(1)}, u32[]{:S(2)}, u32[]{:S(2)}) collective-permute-start(bf16[2,2,4,2,128,128]{5,4,3,2,1,0:T(8,128)(2,1)S(1)} %dynamic-slice_bitcast_fusion), channel_id=1, source_target_pairs={{0,32},{32,0},{1,33},{33,1},{2,34},{34,2},{3,35},{35,3},{4,36},{36... | collective-permute-start | bytes 3145736 | tf_op jit(solution)/shard_map/ppermute | solution.py:115
  101.6 0.0 copy-done.3
  101.6 2.4 %collective-permute-start.1 = (bf16[3,128,256]{2,1,0:T(8,128)(2,1)S(1)}, bf16[3,128,256]{2,1,0:T(8,128)(2,1)S(1)}, u32[]{:S(2)}, u32[]{:S(2)}) collective-permute-start(bf16[3,128,256]{2,1,0:T(8,128)(2,1)S(1)} %copy-done.3), channel_id=1, source_target_pairs={{0,32},{32,0},{1,33},{33,1},{2,34},{34,2},{3,35},{35,3},{4,36},{36... | collective-permute-start | bytes 589832 | tf_op jit(solution)/shard_map/ppermute | solution.py:118
  104.0 0.2 collective-permute-done.other_acts_ref
  104.2 0.0 copy-start.2
  104.2 0.8 collective-permute-done.1.other_grads_ref
  105.0 0.0 copy-start.4
  105.0 0.1 copy-done.2
  105.2 0.5 copy-done.4
  105.7 4.6 %weight_terms.1 = bf16[8,3,256,256]{3,2,1,0:T(8,128)(2,1)} custom-call(s32[1]{0:T(128)} %bitcast.5.core_ref, bf16[8,4,2,128,128]{4,3,2,1,0:T(8,128)(2,1)} %all_to_all.21.acts_ref, bf16[2,2,4,2,128,128]{5,4,3,2,1,0:T(8,128)(2,1)} %copy-done.2, bf16[3,128,256]{2,1,0:T(8,128)(2,1)} %get-tuple-element.5.grads_ref, bf16[3,128,256]{2,1,0:T(8,128)(2,1)} %copy-done.4), custom_call_target="tpu_custom_call" | custom-call | flops 800000000 | bytes 6000000 | tf_op jit(solution)/shard_map/weight_terms/pallas_call | solution.py:93
  110.3 23.7 %all-to-all-done.2 = bf16[32,128,128]{2,1,0:T(8,128)(2,1)S(1)} async-done(((bf16[32,128,128]{2,1,0:T(8,128)(2,1)}), bf16[32,128,128]{2,1,0:T(8,128)(2,1)S(1)}, u32[]{:S(2)}, u32[]{:S(2)}) %all-to-all-start.2) | async-done | bytes 1048608 | tf_op jit(solution)/shard_map/all_to_all | solution.py:119
  134.0 0.0 copy-start.1
  134.0 1.0 copy-done.1
  135.0 5.7 %all-to-all-start.3 = ((bf16[8,3,256,256]{3,2,1,0:T(8,128)(2,1)}), bf16[8,3,256,256]{3,2,1,0:T(8,128)(2,1)S(1)}, u32[]{:S(2)}, u32[]{:S(2)}) async-start(bf16[8,3,256,256]{3,2,1,0:T(8,128)(2,1)} %weight_terms.1), calls=%async_computation.3 | async-start | bytes 6291456 | tf_op jit(solution)/shard_map/all_to_all | solution.py:123
  140.7 2.0 %reduce_sum.21 = bf16[128,128]{1,0:T(8,128)(2,1)} reduce(bf16[32,128,128]{2,1,0:T(8,128)(2,1)} %copy-done.1, bf16[]{:T(256)} %constant.12.clone.1), dimensions={0}, to_apply=%region_0.1 | reduce | flops 507904 | bytes 1081346 | tf_op jit(solution)/shard_map/reduce_sum | solution.py:120
  142.7 32.9 %all-to-all-done.3 = bf16[8,3,256,256]{3,2,1,0:T(8,128)(2,1)S(1)} async-done(((bf16[8,3,256,256]{3,2,1,0:T(8,128)(2,1)}), bf16[8,3,256,256]{3,2,1,0:T(8,128)(2,1)S(1)}, u32[]{:S(2)}, u32[]{:S(2)}) %all-to-all-start.3) | async-done | bytes 3145760 | tf_op jit(solution)/shard_map/all_to_all | solution.py:123
  175.6 1.3 convert_reduce_fusion
  (1 shorter events, 0.0 us)
Async XLA Ops:
  7.2 76.3 %all-gather.3.cloned.1.call-start = ((), (), s32[]{:S(2)}) async-start(), calls=%async_computation.4 | async-start | bytes 6684672 | tf_op jit(solution)/shard_map/all_gather | solution.py:108
  83.4 16.1 %copy-start = (bf16[8,4,2,128,128]{4,3,2,1,0:T(8,128)(2,1)S(1)}, bf16[8,4,2,128,128]{4,3,2,1,0:T(8,128)(2,1)}, u32[]{:S(2)}) copy-start(bf16[8,4,2,128,128]{4,3,2,1,0:T(8,128)(2,1)} %all_to_all.21.acts_ref) | copy-start | bytes 6291460
  90.9 10.6 %copy-start.3 = (bf16[3,128,256]{2,1,0:T(8,128)(2,1)S(1)}, bf16[3,128,256]{2,1,0:T(8,128)(2,1)}, u32[]{:S(2)}) copy-start(bf16[3,128,256]{2,1,0:T(8,128)(2,1)} %get-tuple-element.5.grads_ref) | copy-start | bytes 589828
  90.9 43.0 %all-to-all-start.2 = ((bf16[32,128,128]{2,1,0:T(8,128)(2,1)}), bf16[32,128,128]{2,1,0:T(8,128)(2,1)S(1)}, u32[]{:S(2)}, u32[]{:S(2)}) async-start(bf16[32,128,128]{2,1,0:T(8,128)(2,1)} %bitcast.15), calls=%async_computation.2 | async-start | bytes 2097152 | tf_op jit(solution)/shard_map/all_to_all | solution.py:119
  99.6 4.6 %collective-permute-start = (bf16[2,2,4,2,128,128]{5,4,3,2,1,0:T(8,128)(2,1)S(1)}, bf16[2,2,4,2,128,128]{5,4,3,2,1,0:T(8,128)(2,1)S(1)}, u32[]{:S(2)}, u32[]{:S(2)}) collective-permute-start(bf16[2,2,4,2,128,128]{5,4,3,2,1,0:T(8,128)(2,1)S(1)} %dynamic-slice_bitcast_fusion), channel_id=1, source_target_pairs={{0,32},{32,0},{1,33},{33,1},{2,34},{34,2},{3,35},{35,3},{4,36},{36... | collective-permute-start | bytes 3145736 | tf_op jit(solution)/shard_map/ppermute | solution.py:115
  101.6 3.5 %collective-permute-start.1 = (bf16[3,128,256]{2,1,0:T(8,128)(2,1)S(1)}, bf16[3,128,256]{2,1,0:T(8,128)(2,1)S(1)}, u32[]{:S(2)}, u32[]{:S(2)}) collective-permute-start(bf16[3,128,256]{2,1,0:T(8,128)(2,1)S(1)} %copy-done.3), channel_id=1, source_target_pairs={{0,32},{32,0},{1,33},{33,1},{2,34},{34,2},{3,35},{35,3},{4,36},{36... | collective-permute-start | bytes 589832 | tf_op jit(solution)/shard_map/ppermute | solution.py:118
  104.2 1.0 copy-start.2
  105.0 0.7 copy-start.4
  134.0 1.0 copy-start.1
  135.0 40.7 %all-to-all-start.3 = ((bf16[8,3,256,256]{3,2,1,0:T(8,128)(2,1)}), bf16[8,3,256,256]{3,2,1,0:T(8,128)(2,1)S(1)}, u32[]{:S(2)}, u32[]{:S(2)}) async-start(bf16[8,3,256,256]{3,2,1,0:T(8,128)(2,1)} %weight_terms.1), calls=%async_computation.3 | async-start | bytes 6291456 | tf_op jit(solution)/shard_map/all_to_all | solution.py:123
Sparse Core Ops, SparseCore 0:
  10.7 51.5 all-gather.2

commit v2 on v1

v2 whole, which is shorter than its diff:
```python
import functools

import jax
import jax.numpy as jnp
from jax import lax
from jax.experimental import pallas as pl
from jax.experimental.pallas import tpu as pltpu
from jax.sharding import Mesh, PartitionSpec as P

F32 = jnp.float32
BF16 = jnp.bfloat16
ROW = ("yl", "x", "core")
COL = ("yh", "z")
YL, X, CORE, YH, Z = 2, 4, 2, 4, 8
N_ROW = YL * X * CORE
TOK = 128
VMEM_LIMIT = 56 * 1024 * 1024


def dot(a, b, dims):
    return lax.dot_general(a, b, (dims, ((), ())), preferred_element_type=F32)


def gather_by_swap(block, axis, size):
    copies = jnp.broadcast_to(block[None], (size,) + block.shape)
    return lax.all_to_all(copies, axis, split_axis=0, concat_axis=0, tiled=True)


def fan_out(block, axis, size):
    shifts = [[(i, (i + d) % size) for i in range(size)] for d in range(1, size)]
    return [block] + [lax.ppermute(block, axis, shift) for shift in shifts]


def forward_kernel(place_ref, x_ref, dy_ref, w_ref, grads_ref, dx_ref):
    gate = jnp.zeros((TOK, 256), F32)
    up = jnp.zeros((TOK, 256), F32)
    hidden_grad = jnp.zeros((TOK, 256), F32)
    ys = [lax.rem(place_ref[1] + YH - d, YH) for d in range(YH)]
    for d in range(YH):
        for j in range(Z // 2):
            r = ys[d] * 4 + j
            tokens = jnp.concatenate([x_ref[2 * j, d], x_ref[2 * j + 1, d]], axis=1)
            gate += dot(tokens, w_ref[r, 0], ((1,), (0,)))
            up += dot(tokens, w_ref[r, 1], ((1,), (0,)))
            cots = jnp.concatenate([dy_ref[d, 2 * j], dy_ref[d, 2 * j + 1]], axis=1)
            hidden_grad += dot(cots, w_ref[r, 2], ((1,), (0,)))
    sig = 1.0 / (1.0 + jnp.exp(-gate))
    act = gate * sig
    gate_grad = (hidden_grad * up * sig * (1.0 + gate * (1.0 - sig))).astype(BF16)
    up_grad = (hidden_grad * act).astype(BF16)
    grads_ref[0] = gate_grad
    grads_ref[1] = up_grad
    grads_ref[2] = (act * up).astype(BF16)
    for r in range(N_ROW):
        dx = dot(gate_grad, w_ref[r, 0], ((1,), (1,))) + dot(up_grad, w_ref[r, 1], ((1,), (1,)))
        dx = dx.astype(BF16)
        y, z = r // 4, (r % 4) * 2
        dx_ref[z, y] = dx[:, :128]
        dx_ref[z + 1, y] = dx[:, 128:]


def forward(place, x, dy, weights):
    whole = pl.BlockSpec(memory_space=pltpu.VMEM)
    return pl.pallas_call(
        forward_kernel,
        out_shape=(
            jax.ShapeDtypeStruct((3, TOK, 256), BF16),
            jax.ShapeDtypeStruct((Z, YH, TOK, 128), BF16),
        ),
        in_specs=[pl.BlockSpec(memory_space=pltpu.SMEM)] + [whole] * 3,
        out_specs=(whole, whole),
        compiler_params=pltpu.CompilerParams(vmem_limit_bytes=VMEM_LIMIT),
        cost_estimate=pl.CostEstimate(flops=1400000000, bytes_accessed=10000000, transcendentals=32768),
        name="forward",
    )(place, x, dy, weights)


def weight_kernel(place_ref, x_ref, dy_ref, other_x_ref, other_dy_ref, grads_ref, other_grads_ref, out_ref):
    k = place_ref[0]
    grads = [jnp.concatenate([grads_ref[p], other_grads_ref[p]], axis=0) for p in range(3)]
    for d in range(YH):
        y = lax.rem(place_ref[1] + YH - d, YH)
        for j in range(2):
            z = 4 * j + 2 * k
            x = jnp.concatenate([x_ref[z, d], x_ref[z + 1, d]], axis=1)
            other_x = jnp.concatenate([other_x_ref[j, 0, d], other_x_ref[j, 1, d]], axis=1)
            x = jnp.concatenate([x, other_x], axis=0)
            dy = jnp.concatenate([dy_ref[d, z], dy_ref[d, z + 1]], axis=1)
            other_dy = jnp.concatenate([other_dy_ref[d, j, 0], other_dy_ref[d, j, 1]], axis=1)
            dy = jnp.concatenate([dy, other_dy], axis=0)
            for p in range(3):
                term = dot(dy if p == 2 else x, grads[p], ((0,), (0,)))
                out_ref[2 * y + j, p] = term.astype(BF16)


def weight_terms(place, *arrays):
    whole = pl.BlockSpec(memory_space=pltpu.VMEM)
    return pl.pallas_call(
        weight_kernel,
        out_shape=jax.ShapeDtypeStruct((N_ROW // 2, 3, 256, 256), BF16),
        in_specs=[pl.BlockSpec(memory_space=pltpu.SMEM)] + [whole] * 6,
        out_specs=whole,
        compiler_params=pltpu.CompilerParams(vmem_limit_bytes=VMEM_LIMIT),
        cost_estimate=pl.CostEstimate(flops=800000000, bytes_accessed=6000000, transcendentals=0),
        name="weight_terms",
    )(place, *arrays)


def local(inputs, out_grad, codes, scales):
    core = lax.axis_index("core")
    yh = lax.axis_index("yh")
    place = jnp.stack([core, yh])
    swap = [(0, 1), (1, 0)]
    weights = (codes.astype(F32) * scales.astype(F32)).astype(BF16)
    weights = lax.all_gather(weights, ROW, axis=0, tiled=False)

    x = jnp.stack(fan_out(inputs, "yh", YH))
    dy = gather_by_swap(out_grad, "z", Z)
    x = gather_by_swap(x, "z", Z)
    dy = jnp.stack(fan_out(dy, "yh", YH))

    other_x = x.reshape(2, 2, 2, YH, TOK, 128)
    other_x = lax.dynamic_index_in_dim(other_x, 1 - core, axis=1, keepdims=False)
    other_x = lax.ppermute(other_x, "core", swap)
    other_dy = dy.reshape(YH, 2, 2, 2, TOK, 128)
    other_dy = lax.dynamic_index_in_dim(other_dy, 1 - core, axis=2, keepdims=False)
    other_dy = lax.ppermute(other_dy, "core", swap)

    grads, dx = forward(place, x, dy, weights)
    dx = lax.psum_scatter(dx, "z", scatter_dimension=0, tiled=False)
    other_grads = lax.ppermute(grads, "core", swap)
    terms = weight_terms(place, x, dy, other_x, other_dy, grads, other_grads)
    terms = lax.all_to_all(terms, ("yl", "x"), split_axis=0, concat_axis=0, tiled=True)

    input_grad = lax.dynamic_index_in_dim(dx, yh, axis=0, keepdims=False).astype(F32)
    for d in range(1, YH):
        part = lax.dynamic_index_in_dim(dx, lax.rem(yh + d, YH), axis=0, keepdims=False)
        part = lax.ppermute(part, "yh", [(i, (i + d) % YH) for i in range(YH)])
        input_grad += part.astype(F32)

    weight_grad = jnp.sum(terms.astype(F32), axis=0)
    return input_grad.astype(BF16), weight_grad


def solution(mesh):
    fine = Mesh(mesh.devices.reshape(YL, X, CORE, YH, Z), ROW + COL)
    return jax.shard_map(
        local,
        mesh=fine,
        in_specs=(P(ROW, COL), P(ROW, COL), P(None, ROW, COL), P(None, ROW, COL)),
        out_specs=(P(ROW, COL), P(None, ROW, COL)),
        check_vma=False,
    )
```

time: 184 us -> 191 us (1.038)
  the two profiles are of different devices: /device:TPU:56 before, /device:TPU:48 now
where the time goes in v2:
time: 191 us; the launch traced here: 190 us
  waiting for transfers between devices  89.4 us (47%)
  starting transfers between devices  60.4 us (32%)
  between operations  14.2 us (7%)
  Pallas kernels  11.9 us (6%)
  other arithmetic  9.83 us (5%)
  local copies, waits for them, and re-layouts  4.25 us (2%)
    reduce_scatter x1, waiting for transfers between devices, local(): dx = lax.psum_scatter(dx, 'z', scatter_dimension=0, tiled=False)  46.6 us
    ppermute x6, waiting for transfers between devices, fan_out(): return [block] + [lax.ppermute(block, axis, shift) for shift in shifts]  34.1 us
    ppermute x6, starting transfers between devices, fan_out(): return [block] + [lax.ppermute(block, axis, shift) for shift in shifts]  20.5 us
    all_to_all x2, starting transfers between devices, gather_by_swap(): return lax.all_to_all(copies, axis, split_axis=0, concat_axis=0, tiled=True)  17.5 us
    ppermute x3, starting transfers between devices, local(): part = lax.ppermute(part, 'yh', [(i, (i + d) % YH) for i in range(YH)])  11.6 us
    pallas_call x1, Pallas kernels, forward(): pl.pallas_call(forward_kernel, out_shape=(jax.ShapeDtypeStruct((3, TOK, 2...  7.31 us
    ppermute x3, waiting for transfers between devices, local(): part = lax.ppermute(part, 'yh', [(i, (i + d) % YH) for i in range(YH)])  6.33 us
    pallas_call x1, Pallas kernels, weight_terms(): pl.pallas_call(weight_kernel, out_shape=jax.ShapeDtypeStruct((N_ROW // 2,...  4.61 us
  transfers between devices with their start and end apart: 17, of which 8 were waited for; matrix products, arithmetic and copies ran while one was open for 4% of the time, Pallas kernels for 4%

profile of v2, /device:TPU:48, one launch (start us, length us, event | category | flops | bytes accessed | tf_op | source)
XLA Modules:
  0.0 190.0 jit_solution(18379721014008339272)
XLA Ops:
  7.2 0.0 all-gather.3.cloned.1.call-start
  7.2 0.7 bitcast_convert_fusion
  7.9 1.8 multiply_convert_fusion
  9.7 0.0 all-gather.3.cloned.1.call-update
  9.7 1.5 broadcast_in_dim.5
  11.2 10.3 %all-to-all-start.1 = ((bf16[8,128,128]{2,1,0:T(8,128)(2,1)}), bf16[8,128,128]{2,1,0:T(8,128)(2,1)S(1)}, u32[]{:S(2)}, u32[]{:S(2)}) async-start(bf16[8,128,128]{2,1,0:T(8,128)(2,1)} %broadcast_in_dim.5), calls=%async_computation.1 | async-start | bytes 524288 | tf_op jit(solution)/shard_map/all_to_all | solution.py:26
  21.6 1.9 %collective-permute-start = (bf16[128,128]{1,0:T(8,128)(2,1)}, bf16[128,128]{1,0:T(8,128)(2,1)S(1)}, u32[]{:S(2)}, u32[]{:S(2)}) collective-permute-start(bf16[128,128]{1,0:T(8,128)(2,1)} %param.4), channel_id=1, source_target_pairs={{0,8},{8,16},{16,24},{24,0},{1,9},{9,17},{17,25},{25,1},{2,10},{10... | collective-permute-start | bytes 98312 | tf_op jit(solution)/shard_map/ppermute | solution.py:31
  23.5 7.6 %collective-permute-start.1 = (bf16[128,128]{1,0:T(8,128)(2,1)}, bf16[128,128]{1,0:T(8,128)(2,1)S(1)}, u32[]{:S(2)}, u32[]{:S(2)}) collective-permute-start(bf16[128,128]{1,0:T(8,128)(2,1)} %param.4), channel_id=1, source_target_pairs={{0,16},{8,24},{16,0},{24,8},{1,17},{9,25},{17,1},{25,9},{2,18},{10... | collective-permute-start | bytes 98312 | tf_op jit(solution)/shard_map/ppermute | solution.py:31
  31.1 1.9 %collective-permute-start.2 = (bf16[128,128]{1,0:T(8,128)(2,1)}, bf16[128,128]{1,0:T(8,128)(2,1)S(1)}, u32[]{:S(2)}, u32[]{:S(2)}) collective-permute-start(bf16[128,128]{1,0:T(8,128)(2,1)} %param.4), channel_id=1, source_target_pairs={{0,24},{8,0},{16,8},{24,16},{1,25},{9,1},{17,9},{25,17},{2,26},{10... | collective-permute-start | bytes 98312 | tf_op jit(solution)/shard_map/ppermute | solution.py:31
  33.0 0.0 collective-permute-done
  33.0 0.8 collective-permute-done.1
  33.8 5.6 %collective-permute-done.2 = bf16[128,128]{1,0:T(8,128)(2,1)S(1)} collective-permute-done((bf16[128,128]{1,0:T(8,128)(2,1)}, bf16[128,128]{1,0:T(8,128)(2,1)S(1)}, u32[]{:S(2)}, u32[]{:S(2)}) %collective-permute-start.2) | collective-permute-done | bytes 32800 | tf_op jit(solution)/shard_map/ppermute | solution.py:31
  39.4 0.8 pad_maximum_fusion.1
  40.1 0.0 all-to-all-done.1
  40.2 1.2 broadcast_in_dim.4
  41.4 7.2 %all-to-all-start = ((bf16[8,4,128,128]{3,2,1,0:T(8,128)(2,1)}), bf16[8,4,128,128]{3,2,1,0:T(8,128)(2,1)S(1)}, u32[]{:S(2)}, u32[]{:S(2)}) async-start(bf16[8,4,128,128]{3,2,1,0:T(8,128)(2,1)} %broadcast_in_dim.4), calls=%async_computation | async-start | bytes 2097152 | tf_op jit(solution)/shard_map/all_to_all | solution.py:26
  48.6 1.9 %collective-permute-start.3 = (bf16[8,128,128]{2,1,0:T(8,128)(2,1)S(1)}, bf16[8,128,128]{2,1,0:T(8,128)(2,1)S(1)}, u32[]{:S(2)}, u32[]{:S(2)}) collective-permute-start(bf16[8,128,128]{2,1,0:T(8,128)(2,1)S(1)} %all-to-all-done.1), channel_id=1, source_target_pairs={{0,8},{8,16},{16,24},{24,0},{1,9},{9,17},{17,25},{25,1},{2,10},{10... | collective-permute-start | bytes 786440 | tf_op jit(solution)/shard_map/ppermute | solution.py:31
  50.5 4.3 %collective-permute-start.4 = (bf16[8,128,128]{2,1,0:T(8,128)(2,1)S(1)}, bf16[8,128,128]{2,1,0:T(8,128)(2,1)S(1)}, u32[]{:S(2)}, u32[]{:S(2)}) collective-permute-start(bf16[8,128,128]{2,1,0:T(8,128)(2,1)S(1)} %all-to-all-done.1), channel_id=1, source_target_pairs={{0,16},{8,24},{16,0},{24,8},{1,17},{9,25},{17,1},{25,9},{2,18},{10... | collective-permute-start | bytes 786440 | tf_op jit(solution)/shard_map/ppermute | solution.py:31
  54.8 2.9 %collective-permute-start.5 = (bf16[8,128,128]{2,1,0:T(8,128)(2,1)S(1)}, bf16[8,128,128]{2,1,0:T(8,128)(2,1)S(1)}, u32[]{:S(2)}, u32[]{:S(2)}) collective-permute-start(bf16[8,128,128]{2,1,0:T(8,128)(2,1)S(1)} %all-to-all-done.1), channel_id=1, source_target_pairs={{0,24},{8,0},{16,8},{24,16},{1,25},{9,1},{17,9},{25,17},{2,26},{10... | collective-permute-start | bytes 786440 | tf_op jit(solution)/shard_map/ppermute | solution.py:31
  57.7 11.3 %collective-permute-done.3 = bf16[8,128,128]{2,1,0:T(8,128)(2,1)S(1)} collective-permute-done((bf16[8,128,128]{2,1,0:T(8,128)(2,1)S(1)}, bf16[8,128,128]{2,1,0:T(8,128)(2,1)S(1)}, u32[]{:S(2)}, u32[]{:S(2)}) %collective-permute-start.3) | collective-permute-done | bytes 262176 | tf_op jit(solution)/shard_map/ppermute | solution.py:31
  68.9 16.5 %collective-permute-done.4 = bf16[8,128,128]{2,1,0:T(8,128)(2,1)S(1)} collective-permute-done((bf16[8,128,128]{2,1,0:T(8,128)(2,1)S(1)}, bf16[8,128,128]{2,1,0:T(8,128)(2,1)S(1)}, u32[]{:S(2)}, u32[]{:S(2)}) %collective-permute-start.4) | collective-permute-done | bytes 262176 | tf_op jit(solution)/shard_map/ppermute | solution.py:31
  85.5 0.0 collective-permute-done.5
  85.5 0.1 fusion.3
  85.5 1.9 %collective-permute-start.10 = (bf16[4,2,2,128,128]{4,3,2,1,0:T(8,128)(2,1)S(1)}, bf16[4,2,2,128,128]{4,3,2,1,0:T(8,128)(2,1)}, u32[]{:S(2)}, u32[]{:S(2)}) collective-permute-start(bf16[4,2,2,128,128]{4,3,2,1,0:T(8,128)(2,1)S(1)} %fusion.3), channel_id=1, source_target_pairs={{0,32},{32,0},{1,33},{33,1},{2,34},{34,2},{3,35},{35,3},{4,36},{36... | collective-permute-start | bytes 1572872 | tf_op jit(solution)/shard_map/ppermute | solution.py:127
  87.5 0.0 all-to-all-done.x_ref
  87.5 0.0 copy-start
  87.5 2.4 %collective-permute-start.9 = (bf16[2,2,4,128,128]{4,3,2,1,0:T(8,128)(2,1)S(1)}, bf16[2,2,4,128,128]{4,3,2,1,0:T(8,128)(2,1)}, u32[]{:S(2)}, u32[]{:S(2)}) collective-permute-start(bf16[2,2,4,128,128]{4,3,2,1,0:T(8,128)(2,1)S(1)} %dynamic-slice_bitcast_fusion), channel_id=1, source_target_pairs={{0,32},{32,0},{1,33},{33,1},{2,34},{34,2},{3,35},{35,3},{4,36},{36... | collective-permute-start | bytes 1572872 | tf_op jit(solution)/shard_map/ppermute | solution.py:124
  90.0 0.6 pad_add_fusion.place_ref
  90.6 1.2 pad_maximum_fusion.dy_ref
  91.8 0.0 all-gather.3.cloned.1.call-done
  91.8 0.0 copy-done
  91.8 7.3 %forward.1 = (bf16[3,128,256]{2,1,0:T(8,128)(2,1)}, bf16[8,4,128,128]{3,2,1,0:T(8,128)(2,1)}) custom-call(s32[2]{0:T(128)} %pad_add_fusion.place_ref, bf16[8,4,128,128]{3,2,1,0:T(8,128)(2,1)} %copy-done, bf16[4,8,128,128]{3,2,1,0:T(8,128)(2,1)} %pad_maximum_fusion.dy_ref, bf16[16,3,256,256]{3,2,1,0:T(8,128)(2,1)} %bitcast.37), custom_call_target="tpu_custom_call" | custom-call | flops 1400000000 | bytes 10000000 | tf_op jit(solution)/shard_map/forward/pallas_call | solution.py:64
  99.1 1.9 %collective-permute-start.11 = (bf16[3,128,256]{2,1,0:T(8,128)(2,1)}, bf16[3,128,256]{2,1,0:T(8,128)(2,1)S(1)}, u32[]{:S(2)}, u32[]{:S(2)}) collective-permute-start(bf16[3,128,256]{2,1,0:T(8,128)(2,1)} %get-tuple-element.5.grads_ref), channel_id=1, source_target_pairs={{0,32},{32,0},{1,33},{33,1},{2,34},{34,2},{3,35},{35,3},{4,36},{36... | collective-permute-start | bytes 589832 | tf_op jit(solution)/shard_map/ppermute | solution.py:131
  101.0 0.0 collective-permute-done.10.other_dy_ref
  101.0 0.0 collective-permute-done.9.other_x_ref
  101.0 1.6 collective-permute-done.11.other_grads_ref
  102.6 0.0 copy-start.1
  102.6 0.7 copy-done.1
  103.3 4.6 %weight_terms.1 = bf16[8,3,256,256]{3,2,1,0:T(8,128)(2,1)} custom-call(s32[2]{0:T(128)} %pad_add_fusion.place_ref, bf16[8,4,128,128]{3,2,1,0:T(8,128)(2,1)} %copy-done, bf16[4,8,128,128]{3,2,1,0:T(8,128)(2,1)} %pad_maximum_fusion.dy_ref, bf16[2,2,4,128,128]{4,3,2,1,0:T(8,128)(2,1)} %collective-permute-done.9.other_x_ref, ...), custom_call_target="tpu_custom_call" | custom-call | flops 800000000 | bytes 6000000 | tf_op jit(solution)/shard_map/weight_terms/pallas_call | solution.py:98
  107.9 4.5 %all-to-all-start.2 = ((bf16[8,3,256,256]{3,2,1,0:T(8,128)(2,1)}), bf16[8,3,256,256]{3,2,1,0:T(8,128)(2,1)}, u32[]{:S(2)}, u32[]{:S(2)}) async-start(bf16[8,3,256,256]{3,2,1,0:T(8,128)(2,1)} %weight_terms.1), calls=%async_computation.3 | async-start | bytes 6291456 | tf_op jit(solution)/shard_map/all_to_all | solution.py:133
  112.4 0.0 reduce-scatter.2.cloned.1.call-start
  112.4 0.7 reduce-scatter.2.cloned.1.call-update
  113.2 46.6 %reduce-scatter.2.cloned.1.call-done = bf16[1,4,128,128]{3,2,1,0:T(8,128)(2,1)} async-done(((bf16[8,4,128,128]{3,2,1,0:T(8,128)(2,1)}), bf16[1,4,128,128]{3,2,1,0:T(8,128)(2,1)}) %reduce-scatter.2.cloned.1.call-update) | async-done | bytes 131088 | tf_op jit(solution)/shard_map/reduce_scatter | solution.py:130
  159.7 0.8 dynamic-slice_bitcast_fusion.3
  160.5 2.3 %collective-permute-start.6 = (bf16[128,128]{1,0:T(8,128)(2,1)S(1)}, bf16[128,128]{1,0:T(8,128)(2,1)S(1)}, u32[]{:S(2)}, u32[]{:S(2)}) collective-permute-start(bf16[128,128]{1,0:T(8,128)(2,1)S(1)} %get-tuple-element.6), channel_id=1, source_target_pairs={{0,8},{8,16},{16,24},{24,0},{1,9},{9,17},{17,25},{25,1},{2,10},{10... | collective-permute-start | bytes 98312 | tf_op jit(solution)/shard_map/ppermute | solution.py:138
  162.9 7.4 %collective-permute-start.7 = (bf16[128,128]{1,0:T(8,128)(2,1)S(1)}, bf16[128,128]{1,0:T(8,128)(2,1)S(1)}, u32[]{:S(2)}, u32[]{:S(2)}) collective-permute-start(bf16[128,128]{1,0:T(8,128)(2,1)S(1)} %get-tuple-element.8), channel_id=1, source_target_pairs={{0,16},{8,24},{16,0},{24,8},{1,17},{9,25},{17,1},{25,9},{2,18},{10... | collective-permute-start | bytes 98312 | tf_op jit(solution)/shard_map/ppermute | solution.py:138
  170.2 1.9 %collective-permute-start.8 = (bf16[128,128]{1,0:T(8,128)(2,1)S(1)}, bf16[128,128]{1,0:T(8,128)(2,1)S(1)}, u32[]{:S(2)}, u32[]{:S(2)}) collective-permute-start(bf16[128,128]{1,0:T(8,128)(2,1)S(1)} %get-tuple-element.7), channel_id=1, source_target_pairs={{0,24},{8,0},{16,8},{24,16},{1,25},{9,1},{17,9},{25,17},{2,26},{10... | collective-permute-start | bytes 98312 | tf_op jit(solution)/shard_map/ppermute | solution.py:138
  172.2 0.0 collective-permute-done.6
  172.2 0.4 collective-permute-done.7
  172.6 5.9 %collective-permute-done.8 = bf16[128,128]{1,0:T(8,128)(2,1)S(1)} collective-permute-done((bf16[128,128]{1,0:T(8,128)(2,1)S(1)}, bf16[128,128]{1,0:T(8,128)(2,1)S(1)}, u32[]{:S(2)}, u32[]{:S(2)}) %collective-permute-start.8) | collective-permute-done | bytes 32800 | tf_op jit(solution)/shard_map/ppermute | solution.py:138
  178.5 1.4 fusion.6
  179.9 0.0 all-to-all-done.2
  179.9 3.3 %convert_reduce_fusion = f32[3,256,256]{2,1,0:T(8,128)} fusion(bf16[8,3,256,256]{3,2,1,0:T(8,128)(2,1)} %all-to-all-done.2), kind=kLoop, calls=%fused_computation | loop fusion | flops 2949120 | bytes 3932160 | tf_op jit(solution)/shard_map/reduce_sum | solution.py:141
  (1 shorter events, 0.0 us)
Async XLA Ops:
  7.2 84.6 %all-gather.3.cloned.1.call-start = ((), (), s32[]{:S(2)}) async-start(), calls=%async_computation.5 | async-start | bytes 6684672 | tf_op jit(solution)/shard_map/all_gather | solution.py:115
  11.2 28.9 %all-to-all-start.1 = ((bf16[8,128,128]{2,1,0:T(8,128)(2,1)}), bf16[8,128,128]{2,1,0:T(8,128)(2,1)S(1)}, u32[]{:S(2)}, u32[]{:S(2)}) async-start(bf16[8,128,128]{2,1,0:T(8,128)(2,1)} %broadcast_in_dim.5), calls=%async_computation.1 | async-start | bytes 524288 | tf_op jit(solution)/shard_map/all_to_all | solution.py:26
  21.6 11.5 %collective-permute-start = (bf16[128,128]{1,0:T(8,128)(2,1)}, bf16[128,128]{1,0:T(8,128)(2,1)S(1)}, u32[]{:S(2)}, u32[]{:S(2)}) collective-permute-start(bf16[128,128]{1,0:T(8,128)(2,1)} %param.4), channel_id=1, source_target_pairs={{0,8},{8,16},{16,24},{24,0},{1,9},{9,17},{17,25},{25,1},{2,10},{10... | collective-permute-start | bytes 98312 | tf_op jit(solution)/shard_map/ppermute | solution.py:31
  23.5 10.3 %collective-permute-start.1 = (bf16[128,128]{1,0:T(8,128)(2,1)}, bf16[128,128]{1,0:T(8,128)(2,1)S(1)}, u32[]{:S(2)}, u32[]{:S(2)}) collective-permute-start(bf16[128,128]{1,0:T(8,128)(2,1)} %param.4), channel_id=1, source_target_pairs={{0,16},{8,24},{16,0},{24,8},{1,17},{9,25},{17,1},{25,9},{2,18},{10... | collective-permute-start | bytes 98312 | tf_op jit(solution)/shard_map/ppermute | solution.py:31
  31.1 8.3 %collective-permute-start.2 = (bf16[128,128]{1,0:T(8,128)(2,1)}, bf16[128,128]{1,0:T(8,128)(2,1)S(1)}, u32[]{:S(2)}, u32[]{:S(2)}) collective-permute-start(bf16[128,128]{1,0:T(8,128)(2,1)} %param.4), channel_id=1, source_target_pairs={{0,24},{8,0},{16,8},{24,16},{1,25},{9,1},{17,9},{25,17},{2,26},{10... | collective-permute-start | bytes 98312 | tf_op jit(solution)/shard_map/ppermute | solution.py:31
  41.4 46.1 %all-to-all-start = ((bf16[8,4,128,128]{3,2,1,0:T(8,128)(2,1)}), bf16[8,4,128,128]{3,2,1,0:T(8,128)(2,1)S(1)}, u32[]{:S(2)}, u32[]{:S(2)}) async-start(bf16[8,4,128,128]{3,2,1,0:T(8,128)(2,1)} %broadcast_in_dim.4), calls=%async_computation | async-start | bytes 2097152 | tf_op jit(solution)/shard_map/all_to_all | solution.py:26
  48.6 20.4 %collective-permute-start.3 = (bf16[8,128,128]{2,1,0:T(8,128)(2,1)S(1)}, bf16[8,128,128]{2,1,0:T(8,128)(2,1)S(1)}, u32[]{:S(2)}, u32[]{:S(2)}) collective-permute-start(bf16[8,128,128]{2,1,0:T(8,128)(2,1)S(1)} %all-to-all-done.1), channel_id=1, source_target_pairs={{0,8},{8,16},{16,24},{24,0},{1,9},{9,17},{17,25},{25,1},{2,10},{10... | collective-permute-start | bytes 786440 | tf_op jit(solution)/shard_map/ppermute | solution.py:31
  50.5 35.0 %collective-permute-start.4 = (bf16[8,128,128]{2,1,0:T(8,128)(2,1)S(1)}, bf16[8,128,128]{2,1,0:T(8,128)(2,1)S(1)}, u32[]{:S(2)}, u32[]{:S(2)}) collective-permute-start(bf16[8,128,128]{2,1,0:T(8,128)(2,1)S(1)} %all-to-all-done.1), channel_id=1, source_target_pairs={{0,16},{8,24},{16,0},{24,8},{1,17},{9,25},{17,1},{25,9},{2,18},{10... | collective-permute-start | bytes 786440 | tf_op jit(solution)/shard_map/ppermute | solution.py:31
  54.8 30.7 %collective-permute-start.5 = (bf16[8,128,128]{2,1,0:T(8,128)(2,1)S(1)}, bf16[8,128,128]{2,1,0:T(8,128)(2,1)S(1)}, u32[]{:S(2)}, u32[]{:S(2)}) collective-permute-start(bf16[8,128,128]{2,1,0:T(8,128)(2,1)S(1)} %all-to-all-done.1), channel_id=1, source_target_pairs={{0,24},{8,0},{16,8},{24,16},{1,25},{9,1},{17,9},{25,17},{2,26},{10... | collective-permute-start | bytes 786440 | tf_op jit(solution)/shard_map/ppermute | solution.py:31
  85.5 15.5 %collective-permute-start.10 = (bf16[4,2,2,128,128]{4,3,2,1,0:T(8,128)(2,1)S(1)}, bf16[4,2,2,128,128]{4,3,2,1,0:T(8,128)(2,1)}, u32[]{:S(2)}, u32[]{:S(2)}) collective-permute-start(bf16[4,2,2,128,128]{4,3,2,1,0:T(8,128)(2,1)S(1)} %fusion.3), channel_id=1, source_target_pairs={{0,32},{32,0},{1,33},{33,1},{2,34},{34,2},{3,35},{35,3},{4,36},{36... | collective-permute-start | bytes 1572872 | tf_op jit(solution)/shard_map/ppermute | solution.py:127
  87.5 4.3 %copy-start = (bf16[8,4,128,128]{3,2,1,0:T(8,128)(2,1)}, bf16[8,4,128,128]{3,2,1,0:T(8,128)(2,1)S(1)}, u32[]{:S(2)}) copy-start(bf16[8,4,128,128]{3,2,1,0:T(8,128)(2,1)S(1)} %all-to-all-done.x_ref) | copy-start | bytes 3145732
  87.5 13.5 %collective-permute-start.9 = (bf16[2,2,4,128,128]{4,3,2,1,0:T(8,128)(2,1)S(1)}, bf16[2,2,4,128,128]{4,3,2,1,0:T(8,128)(2,1)}, u32[]{:S(2)}, u32[]{:S(2)}) collective-permute-start(bf16[2,2,4,128,128]{4,3,2,1,0:T(8,128)(2,1)S(1)} %dynamic-slice_bitcast_fusion), channel_id=1, source_target_pairs={{0,32},{32,0},{1,33},{33,1},{2,34},{34,2},{3,35},{35,3},{4,36},{36... | collective-permute-start | bytes 1572872 | tf_op jit(solution)/shard_map/ppermute | solution.py:124
  99.1 3.5 %collective-permute-start.11 = (bf16[3,128,256]{2,1,0:T(8,128)(2,1)}, bf16[3,128,256]{2,1,0:T(8,128)(2,1)S(1)}, u32[]{:S(2)}, u32[]{:S(2)}) collective-permute-start(bf16[3,128,256]{2,1,0:T(8,128)(2,1)} %get-tuple-element.5.grads_ref), channel_id=1, source_target_pairs={{0,32},{32,0},{1,33},{33,1},{2,34},{34,2},{3,35},{35,3},{4,36},{36... | collective-permute-start | bytes 589832 | tf_op jit(solution)/shard_map/ppermute | solution.py:131
  102.6 0.7 copy-start.1
  107.9 72.0 %all-to-all-start.2 = ((bf16[8,3,256,256]{3,2,1,0:T(8,128)(2,1)}), bf16[8,3,256,256]{3,2,1,0:T(8,128)(2,1)}, u32[]{:S(2)}, u32[]{:S(2)}) async-start(bf16[8,3,256,256]{3,2,1,0:T(8,128)(2,1)} %weight_terms.1), calls=%async_computation.3 | async-start | bytes 6291456 | tf_op jit(solution)/shard_map/all_to_all | solution.py:133
  112.4 47.4 %reduce-scatter.2.cloned.1.call-start = ((), (), s32[]{:S(2)}) async-start(), calls=%async_computation.4 | async-start | bytes 1179648 | tf_op jit(solution)/shard_map/reduce_scatter | solution.py:130
  160.5 11.6 %collective-permute-start.6 = (bf16[128,128]{1,0:T(8,128)(2,1)S(1)}, bf16[128,128]{1,0:T(8,128)(2,1)S(1)}, u32[]{:S(2)}, u32[]{:S(2)}) collective-permute-start(bf16[128,128]{1,0:T(8,128)(2,1)S(1)} %get-tuple-element.6), channel_id=1, source_target_pairs={{0,8},{8,16},{16,24},{24,0},{1,9},{9,17},{17,25},{25,1},{2,10},{10... | collective-permute-start | bytes 98312 | tf_op jit(solution)/shard_map/ppermute | solution.py:138
  162.9 9.7 %collective-permute-start.7 = (bf16[128,128]{1,0:T(8,128)(2,1)S(1)}, bf16[128,128]{1,0:T(8,128)(2,1)S(1)}, u32[]{:S(2)}, u32[]{:S(2)}) collective-permute-start(bf16[128,128]{1,0:T(8,128)(2,1)S(1)} %get-tuple-element.8), channel_id=1, source_target_pairs={{0,16},{8,24},{16,0},{24,8},{1,17},{9,25},{17,1},{25,9},{2,18},{10... | collective-permute-start | bytes 98312 | tf_op jit(solution)/shard_map/ppermute | solution.py:138
  170.2 8.3 %collective-permute-start.8 = (bf16[128,128]{1,0:T(8,128)(2,1)S(1)}, bf16[128,128]{1,0:T(8,128)(2,1)S(1)}, u32[]{:S(2)}, u32[]{:S(2)}) collective-permute-start(bf16[128,128]{1,0:T(8,128)(2,1)S(1)} %get-tuple-element.7), channel_id=1, source_target_pairs={{0,24},{8,0},{16,8},{24,16},{1,25},{9,1},{17,9},{25,17},{2,26},{10... | collective-permute-start | bytes 98312 | tf_op jit(solution)/shard_map/ppermute | solution.py:138
Sparse Core Ops, SparseCore 0:
  10.7 74.8 all-gather.2
  116.1 43.6 reduce-scatter.1

commit v3 on v1

v3 whole, which is shorter than its diff:
```python
import jax
import jax.numpy as jnp
from jax import lax
from jax.experimental import pallas as pl
from jax.experimental.pallas import tpu as pltpu
from jax.sharding import Mesh, PartitionSpec as P

F32 = jnp.float32
BF16 = jnp.bfloat16
ROW = ("yl", "x", "core")
Z = ("zh", "zl")
COL = ("yh",) + Z
SIZES = {"yl": 2, "x": 4, "core": 2, "yh": 4, "zh": 4, "zl": 2}
N_ROW, N_YH, N_Z = 16, 4, 8
HALF = N_ROW // 2
TOK = 128
VMEM_LIMIT = 56 * 1024 * 1024
WHOLE = pl.BlockSpec(memory_space=pltpu.VMEM)
SCALARS = pl.BlockSpec(memory_space=pltpu.SMEM)


def dot(a, b, dims):
    return lax.dot_general(a, b, (dims, ((), ())), preferred_element_type=F32)


def gather_by_swap(block, axis, size):
    copies = jnp.broadcast_to(block[None], (size,) + block.shape)
    return lax.all_to_all(copies, axis, split_axis=0, concat_axis=0, tiled=True)


def forward_kernel(place_ref, even_ref, x_ref, dy_ref, w_ref, keep_ref, send_ref, dx_ref):
    core, first = place_ref[0], place_ref[1] == 0
    gate = jnp.zeros((TOK, 256), F32)
    up = jnp.zeros((TOK, 256), F32)
    hidden_grad = jnp.zeros((TOK, 256), F32)
    for side in range(2):
        parity = core if side == 0 else 1 - core
        for q in range(HALF):
            y, zh = q // 2, (q % 2) * 2 + parity
            r = 2 * q + parity
            both = []
            for p, other_ref in enumerate((x_ref, dy_ref)):
                mine, other = even_ref[y, zh, p], other_ref[y, zh]
                low = jnp.where(first, mine, other)
                high = jnp.where(first, other, mine)
                both.append(jnp.concatenate([low, high], axis=1))
                if side == 0:
                    keep_ref[2 * q + p] = both[p]
                else:
                    send_ref[2 * q + p] = both[p]
            gate += dot(both[0], w_ref[r, 0], ((1,), (0,)))
            up += dot(both[0], w_ref[r, 1], ((1,), (0,)))
            hidden_grad += dot(both[1], w_ref[r, 2], ((1,), (0,)))
    sig = 1.0 / (1.0 + jnp.exp(-gate))
    act = gate * sig
    gate_grad = (hidden_grad * up * sig * (1.0 + gate * (1.0 - sig))).astype(BF16)
    up_grad = (hidden_grad * act).astype(BF16)
    hidden = (act * up).astype(BF16)
    for p, value in enumerate((gate_grad, up_grad, hidden)):
        keep_ref[N_ROW + p] = value
        send_ref[N_ROW + p] = value
    for r in range(N_ROW):
        dx = dot(gate_grad, w_ref[r, 0], ((1,), (1,))) + dot(up_grad, w_ref[r, 1], ((1,), (1,)))
        dx = dx.astype(BF16)
        y, z = r // 4, (r % 4) * 2
        dx_ref[z, y] = dx[:, :128]
        dx_ref[z + 1, y] = dx[:, 128:]


def forward(place, *arrays):
    pack = jax.ShapeDtypeStruct((N_ROW + 3, TOK, 256), BF16)
    return pl.pallas_call(
        forward_kernel,
        out_shape=(pack, pack, jax.ShapeDtypeStruct((N_Z, N_YH, TOK, 128), BF16)),
        in_specs=[SCALARS] + [WHOLE] * 4,
        out_specs=(WHOLE,) * 3,
        compiler_params=pltpu.CompilerParams(vmem_limit_bytes=VMEM_LIMIT),
        cost_estimate=pl.CostEstimate(flops=1400000000, bytes_accessed=10000000, transcendentals=32768),
        name="forward",
    )(place, *arrays)


def weight_kernel(mine_ref, other_ref, out_ref):
    grads = [
        jnp.concatenate([mine_ref[N_ROW + p], other_ref[N_ROW + p]], axis=0) for p in range(3)
    ]
    for q in range(HALF):
        x = jnp.concatenate([mine_ref[2 * q], other_ref[2 * q]], axis=0)
        dy = jnp.concatenate([mine_ref[2 * q + 1], other_ref[2 * q + 1]], axis=0)
        for p in range(3):
            term = dot(dy if p == 2 else x, grads[p], ((0,), (0,)))
            out_ref[q, p] = term.astype(BF16)


def weight_terms(mine, other):
    return pl.pallas_call(
        weight_kernel,
        out_shape=jax.ShapeDtypeStruct((HALF, 3, 256, 256), BF16),
        in_specs=[WHOLE] * 2,
        out_specs=WHOLE,
        compiler_params=pltpu.CompilerParams(vmem_limit_bytes=VMEM_LIMIT),
        cost_estimate=pl.CostEstimate(flops=8000000, bytes_accessed=60000, transcendentals=0),
        name="weight_terms",
    )(mine, other)


def local(inputs, out_grad, codes, scales):
    place = jnp.stack([lax.axis_index("core"), lax.axis_index("zl")])
    weights = (codes.astype(F32) * scales.astype(F32)).astype(BF16)
    weights = lax.all_gather(weights, ROW, axis=0, tiled=False)

    even = gather_by_swap(jnp.stack([inputs, out_grad]), ("yh", "zh"), 16)
    even = even.reshape(N_YH, 4, 2, TOK, 128)
    x = lax.ppermute(even[:, :, 0], Z, [(i, (i - 1) % N_Z) for i in range(N_Z)])
    dy = lax.ppermute(even[:, :, 1], Z, [(i, (i + 1) % N_Z) for i in range(N_Z)])

    keep, send, dx = forward(place, even, x, dy, weights)
    dx = lax.psum_scatter(dx, Z, scatter_dimension=0, tiled=False)
    other = lax.ppermute(send, "core", [(0, 1), (1, 0)])
    terms = weight_terms(keep, other)
    terms = lax.all_to_all(terms, ("yl", "x"), split_axis=0, concat_axis=0, tiled=True)

    dx, terms = lax.optimization_barrier((dx, terms))
    dx = lax.all_to_all(dx, "yh", split_axis=0, concat_axis=0, tiled=True)
    input_grad = jnp.sum(dx.astype(F32), axis=0).astype(BF16)
    weight_grad = jnp.sum(terms.astype(F32), axis=0)
    return input_grad, weight_grad


def solution(mesh):
    fine = Mesh(mesh.devices.reshape(tuple(SIZES.values())), tuple(SIZES))
    return jax.shard_map(
        local,
        mesh=fine,
        in_specs=(P(ROW, COL), P(ROW, COL), P(None, ROW, COL), P(None, ROW, COL)),
        out_specs=(P(ROW, COL), P(None, ROW, COL)),
        check_vma=False,
    )
```

time: 184 us -> 173 us (0.940)
  the two profiles are of different devices: /device:TPU:56 before, /device:TPU:4 now
where the time goes in v3:
time: 173 us
  waiting for transfers between devices  63.5 us (37%)
  blocking collectives  51.4 us (30%)
  starting transfers between devices  24.7 us (14%)
  between operations  14.1 us (8%)
  Pallas kernels  11.7 us (7%)
  other arithmetic  5.88 us (3%)
    all_to_all x1, blocking collectives, gather_by_swap(): return lax.all_to_all(copies, axis, split_axis=0, concat_axis=0, tiled=True)  51.4 us
    reduce_scatter x1, waiting for transfers between devices, local(): dx = lax.psum_scatter(dx, Z, scatter_dimension=0, tiled=False)  42 us
    all_to_all x1, starting transfers between devices, local(): lax.all_to_all(terms, ('yl', 'x'), split_axis=0, concat_axis=0, tiled=True)  8.83 us
    ppermute x1, waiting for transfers between devices, local(): lax.ppermute(even[:, :, 1], Z, [(i, (i + 1) % N_Z) for i in range(N_Z)])  7.69 us
    all_to_all x1, waiting for transfers between devices, local(): dx = lax.all_to_all(dx, 'yh', split_axis=0, concat_axis=0, tiled=True)  7.43 us
    pallas_call x1, Pallas kernels, forward(): pl.pallas_call(forward_kernel, out_shape=(pack, pack, jax.ShapeDtypeStruc...  7.39 us
    all_to_all x1, starting transfers between devices, local(): dx = lax.all_to_all(dx, 'yh', split_axis=0, concat_axis=0, tiled=True)  6.69 us
    ppermute x1, starting transfers between devices, local(): x = lax.ppermute(even[:, :, 0], Z, [(i, (i - 1) % N_Z) for i in range(N_Z)])  5.13 us
  transfers between devices with their start and end apart: 7, of which 6 were waited for; matrix products, arithmetic and copies ran while one was open for 2% of the time, Pallas kernels for 0%

profile of v3, /device:TPU:4, one launch (start us, length us, event | category | flops | bytes accessed | tf_op | source)
XLA Modules:
  0.0 172.9 jit_solution(10811187921501521673)
XLA Ops:
  7.2 0.0 all-gather.3.cloned.1.call-start
  7.2 0.7 bitcast_convert_fusion
  7.9 1.8 %multiply_convert_fusion = bf16[3,256,256]{2,1,0:T(8,128)(2,1)} fusion(bf16[3,256,256]{2,1,0:T(8,128)(2,1)} %param.6, f32[3,256]{1,0:T(4,128)S(1)} %bitcast_convert_fusion), kind=kLoop, calls=%fused_computation.1 | loop fusion | flops 589824 | bytes 789504 | tf_op jit(solution)/shard_map/convert_element_type | solution.py:109
  9.7 0.0 all-gather.3.cloned.1.call-update
  9.7 0.8 pad_maximum_fusion
  10.5 0.2 broadcast_in_dim.2
  10.8 51.4 %all_to_all.15 = bf16[16,2,128,128]{3,2,1,0:T(8,128)(2,1)S(1)} all-to-all(bf16[16,2,128,128]{3,2,1,0:T(8,128)(2,1)S(1)} %broadcast_in_dim.2), channel_id=1, replica_groups=mesh['yl'=2,'x'=4,'core'=2,'yh'=4,'zh'=4,'zl'=2] {'yh','zh'}, dimensions={0} | all-to-all | bytes 2097152 | tf_op jit(solution)/shard_map/all_to_all | solution.py:28
  62.2 0.0 copy-start
  62.2 0.1 copy.7
  62.3 0.1 slice_bitcast_fusion
  62.4 1.9 %collective-permute-start.1 = (bf16[4,4,128,128]{3,2,1,0:T(8,128)(2,1)S(1)}, bf16[4,4,128,128]{3,2,1,0:T(8,128)(2,1)S(1)}, u32[]{:S(2)}, u32[]{:S(2)}) collective-permute-start(bf16[4,4,128,128]{3,2,1,0:T(8,128)(2,1)S(1)} %get-tuple-element.12), channel_id=1, source_target_pairs={{0,1},{1,2},{2,3},{3,4},{4,5},{5,6},{6,7},{7,0},{8,9},{9,10},{10,1... | collective-permute-start | bytes 1572872 | tf_op jit(solution)/shard_map/ppermute | solution.py:115
  64.4 5.1 %collective-permute-start = (bf16[4,4,128,128]{3,2,1,0:T(8,128)(2,1)S(1)}, bf16[4,4,128,128]{3,2,1,0:T(8,128)(2,1)S(1)}, u32[]{:S(2)}, u32[]{:S(2)}) collective-permute-start(bf16[4,4,128,128]{3,2,1,0:T(8,128)(2,1)S(1)} %get-tuple-element.13), channel_id=1, source_target_pairs={{0,7},{1,0},{2,1},{3,2},{4,3},{5,4},{6,5},{7,6},{8,15},{9,8},{10,9... | collective-permute-start | bytes 1572872 | tf_op jit(solution)/shard_map/ppermute | solution.py:114
  69.5 0.6 pad_add_fusion.place_ref
  70.2 7.7 %collective-permute-done.1.dy_ref = bf16[4,4,128,128]{3,2,1,0:T(8,128)(2,1)S(1)} collective-permute-done((bf16[4,4,128,128]{3,2,1,0:T(8,128)(2,1)S(1)}, bf16[4,4,128,128]{3,2,1,0:T(8,128)(2,1)S(1)}, u32[]{:S(2)}, u32[]{:S(2)}) %collective-permute-start.1) | collective-permute-done | bytes 524320 | tf_op jit(solution)/shard_map/ppermute | solution.py:115
  77.8 0.0 copy-start.2
  77.8 1.2 collective-permute-done.x_ref
  79.0 0.0 copy-start.3
  79.0 1.5 all-gather.3.cloned.1.call-done
  80.6 0.0 copy-done
  80.6 0.0 copy-done.2
  80.6 0.0 copy-done.3
  80.6 7.4 %forward.1 = (bf16[19,128,256]{2,1,0:T(8,128)(2,1)}, bf16[19,128,256]{2,1,0:T(8,128)(2,1)}, bf16[8,4,128,128]{3,2,1,0:T(8,128)(2,1)}) custom-call(s32[2]{0:T(128)} %pad_add_fusion.place_ref, bf16[4,4,2,128,128]{4,3,2,1,0:T(8,128)(2,1)} %bitcast.15, bf16[4,4,128,128]{3,2,1,0:T(8,128)(2,1)} %copy-done.3, bf16[4,4,128,128]{3,2,1,0:T(8,128)(2,1)} %copy-done.2, ...), custom_call_target="tpu_custom_call" | custom-call | flops 1400000000 | bytes 10000000 | tf_op jit(solution)/shard_map/forward/pallas_call | solution.py:72
  88.0 2.1 %collective-permute-start.2 = (bf16[19,128,256]{2,1,0:T(8,128)(2,1)}, bf16[19,128,256]{2,1,0:T(8,128)(2,1)S(1)}, u32[]{:S(2)}, u32[]{:S(2)}) collective-permute-start(bf16[19,128,256]{2,1,0:T(8,128)(2,1)} %get-tuple-element.9), channel_id=1, source_target_pairs={{0,32},{32,0},{1,33},{33,1},{2,34},{34,2},{3,35},{35,3},{4,36},{36... | collective-permute-start | bytes 3735560 | tf_op jit(solution)/shard_map/ppermute | solution.py:119
  90.1 2.9 %collective-permute-done.2.other_ref = bf16[19,128,256]{2,1,0:T(8,128)(2,1)S(1)} collective-permute-done((bf16[19,128,256]{2,1,0:T(8,128)(2,1)}, bf16[19,128,256]{2,1,0:T(8,128)(2,1)S(1)}, u32[]{:S(2)}, u32[]{:S(2)}) %collective-permute-start.2) | collective-permute-done | bytes 1245216 | tf_op jit(solution)/shard_map/ppermute | solution.py:119
  93.0 0.0 copy-start.1
  93.0 1.0 copy-done.1
  94.0 4.3 %weight_terms.1 = bf16[8,3,256,256]{3,2,1,0:T(8,128)(2,1)} custom-call(bf16[19,128,256]{2,1,0:T(8,128)(2,1)} %get-tuple-element.8.mine_ref, bf16[19,128,256]{2,1,0:T(8,128)(2,1)} %copy-done.1), custom_call_target="tpu_custom_call" | custom-call | flops 8000000 | bytes 60000 | tf_op jit(solution)/shard_map/weight_terms/pallas_call | solution.py:96
  98.4 8.8 %all-to-all-start.1 = ((bf16[8,3,256,256]{3,2,1,0:T(8,128)(2,1)}), bf16[8,3,256,256]{3,2,1,0:T(8,128)(2,1)S(1)}, u32[]{:S(2)}, u32[]{:S(2)}) async-start(bf16[8,3,256,256]{3,2,1,0:T(8,128)(2,1)} %weight_terms.1), calls=%async_computation.2 | async-start | bytes 6291456 | tf_op jit(solution)/shard_map/all_to_all | solution.py:121
  107.2 0.0 reduce-scatter.2.cloned.1.call-start
  107.2 0.7 reduce-scatter.2.cloned.1.call-update
  107.9 42.0 %reduce-scatter.2.cloned.1.call-done = bf16[1,4,128,128]{3,2,1,0:T(8,128)(2,1)} async-done(((bf16[8,4,128,128]{3,2,1,0:T(8,128)(2,1)}), bf16[1,4,128,128]{3,2,1,0:T(8,128)(2,1)}) %reduce-scatter.2.cloned.1.call-update) | async-done | bytes 131088 | tf_op jit(solution)/shard_map/reduce_scatter | solution.py:118
  150.0 0.0 all-to-all-done.1
  150.0 6.7 %all-to-all-start.2 = ((bf16[4,128,128]{2,1,0:T(8,128)(2,1)}), bf16[4,128,128]{2,1,0:T(8,128)(2,1)S(1)}, u32[]{:S(2)}, u32[]{:S(2)}) async-start(bf16[4,128,128]{2,1,0:T(8,128)(2,1)} %bitcast.18), calls=%async_computation.3 | async-start | bytes 262144 | tf_op jit(solution)/shard_map/all_to_all | solution.py:124
  156.6 1.3 convert_reduce_fusion
  157.9 7.4 %all-to-all-done.2 = bf16[4,128,128]{2,1,0:T(8,128)(2,1)S(1)} async-done(((bf16[4,128,128]{2,1,0:T(8,128)(2,1)}), bf16[4,128,128]{2,1,0:T(8,128)(2,1)S(1)}, u32[]{:S(2)}, u32[]{:S(2)}) %all-to-all-start.2) | async-done | bytes 131104 | tf_op jit(solution)/shard_map/all_to_all | solution.py:124
  165.4 0.6 reduce_sum.21
Async XLA Ops:
  7.2 73.4 %all-gather.3.cloned.1.call-start = ((), (), s32[]{:S(2)}) async-start(), calls=%async_computation.5 | async-start | bytes 6684672 | tf_op jit(solution)/shard_map/all_gather | solution.py:110
  62.2 18.4 %copy-start = (bf16[16,2,128,128]{3,2,1,0:T(8,128)(2,1)}, bf16[16,2,128,128]{3,2,1,0:T(8,128)(2,1)S(1)}, u32[]{:S(2)}) copy-start(bf16[16,2,128,128]{3,2,1,0:T(8,128)(2,1)S(1)} %all_to_all.15) | copy-start | bytes 3145732
  62.4 15.4 %collective-permute-start.1 = (bf16[4,4,128,128]{3,2,1,0:T(8,128)(2,1)S(1)}, bf16[4,4,128,128]{3,2,1,0:T(8,128)(2,1)S(1)}, u32[]{:S(2)}, u32[]{:S(2)}) collective-permute-start(bf16[4,4,128,128]{3,2,1,0:T(8,128)(2,1)S(1)} %get-tuple-element.12), channel_id=1, source_target_pairs={{0,1},{1,2},{2,3},{3,4},{4,5},{5,6},{6,7},{7,0},{8,9},{9,10},{10,1... | collective-permute-start | bytes 1572872 | tf_op jit(solution)/shard_map/ppermute | solution.py:115
  64.4 14.7 %collective-permute-start = (bf16[4,4,128,128]{3,2,1,0:T(8,128)(2,1)S(1)}, bf16[4,4,128,128]{3,2,1,0:T(8,128)(2,1)S(1)}, u32[]{:S(2)}, u32[]{:S(2)}) collective-permute-start(bf16[4,4,128,128]{3,2,1,0:T(8,128)(2,1)S(1)} %get-tuple-element.13), channel_id=1, source_target_pairs={{0,7},{1,0},{2,1},{3,2},{4,3},{5,4},{6,5},{7,6},{8,15},{9,8},{10,9... | collective-permute-start | bytes 1572872 | tf_op jit(solution)/shard_map/ppermute | solution.py:114
  77.8 2.7 %copy-start.2 = (bf16[4,4,128,128]{3,2,1,0:T(8,128)(2,1)}, bf16[4,4,128,128]{3,2,1,0:T(8,128)(2,1)S(1)}, u32[]{:S(2)}) copy-start(bf16[4,4,128,128]{3,2,1,0:T(8,128)(2,1)S(1)} %collective-permute-done.1.dy_ref) | copy-start | bytes 1572868
  79.0 1.6 copy-start.3
  88.0 5.0 %collective-permute-start.2 = (bf16[19,128,256]{2,1,0:T(8,128)(2,1)}, bf16[19,128,256]{2,1,0:T(8,128)(2,1)S(1)}, u32[]{:S(2)}, u32[]{:S(2)}) collective-permute-start(bf16[19,128,256]{2,1,0:T(8,128)(2,1)} %get-tuple-element.9), channel_id=1, source_target_pairs={{0,32},{32,0},{1,33},{33,1},{2,34},{34,2},{3,35},{35,3},{4,36},{36... | collective-permute-start | bytes 3735560 | tf_op jit(solution)/shard_map/ppermute | solution.py:119
  93.0 1.0 copy-start.1
  98.4 51.6 %all-to-all-start.1 = ((bf16[8,3,256,256]{3,2,1,0:T(8,128)(2,1)}), bf16[8,3,256,256]{3,2,1,0:T(8,128)(2,1)S(1)}, u32[]{:S(2)}, u32[]{:S(2)}) async-start(bf16[8,3,256,256]{3,2,1,0:T(8,128)(2,1)} %weight_terms.1), calls=%async_computation.2 | async-start | bytes 6291456 | tf_op jit(solution)/shard_map/all_to_all | solution.py:121
  107.2 42.8 %reduce-scatter.2.cloned.1.call-start = ((), (), s32[]{:S(2)}) async-start(), calls=%async_computation.4 | async-start | bytes 1179648 | tf_op jit(solution)/shard_map/reduce_scatter | solution.py:118
  150.0 15.4 %all-to-all-start.2 = ((bf16[4,128,128]{2,1,0:T(8,128)(2,1)}), bf16[4,128,128]{2,1,0:T(8,128)(2,1)S(1)}, u32[]{:S(2)}, u32[]{:S(2)}) async-start(bf16[4,128,128]{2,1,0:T(8,128)(2,1)} %bitcast.18), calls=%async_computation.3 | async-start | bytes 262144 | tf_op jit(solution)/shard_map/all_to_all | solution.py:124
Sparse Core Ops, SparseCore 0:
  10.1 70.3 all-gather.2
  110.8 39.0 reduce-scatter.1

commit v4 on v3

--- a/solution.py
+++ b/solution.py
@@ -40,7 +40,7 @@
             r = 2 * q + parity
             both = []
             for p, other_ref in enumerate((x_ref, dy_ref)):
-                mine, other = even_ref[y, zh, p], other_ref[y, zh]
+                mine, other = even_ref[zh, y, p], other_ref[zh, y]
                 low = jnp.where(first, mine, other)
                 high = jnp.where(first, other, mine)
                 both.append(jnp.concatenate([low, high], axis=1))
@@ -62,16 +62,15 @@
     for r in range(N_ROW):
         dx = dot(gate_grad, w_ref[r, 0], ((1,), (1,))) + dot(up_grad, w_ref[r, 1], ((1,), (1,)))
         dx = dx.astype(BF16)
-        y, z = r // 4, (r % 4) * 2
-        dx_ref[z, y] = dx[:, :128]
-        dx_ref[z + 1, y] = dx[:, 128:]
+        dx_ref[2 * r] = dx[:, :128]
+        dx_ref[2 * r + 1] = dx[:, 128:]
 
 
 def forward(place, *arrays):
     pack = jax.ShapeDtypeStruct((N_ROW + 3, TOK, 256), BF16)
     return pl.pallas_call(
         forward_kernel,
-        out_shape=(pack, pack, jax.ShapeDtypeStruct((N_Z, N_YH, TOK, 128), BF16)),
+        out_shape=(pack, pack, jax.ShapeDtypeStruct((N_YH * N_Z, TOK, 128), BF16)),
         in_specs=[SCALARS] + [WHOLE] * 4,
         out_specs=(WHOLE,) * 3,
         compiler_params=pltpu.CompilerParams(vmem_limit_bytes=VMEM_LIMIT),
@@ -80,7 +79,7 @@
     )(place, *arrays)
 
 
-def weight_kernel(mine_ref, other_ref, out_ref):
+def weight_kernel(mine_ref, other_ref, top_ref, low_ref):
     grads = [
         jnp.concatenate([mine_ref[N_ROW + p], other_ref[N_ROW + p]], axis=0) for p in range(3)
     ]
@@ -89,17 +88,20 @@
         dy = jnp.concatenate([mine_ref[2 * q + 1], other_ref[2 * q + 1]], axis=0)
         for p in range(3):
             term = dot(dy if p == 2 else x, grads[p], ((0,), (0,)))
-            out_ref[q, p] = term.astype(BF16)
+            term = term.astype(BF16)
+            top_ref[q, p] = term[:TOK]
+            low_ref[q, p] = term[TOK:]
 
 
 def weight_terms(mine, other):
+    rows = jax.ShapeDtypeStruct((HALF, 3, TOK, 256), BF16)
     return pl.pallas_call(
         weight_kernel,
-        out_shape=jax.ShapeDtypeStruct((HALF, 3, 256, 256), BF16),
+        out_shape=(rows, rows),
         in_specs=[WHOLE] * 2,
-        out_specs=WHOLE,
+        out_specs=(WHOLE, WHOLE),
         compiler_params=pltpu.CompilerParams(vmem_limit_bytes=VMEM_LIMIT),
-        cost_estimate=pl.CostEstimate(flops=8000000, bytes_accessed=60000, transcendentals=0),
+        cost_estimate=pl.CostEstimate(flops=800000000, bytes_accessed=6000000, transcendentals=0),
         name="weight_terms",
     )(mine, other)
 
@@ -109,22 +111,21 @@
     weights = (codes.astype(F32) * scales.astype(F32)).astype(BF16)
     weights = lax.all_gather(weights, ROW, axis=0, tiled=False)
 
-    even = gather_by_swap(jnp.stack([inputs, out_grad]), ("yh", "zh"), 16)
-    even = even.reshape(N_YH, 4, 2, TOK, 128)
+    even = gather_by_swap(jnp.stack([inputs, out_grad]), "yh", N_YH)
+    even = gather_by_swap(even, "zh", 4)
     x = lax.ppermute(even[:, :, 0], Z, [(i, (i - 1) % N_Z) for i in range(N_Z)])
     dy = lax.ppermute(even[:, :, 1], Z, [(i, (i + 1) % N_Z) for i in range(N_Z)])
 
     keep, send, dx = forward(place, even, x, dy, weights)
-    dx = lax.psum_scatter(dx, Z, scatter_dimension=0, tiled=False)
+    dx = lax.all_to_all(dx, COL, split_axis=0, concat_axis=0, tiled=True)
+    input_grad = jnp.sum(dx.astype(F32), axis=0).astype(BF16)
+
     other = lax.ppermute(send, "core", [(0, 1), (1, 0)])
-    terms = weight_terms(keep, other)
-    terms = lax.all_to_all(terms, ("yl", "x"), split_axis=0, concat_axis=0, tiled=True)
-
-    dx, terms = lax.optimization_barrier((dx, terms))
-    dx = lax.all_to_all(dx, "yh", split_axis=0, concat_axis=0, tiled=True)
-    input_grad = jnp.sum(dx.astype(F32), axis=0).astype(BF16)
-    weight_grad = jnp.sum(terms.astype(F32), axis=0)
-    return input_grad, weight_grad
+    top, low = weight_terms(keep, other)
+    low = lax.psum_scatter(low, ("yl", "x"), scatter_dimension=0, tiled=False)
+    top = lax.all_to_all(top, ("yl", "x"), split_axis=0, concat_axis=0, tiled=True)
+    top = jnp.sum(top.astype(F32), axis=0)
+    return input_grad, jnp.concatenate([top, low.astype(F32)], axis=1)
 
 
 def solution(mesh):

time: 173 us -> 175 us (1.012)
  the two profiles are of different devices: /device:TPU:4 before, /device:TPU:40 now
where the time goes in v4:
time: 175 us; the launch traced here: 174 us
  waiting for transfers between devices  66.4 us (38%)
  blocking collectives  46.5 us (27%)
  starting transfers between devices  25.6 us (15%)
  between operations  14.1 us (8%)
  Pallas kernels  11.7 us (7%)
  other arithmetic  6.75 us (4%)
  local copies, waits for them, and re-layouts  3.28 us (2%)
    all_to_all x2, blocking collectives, gather_by_swap(): return lax.all_to_all(copies, axis, split_axis=0, concat_axis=0, tiled=True)  46.5 us
    all_to_all x1, waiting for transfers between devices, local(): lax.all_to_all(top, ('yl', 'x'), split_axis=0, concat_axis=0, tiled=True)  27.4 us
    all_to_all x1, waiting for transfers between devices, local(): dx = lax.all_to_all(dx, COL, split_axis=0, concat_axis=0, tiled=True)  20.9 us
    all_to_all x1, starting transfers between devices, local(): dx = lax.all_to_all(dx, COL, split_axis=0, concat_axis=0, tiled=True)  10.3 us
    ppermute x1, waiting for transfers between devices, local(): lax.ppermute(even[:, :, 1], Z, [(i, (i + 1) % N_Z) for i in range(N_Z)])  8.21 us
    pallas_call x1, Pallas kernels, forward(): pl.pallas_call(forward_kernel, out_shape=(pack, pack, jax.ShapeDtypeStruc...  7.38 us
    all_to_all x1, starting transfers between devices, local(): lax.all_to_all(top, ('yl', 'x'), split_axis=0, concat_axis=0, tiled=True)  5.79 us
    ppermute x1, starting transfers between devices, local(): lax.ppermute(even[:, :, 1], Z, [(i, (i + 1) % N_Z) for i in range(N_Z)])  5.6 us
  transfers between devices with their start and end apart: 7, of which 6 were waited for; matrix products, arithmetic and copies ran while one was open for 2% of the time, Pallas kernels for 2%

profile of v4, /device:TPU:40, one launch (start us, length us, event | category | flops | bytes accessed | tf_op | source)
XLA Modules:
  0.0 174.3 jit_solution(13644384804282644957)
XLA Ops:
  7.2 0.0 all-gather.3.cloned.1.call-start
  7.2 0.7 bitcast_convert_fusion.1
  7.9 1.8 %multiply_convert_fusion = bf16[3,256,256]{2,1,0:T(8,128)(2,1)} fusion(bf16[3,256,256]{2,1,0:T(8,128)(2,1)} %param.6, f32[3,256]{1,0:T(4,128)S(1)} %bitcast_convert_fusion.1), kind=kLoop, calls=%fused_computation.2 | loop fusion | flops 589824 | bytes 789504 | tf_op jit(solution)/shard_map/convert_element_type | solution.py:111
  9.7 0.0 all-gather.3.cloned.1.call-update
  9.7 0.8 pad_maximum_fusion.1
  10.6 13.6 %all_to_all.20 = bf16[4,2,128,128]{3,2,1,0:T(8,128)(2,1)S(1)} all-to-all(bf16[4,2,128,128]{3,2,1,0:T(8,128)(2,1)S(1)} %broadcast_in_dim.4), channel_id=1, replica_groups=mesh['yl'=2,'x'=4,'core'=2,'yh'=4,'zh'=4,'zl'=2] {'yh'}, dimensions={0} | all-to-all | bytes 524288 | tf_op jit(solution)/shard_map/all_to_all | solution.py:28
  24.2 0.2 broadcast_in_dim.5
  24.5 32.8 %all_to_all.21 = bf16[4,4,2,128,128]{4,3,1,2,0:T(8,128)(2,1)S(1)} all-to-all(bf16[4,4,2,128,128]{4,3,1,2,0:T(8,128)(2,1)S(1)} %broadcast_in_dim.5), channel_id=1, replica_groups=mesh['yl'=2,'x'=4,'core'=2,'yh'=4,'zh'=4,'zl'=2] {'zh'}, dimensions={0} | all-to-all | bytes 2097152 | tf_op jit(solution)/shard_map/all_to_all | solution.py:28
  57.3 0.1 slice_bitcast_fusion
  57.4 5.6 %collective-permute-start.1 = (bf16[4,4,128,128]{3,2,1,0:T(8,128)(2,1)S(1)}, bf16[4,4,128,128]{3,2,1,0:T(8,128)(2,1)S(1)}, u32[]{:S(2)}, u32[]{:S(2)}) collective-permute-start(bf16[4,4,128,128]{3,2,1,0:T(8,128)(2,1)S(1)} %get-tuple-element.12), channel_id=1, source_target_pairs={{0,1},{1,2},{2,3},{3,4},{4,5},{5,6},{6,7},{7,0},{8,9},{9,10},{10,1... | collective-permute-start | bytes 1572872 | tf_op jit(solution)/shard_map/ppermute | solution.py:117
  63.0 1.9 %collective-permute-start = (bf16[4,4,128,128]{3,2,1,0:T(8,128)(2,1)S(1)}, bf16[4,4,128,128]{3,2,1,0:T(8,128)(2,1)S(1)}, u32[]{:S(2)}, u32[]{:S(2)}) collective-permute-start(bf16[4,4,128,128]{3,2,1,0:T(8,128)(2,1)S(1)} %get-tuple-element.13), channel_id=1, source_target_pairs={{0,7},{1,0},{2,1},{3,2},{4,3},{5,4},{6,5},{7,6},{8,15},{9,8},{10,9... | collective-permute-start | bytes 1572872 | tf_op jit(solution)/shard_map/ppermute | solution.py:116
  64.9 0.6 pad_add_fusion.place_ref
  65.5 1.1 copy.10.even_ref
  66.6 8.2 %collective-permute-done.1.dy_ref = bf16[4,4,128,128]{3,2,1,0:T(8,128)(2,1)S(1)} collective-permute-done((bf16[4,4,128,128]{3,2,1,0:T(8,128)(2,1)S(1)}, bf16[4,4,128,128]{3,2,1,0:T(8,128)(2,1)S(1)}, u32[]{:S(2)}, u32[]{:S(2)}) %collective-permute-start.1) | collective-permute-done | bytes 524320 | tf_op jit(solution)/shard_map/ppermute | solution.py:117
  74.8 0.0 copy-start
  74.8 2.7 %collective-permute-done.x_ref = bf16[4,4,128,128]{3,2,1,0:T(8,128)(2,1)S(1)} collective-permute-done((bf16[4,4,128,128]{3,2,1,0:T(8,128)(2,1)S(1)}, bf16[4,4,128,128]{3,2,1,0:T(8,128)(2,1)S(1)}, u32[]{:S(2)}, u32[]{:S(2)}) %collective-permute-start) | collective-permute-done | bytes 524320 | tf_op jit(solution)/shard_map/ppermute | solution.py:116
  77.5 0.0 copy-start.1
  77.5 0.0 all-gather.3.cloned.1.call-done
  77.5 0.0 copy-done
  77.5 0.8 copy-done.1
  78.3 7.4 %forward.1 = (bf16[19,128,256]{2,1,0:T(8,128)(2,1)}, bf16[19,128,256]{2,1,0:T(8,128)(2,1)}, bf16[32,128,128]{2,1,0:T(8,128)(2,1)}) custom-call(s32[2]{0:T(128)} %pad_add_fusion.place_ref, bf16[4,4,2,128,128]{4,3,2,1,0:T(8,128)(2,1)} %copy.10.even_ref, bf16[4,4,128,128]{3,2,1,0:T(8,128)(2,1)} %copy-done.1, bf16[4,4,128,128]{3,2,1,0:T(8,128)(2,1)} %copy-done, ...), custom_call_target="tpu_custom_call" | custom-call | flops 1400000000 | bytes 10000000 | tf_op jit(solution)/shard_map/forward/pallas_call | solution.py:71
  85.7 0.0 copy-start.2
  85.7 10.3 %all-to-all-start.2 = ((bf16[32,128,128]{2,1,0:T(8,128)(2,1)}), bf16[32,128,128]{2,1,0:T(8,128)(2,1)S(1)}, u32[]{:S(2)}, u32[]{:S(2)}) async-start(bf16[32,128,128]{2,1,0:T(8,128)(2,1)} %get-tuple-element.7), calls=%async_computation.2 | async-start | bytes 2097152 | tf_op jit(solution)/shard_map/all_to_all | solution.py:120
  96.0 0.0 reduce-scatter.2.cloned.1.call-start
  96.1 0.0 copy-done.2
  96.1 1.9 %collective-permute-start.2 = (bf16[19,128,256]{2,1,0:T(8,128)(2,1)S(1)}, bf16[19,128,256]{2,1,0:T(8,128)(2,1)S(1)}, u32[]{:S(2)}, u32[]{:S(2)}) collective-permute-start(bf16[19,128,256]{2,1,0:T(8,128)(2,1)S(1)} %copy-done.2), channel_id=1, source_target_pairs={{0,32},{32,0},{1,33},{33,1},{2,34},{34,2},{3,35},{35,3},{4,36},{36... | collective-permute-start | bytes 3735560 | tf_op jit(solution)/shard_map/ppermute | solution.py:123
  98.0 2.9 %collective-permute-done.2.other_ref = bf16[19,128,256]{2,1,0:T(8,128)(2,1)S(1)} collective-permute-done((bf16[19,128,256]{2,1,0:T(8,128)(2,1)S(1)}, bf16[19,128,256]{2,1,0:T(8,128)(2,1)S(1)}, u32[]{:S(2)}, u32[]{:S(2)}) %collective-permute-start.2) | collective-permute-done | bytes 1245216 | tf_op jit(solution)/shard_map/ppermute | solution.py:123
  100.9 0.0 copy-start.3
  100.9 1.0 copy-done.3
  102.0 4.3 %weight_terms.1 = (bf16[8,3,128,256]{3,2,1,0:T(8,128)(2,1)}, bf16[8,3,128,256]{3,2,1,0:T(8,128)(2,1)}) custom-call(bf16[19,128,256]{2,1,0:T(8,128)(2,1)} %get-tuple-element.8.mine_ref, bf16[19,128,256]{2,1,0:T(8,128)(2,1)} %copy-done.3), custom_call_target="tpu_custom_call" | custom-call | flops 800000000 | bytes 6000000 | tf_op jit(solution)/shard_map/weight_terms/pallas_call | solution.py:98
  106.2 0.0 reduce-scatter.2.cloned.1.call-update
  106.3 20.9 %all-to-all-done.2 = bf16[32,128,128]{2,1,0:T(8,128)(2,1)S(1)} async-done(((bf16[32,128,128]{2,1,0:T(8,128)(2,1)}), bf16[32,128,128]{2,1,0:T(8,128)(2,1)S(1)}, u32[]{:S(2)}, u32[]{:S(2)}) %all-to-all-start.2) | async-done | bytes 1048608 | tf_op jit(solution)/shard_map/all_to_all | solution.py:120
  127.2 5.8 %all-to-all-start.3 = ((bf16[8,3,128,256]{3,2,1,0:T(8,128)(2,1)}), bf16[8,3,128,256]{3,2,1,0:T(8,128)(2,1)S(1)}, u32[]{:S(2)}, u32[]{:S(2)}) async-start(bf16[8,3,128,256]{3,2,1,0:T(8,128)(2,1)} %get-tuple-element.10), calls=%async_computation.3 | async-start | bytes 3145728 | tf_op jit(solution)/shard_map/all_to_all | solution.py:126
  133.0 0.8 reduce_sum.21
  133.7 27.4 %all-to-all-done.3 = bf16[8,3,128,256]{3,2,1,0:T(8,128)(2,1)S(1)} async-done(((bf16[8,3,128,256]{3,2,1,0:T(8,128)(2,1)}), bf16[8,3,128,256]{3,2,1,0:T(8,128)(2,1)S(1)}, u32[]{:S(2)}, u32[]{:S(2)}) %all-to-all-start.3) | async-done | bytes 1572896 | tf_op jit(solution)/shard_map/all_to_all | solution.py:126
  161.1 0.2 convert_reduce_fusion
  161.3 4.2 %reduce-scatter.2.cloned.1.call-done = bf16[1,3,128,256]{3,2,1,0:T(8,128)(2,1)} async-done(((bf16[8,3,128,256]{3,2,1,0:T(8,128)(2,1)}), bf16[1,3,128,256]{3,2,1,0:T(8,128)(2,1)}) %reduce-scatter.2.cloned.1.call-update) | async-done | bytes 196624 | tf_op jit(solution)/shard_map/reduce_scatter | solution.py:125
  165.5 1.0 bitcast_convert_fusion
  166.5 0.9 pad_maximum_fusion
  (2 shorter events, 0.1 us)
Async XLA Ops:
  7.2 70.4 %all-gather.3.cloned.1.call-start = ((), (), s32[]{:S(2)}) async-start(), calls=%async_computation.6 | async-start | bytes 6684672 | tf_op jit(solution)/shard_map/all_gather | solution.py:112
  57.4 17.4 %collective-permute-start.1 = (bf16[4,4,128,128]{3,2,1,0:T(8,128)(2,1)S(1)}, bf16[4,4,128,128]{3,2,1,0:T(8,128)(2,1)S(1)}, u32[]{:S(2)}, u32[]{:S(2)}) collective-permute-start(bf16[4,4,128,128]{3,2,1,0:T(8,128)(2,1)S(1)} %get-tuple-element.12), channel_id=1, source_target_pairs={{0,1},{1,2},{2,3},{3,4},{4,5},{5,6},{6,7},{7,0},{8,9},{9,10},{10,1... | collective-permute-start | bytes 1572872 | tf_op jit(solution)/shard_map/ppermute | solution.py:117
  63.0 14.5 %collective-permute-start = (bf16[4,4,128,128]{3,2,1,0:T(8,128)(2,1)S(1)}, bf16[4,4,128,128]{3,2,1,0:T(8,128)(2,1)S(1)}, u32[]{:S(2)}, u32[]{:S(2)}) collective-permute-start(bf16[4,4,128,128]{3,2,1,0:T(8,128)(2,1)S(1)} %get-tuple-element.13), channel_id=1, source_target_pairs={{0,7},{1,0},{2,1},{3,2},{4,3},{5,4},{6,5},{7,6},{8,15},{9,8},{10,9... | collective-permute-start | bytes 1572872 | tf_op jit(solution)/shard_map/ppermute | solution.py:116
  74.8 2.7 %copy-start = (bf16[4,4,128,128]{3,2,1,0:T(8,128)(2,1)}, bf16[4,4,128,128]{3,2,1,0:T(8,128)(2,1)S(1)}, u32[]{:S(2)}) copy-start(bf16[4,4,128,128]{3,2,1,0:T(8,128)(2,1)S(1)} %collective-permute-done.1.dy_ref) | copy-start | bytes 1572868
  77.5 0.8 copy-start.1
  85.7 10.4 %copy-start.2 = (bf16[19,128,256]{2,1,0:T(8,128)(2,1)S(1)}, bf16[19,128,256]{2,1,0:T(8,128)(2,1)}, u32[]{:S(2)}) copy-start(bf16[19,128,256]{2,1,0:T(8,128)(2,1)} %get-tuple-element.9) | copy-start | bytes 3735556
  85.7 41.5 %all-to-all-start.2 = ((bf16[32,128,128]{2,1,0:T(8,128)(2,1)}), bf16[32,128,128]{2,1,0:T(8,128)(2,1)S(1)}, u32[]{:S(2)}, u32[]{:S(2)}) async-start(bf16[32,128,128]{2,1,0:T(8,128)(2,1)} %get-tuple-element.7), calls=%async_computation.2 | async-start | bytes 2097152 | tf_op jit(solution)/shard_map/all_to_all | solution.py:120
  96.0 69.5 %reduce-scatter.2.cloned.1.call-start = ((), (), s32[]{:S(2)}) async-start(), calls=%async_computation.5 | async-start | bytes 1769472 | tf_op jit(solution)/shard_map/reduce_scatter | solution.py:125
  96.1 4.8 %collective-permute-start.2 = (bf16[19,128,256]{2,1,0:T(8,128)(2,1)S(1)}, bf16[19,128,256]{2,1,0:T(8,128)(2,1)S(1)}, u32[]{:S(2)}, u32[]{:S(2)}) collective-permute-start(bf16[19,128,256]{2,1,0:T(8,128)(2,1)S(1)} %copy-done.2), channel_id=1, source_target_pairs={{0,32},{32,0},{1,33},{33,1},{2,34},{34,2},{3,35},{35,3},{4,36},{36... | collective-permute-start | bytes 3735560 | tf_op jit(solution)/shard_map/ppermute | solution.py:123
  100.9 1.0 copy-start.3
  127.2 33.9 %all-to-all-start.3 = ((bf16[8,3,128,256]{3,2,1,0:T(8,128)(2,1)}), bf16[8,3,128,256]{3,2,1,0:T(8,128)(2,1)S(1)}, u32[]{:S(2)}, u32[]{:S(2)}) async-start(bf16[8,3,128,256]{3,2,1,0:T(8,128)(2,1)} %get-tuple-element.10), calls=%async_computation.3 | async-start | bytes 3145728 | tf_op jit(solution)/shard_map/all_to_all | solution.py:126
Sparse Core Ops, SparseCore 0:
  10.1 51.7 all-gather.2
  106.4 59.0 reduce-scatter.1

commit v5 on v4

v5 whole, which is shorter than its diff:
```python
import jax
import jax.numpy as jnp
from jax import lax
from jax.experimental import pallas as pl
from jax.experimental.pallas import tpu as pltpu
from jax.sharding import Mesh, PartitionSpec as P

F32 = jnp.float32
BF16 = jnp.bfloat16
ROW = ("yl", "x", "core")
Z = ("zh", "zl")
COL = ("yh",) + Z
SIZES = {"yl": 2, "x": 4, "core": 2, "yh": 4, "zh": 4, "zl": 2}
N_ROW, N_YH, N_Z = 16, 4, 8
HALF = N_ROW // 2
TOK = 128
BLOCK = 256
SIDE = HALF * BLOCK
PACK = 2 * SIDE + 3 * BLOCK
TOP = 96
FORWARD_VMEM = 49 * 1024 * 1024
WEIGHT_VMEM = 24 * 1024 * 1024
ANYWHERE = pl.BlockSpec(memory_space=pl.ANY)
SCALARS = pl.BlockSpec(memory_space=pltpu.SMEM)


def dot(a, b, dims):
    return lax.dot_general(a, b, (dims, ((), ())), preferred_element_type=F32)


def gather_by_swap(block, axis, size):
    copies = jnp.broadcast_to(block[None], (size,) + block.shape)
    return lax.all_to_all(copies, axis, split_axis=0, concat_axis=0, tiled=True)


def forward_kernel(
    place_ref, same_in, upper_in, lower_in, w_in, keep_out, send_out, dx_out,
    same_ref, upper_ref, lower_ref, w_ref, pack_ref, dx_ref, in_sems, w_sems, out_sems,
):
    core, first = place_ref[0], place_ref[1] == 0

    def row(i):
        return 2 * (i % HALF) + (core if i < HALF else 1 - core)

    loads = [
        pltpu.make_async_copy(src, dst, in_sems.at[i])
        for i, (src, dst) in enumerate(((same_in, same_ref), (upper_in, upper_ref), (lower_in, lower_ref)))
    ]
    w_loads = [
        pltpu.make_async_copy(w_in.at[row(i)], w_ref.at[:, pl.ds(i * BLOCK, BLOCK)], w_sems.at[i])
        for i in range(N_ROW)
    ]
    for load in loads + w_loads:
        load.start()
    for load in loads:
        load.wait()
    sums = [jnp.zeros((TOK, BLOCK), F32) for _ in range(3)]
    stores = []
    for side in range(2):
        parity = core if side == 0 else 1 - core
        for half in range(2):
            for q in range(4 * half, 4 * half + 4):
                y, zh = q // 2, (q % 2) * 2 + parity
                other_ref = lower_ref if q % 2 else upper_ref
                for p in range(2):
                    mine, other = same_ref[zh, y, p], other_ref[parity, y, p]
                    low = jnp.where(first, mine, other)
                    high = jnp.where(first, other, mine)
                    at = p * SIDE + q * BLOCK
                    pack_ref[side, :, pl.ds(at, BLOCK)] = jnp.concatenate([low, high], axis=1)
                w_loads[side * HALF + q].wait()
            rows = pl.ds((side * 2 + half) * 4 * BLOCK, 4 * BLOCK)
            x = pack_ref[side, :, pl.ds(half * 4 * BLOCK, 4 * BLOCK)]
            dy = pack_ref[side, :, pl.ds(SIDE + half * 4 * BLOCK, 4 * BLOCK)]
            for p in range(3):
                sums[p] += dot(dy if p == 2 else x, w_ref[p, rows], ((1,), (0,)))
        out = keep_out if side == 0 else send_out
        cols = pl.ds(0, 2 * SIDE)
        stores.append(
            pltpu.make_async_copy(pack_ref.at[side, :, cols], out.at[:, cols], out_sems.at[side])
        )
        stores[-1].start()
    gate, up, hidden_grad = sums
    sig = 1.0 / (1.0 + jnp.exp(-gate))
    act = gate * sig
    gate_grad = (hidden_grad * up * sig * (1.0 + gate * (1.0 - sig))).astype(BF16)
    up_grad = (hidden_grad * act).astype(BF16)
    hidden = (act * up).astype(BF16)
    for side in range(2):
        for p, value in enumerate((gate_grad, up_grad, hidden)):
            pack_ref[side, :, pl.ds(2 * SIDE + p * BLOCK, BLOCK)] = value
        out = keep_out if side == 0 else send_out
        cols = pl.ds(2 * SIDE, 3 * BLOCK)
        stores.append(
            pltpu.make_async_copy(pack_ref.at[side, :, cols], out.at[:, cols], out_sems.at[2 + side])
        )
        stores[-1].start()
    for i in range(N_ROW):
        q, parity = i % HALF, (core if i < HALF else 1 - core)
        rows = pl.ds(i * BLOCK, BLOCK)
        dx = dot(gate_grad, w_ref[0, rows], ((1,), (1,)))
        dx = (dx + dot(up_grad, w_ref[1, rows], ((1,), (1,)))).astype(BF16)
        y, z = q // 2, 4 * (q % 2) + 2 * parity
        dx_ref[z, y] = dx[:, :TOK]
        dx_ref[z + 1, y] = dx[:, TOK:]
    stores.append(pltpu.make_async_copy(dx_ref, dx_out, out_sems.at[4]))
    stores[-1].start()
    for store in stores:
        store.wait()


def forward(place, same, upper, lower, weights):
    pack = jax.ShapeDtypeStruct((TOK, PACK), BF16)
    return pl.pallas_call(
        forward_kernel,
        out_shape=(pack, pack, jax.ShapeDtypeStruct((N_Z, N_YH, TOK, 128), BF16)),
        in_specs=[SCALARS] + [ANYWHERE] * 4,
        out_specs=(ANYWHERE,) * 3,
        scratch_shapes=[
            pltpu.VMEM(same.shape, BF16),
            pltpu.VMEM(upper.shape, BF16),
            pltpu.VMEM(lower.shape, BF16),
            pltpu.VMEM((3, N_ROW * BLOCK, BLOCK), BF16),
            pltpu.VMEM((2, TOK, PACK), BF16),
            pltpu.VMEM((N_Z, N_YH, TOK, 128), BF16),
            pltpu.SemaphoreType.DMA((3,)),
            pltpu.SemaphoreType.DMA((N_ROW,)),
            pltpu.SemaphoreType.DMA((5,)),
        ],
        compiler_params=pltpu.CompilerParams(vmem_limit_bytes=FORWARD_VMEM),
        cost_estimate=pl.CostEstimate(flops=1400000000, bytes_accessed=10000000, transcendentals=32768),
        name="forward",
    )(place, same, upper, lower, weights)


def weight_kernel(mine_in, other_in, top_out, low_out, both_ref, terms_ref, in_sems, out_sems):
    loads = [
        pltpu.make_async_copy(src, both_ref.at[pl.ds(i * TOK, TOK)], in_sems.at[i])
        for i, src in enumerate((mine_in, other_in))
    ]
    for load in loads:
        load.start()
    for load in loads:
        load.wait()
    stores = []
    for q in range(HALF):
        x = both_ref[:, pl.ds(q * BLOCK, BLOCK)]
        dy = both_ref[:, pl.ds(SIDE + q * BLOCK, BLOCK)]
        gate_up = dot(x, both_ref[:, pl.ds(2 * SIDE, 2 * BLOCK)], ((0,), (0,)))
        down = dot(dy, both_ref[:, pl.ds(2 * SIDE + 2 * BLOCK, BLOCK)], ((0,), (0,)))
        terms_ref[q, 0] = gate_up[:, :BLOCK].astype(BF16)
        terms_ref[q, 1] = gate_up[:, BLOCK:].astype(BF16)
        terms_ref[q, 2] = down.astype(BF16)
        for i, (out, rows) in enumerate(((top_out, pl.ds(0, TOP)), (low_out, pl.ds(TOP, BLOCK - TOP)))):
            stores.append(
                pltpu.make_async_copy(terms_ref.at[q, :, rows], out.at[q], out_sems.at[2 * q + i])
            )
            stores[-1].start()
    for store in stores:
        store.wait()


def weight_terms(mine, other):
    return pl.pallas_call(
        weight_kernel,
        out_shape=(
            jax.ShapeDtypeStruct((HALF, 3, TOP, BLOCK), BF16),
            jax.ShapeDtypeStruct((HALF, 3, BLOCK - TOP, BLOCK), BF16),
        ),
        in_specs=[ANYWHERE] * 2,
        out_specs=(ANYWHERE,) * 2,
        scratch_shapes=[
            pltpu.VMEM((2 * TOK, PACK), BF16),
            pltpu.VMEM((HALF, 3, BLOCK, BLOCK), BF16),
            pltpu.SemaphoreType.DMA((2,)),
            pltpu.SemaphoreType.DMA((2 * HALF,)),
        ],
        compiler_params=pltpu.CompilerParams(vmem_limit_bytes=WEIGHT_VMEM),
        cost_estimate=pl.CostEstimate(flops=800000000, bytes_accessed=6000000, transcendentals=0),
        name="weight_terms",
    )(mine, other)


def local(inputs, out_grad, codes, scales):
    place = jnp.stack([lax.axis_index("core"), lax.axis_index("zl")])
    acts = jnp.broadcast_to(jnp.stack([inputs, out_grad])[None], (N_YH, 2, TOK, 128))
    acts, codes = lax.optimization_barrier((acts, codes))
    acts = lax.all_to_all(acts, "yh", split_axis=0, concat_axis=0, tiled=True)

    weights = (codes.astype(F32) * scales.astype(F32)).astype(BF16)
    weights = lax.all_gather(weights, ROW, axis=0, tiled=False)

    same = gather_by_swap(acts, "zh", 4)
    upper = lax.ppermute(same[:2], Z, [(i, (i - 1) % N_Z) for i in range(N_Z)])
    lower = lax.ppermute(same[2:], Z, [(i, (i + 1) % N_Z) for i in range(N_Z)])

    keep, send, dx = forward(place, same, upper, lower, weights)
    dx = lax.all_to_all(dx, Z, split_axis=0, concat_axis=0, tiled=True)
    dx = jnp.sum(dx.astype(F32), axis=0).astype(BF16)
    dx = lax.all_to_all(dx, "yh", split_axis=0, concat_axis=0, tiled=True)
    input_grad = jnp.sum(dx.astype(F32), axis=0).astype(BF16)

    other = lax.ppermute(send, "core", [(0, 1), (1, 0)])
    top, low = weight_terms(keep, other)
    low = lax.psum_scatter(low, ("yl", "x"), scatter_dimension=0, tiled=False)
    top = lax.all_to_all(top, ("yl", "x"), split_axis=0, concat_axis=0, tiled=True)
    top = jnp.sum(top.astype(F32), axis=0)
    return input_grad, jnp.concatenate([top, low.astype(F32)], axis=1)


def solution(mesh):
    fine = Mesh(mesh.devices.reshape(tuple(SIZES.values())), tuple(SIZES))
    return jax.shard_map(
        local,
        mesh=fine,
        in_specs=(P(ROW, COL), P(ROW, COL), P(None, ROW, COL), P(None, ROW, COL)),
        out_specs=(P(ROW, COL), P(None, ROW, COL)),
        check_vma=False,
    )
```

time: 175 us -> 169 us (0.966)
  the two profiles are of different devices: /device:TPU:40 before, /device:TPU:8 now
where the time goes in v5:
time: 169 us
  blocking collectives  64.9 us (38%)
  waiting for transfers between devices  52.8 us (31%)
  starting transfers between devices  19.4 us (11%)
  between operations  14.1 us (8%)
  Pallas kernels  9.73 us (6%)
  other arithmetic  7.44 us (4%)
    all_to_all x1, blocking collectives, gather_by_swap(): return lax.all_to_all(copies, axis, split_axis=0, concat_axis=0, tiled=True)  33.8 us
    all_to_all x1, waiting for transfers between devices, local(): dx = lax.all_to_all(dx, Z, split_axis=0, concat_axis=0, tiled=True)  26.8 us
    all_to_all x1, blocking collectives, local(): acts = lax.all_to_all(acts, 'yh', split_axis=0, concat_axis=0, tiled=True)  16.8 us
    all_to_all x1, blocking collectives, local(): dx = lax.all_to_all(dx, 'yh', split_axis=0, concat_axis=0, tiled=True)  14.2 us
    all_to_all x1, waiting for transfers between devices, local(): lax.all_to_all(top, ('yl', 'x'), split_axis=0, concat_axis=0, tiled=True)  13.4 us
    ppermute x1, waiting for transfers between devices, local(): lower = lax.ppermute(same[2:], Z, [(i, (i + 1) % N_Z) for i in range(N_Z)])  9.82 us
    pallas_call x1, Pallas kernels, forward(): pl.pallas_call(forward_kernel, out_shape=(pack, pack, jax.ShapeDtypeStruc...  6.93 us
    all_to_all x1, starting transfers between devices, local(): lax.all_to_all(top, ('yl', 'x'), split_axis=0, concat_axis=0, tiled=True)  5.75 us
  transfers between devices with their start and end apart: 7, of which 4 were waited for; matrix products, arithmetic and copies ran while one was open for 2% of the time, Pallas kernels for 2%

profile of v5, /device:TPU:8, one launch (start us, length us, event | category | flops | bytes accessed | tf_op | source)
XLA Modules:
  0.0 168.8 jit_solution(9303171495368335686)
XLA Ops:
  7.2 0.0 all-gather.3.cloned.1.call-start
  7.2 0.7 bitcast_convert_fusion.1
  7.9 0.8 pad_maximum_fusion.1
  8.7 1.8 %multiply_convert_fusion = bf16[3,256,256]{2,1,0:T(8,128)(2,1)} fusion(bf16[3,256,256]{2,1,0:T(8,128)(2,1)} %param.6, f32[3,256]{1,0:T(4,128)S(1)} %bitcast_convert_fusion.1), kind=kLoop, calls=%fused_computation.2 | loop fusion | flops 589824 | bytes 789504 | tf_op jit(solution)/shard_map/convert_element_type | solution.py:190
  10.5 0.0 all-gather.3.cloned.1.call-update
  10.6 16.8 %all_to_all.25 = bf16[4,2,128,128]{3,2,1,0:T(8,128)(2,1)S(1)} all-to-all(bf16[4,2,128,128]{3,2,1,0:T(8,128)(2,1)S(1)} %broadcast_in_dim.4), channel_id=1, replica_groups=mesh['yl'=2,'x'=4,'core'=2,'yh'=4,'zh'=4,'zl'=2] {'yh'}, dimensions={0} | all-to-all | bytes 524288 | tf_op jit(solution)/shard_map/all_to_all | solution.py:188
  27.4 0.2 broadcast_in_dim.5
  27.6 33.8 %all_to_all.26.same_in = bf16[4,4,2,128,128]{4,3,2,1,0:T(8,128)(2,1)S(1)} all-to-all(bf16[4,4,2,128,128]{4,3,2,1,0:T(8,128)(2,1)S(1)} %broadcast_in_dim.5), channel_id=1, replica_groups=mesh['yl'=2,'x'=4,'core'=2,'yh'=4,'zh'=4,'zl'=2] {'zh'}, dimensions={0} | all-to-all | bytes 2097152 | tf_op jit(solution)/shard_map/all_to_all | solution.py:33
  61.5 0.1 fusion
  61.6 5.5 %collective-permute-start.1 = (bf16[2,4,2,128,128]{4,3,2,1,0:T(8,128)(2,1)S(1)}, bf16[2,4,2,128,128]{4,3,2,1,0:T(8,128)(2,1)S(1)}, u32[]{:S(2)}, u32[]{:S(2)}) collective-permute-start(bf16[2,4,2,128,128]{4,3,2,1,0:T(8,128)(2,1)S(1)} %get-tuple-element.16), channel_id=1, source_target_pairs={{0,1},{1,2},{2,3},{3,4},{4,5},{5,6},{6,7},{7,0},{8,9},{9,10},{10,1... | collective-permute-start | bytes 1572872 | tf_op jit(solution)/shard_map/ppermute | solution.py:195
  67.1 1.9 %collective-permute-start = (bf16[2,4,2,128,128]{4,3,2,1,0:T(8,128)(2,1)S(1)}, bf16[2,4,2,128,128]{4,3,2,1,0:T(8,128)(2,1)S(1)}, u32[]{:S(2)}, u32[]{:S(2)}) collective-permute-start(bf16[2,4,2,128,128]{4,3,2,1,0:T(8,128)(2,1)S(1)} %get-tuple-element.17), channel_id=1, source_target_pairs={{0,7},{1,0},{2,1},{3,2},{4,3},{5,4},{6,5},{7,6},{8,15},{9,8},{10,9... | collective-permute-start | bytes 1572872 | tf_op jit(solution)/shard_map/ppermute | solution.py:194
  69.0 0.1 pad_add_fusion.place_ref
  69.1 9.8 %collective-permute-done.1.lower_in = bf16[2,4,2,128,128]{4,3,2,1,0:T(8,128)(2,1)S(1)} collective-permute-done((bf16[2,4,2,128,128]{4,3,2,1,0:T(8,128)(2,1)S(1)}, bf16[2,4,2,128,128]{4,3,2,1,0:T(8,128)(2,1)S(1)}, u32[]{:S(2)}, u32[]{:S(2)}) %collective-permute-start.1) | collective-permute-done | bytes 524320 | tf_op jit(solution)/shard_map/ppermute | solution.py:195
  78.9 2.7 %collective-permute-done.upper_in = bf16[2,4,2,128,128]{4,3,2,1,0:T(8,128)(2,1)S(1)} collective-permute-done((bf16[2,4,2,128,128]{4,3,2,1,0:T(8,128)(2,1)S(1)}, bf16[2,4,2,128,128]{4,3,2,1,0:T(8,128)(2,1)S(1)}, u32[]{:S(2)}, u32[]{:S(2)}) %collective-permute-start) | collective-permute-done | bytes 524320 | tf_op jit(solution)/shard_map/ppermute | solution.py:194
  81.6 0.0 all-gather.3.cloned.1.call-done
  81.6 6.9 %forward.1 = (bf16[128,4864]{1,0:T(8,128)(2,1)S(1)}, bf16[128,4864]{1,0:T(8,128)(2,1)}, bf16[8,4,128,128]{3,2,1,0:T(8,128)(2,1)}) custom-call(s32[2]{0:T(128)S(1)} %pad_add_fusion.place_ref, bf16[4,4,2,128,128]{4,3,2,1,0:T(8,128)(2,1)S(1)} %all_to_all.26.same_in, bf16[2,4,2,128,128]{4,3,2,1,0:T(8,128)(2,1)S(1)} %collective-permute-done.upper_in, ...), custom_call_target="tpu_custom_call" | custom-call | flops 1400000000 | bytes 10000000 | tf_op jit(solution)/shard_map/forward/pallas_call | solution.py:114
  88.6 1.9 %collective-permute-start.2 = (bf16[128,4864]{1,0:T(8,128)(2,1)}, bf16[128,4864]{1,0:T(8,128)(2,1)S(1)}, u32[]{:S(2)}, u32[]{:S(2)}) collective-permute-start(bf16[128,4864]{1,0:T(8,128)(2,1)} %get-tuple-element.13), channel_id=1, source_target_pairs={{0,32},{32,0},{1,33},{33,1},{2,34},{34,2},{3,35},{35,3},{4,36},{36... | collective-permute-start | bytes 3735560 | tf_op jit(solution)/shard_map/ppermute | solution.py:203
  90.5 4.3 %all-to-all-start.2 = ((bf16[8,4,128,128]{3,2,1,0:T(8,128)(2,1)}), bf16[8,4,128,128]{3,2,1,0:T(8,128)(2,1)}, u32[]{:S(2)}, u32[]{:S(2)}) async-start(bf16[8,4,128,128]{3,2,1,0:T(8,128)(2,1)} %get-tuple-element.11), calls=%async_computation.2 | async-start | bytes 2097152 | tf_op jit(solution)/shard_map/all_to_all | solution.py:198
  94.7 0.0 reduce-scatter.2.cloned.1.call-start
  94.8 0.0 collective-permute-done.2.other_in
  94.8 2.8 %weight_terms.1 = (bf16[8,3,96,256]{3,2,1,0:T(8,128)(2,1)}, bf16[8,3,160,256]{3,2,1,0:T(8,128)(2,1)}) custom-call(bf16[128,4864]{1,0:T(8,128)(2,1)S(1)} %get-tuple-element.12.mine_in, bf16[128,4864]{1,0:T(8,128)(2,1)S(1)} %collective-permute-done.2.other_in), custom_call_target="tpu_custom_call" | custom-call | flops 800000000 | bytes 6000000 | tf_op jit(solution)/shard_map/weight_terms/pallas_call | solution.py:164
  97.6 0.0 reduce-scatter.2.cloned.1.call-update
  97.6 26.8 %all-to-all-done.2 = bf16[8,4,128,128]{3,2,1,0:T(8,128)(2,1)} async-done(((bf16[8,4,128,128]{3,2,1,0:T(8,128)(2,1)}), bf16[8,4,128,128]{3,2,1,0:T(8,128)(2,1)}, u32[]{:S(2)}, u32[]{:S(2)}) %all-to-all-start.2) | async-done | bytes 1048608 | tf_op jit(solution)/shard_map/all_to_all | solution.py:198
  124.5 1.4 reduce_sum.33
  125.8 14.2 %all_to_all.27 = bf16[4,128,128]{2,1,0:T(8,128)(2,1)S(1)} all-to-all(bf16[4,128,128]{2,1,0:T(8,128)(2,1)S(1)} %reduce_sum.33), channel_id=1, replica_groups=mesh['yl'=2,'x'=4,'core'=2,'yh'=4,'zh'=4,'zl'=2] {'yh'}, dimensions={0} | all-to-all | bytes 262144 | tf_op jit(solution)/shard_map/all_to_all | solution.py:200
  140.1 5.8 %all-to-all-start.4 = ((bf16[8,3,96,256]{3,2,1,0:T(8,128)(2,1)}), bf16[8,3,96,256]{3,2,1,0:T(8,128)(2,1)S(1)}, u32[]{:S(2)}, u32[]{:S(2)}) async-start(bf16[8,3,96,256]{3,2,1,0:T(8,128)(2,1)} %get-tuple-element.14), calls=%async_computation.4 | async-start | bytes 2359296 | tf_op jit(solution)/shard_map/all_to_all | solution.py:206
  145.8 0.6 reduce_sum.34
  146.5 13.4 %all-to-all-done.4 = bf16[8,3,96,256]{3,2,1,0:T(8,128)(2,1)S(1)} async-done(((bf16[8,3,96,256]{3,2,1,0:T(8,128)(2,1)}), bf16[8,3,96,256]{3,2,1,0:T(8,128)(2,1)S(1)}, u32[]{:S(2)}, u32[]{:S(2)}) %all-to-all-start.4) | async-done | bytes 1179680 | tf_op jit(solution)/shard_map/all_to_all | solution.py:206
  159.9 0.2 convert_reduce_fusion
  160.0 0.0 reduce-scatter.2.cloned.1.call-done
  160.0 1.0 bitcast_convert_fusion
  161.0 0.9 pad_maximum_fusion
  (1 shorter events, 0.0 us)
Async XLA Ops:
  7.2 74.4 %all-gather.3.cloned.1.call-start = ((), (), s32[]{:S(2)}) async-start(), calls=%async_computation.7 | async-start | bytes 6684672 | tf_op jit(solution)/shard_map/all_gather | solution.py:191
  61.6 17.3 %collective-permute-start.1 = (bf16[2,4,2,128,128]{4,3,2,1,0:T(8,128)(2,1)S(1)}, bf16[2,4,2,128,128]{4,3,2,1,0:T(8,128)(2,1)S(1)}, u32[]{:S(2)}, u32[]{:S(2)}) collective-permute-start(bf16[2,4,2,128,128]{4,3,2,1,0:T(8,128)(2,1)S(1)} %get-tuple-element.16), channel_id=1, source_target_pairs={{0,1},{1,2},{2,3},{3,4},{4,5},{5,6},{6,7},{7,0},{8,9},{9,10},{10,1... | collective-permute-start | bytes 1572872 | tf_op jit(solution)/shard_map/ppermute | solution.py:195
  67.1 14.5 %collective-permute-start = (bf16[2,4,2,128,128]{4,3,2,1,0:T(8,128)(2,1)S(1)}, bf16[2,4,2,128,128]{4,3,2,1,0:T(8,128)(2,1)S(1)}, u32[]{:S(2)}, u32[]{:S(2)}) collective-permute-start(bf16[2,4,2,128,128]{4,3,2,1,0:T(8,128)(2,1)S(1)} %get-tuple-element.17), channel_id=1, source_target_pairs={{0,7},{1,0},{2,1},{3,2},{4,3},{5,4},{6,5},{7,6},{8,15},{9,8},{10,9... | collective-permute-start | bytes 1572872 | tf_op jit(solution)/shard_map/ppermute | solution.py:194
  88.6 6.2 %collective-permute-start.2 = (bf16[128,4864]{1,0:T(8,128)(2,1)}, bf16[128,4864]{1,0:T(8,128)(2,1)S(1)}, u32[]{:S(2)}, u32[]{:S(2)}) collective-permute-start(bf16[128,4864]{1,0:T(8,128)(2,1)} %get-tuple-element.13), channel_id=1, source_target_pairs={{0,32},{32,0},{1,33},{33,1},{2,34},{34,2},{3,35},{35,3},{4,36},{36... | collective-permute-start | bytes 3735560 | tf_op jit(solution)/shard_map/ppermute | solution.py:203
  90.5 34.0 %all-to-all-start.2 = ((bf16[8,4,128,128]{3,2,1,0:T(8,128)(2,1)}), bf16[8,4,128,128]{3,2,1,0:T(8,128)(2,1)}, u32[]{:S(2)}, u32[]{:S(2)}) async-start(bf16[8,4,128,128]{3,2,1,0:T(8,128)(2,1)} %get-tuple-element.11), calls=%async_computation.2 | async-start | bytes 2097152 | tf_op jit(solution)/shard_map/all_to_all | solution.py:198
  94.7 65.3 %reduce-scatter.2.cloned.1.call-start = ((), (), s32[]{:S(2)}) async-start(), calls=%async_computation.6 | async-start | bytes 2211840 | tf_op jit(solution)/shard_map/reduce_scatter | solution.py:205
  140.1 19.8 %all-to-all-start.4 = ((bf16[8,3,96,256]{3,2,1,0:T(8,128)(2,1)}), bf16[8,3,96,256]{3,2,1,0:T(8,128)(2,1)S(1)}, u32[]{:S(2)}, u32[]{:S(2)}) async-start(bf16[8,3,96,256]{3,2,1,0:T(8,128)(2,1)} %get-tuple-element.14), calls=%async_computation.4 | async-start | bytes 2359296 | tf_op jit(solution)/shard_map/all_to_all | solution.py:206
Sparse Core Ops, SparseCore 0:
  10.7 52.1 all-gather.2
  98.5 47.2 reduce-scatter.1

commit v6 on v5

v6 whole, which is shorter than its diff:
```python
import jax
import jax.numpy as jnp
from jax import lax
from jax.experimental import pallas as pl
from jax.experimental.pallas import tpu as pltpu
from jax.sharding import Mesh, PartitionSpec as P

F32 = jnp.float32
BF16 = jnp.bfloat16
ROW = ("yl", "x", "core")
Z = ("zh", "zl")
COL = ("yh",) + Z
SIZES = {"yl": 2, "x": 4, "core": 2, "yh": 4, "zh": 4, "zl": 2}
N_ROW, N_YH, N_Z = 16, 4, 8
HALF = N_ROW // 2
TOK = 128
BLOCK = 256
SIDE = HALF * BLOCK
PACK = SIDE + 3 * BLOCK
FORWARD_VMEM = 49 * 1024 * 1024
WEIGHT_VMEM = 24 * 1024 * 1024
ANYWHERE = pl.BlockSpec(memory_space=pl.ANY)
SCALARS = pl.BlockSpec(memory_space=pltpu.SMEM)


def dot(a, b, dims):
    return lax.dot_general(a, b, (dims, ((), ())), preferred_element_type=F32)


def gather_by_swap(block, axis, size):
    copies = jnp.broadcast_to(block[None], (size,) + block.shape)
    return lax.all_to_all(copies, axis, split_axis=0, concat_axis=0, tiled=True)


def from_neighbours(same):
    upper = lax.ppermute(same[:2], Z, [(i, (i - 1) % N_Z) for i in range(N_Z)])
    lower = lax.ppermute(same[2:], Z, [(i, (i + 1) % N_Z) for i in range(N_Z)])
    return upper, lower


def prepare_kernel(x_ref, dy_ref, codes_ref, scales_ref, acts_ref, weights_ref):
    for y in range(N_YH):
        acts_ref[y, 0] = x_ref[...]
        acts_ref[y, 1] = dy_ref[...]
    weights_ref[...] = (codes_ref[...].astype(F32) * scales_ref[...].astype(F32)).astype(BF16)


def prepare(x, dy, codes, scales):
    whole = pl.BlockSpec(memory_space=pltpu.VMEM)
    return pl.pallas_call(
        prepare_kernel,
        out_shape=(
            jax.ShapeDtypeStruct((N_YH, 2, TOK, 128), BF16),
            jax.ShapeDtypeStruct(codes.shape, BF16),
        ),
        in_specs=[whole] * 4,
        out_specs=(whole,) * 2,
        compiler_params=pltpu.CompilerParams(vmem_limit_bytes=WEIGHT_VMEM),
        cost_estimate=pl.CostEstimate(flops=200000, bytes_accessed=1200000, transcendentals=0),
        name="prepare",
    )(x, dy, codes, scales)


def load_acts(same_in, upper_in, lower_in, same_ref, upper_ref, lower_ref, sems):
    loads = [
        pltpu.make_async_copy(src, dst, sems.at[i])
        for i, (src, dst) in enumerate(
            ((same_in, same_ref), (upper_in, upper_ref), (lower_in, lower_ref))
        )
    ]
    for load in loads:
        load.start()
    return loads


def load_weights(core, first, count, w_in, w_ref, sems):
    loads = []
    for i in range(N_ROW):
        r = 2 * (i % HALF) + (core if i < HALF else 1 - core)
        src = w_in.at[r, pl.ds(first, count)]
        dst = w_ref.at[pl.ds(first, count), pl.ds(i * BLOCK, BLOCK)]
        loads.append(pltpu.make_async_copy(src, dst, sems.at[i]))
        loads[-1].start()
    return loads


def widen(place_ref, side, q, same_ref, upper_ref, lower_ref):
    core, first = place_ref[0], place_ref[1] == 0
    parity = core if side == 0 else 1 - core
    y, zh = q // 2, (q % 2) * 2 + parity
    mine, other = same_ref[zh, y], (lower_ref if q % 2 else upper_ref)[parity, y]
    return jnp.concatenate([jnp.where(first, mine, other), jnp.where(first, other, mine)], axis=1)


def gates_kernel(
    place_ref, same_in, upper_in, lower_in, w_in, keep_out, send_out, gate_out,
    same_ref, upper_ref, lower_ref, w_ref, acts_ref, gate_ref, in_sems, w_sems, out_sems,
):
    loads = load_acts(same_in, upper_in, lower_in, same_ref, upper_ref, lower_ref, in_sems)
    w_loads = load_weights(place_ref[0], 0, 2, w_in, w_ref, w_sems)
    for load in loads:
        load.wait()
    sums = [jnp.zeros((TOK, BLOCK), F32) for _ in range(2)]
    stores = []
    for side in range(2):
        for half in range(2):
            for q in range(4 * half, 4 * half + 4):
                wide = widen(place_ref, side, q, same_ref, upper_ref, lower_ref)
                acts_ref[side, :, pl.ds(q * BLOCK, BLOCK)] = wide
                w_loads[side * HALF + q].wait()
            rows = pl.ds((side * 2 + half) * 4 * BLOCK, 4 * BLOCK)
            x = acts_ref[side, :, pl.ds(half * 4 * BLOCK, 4 * BLOCK)]
            for p in range(2):
                sums[p] += dot(x, w_ref[p, rows], ((1,), (0,)))
        out = keep_out if side == 0 else send_out
        stores.append(pltpu.make_async_copy(acts_ref.at[side], out, out_sems.at[side]))
        stores[-1].start()
    for p in range(2):
        gate_ref[p] = sums[p]
    stores.append(pltpu.make_async_copy(gate_ref, gate_out, out_sems.at[2]))
    stores[-1].start()
    for store in stores:
        store.wait()


def gates(place, same, upper, lower, weights):
    acts = jax.ShapeDtypeStruct((TOK, SIDE), BF16)
    return pl.pallas_call(
        gates_kernel,
        out_shape=(acts, acts, jax.ShapeDtypeStruct((2, TOK, BLOCK), F32)),
        in_specs=[SCALARS] + [ANYWHERE] * 4,
        out_specs=(ANYWHERE,) * 3,
        scratch_shapes=[
            pltpu.VMEM(same.shape, BF16),
            pltpu.VMEM(upper.shape, BF16),
            pltpu.VMEM(lower.shape, BF16),
            pltpu.VMEM((2, N_ROW * BLOCK, BLOCK), BF16),
            pltpu.VMEM((2, TOK, SIDE), BF16),
            pltpu.VMEM((2, TOK, BLOCK), F32),
            pltpu.SemaphoreType.DMA((3,)),
            pltpu.SemaphoreType.DMA((N_ROW,)),
            pltpu.SemaphoreType.DMA((3,)),
        ],
        compiler_params=pltpu.CompilerParams(vmem_limit_bytes=FORWARD_VMEM),
        cost_estimate=pl.CostEstimate(flops=540000000, bytes_accessed=6000000, transcendentals=0),
        name="gates",
    )(place, same, upper, lower, weights)


def hidden_kernel(
    place_ref, same_in, upper_in, lower_in, w_in, gate_in, keep_out, send_out, dx_out,
    same_ref, upper_ref, lower_ref, w_ref, gate_ref, pack_ref, dx_ref, in_sems, w_sems, w_sems2, out_sems,
):
    core = place_ref[0]
    loads = load_acts(same_in, upper_in, lower_in, same_ref, upper_ref, lower_ref, in_sems)
    loads.append(pltpu.make_async_copy(gate_in, gate_ref, in_sems.at[3]))
    loads[-1].start()
    w_loads = load_weights(core, 2, 1, w_in, w_ref, w_sems)
    w_loads2 = load_weights(core, 0, 2, w_in, w_ref, w_sems2)
    for load in loads:
        load.wait()
    hidden_grad = jnp.zeros((TOK, BLOCK), F32)
    stores = []
    for side in range(2):
        for half in range(2):
            for q in range(4 * half, 4 * half + 4):
                wide = widen(place_ref, side, q, same_ref, upper_ref, lower_ref)
                pack_ref[side, :, pl.ds(q * BLOCK, BLOCK)] = wide
                w_loads[side * HALF + q].wait()
            rows = pl.ds((side * 2 + half) * 4 * BLOCK, 4 * BLOCK)
            dy = pack_ref[side, :, pl.ds(half * 4 * BLOCK, 4 * BLOCK)]
            hidden_grad += dot(dy, w_ref[2, rows], ((1,), (0,)))
        out, cols = (keep_out if side == 0 else send_out), pl.ds(0, SIDE)
        stores.append(
            pltpu.make_async_copy(pack_ref.at[side, :, cols], out.at[:, cols], out_sems.at[side])
        )
        stores[-1].start()
    gate, up = gate_ref[0], gate_ref[1]
    sig = 1.0 / (1.0 + jnp.exp(-gate))
    act = gate * sig
    gate_grad = (hidden_grad * up * sig * (1.0 + gate * (1.0 - sig))).astype(BF16)
    up_grad = (hidden_grad * act).astype(BF16)
    hidden = (act * up).astype(BF16)
    for side in range(2):
        for p, value in enumerate((gate_grad, up_grad, hidden)):
            pack_ref[side, :, pl.ds(SIDE + p * BLOCK, BLOCK)] = value
        out, cols = (keep_out if side == 0 else send_out), pl.ds(SIDE, 3 * BLOCK)
        stores.append(
            pltpu.make_async_copy(pack_ref.at[side, :, cols], out.at[:, cols], out_sems.at[2 + side])
        )
        stores[-1].start()
    for i in range(N_ROW):
        q, parity = i % HALF, (core if i < HALF else 1 - core)
        rows = pl.ds(i * BLOCK, BLOCK)
        w_loads2[i].wait()
        dx = dot(gate_grad, w_ref[0, rows], ((1,), (1,)))
        dx = (dx + dot(up_grad, w_ref[1, rows], ((1,), (1,)))).astype(BF16)
        y, z = q // 2, 4 * (q % 2) + 2 * parity
        dx_ref[z, y] = dx[:, :TOK]
        dx_ref[z + 1, y] = dx[:, TOK:]
    stores.append(pltpu.make_async_copy(dx_ref, dx_out, out_sems.at[4]))
    stores[-1].start()
    for store in stores:
        store.wait()


def hidden_grads(place, same, upper, lower, weights, gate):
    pack = jax.ShapeDtypeStruct((TOK, PACK), BF16)
    return pl.pallas_call(
        hidden_kernel,
        out_shape=(pack, pack, jax.ShapeDtypeStruct((N_Z, N_YH, TOK, 128), BF16)),
        in_specs=[SCALARS] + [ANYWHERE] * 5,
        out_specs=(ANYWHERE,) * 3,
        scratch_shapes=[
            pltpu.VMEM(same.shape, BF16),
            pltpu.VMEM(upper.shape, BF16),
            pltpu.VMEM(lower.shape, BF16),
            pltpu.VMEM((3, N_ROW * BLOCK, BLOCK), BF16),
            pltpu.VMEM((2, TOK, BLOCK), F32),
            pltpu.VMEM((2, TOK, PACK), BF16),
            pltpu.VMEM((N_Z, N_YH, TOK, 128), BF16),
            pltpu.SemaphoreType.DMA((4,)),
            pltpu.SemaphoreType.DMA((N_ROW,)),
            pltpu.SemaphoreType.DMA((N_ROW,)),
            pltpu.SemaphoreType.DMA((5,)),
        ],
        compiler_params=pltpu.CompilerParams(vmem_limit_bytes=FORWARD_VMEM),
        cost_estimate=pl.CostEstimate(flops=800000000, bytes_accessed=9000000, transcendentals=32768),
        name="hidden_grads",
    )(place, same, upper, lower, weights, gate)


def weight_kernel(
    x_in, other_x_in, pack_in, other_pack_in, out, x_ref, pack_ref, terms_ref, in_sems, out_sems
):
    loads = []
    for i, (src, dst) in enumerate(
        ((x_in, x_ref), (other_x_in, x_ref), (pack_in, pack_ref), (other_pack_in, pack_ref))
    ):
        rows = pl.ds((i % 2) * TOK, TOK)
        loads.append(pltpu.make_async_copy(src, dst.at[rows], in_sems.at[i]))
        loads[-1].start()
    for load in loads:
        load.wait()
    stores = []
    for q in range(HALF):
        cols = pl.ds(q * BLOCK, BLOCK)
        gate_up = dot(x_ref[:, cols], pack_ref[:, pl.ds(SIDE, 2 * BLOCK)], ((0,), (0,)))
        down = dot(pack_ref[:, cols], pack_ref[:, pl.ds(SIDE + 2 * BLOCK, BLOCK)], ((0,), (0,)))
        terms_ref[q, 0] = gate_up[:, :BLOCK].astype(BF16)
        terms_ref[q, 1] = gate_up[:, BLOCK:].astype(BF16)
        terms_ref[q, 2] = down.astype(BF16)
        stores.append(pltpu.make_async_copy(terms_ref.at[q], out.at[q], out_sems.at[q]))
        stores[-1].start()
    for store in stores:
        store.wait()


def weight_terms(x, other_x, pack, other_pack):
    return pl.pallas_call(
        weight_kernel,
        out_shape=jax.ShapeDtypeStruct((HALF, 3, BLOCK, BLOCK), BF16),
        in_specs=[ANYWHERE] * 4,
        out_specs=ANYWHERE,
        scratch_shapes=[
            pltpu.VMEM((2 * TOK, SIDE), BF16),
            pltpu.VMEM((2 * TOK, PACK), BF16),
            pltpu.VMEM((HALF, 3, BLOCK, BLOCK), BF16),
            pltpu.SemaphoreType.DMA((4,)),
            pltpu.SemaphoreType.DMA((HALF,)),
        ],
        compiler_params=pltpu.CompilerParams(vmem_limit_bytes=WEIGHT_VMEM),
        cost_estimate=pl.CostEstimate(flops=800000000, bytes_accessed=6000000, transcendentals=0),
        name="weight_terms",
    )(x, other_x, pack, other_pack)


def local(inputs, out_grad, codes, scales):
    place = jnp.stack([lax.axis_index("core"), lax.axis_index("zl")])
    swap = [(0, 1), (1, 0)]
    acts, weights = prepare(inputs, out_grad, codes, scales)
    weights = lax.all_gather(weights, ROW, axis=0, tiled=False)

    acts = lax.all_to_all(acts, "yh", split_axis=0, concat_axis=0, tiled=True)
    x = gather_by_swap(acts[:, 0], "zh", 4)
    x_upper, x_lower = from_neighbours(x)
    dy = gather_by_swap(acts[:, 1], "zh", 4)
    dy_upper, dy_lower = from_neighbours(dy)

    keep_x, send_x, gate = gates(place, x, x_upper, x_lower, weights)
    other_x = lax.ppermute(send_x, "core", swap)
    keep, send, dx = hidden_grads(place, dy, dy_upper, dy_lower, weights, gate)
    other = lax.ppermute(send, "core", swap)
    terms = weight_terms(keep_x, other_x, keep, other)
    terms = lax.psum_scatter(terms, ("yl", "x"), scatter_dimension=0, tiled=False)

    dx = lax.all_to_all(dx, Z, split_axis=0, concat_axis=0, tiled=True)
    dx = jnp.sum(dx.astype(F32), axis=0).astype(BF16)
    dx = lax.all_to_all(dx, "yh", split_axis=0, concat_axis=0, tiled=True)
    input_grad = jnp.sum(dx.astype(F32), axis=0).astype(BF16)
    return input_grad, terms.astype(F32)


def solution(mesh):
    fine = Mesh(mesh.devices.reshape(tuple(SIZES.values())), tuple(SIZES))
    return jax.shard_map(
        local,
        mesh=fine,
        in_specs=(P(ROW, COL), P(ROW, COL), P(None, ROW, COL), P(None, ROW, COL)),
        out_specs=(P(ROW, COL), P(None, ROW, COL)),
        check_vma=False,
    )
```

time: 169 us -> 164 us (0.970)
  the two profiles are of different devices: /device:TPU:8 before, /device:TPU:40 now
where the time goes in v6:
time: 164 us; the launch traced here: 163 us
  blocking collectives  84.4 us (51%)
  starting transfers between devices  22 us (13%)
  waiting for transfers between devices  20.7 us (13%)
  Pallas kernels  15 us (9%)
  between operations  14.2 us (9%)
  local copies, waits for them, and re-layouts  4.29 us (3%)
  other arithmetic  2.8 us (2%)
    all_to_all x1, blocking collectives, local(): dx = lax.all_to_all(dx, Z, split_axis=0, concat_axis=0, tiled=True)  33.6 us
    all_to_all x1, blocking collectives, gather_by_swap(): return lax.all_to_all(copies, axis, split_axis=0, concat_axis=0, tiled=True)  24.4 us
    all_to_all x1, blocking collectives, local(): acts = lax.all_to_all(acts, 'yh', split_axis=0, concat_axis=0, tiled=True)  13.6 us
    all_to_all x1, blocking collectives, local(): dx = lax.all_to_all(dx, 'yh', split_axis=0, concat_axis=0, tiled=True)  12.8 us
    reduce_scatter x1, waiting for transfers between devices, local(): lax.psum_scatter(terms, ('yl', 'x'), scatter_dimension=0, tiled=False)  9.78 us
    ppermute x2, starting transfers between devices, from_neighbours(): upper = lax.ppermute(same[:2], Z, [(i, (i - 1) % N_Z) for i in range(N_Z)])  8.52 us
    all_to_all x1, waiting for transfers between devices, gather_by_swap(): return lax.all_to_all(copies, axis, split_axis=0, concat_axis=0, tiled=True)  8.51 us
    pallas_call x1, Pallas kernels, hidden_grads(): pl.pallas_call(hidden_kernel, out_shape=(pack, pack, jax.ShapeDtypeStruct...  8 us
  transfers between devices with their start and end apart: 9, of which 4 were waited for; matrix products, arithmetic and copies ran while one was open for 1% of the time, Pallas kernels for 2%

profile of v6, /device:TPU:40, one launch (start us, length us, event | category | flops | bytes accessed | tf_op | source)
XLA Modules:
  0.0 163.3 jit_solution(6485147561449767575)
XLA Ops:
  7.2 0.0 all-gather.3.cloned.1.call-start
  7.2 0.7 copy.8.scales_ref
  7.9 0.0 copy-start
  7.9 1.0 copy-done
  8.9 0.0 copy-start.1
  8.9 0.8 copy-done.1
  9.7 0.0 copy-start.2
  9.7 0.8 copy-done.2
  10.4 0.9 prepare.1
  11.3 0.0 all-gather.3.cloned.1.call-update
  11.3 13.6 %all_to_all.25 = bf16[4,2,128,128]{3,2,1,0:T(8,128)(2,1)S(1)} all-to-all(bf16[4,2,128,128]{3,2,1,0:T(8,128)(2,1)S(1)} %get-tuple-element.10), channel_id=1, replica_groups=mesh['yl'=2,'x'=4,'core'=2,'yh'=4,'zh'=4,'zl'=2] {'yh'}, dimensions={0} | all-to-all | bytes 524288 | tf_op jit(solution)/shard_map/all_to_all | solution.py:284
  24.9 0.1 broadcast_in_dim.17
  25.0 24.4 %all_to_all.26.same_in = bf16[4,4,128,128]{3,2,1,0:T(8,128)(2,1)S(1)} all-to-all(bf16[4,4,128,128]{3,2,1,0:T(8,128)(2,1)S(1)} %broadcast_in_dim.17), channel_id=1, replica_groups=mesh['yl'=2,'x'=4,'core'=2,'yh'=4,'zh'=4,'zl'=2] {'zh'}, dimensions={0} | all-to-all | bytes 1048576 | tf_op jit(solution)/shard_map/all_to_all | solution.py:32
  49.4 0.9 broadcast_in_dim.15
  50.3 3.5 %all-to-all-start.1 = ((bf16[4,4,128,128]{3,2,1,0:T(8,128)(2,1)}), bf16[4,4,128,128]{3,2,1,0:T(8,128)(2,1)S(1)}, u32[]{:S(2)}, u32[]{:S(2)}) async-start(bf16[4,4,128,128]{3,2,1,0:T(8,128)(2,1)} %broadcast_in_dim.15), calls=%async_computation.1 | async-start | bytes 1048576 | tf_op jit(solution)/shard_map/all_to_all | solution.py:32
  53.8 0.0 reduce-scatter.2.cloned.1.call-start
  53.9 2.5 %collective-permute-start.3 = (bf16[2,4,128,128]{3,2,1,0:T(8,128)(2,1)S(1)}, bf16[2,4,128,128]{3,2,1,0:T(8,128)(2,1)S(1)}, u32[]{:S(2)}, u32[]{:S(2)}) collective-permute-start(bf16[2,4,128,128]{3,2,1,0:T(8,128)(2,1)S(1)} %get-tuple-element.18), channel_id=1, source_target_pairs={{0,1},{1,2},{2,3},{3,4},{4,5},{5,6},{6,7},{7,0},{8,9},{9,10},{10,1... | collective-permute-start | bytes 786440 | tf_op jit(solution)/shard_map/ppermute | solution.py:37
  56.4 4.5 %collective-permute-start.2 = (bf16[2,4,128,128]{3,2,1,0:T(8,128)(2,1)S(1)}, bf16[2,4,128,128]{3,2,1,0:T(8,128)(2,1)S(1)}, u32[]{:S(2)}, u32[]{:S(2)}) collective-permute-start(bf16[2,4,128,128]{3,2,1,0:T(8,128)(2,1)S(1)} %get-tuple-element.19), channel_id=1, source_target_pairs={{0,7},{1,0},{2,1},{3,2},{4,3},{5,4},{6,5},{7,6},{8,15},{9,8},{10,9... | collective-permute-start | bytes 786440 | tf_op jit(solution)/shard_map/ppermute | solution.py:36
  61.0 8.5 %all-to-all-done.1.same_in = bf16[4,4,128,128]{3,2,1,0:T(8,128)(2,1)S(1)} async-done(((bf16[4,4,128,128]{3,2,1,0:T(8,128)(2,1)}), bf16[4,4,128,128]{3,2,1,0:T(8,128)(2,1)S(1)}, u32[]{:S(2)}, u32[]{:S(2)}) %all-to-all-start.1) | async-done | bytes 524320 | tf_op jit(solution)/shard_map/all_to_all | solution.py:32
  69.5 3.1 %collective-permute-start.1 = (bf16[2,4,128,128]{3,2,1,0:T(8,128)(2,1)S(1)}, bf16[2,4,128,128]{3,2,1,0:T(8,128)(2,1)S(1)}, u32[]{:S(2)}, u32[]{:S(2)}) collective-permute-start(bf16[2,4,128,128]{3,2,1,0:T(8,128)(2,1)S(1)} %get-tuple-element.20), channel_id=1, source_target_pairs={{0,1},{1,2},{2,3},{3,4},{4,5},{5,6},{6,7},{7,0},{8,9},{9,10},{10,1... | collective-permute-start | bytes 786440 | tf_op jit(solution)/shard_map/ppermute | solution.py:37
  72.6 4.0 %collective-permute-start = (bf16[2,4,128,128]{3,2,1,0:T(8,128)(2,1)S(1)}, bf16[2,4,128,128]{3,2,1,0:T(8,128)(2,1)S(1)}, u32[]{:S(2)}, u32[]{:S(2)}) collective-permute-start(bf16[2,4,128,128]{3,2,1,0:T(8,128)(2,1)S(1)} %get-tuple-element.21), channel_id=1, source_target_pairs={{0,7},{1,0},{2,1},{3,2},{4,3},{5,4},{6,5},{7,6},{8,15},{9,8},{10,9... | collective-permute-start | bytes 786440 | tf_op jit(solution)/shard_map/ppermute | solution.py:36
  76.6 0.1 pad_add_fusion.place_ref
  76.7 0.0 collective-permute-done.3.lower_in
  76.7 0.0 collective-permute-done.2.upper_in
  76.7 0.0 all-gather.3.cloned.1.call-done
  76.7 3.4 %gates.1 = (bf16[128,2048]{1,0:T(8,128)(2,1)S(1)}, bf16[128,2048]{1,0:T(8,128)(2,1)S(1)}, f32[2,128,256]{2,1,0:T(8,128)S(1)}) custom-call(s32[2]{0:T(128)S(1)} %pad_add_fusion.place_ref, bf16[4,4,128,128]{3,2,1,0:T(8,128)(2,1)S(1)} %all_to_all.26.same_in, bf16[2,4,128,128]{3,2,1,0:T(8,128)(2,1)S(1)} %collective-permute-done.2.upper_in, ...), custom_call_target="tpu_custom_call" | custom-call | flops 540000000 | bytes 6000000 | tf_op jit(solution)/shard_map/gates/pallas_call | solution.py:128
  80.1 0.0 collective-permute-done.1.lower_in
  80.1 0.8 collective-permute-done.upper_in
  80.9 8.0 %hidden_grads.1 = (bf16[128,2816]{1,0:T(8,128)(2,1)S(1)}, bf16[128,2816]{1,0:T(8,128)(2,1)S(1)}, bf16[8,4,128,128]{3,2,1,0:T(8,128)(2,1)S(1)}) custom-call(s32[2]{0:T(128)S(1)} %pad_add_fusion.place_ref, bf16[4,4,128,128]{3,2,1,0:T(8,128)(2,1)S(1)} %all-to-all-done.1.same_in, bf16[2,4,128,128]{3,2,1,0:T(8,128)(2,1)S(1)} %collective-permute-done.upper_in, ...), custom_call_target="tpu_custom_call" | custom-call | flops 800000000 | bytes 9000000 | tf_op jit(solution)/shard_map/hidden_grads/pallas_call | solution.py:209
  88.9 1.9 %collective-permute-start.5 = (bf16[128,2816]{1,0:T(8,128)(2,1)S(1)}, bf16[128,2816]{1,0:T(8,128)(2,1)S(1)}, u32[]{:S(2)}, u32[]{:S(2)}) collective-permute-start(bf16[128,2816]{1,0:T(8,128)(2,1)S(1)} %get-tuple-element.17), channel_id=1, source_target_pairs={{0,32},{32,0},{1,33},{33,1},{2,34},{34,2},{3,35},{35,3},{4,36},{36... | collective-permute-start | bytes 2162696 | tf_op jit(solution)/shard_map/ppermute | solution.py:293
  90.8 2.4 %collective-permute-start.4 = (bf16[128,2048]{1,0:T(8,128)(2,1)S(1)}, bf16[128,2048]{1,0:T(8,128)(2,1)S(1)}, u32[]{:S(2)}, u32[]{:S(2)}) collective-permute-start(bf16[128,2048]{1,0:T(8,128)(2,1)S(1)} %get-tuple-element.15), channel_id=1, source_target_pairs={{0,32},{32,0},{1,33},{33,1},{2,34},{34,2},{3,35},{35,3},{4,36},{36... | collective-permute-start | bytes 1572872 | tf_op jit(solution)/shard_map/ppermute | solution.py:291
  93.2 1.5 collective-permute-done.4.other_x_in
  94.7 0.0 collective-permute-done.5.other_pack_in
  94.7 2.7 %weight_terms.1 = bf16[8,3,256,256]{3,2,1,0:T(8,128)(2,1)} custom-call(bf16[128,2048]{1,0:T(8,128)(2,1)S(1)} %get-tuple-element.14.x_in, bf16[128,2048]{1,0:T(8,128)(2,1)S(1)} %collective-permute-done.4.other_x_in, bf16[128,2816]{1,0:T(8,128)(2,1)S(1)} %get-tuple-element.16.pack_in, bf16[128,2816]{1,0:T(8,128)(2,1)S(1)} %collective-permute-done.5.other_pack_in), custom_call_target="tpu_custom_call" | custom-call | flops 800000000 | bytes 6000000 | tf_op jit(solution)/shard_map/weight_terms/pallas_call | solution.py:260
  97.5 0.0 reduce-scatter.2.cloned.1.call-update
  97.5 33.6 %all_to_all.27 = bf16[8,4,128,128]{3,2,1,0:T(8,128)(2,1)S(1)} all-to-all(bf16[8,4,128,128]{3,2,1,0:T(8,128)(2,1)S(1)} %get-tuple-element.13), channel_id=1, replica_groups=mesh['yl'=2,'x'=4,'core'=2,'yh'=4,'zh'=4,'zl'=2] {'zh','zl'}, dimensions={0} | all-to-all | bytes 2097152 | tf_op jit(solution)/shard_map/all_to_all | solution.py:297
  131.1 0.1 reduce_sum.24
  131.3 12.8 %all_to_all.28 = bf16[4,128,128]{2,1,0:T(8,128)(2,1)S(1)} all-to-all(bf16[4,128,128]{2,1,0:T(8,128)(2,1)S(1)} %reduce_sum.24), channel_id=1, replica_groups=mesh['yl'=2,'x'=4,'core'=2,'yh'=4,'zh'=4,'zl'=2] {'yh'}, dimensions={0} | all-to-all | bytes 262144 | tf_op jit(solution)/shard_map/all_to_all | solution.py:299
  144.1 0.6 reduce_sum.25
  144.7 9.8 %reduce-scatter.2.cloned.1.call-done = bf16[1,3,256,256]{3,2,1,0:T(8,128)(2,1)} async-done(((bf16[8,3,256,256]{3,2,1,0:T(8,128)(2,1)}), bf16[1,3,256,256]{3,2,1,0:T(8,128)(2,1)}) %reduce-scatter.2.cloned.1.call-update) | async-done | bytes 393232 | tf_op jit(solution)/shard_map/reduce_scatter | solution.py:295
  154.5 1.9 %bitcast_convert_fusion = f32[3,256,256]{2,1,0:T(8,128)} fusion(bf16[1,3,256,256]{3,2,1,0:T(8,128)(2,1)} %reduce-scatter.2.cloned.1.call-done), kind=kLoop, calls=%fused_computation | loop fusion | flops 196608 | bytes 1179648 | tf_op jit(solution)/shard_map/convert_element_type | solution.py:301
  (3 shorter events, 0.1 us)
Async XLA Ops:
  7.2 69.5 %all-gather.3.cloned.1.call-start = ((), (), s32[]{:S(2)}) async-start(), calls=%async_computation.7 | async-start | bytes 6684672 | tf_op jit(solution)/shard_map/all_gather | solution.py:282
  7.9 1.0 copy-start
  8.9 0.8 copy-start.1
  9.7 0.8 copy-start.2
  50.3 19.2 %all-to-all-start.1 = ((bf16[4,4,128,128]{3,2,1,0:T(8,128)(2,1)}), bf16[4,4,128,128]{3,2,1,0:T(8,128)(2,1)S(1)}, u32[]{:S(2)}, u32[]{:S(2)}) async-start(bf16[4,4,128,128]{3,2,1,0:T(8,128)(2,1)} %broadcast_in_dim.15), calls=%async_computation.1 | async-start | bytes 1048576 | tf_op jit(solution)/shard_map/all_to_all | solution.py:32
  53.8 100.7 %reduce-scatter.2.cloned.1.call-start = ((), (), s32[]{:S(2)}) async-start(), calls=%async_computation.6 | async-start | bytes 3538944 | tf_op jit(solution)/shard_map/reduce_scatter | solution.py:295
  53.9 22.8 %collective-permute-start.3 = (bf16[2,4,128,128]{3,2,1,0:T(8,128)(2,1)S(1)}, bf16[2,4,128,128]{3,2,1,0:T(8,128)(2,1)S(1)}, u32[]{:S(2)}, u32[]{:S(2)}) collective-permute-start(bf16[2,4,128,128]{3,2,1,0:T(8,128)(2,1)S(1)} %get-tuple-element.18), channel_id=1, source_target_pairs={{0,1},{1,2},{2,3},{3,4},{4,5},{5,6},{6,7},{7,0},{8,9},{9,10},{10,1... | collective-permute-start | bytes 786440 | tf_op jit(solution)/shard_map/ppermute | solution.py:37
  56.4 20.3 %collective-permute-start.2 = (bf16[2,4,128,128]{3,2,1,0:T(8,128)(2,1)S(1)}, bf16[2,4,128,128]{3,2,1,0:T(8,128)(2,1)S(1)}, u32[]{:S(2)}, u32[]{:S(2)}) collective-permute-start(bf16[2,4,128,128]{3,2,1,0:T(8,128)(2,1)S(1)} %get-tuple-element.19), channel_id=1, source_target_pairs={{0,7},{1,0},{2,1},{3,2},{4,3},{5,4},{6,5},{7,6},{8,15},{9,8},{10,9... | collective-permute-start | bytes 786440 | tf_op jit(solution)/shard_map/ppermute | solution.py:36
  69.5 10.5 %collective-permute-start.1 = (bf16[2,4,128,128]{3,2,1,0:T(8,128)(2,1)S(1)}, bf16[2,4,128,128]{3,2,1,0:T(8,128)(2,1)S(1)}, u32[]{:S(2)}, u32[]{:S(2)}) collective-permute-start(bf16[2,4,128,128]{3,2,1,0:T(8,128)(2,1)S(1)} %get-tuple-element.20), channel_id=1, source_target_pairs={{0,1},{1,2},{2,3},{3,4},{4,5},{5,6},{6,7},{7,0},{8,9},{9,10},{10,1... | collective-permute-start | bytes 786440 | tf_op jit(solution)/shard_map/ppermute | solution.py:37
  72.6 8.3 %collective-permute-start = (bf16[2,4,128,128]{3,2,1,0:T(8,128)(2,1)S(1)}, bf16[2,4,128,128]{3,2,1,0:T(8,128)(2,1)S(1)}, u32[]{:S(2)}, u32[]{:S(2)}) collective-permute-start(bf16[2,4,128,128]{3,2,1,0:T(8,128)(2,1)S(1)} %get-tuple-element.21), channel_id=1, source_target_pairs={{0,7},{1,0},{2,1},{3,2},{4,3},{5,4},{6,5},{7,6},{8,15},{9,8},{10,9... | collective-permute-start | bytes 786440 | tf_op jit(solution)/shard_map/ppermute | solution.py:36
  88.9 5.9 %collective-permute-start.5 = (bf16[128,2816]{1,0:T(8,128)(2,1)S(1)}, bf16[128,2816]{1,0:T(8,128)(2,1)S(1)}, u32[]{:S(2)}, u32[]{:S(2)}) collective-permute-start(bf16[128,2816]{1,0:T(8,128)(2,1)S(1)} %get-tuple-element.17), channel_id=1, source_target_pairs={{0,32},{32,0},{1,33},{33,1},{2,34},{34,2},{3,35},{35,3},{4,36},{36... | collective-permute-start | bytes 2162696 | tf_op jit(solution)/shard_map/ppermute | solution.py:293
  90.8 3.9 %collective-permute-start.4 = (bf16[128,2048]{1,0:T(8,128)(2,1)S(1)}, bf16[128,2048]{1,0:T(8,128)(2,1)S(1)}, u32[]{:S(2)}, u32[]{:S(2)}) collective-permute-start(bf16[128,2048]{1,0:T(8,128)(2,1)S(1)} %get-tuple-element.15), channel_id=1, source_target_pairs={{0,32},{32,0},{1,33},{33,1},{2,34},{34,2},{3,35},{35,3},{4,36},{36... | collective-permute-start | bytes 1572872 | tf_op jit(solution)/shard_map/ppermute | solution.py:291
Sparse Core Ops, SparseCore 0:
  11.4 51.7 all-gather.2
  97.6 56.7 reduce-scatter.1

commit v7 on v5

v7 whole, which is shorter than its diff:
```python
import jax
import jax.numpy as jnp
from jax import lax
from jax.experimental import pallas as pl
from jax.experimental.pallas import tpu as pltpu
from jax.sharding import Mesh, PartitionSpec as P

F32 = jnp.float32
BF16 = jnp.bfloat16
ROW = ("yl", "x", "core")
Z = ("zh", "zl")
COL = ("yh",) + Z
SIZES = {"yl": 2, "x": 4, "core": 2, "yh": 4, "zh": 4, "zl": 2}
N_ROW, N_YH, N_Z = 16, 4, 8
HALF = N_ROW // 2
TOK = 128
BLOCK = 256
SIDE = HALF * BLOCK
SMALL_VMEM = 24 * 1024 * 1024
LARGE_VMEM = 50 * 1024 * 1024
ANYWHERE = pl.BlockSpec(memory_space=pl.ANY)
SCALARS = pl.BlockSpec(memory_space=pltpu.SMEM)


def dot(a, b, dims):
    return lax.dot_general(a, b, (dims, ((), ())), preferred_element_type=F32)


def gather_by_swap(block, axis, size):
    copies = jnp.broadcast_to(block[None], (size,) + block.shape)
    return lax.all_to_all(copies, axis, split_axis=0, concat_axis=0, tiled=True)


def arrange_kernel(place_ref, acts_in, keep_out, send_out, sems):
    copies = []
    for side, out in enumerate((keep_out, send_out)):
        parity = place_ref[0] if side == 0 else 1 - place_ref[0]
        for q in range(HALF):
            y, z = q // 2, 4 * (q % 2) + 2 * parity
            for p in range(2):
                for b in range(2):
                    at = p * SIDE + q * BLOCK + b * TOK
                    copies.append(
                        pltpu.make_async_copy(
                            acts_in.at[z + b, y, p], out.at[:, pl.ds(at, TOK)], sems.at[len(copies)]
                        )
                    )
                    copies[-1].start()
    for copy in copies:
        copy.wait()


def arrange(place, acts):
    side = jax.ShapeDtypeStruct((TOK, 2 * SIDE), BF16)
    return pl.pallas_call(
        arrange_kernel,
        out_shape=(side, side),
        in_specs=[SCALARS, ANYWHERE],
        out_specs=(ANYWHERE,) * 2,
        scratch_shapes=[pltpu.SemaphoreType.DMA((2 * HALF * 4,))],
        compiler_params=pltpu.CompilerParams(vmem_limit_bytes=LARGE_VMEM),
        cost_estimate=pl.CostEstimate(flops=1000000, bytes_accessed=4000000, transcendentals=0),
        name="arrange",
    )(place, acts)


def forward_kernel(
    place_ref, keep_in, send_in, w_in, other_w_in, grads_out, dx_out,
    acts_ref, w_ref, grads_ref, dx_ref, in_sems, w_sems, out_sems,
):
    core = place_ref[0]
    loads = [
        pltpu.make_async_copy(src, acts_ref.at[side], in_sems.at[side])
        for side, src in enumerate((keep_in, send_in))
    ]
    w_loads = [
        pltpu.make_async_copy(
            (w_in if i < HALF else other_w_in).at[i % HALF],
            w_ref.at[:, pl.ds(i * BLOCK, BLOCK)],
            w_sems.at[i],
        )
        for i in range(N_ROW)
    ]
    for load in loads + w_loads:
        load.start()
    sums = [jnp.zeros((TOK, BLOCK), F32) for _ in range(3)]
    for side in range(2):
        loads[side].wait()
        for half in range(2):
            for q in range(4 * half, 4 * half + 4):
                w_loads[side * HALF + q].wait()
            rows = pl.ds((side * 2 + half) * 4 * BLOCK, 4 * BLOCK)
            x = acts_ref[side, :, pl.ds(half * 4 * BLOCK, 4 * BLOCK)]
            dy = acts_ref[side, :, pl.ds(SIDE + half * 4 * BLOCK, 4 * BLOCK)]
            for p in range(3):
                sums[p] += dot(dy if p == 2 else x, w_ref[p, rows], ((1,), (0,)))
    gate, up, hidden_grad = sums
    sig = 1.0 / (1.0 + jnp.exp(-gate))
    act = gate * sig
    gate_grad = (hidden_grad * up * sig * (1.0 + gate * (1.0 - sig))).astype(BF16)
    up_grad = (hidden_grad * act).astype(BF16)
    hidden = (act * up).astype(BF16)
    for p, value in enumerate((gate_grad, up_grad, hidden)):
        grads_ref[:, pl.ds(p * BLOCK, BLOCK)] = value
    stores = [pltpu.make_async_copy(grads_ref, grads_out, out_sems.at[0])]
    stores[-1].start()
    for i in range(N_ROW):
        q, parity = i % HALF, (core if i < HALF else 1 - core)
        rows = pl.ds(i * BLOCK, BLOCK)
        dx = dot(gate_grad, w_ref[0, rows], ((1,), (1,)))
        dx = (dx + dot(up_grad, w_ref[1, rows], ((1,), (1,)))).astype(BF16)
        y, z = q // 2, 4 * (q % 2) + 2 * parity
        dx_ref[z, y] = dx[:, :TOK]
        dx_ref[z + 1, y] = dx[:, TOK:]
    stores.append(pltpu.make_async_copy(dx_ref, dx_out, out_sems.at[1]))
    stores[-1].start()
    for store in stores:
        store.wait()


def forward(place, keep, send, weights, other_weights):
    return pl.pallas_call(
        forward_kernel,
        out_shape=(
            jax.ShapeDtypeStruct((TOK, 3 * BLOCK), BF16),
            jax.ShapeDtypeStruct((N_Z, N_YH, TOK, 128), BF16),
        ),
        in_specs=[SCALARS] + [ANYWHERE] * 4,
        out_specs=(ANYWHERE,) * 2,
        scratch_shapes=[
            pltpu.VMEM((2, TOK, 2 * SIDE), BF16),
            pltpu.VMEM((3, N_ROW * BLOCK, BLOCK), BF16),
            pltpu.VMEM((TOK, 3 * BLOCK), BF16),
            pltpu.VMEM((N_Z, N_YH, TOK, 128), BF16),
            pltpu.SemaphoreType.DMA((2,)),
            pltpu.SemaphoreType.DMA((N_ROW,)),
            pltpu.SemaphoreType.DMA((2,)),
        ],
        compiler_params=pltpu.CompilerParams(vmem_limit_bytes=SMALL_VMEM),
        cost_estimate=pl.CostEstimate(flops=1400000000, bytes_accessed=10000000, transcendentals=32768),
        name="forward",
    )(place, keep, send, weights, other_weights)


def weight_kernel(
    acts_in, other_acts_in, grads_in, other_grads_in, out, acts_ref, grads_ref, terms_ref, in_sems, out_sems
):
    loads = []
    for i, (src, dst) in enumerate(
        ((acts_in, acts_ref), (other_acts_in, acts_ref), (grads_in, grads_ref), (other_grads_in, grads_ref))
    ):
        rows = pl.ds((i % 2) * TOK, TOK)
        loads.append(pltpu.make_async_copy(src, dst.at[rows], in_sems.at[i]))
        loads[-1].start()
    for load in loads:
        load.wait()
    stores = []
    for q in range(HALF):
        x = acts_ref[:, pl.ds(q * BLOCK, BLOCK)]
        dy = acts_ref[:, pl.ds(SIDE + q * BLOCK, BLOCK)]
        gate_up = dot(x, grads_ref[:, pl.ds(0, 2 * BLOCK)], ((0,), (0,)))
        down = dot(dy, grads_ref[:, pl.ds(2 * BLOCK, BLOCK)], ((0,), (0,)))
        terms_ref[q, 0] = gate_up[:, :BLOCK].astype(BF16)
        terms_ref[q, 1] = gate_up[:, BLOCK:].astype(BF16)
        terms_ref[q, 2] = down.astype(BF16)
        stores.append(pltpu.make_async_copy(terms_ref.at[q], out.at[q], out_sems.at[q]))
        stores[-1].start()
    for store in stores:
        store.wait()


def weight_terms(acts, other_acts, grads, other_grads):
    return pl.pallas_call(
        weight_kernel,
        out_shape=jax.ShapeDtypeStruct((HALF, 3, BLOCK, BLOCK), BF16),
        in_specs=[ANYWHERE] * 4,
        out_specs=ANYWHERE,
        scratch_shapes=[
            pltpu.VMEM((2 * TOK, 2 * SIDE), BF16),
            pltpu.VMEM((2 * TOK, 3 * BLOCK), BF16),
            pltpu.VMEM((HALF, 3, BLOCK, BLOCK), BF16),
            pltpu.SemaphoreType.DMA((4,)),
            pltpu.SemaphoreType.DMA((HALF,)),
        ],
        compiler_params=pltpu.CompilerParams(vmem_limit_bytes=SMALL_VMEM),
        cost_estimate=pl.CostEstimate(flops=800000000, bytes_accessed=6000000, transcendentals=0),
        name="weight_terms",
    )(acts, other_acts, grads, other_grads)


def local(inputs, out_grad, codes, scales):
    place = lax.axis_index("core").reshape(1)
    swap = [(0, 1), (1, 0)]
    acts = gather_by_swap(jnp.stack([inputs, out_grad]), "yh", N_YH)
    acts = lax.all_gather(acts, Z, axis=0, tiled=False)

    weights = (codes.astype(F32) * scales.astype(F32)).astype(BF16)
    weights = gather_by_swap(weights, ("yl", "x"), HALF)
    other_weights = lax.ppermute(weights, "core", swap)

    keep, send = arrange(place, acts)
    other = lax.ppermute(send, "core", swap)
    grads, dx = forward(place, keep, send, weights, other_weights)
    dx = lax.all_to_all(dx, Z, split_axis=0, concat_axis=0, tiled=True)
    dx = jnp.sum(dx.astype(F32), axis=0).astype(BF16)
    dx = lax.all_to_all(dx, "yh", split_axis=0, concat_axis=0, tiled=True)
    input_grad = jnp.sum(dx.astype(F32), axis=0).astype(BF16)

    other_grads = lax.ppermute(grads, "core", swap)
    terms = weight_terms(keep, other, grads, other_grads)
    terms = lax.psum_scatter(terms, ("yl", "x"), scatter_dimension=0, tiled=False)
    return input_grad, terms.astype(F32)


def solution(mesh):
    fine = Mesh(mesh.devices.reshape(tuple(SIZES.values())), tuple(SIZES))
    return jax.shard_map(
        local,
        mesh=fine,
        in_specs=(P(ROW, COL), P(ROW, COL), P(None, ROW, COL), P(None, ROW, COL)),
        out_specs=(P(ROW, COL), P(None, ROW, COL)),
        check_vma=False,
    )
```

time: 169 us -> 161 us (0.953)
  the two profiles are of different devices: /device:TPU:8 before, /device:TPU:16 now
where the time goes in v7:
time: 161 us
  waiting for transfers between devices  59.8 us (37%)
  blocking collectives  48 us (30%)
  starting transfers between devices  19.8 us (12%)
  between operations  14.1 us (9%)
  Pallas kernels  9.79 us (6%)
  other arithmetic  5.26 us (3%)
  local copies, waits for them, and re-layouts  3.71 us (2%)
    all_to_all x2, waiting for transfers between devices, gather_by_swap(): return lax.all_to_all(copies, axis, split_axis=0, concat_axis=0, tiled=True)  42.5 us
    all_to_all x1, blocking collectives, local(): dx = lax.all_to_all(dx, Z, split_axis=0, concat_axis=0, tiled=True)  33.2 us
    all_to_all x1, blocking collectives, local(): dx = lax.all_to_all(dx, 'yh', split_axis=0, concat_axis=0, tiled=True)  14.8 us
    all_to_all x2, starting transfers between devices, gather_by_swap(): return lax.all_to_all(copies, axis, split_axis=0, concat_axis=0, tiled=True)  13.4 us
    all_gather x1, waiting for transfers between devices, local(): acts = lax.all_gather(acts, Z, axis=0, tiled=False)  11.7 us
    pallas_call x1, Pallas kernels, forward(): pl.pallas_call(forward_kernel, out_shape=(jax.ShapeDtypeStruct((TOK, 3 *...  5.02 us
    reduce_scatter x1, waiting for transfers between devices, local(): lax.psum_scatter(terms, ('yl', 'x'), scatter_dimension=0, tiled=False)  3.84 us
  transfers between devices with their start and end apart: 7, of which 5 were waited for; matrix products, arithmetic and copies ran while one was open for 2% of the time, Pallas kernels for 4%

profile of v7, /device:TPU:16, one launch (start us, length us, event | category | flops | bytes accessed | tf_op | source)
XLA Modules:
  0.0 160.5 jit_solution(5746223187531784747)
XLA Ops:
  7.2 0.8 pad_maximum_fusion
  7.9 0.7 broadcast_in_dim.4
  8.7 9.1 %all-to-all-start = ((bf16[4,2,128,128]{3,2,1,0:T(8,128)(2,1)}), bf16[4,2,128,128]{3,2,1,0:T(8,128)(2,1)S(1)}, u32[]{:S(2)}, u32[]{:S(2)}) async-start(bf16[4,2,128,128]{3,2,1,0:T(8,128)(2,1)} %broadcast_in_dim.4), calls=%async_computation | async-start | bytes 524288 | tf_op jit(solution)/shard_map/all_to_all | solution.py:31
  17.8 0.7 bitcast_convert_fusion.1
  18.5 1.1 multiply_convert_fusion
  19.5 6.1 %all-to-all-done = bf16[4,2,128,128]{3,2,1,0:T(8,128)(2,1)S(1)} async-done(((bf16[4,2,128,128]{3,2,1,0:T(8,128)(2,1)}), bf16[4,2,128,128]{3,2,1,0:T(8,128)(2,1)S(1)}, u32[]{:S(2)}, u32[]{:S(2)}) %all-to-all-start) | async-done | bytes 262176 | tf_op jit(solution)/shard_map/all_to_all | solution.py:31
  25.6 0.0 copy-start.2
  25.6 2.0 %broadcast_in_dim.5 = bf16[8,3,256,256]{3,2,1,0:T(8,128)(2,1)} broadcast(bf16[3,256,256]{2,1,0:T(8,128)(2,1)S(1)} %multiply_convert_fusion), dimensions={1,2,3} | broadcast | bytes 3538944 | tf_op jit(solution)/shard_map/broadcast_in_dim | solution.py:30
  27.6 0.0 copy-done.2
  27.6 4.3 %all-to-all-start.1 = ((bf16[8,3,256,256]{3,2,1,0:T(8,128)(2,1)}), bf16[8,3,256,256]{3,2,1,0:T(8,128)(2,1)S(1)}, u32[]{:S(2)}, u32[]{:S(2)}) async-start(bf16[8,3,256,256]{3,2,1,0:T(8,128)(2,1)} %broadcast_in_dim.5), calls=%async_computation.1 | async-start | bytes 6291456 | tf_op jit(solution)/shard_map/all_to_all | solution.py:31
  31.9 0.0 all-gather.3.cloned.1.call-start
  32.0 0.7 all-gather.3.cloned.1.call-update
  32.6 0.0 reduce-scatter.2.cloned.1.call-start
  32.7 36.4 %all-to-all-done.1.w_in = bf16[8,3,256,256]{3,2,1,0:T(8,128)(2,1)S(1)} async-done(((bf16[8,3,256,256]{3,2,1,0:T(8,128)(2,1)}), bf16[8,3,256,256]{3,2,1,0:T(8,128)(2,1)S(1)}, u32[]{:S(2)}, u32[]{:S(2)}) %all-to-all-start.1) | async-done | bytes 3145760 | tf_op jit(solution)/shard_map/all_to_all | solution.py:31
  69.1 1.9 %collective-permute-start = (bf16[8,3,256,256]{3,2,1,0:T(8,128)(2,1)S(1)}, bf16[8,3,256,256]{3,2,1,0:T(8,128)(2,1)}, u32[]{:S(2)}, u32[]{:S(2)}) collective-permute-start(bf16[8,3,256,256]{3,2,1,0:T(8,128)(2,1)S(1)} %all-to-all-done.1.w_in), channel_id=1, source_target_pairs={{0,32},{32,0},{1,33},{33,1},{2,34},{34,2},{3,35},{35,3},{4,36},{36... | collective-permute-start | bytes 9437192 | tf_op jit(solution)/shard_map/ppermute | solution.py:199
  71.0 11.7 %all-gather.3.cloned.1.call-done = bf16[32,2,128,128]{3,2,1,0:T(8,128)(2,1)} async-done(((bf16[4,2,128,128]{3,2,1,0:T(8,128)(2,1)}), bf16[32,2,128,128]{3,2,1,0:T(8,128)(2,1)}) %all-gather.3.cloned.1.call-update) | async-done | bytes 2097168 | tf_op jit(solution)/shard_map/all_gather | solution.py:195
  82.7 2.0 %arrange.1 = (bf16[128,4096]{1,0:T(8,128)(2,1)S(1)}, bf16[128,4096]{1,0:T(8,128)(2,1)S(1)}) custom-call(s32[1]{0:T(128)} %bitcast.place_ref, bf16[8,4,2,128,128]{4,3,2,1,0:T(8,128)(2,1)} %bitcast.10), custom_call_target="tpu_custom_call" | custom-call | flops 1000000 | bytes 4000000 | tf_op jit(solution)/shard_map/arrange/pallas_call | solution.py:55
  84.8 1.9 %collective-permute-start.1 = (bf16[128,4096]{1,0:T(8,128)(2,1)S(1)}, bf16[128,4096]{1,0:T(8,128)(2,1)S(1)}, u32[]{:S(2)}, u32[]{:S(2)}) collective-permute-start(bf16[128,4096]{1,0:T(8,128)(2,1)S(1)} %get-tuple-element.7.send_in), channel_id=1, source_target_pairs={{0,32},{32,0},{1,33},{33,1},{2,34},{34,2},{3,35},{35,3},{4,36},{36... | collective-permute-start | bytes 3145736 | tf_op jit(solution)/shard_map/ppermute | solution.py:202
  86.7 0.0 collective-permute-done.other_w_in
  86.7 5.0 %forward.1 = (bf16[128,768]{1,0:T(8,128)(2,1)S(1)}, bf16[8,4,128,128]{3,2,1,0:T(8,128)(2,1)S(1)}) custom-call(s32[1]{0:T(128)} %bitcast.place_ref, bf16[128,4096]{1,0:T(8,128)(2,1)S(1)} %get-tuple-element.6.keep_in.acts_in, bf16[128,4096]{1,0:T(8,128)(2,1)S(1)} %get-tuple-element.7.send_in, bf16[8,3,256,256]{3,2,1,0:T(8,128)(2,1)S(1)} %all-to-all-done.1.w_in, ...), custom_call_target="tpu_custom_call" | custom-call | flops 1400000000 | bytes 10000000 | tf_op jit(solution)/shard_map/forward/pallas_call | solution.py:122
  91.7 0.0 copy-start
  91.7 1.0 copy-done
  92.7 0.0 copy-start.1
  92.7 2.5 %collective-permute-start.2 = (bf16[128,768]{1,0:T(8,128)(2,1)S(1)}, bf16[128,768]{1,0:T(8,128)(2,1)S(1)}, u32[]{:S(2)}, u32[]{:S(2)}) collective-permute-start(bf16[128,768]{1,0:T(8,128)(2,1)S(1)} %get-tuple-element.9.grads_in), channel_id=1, source_target_pairs={{0,32},{32,0},{1,33},{33,1},{2,34},{34,2},{3,35},{35,3},{4,36},{36... | collective-permute-start | bytes 589832 | tf_op jit(solution)/shard_map/ppermute | solution.py:209
  95.3 0.0 collective-permute-done.1.other_acts_in
  95.3 1.0 collective-permute-done.2.other_grads_in
  96.3 2.7 %weight_terms.1 = bf16[8,3,256,256]{3,2,1,0:T(8,128)(2,1)} custom-call(bf16[128,4096]{1,0:T(8,128)(2,1)S(1)} %get-tuple-element.6.keep_in.acts_in, bf16[128,4096]{1,0:T(8,128)(2,1)S(1)} %collective-permute-done.1.other_acts_in, bf16[128,768]{1,0:T(8,128)(2,1)S(1)} %get-tuple-element.9.grads_in, bf16[128,768]{1,0:T(8,128)(2,1)S(1)} %collective-permute-done.2.other_grads_in), custom_call_target="tpu_custom_call" | custom-call | flops 800000000 | bytes 6000000 | tf_op jit(solution)/shard_map/weight_terms/pallas_call | solution.py:173
  99.1 0.0 reduce-scatter.2.cloned.1.call-update
  99.1 0.0 copy-done.1
  99.1 33.2 %all_to_all.20 = bf16[8,4,128,128]{3,2,1,0:T(8,128)(2,1)S(1)} all-to-all(bf16[8,4,128,128]{3,2,1,0:T(8,128)(2,1)S(1)} %copy-done.1), channel_id=1, replica_groups=mesh['yl'=2,'x'=4,'core'=2,'yh'=4,'zh'=4,'zl'=2] {'zh','zl'}, dimensions={0} | all-to-all | bytes 2097152 | tf_op jit(solution)/shard_map/all_to_all | solution.py:204
  132.3 0.1 reduce_sum.24
  132.5 14.8 %all_to_all.21 = bf16[4,128,128]{2,1,0:T(8,128)(2,1)S(1)} all-to-all(bf16[4,128,128]{2,1,0:T(8,128)(2,1)S(1)} %reduce_sum.24), channel_id=1, replica_groups=mesh['yl'=2,'x'=4,'core'=2,'yh'=4,'zh'=4,'zl'=2] {'yh'}, dimensions={0} | all-to-all | bytes 262144 | tf_op jit(solution)/shard_map/all_to_all | solution.py:206
  147.3 0.6 reduce_sum.25
  147.9 3.8 %reduce-scatter.2.cloned.1.call-done = bf16[1,3,256,256]{3,2,1,0:T(8,128)(2,1)} async-done(((bf16[8,3,256,256]{3,2,1,0:T(8,128)(2,1)}), bf16[1,3,256,256]{3,2,1,0:T(8,128)(2,1)}) %reduce-scatter.2.cloned.1.call-update) | async-done | bytes 393232 | tf_op jit(solution)/shard_map/reduce_scatter | solution.py:211
  151.7 1.9 %bitcast_convert_fusion = f32[3,256,256]{2,1,0:T(8,128)} fusion(bf16[1,3,256,256]{3,2,1,0:T(8,128)(2,1)} %reduce-scatter.2.cloned.1.call-done), kind=kLoop, calls=%fused_computation.1 | loop fusion | flops 196608 | bytes 1179648 | tf_op jit(solution)/shard_map/convert_element_type | solution.py:212
Async XLA Ops:
  8.7 16.9 %all-to-all-start = ((bf16[4,2,128,128]{3,2,1,0:T(8,128)(2,1)}), bf16[4,2,128,128]{3,2,1,0:T(8,128)(2,1)S(1)}, u32[]{:S(2)}, u32[]{:S(2)}) async-start(bf16[4,2,128,128]{3,2,1,0:T(8,128)(2,1)} %broadcast_in_dim.4), calls=%async_computation | async-start | bytes 524288 | tf_op jit(solution)/shard_map/all_to_all | solution.py:31
  25.6 2.0 %copy-start.2 = (bf16[4,2,128,128]{3,2,1,0:T(8,128)(2,1)}, bf16[4,2,128,128]{3,2,1,0:T(8,128)(2,1)S(1)}, u32[]{:S(2)}) copy-start(bf16[4,2,128,128]{3,2,1,0:T(8,128)(2,1)S(1)} %all-to-all-done) | copy-start | bytes 786436
  27.6 41.5 %all-to-all-start.1 = ((bf16[8,3,256,256]{3,2,1,0:T(8,128)(2,1)}), bf16[8,3,256,256]{3,2,1,0:T(8,128)(2,1)S(1)}, u32[]{:S(2)}, u32[]{:S(2)}) async-start(bf16[8,3,256,256]{3,2,1,0:T(8,128)(2,1)} %broadcast_in_dim.5), calls=%async_computation.1 | async-start | bytes 6291456 | tf_op jit(solution)/shard_map/all_to_all | solution.py:31
  31.9 50.8 %all-gather.3.cloned.1.call-start = ((), (), s32[]{:S(2)}) async-start(), calls=%async_computation.6 | async-start | bytes 2359296 | tf_op jit(solution)/shard_map/all_gather | solution.py:195
  32.6 119.1 %reduce-scatter.2.cloned.1.call-start = ((), (), s32[]{:S(2)}) async-start(), calls=%async_computation.5 | async-start | bytes 3538944 | tf_op jit(solution)/shard_map/reduce_scatter | solution.py:211
  69.1 17.6 %collective-permute-start = (bf16[8,3,256,256]{3,2,1,0:T(8,128)(2,1)S(1)}, bf16[8,3,256,256]{3,2,1,0:T(8,128)(2,1)}, u32[]{:S(2)}, u32[]{:S(2)}) collective-permute-start(bf16[8,3,256,256]{3,2,1,0:T(8,128)(2,1)S(1)} %all-to-all-done.1.w_in), channel_id=1, source_target_pairs={{0,32},{32,0},{1,33},{33,1},{2,34},{34,2},{3,35},{35,3},{4,36},{36... | collective-permute-start | bytes 9437192 | tf_op jit(solution)/shard_map/ppermute | solution.py:199
  84.8 10.5 %collective-permute-start.1 = (bf16[128,4096]{1,0:T(8,128)(2,1)S(1)}, bf16[128,4096]{1,0:T(8,128)(2,1)S(1)}, u32[]{:S(2)}, u32[]{:S(2)}) collective-permute-start(bf16[128,4096]{1,0:T(8,128)(2,1)S(1)} %get-tuple-element.7.send_in), channel_id=1, source_target_pairs={{0,32},{32,0},{1,33},{33,1},{2,34},{34,2},{3,35},{35,3},{4,36},{36... | collective-permute-start | bytes 3145736 | tf_op jit(solution)/shard_map/ppermute | solution.py:202
  91.7 1.0 copy-start
  92.7 6.4 %copy-start.1 = (bf16[8,4,128,128]{3,2,1,0:T(8,128)(2,1)S(1)}, bf16[8,4,128,128]{3,2,1,0:T(8,128)(2,1)}, u32[]{:S(2)}) copy-start(bf16[8,4,128,128]{3,2,1,0:T(8,128)(2,1)} %copy-done) | copy-start | bytes 3145732
  92.7 3.6 %collective-permute-start.2 = (bf16[128,768]{1,0:T(8,128)(2,1)S(1)}, bf16[128,768]{1,0:T(8,128)(2,1)S(1)}, u32[]{:S(2)}, u32[]{:S(2)}) collective-permute-start(bf16[128,768]{1,0:T(8,128)(2,1)S(1)} %get-tuple-element.9.grads_in), channel_id=1, source_target_pairs={{0,32},{32,0},{1,33},{33,1},{2,34},{34,2},{3,35},{35,3},{4,36},{36... | collective-permute-start | bytes 589832 | tf_op jit(solution)/shard_map/ppermute | solution.py:209
Sparse Core Ops, SparseCore 0:
  35.4 47.2 all-gather.2
  99.2 52.4 reduce-scatter.1

commit v8 on v1

v8 whole, which is shorter than its diff:
```python
import itertools

import jax
import jax.numpy as jnp
from jax import lax
from jax.experimental import pallas as pl
from jax.experimental.pallas import tpu as pltpu
from jax.sharding import Mesh, PartitionSpec as P

F32 = jnp.float32
BF16 = jnp.bfloat16
ROW = ("yl", "x1", "x0", "core")
COL = ("yh1", "yh0", "zh1", "zh0", "zl")
AXES = ROW + COL
SPREAD = ("yh1", "yh0", "zh1", "zh0")
REST = ("yl", "x1")
SWAP = [(0, 1), (1, 0)]
TOK = 128
BLOCK = 256
WIDE = 2 * BLOCK
HALF = 2 * TOK
SHARE = HALF // 4
GRADS = 3 * WIDE
VMEM_LIMIT = 24 * 1024 * 1024
ANYWHERE = pl.BlockSpec(memory_space=pl.ANY)
SCALARS = pl.BlockSpec(memory_space=pltpu.SMEM)


def turned():
    pairs = []
    for bits in itertools.product(range(2), repeat=len(AXES)):
        yl, x1, x0, core, yh1, yh0, zh1, zh0, zl = bits
        there = (yh1, yh0, x0, zh0, yl, x1, zh1, zl, core)
        pairs.append(tuple(sum(b << (8 - i) for i, b in enumerate(at)) for at in (bits, there)))
    return pairs


def dot(a, b, dims):
    return lax.dot_general(a, b, (dims, ((), ())), preferred_element_type=F32)


def params():
    return pltpu.CompilerParams(vmem_limit_bytes=VMEM_LIMIT)


def chunk(place_ref, i, f):
    core, x0 = place_ref[0], place_ref[1]
    t = 2 * (core if i < 2 else 1 - core) + i % 2
    return 4 * t + 2 * (x0 if f < 2 else 1 - x0) + f % 2


def load_weights(w_in, w_z_in, w_x_in, w_ref, count, sems):
    loads = []
    for i, src in enumerate((w_in, w_z_in, w_x_in.at[0], w_x_in.at[1])):
        rows, cols = pl.ds(i // 2 * BLOCK, BLOCK), pl.ds(i % 2 * BLOCK, BLOCK)
        loads.append(
            pltpu.make_async_copy(src.at[pl.ds(0, count)], w_ref.at[:, rows, cols], sems.at[i])
        )
        loads[-1].start()
    return loads


def gates_kernel(
    place_ref, acts_in, w_in, w_z_in, w_x_in, keep_out, send_out, acts_out,
    acts_ref, w_ref, keep_ref, send_ref, act_sems, w_sems, out_sems,
):
    w_loads = load_weights(w_in, w_z_in, w_x_in, w_ref, 3, w_sems)
    loads = []
    for p in range(2):
        for i in range(4):
            for f in range(4):
                src = acts_in.at[chunk(place_ref, i, f), p]
                dst = acts_ref.at[p, pl.ds(i * TOK, TOK), pl.ds(f * TOK, TOK)]
                loads.append(pltpu.make_async_copy(src, dst, act_sems.at[len(loads)]))
                loads[-1].start()
    for load in loads:
        load.wait()
    stores = [pltpu.make_async_copy(acts_ref, acts_out, out_sems.at[0])]
    stores[0].start()
    for load in w_loads:
        load.wait()
    for p in range(3):
        cols = pl.ds(p * WIDE, WIDE)
        sums = dot(acts_ref[p // 2], w_ref[p], ((1,), (0,)))
        send_ref[:, cols] = sums[HALF:].astype(BF16)
        keep_ref[:, cols] = sums[:HALF]
    for i, (src, dst) in enumerate(((send_ref, send_out), (keep_ref, keep_out))):
        stores.append(pltpu.make_async_copy(src, dst, out_sems.at[1 + i]))
        stores[-1].start()
    for store in stores:
        store.wait()


def gates(place, acts, w, w_z, w_x):
    return pl.pallas_call(
        gates_kernel,
        out_shape=(
            jax.ShapeDtypeStruct((HALF, GRADS), F32),
            jax.ShapeDtypeStruct((HALF, GRADS), BF16),
            jax.ShapeDtypeStruct((2, 2 * HALF, WIDE), BF16),
        ),
        in_specs=[SCALARS] + [ANYWHERE] * 4,
        out_specs=(ANYWHERE,) * 3,
        scratch_shapes=[
            pltpu.VMEM((2, 2 * HALF, WIDE), BF16),
            pltpu.VMEM((3, WIDE, WIDE), BF16),
            pltpu.VMEM((HALF, GRADS), F32),
            pltpu.VMEM((HALF, GRADS), BF16),
            pltpu.SemaphoreType.DMA((32,)),
            pltpu.SemaphoreType.DMA((4,)),
            pltpu.SemaphoreType.DMA((3,)),
        ],
        compiler_params=params(),
        cost_estimate=pl.CostEstimate(flops=800000000, bytes_accessed=6000000, transcendentals=0),
        name="gates",
    )(place, acts, w, w_z, w_x)


def hidden_kernel(parts_ref, out_ref):
    total = parts_ref[0].astype(F32)
    for i in range(1, 4):
        total += parts_ref[i].astype(F32)
    gate, up, hidden_grad = (total[:, p * WIDE : (p + 1) * WIDE] for p in range(3))
    sig = 1.0 / (1.0 + jnp.exp(-gate))
    act = gate * sig
    gate_grad = (hidden_grad * up * sig * (1.0 + gate * (1.0 - sig))).astype(BF16)
    up_grad = (hidden_grad * act).astype(BF16)
    hidden = (act * up).astype(BF16)
    for i in range(4):
        for p, value in enumerate((gate_grad, up_grad, hidden)):
            out_ref[i, :, pl.ds(p * WIDE, WIDE)] = value


def hidden_grads(parts):
    whole = pl.BlockSpec(memory_space=pltpu.VMEM)
    return pl.pallas_call(
        hidden_kernel,
        out_shape=jax.ShapeDtypeStruct(parts.shape, BF16),
        in_specs=[whole],
        out_specs=whole,
        compiler_params=params(),
        cost_estimate=pl.CostEstimate(flops=2000000, bytes_accessed=1600000, transcendentals=32768),
        name="hidden_grads",
    )(parts)


def load_grads(own_in, other_in, grads_ref, sems):
    loads = []
    for i, src in enumerate((own_in, other_in)):
        loads.append(
            pltpu.make_async_copy(src, grads_ref.at[pl.ds(i * HALF, HALF)], sems.at[i])
        )
        loads[-1].start()
    return loads


def input_kernel(
    place_ref, own_in, other_in, w_in, w_z_in, w_x_in, dx_out, grads_ref, w_ref, dx_ref, in_sems, w_sems, out_sem
):
    loads = load_grads(own_in, other_in, grads_ref, in_sems)
    loads += load_weights(w_in, w_z_in, w_x_in, w_ref, 2, w_sems)
    for load in loads:
        load.wait()
    dx = dot(grads_ref[:, pl.ds(0, WIDE)], w_ref[0], ((1,), (1,)))
    dx = (dx + dot(grads_ref[:, pl.ds(WIDE, WIDE)], w_ref[1], ((1,), (1,)))).astype(BF16)
    for i in range(4):
        for f in range(4):
            dx_ref[chunk(place_ref, i, f)] = dx[i * TOK : (i + 1) * TOK, f * TOK : (f + 1) * TOK]
    store = pltpu.make_async_copy(dx_ref, dx_out, out_sem)
    store.start()
    store.wait()


def input_terms(place, own, other, w, w_z, w_x):
    return pl.pallas_call(
        input_kernel,
        out_shape=jax.ShapeDtypeStruct((16, TOK, TOK), BF16),
        in_specs=[SCALARS] + [ANYWHERE] * 5,
        out_specs=ANYWHERE,
        scratch_shapes=[
            pltpu.VMEM((2 * HALF, GRADS), BF16),
            pltpu.VMEM((2, WIDE, WIDE), BF16),
            pltpu.VMEM((16, TOK, TOK), BF16),
            pltpu.SemaphoreType.DMA((2,)),
            pltpu.SemaphoreType.DMA((4,)),
            pltpu.SemaphoreType.DMA,
        ],
        compiler_params=params(),
        cost_estimate=pl.CostEstimate(flops=540000000, bytes_accessed=4000000, transcendentals=0),
        name="input_terms",
    )(place, own, other, w, w_z, w_x)


def weight_kernel(
    acts_in, own_in, other_in, keep_out, send_out,
    acts_ref, grads_ref, keep_ref, send_ref, in_sems, out_sems,
):
    loads = load_grads(own_in, other_in, grads_ref, in_sems)
    loads.append(pltpu.make_async_copy(acts_in, acts_ref, in_sems.at[2]))
    loads[-1].start()
    for load in loads:
        load.wait()
    stores = []
    for side in (1, 0):
        for p in range(3):
            x = acts_ref[p // 2, :, pl.ds(side * BLOCK, BLOCK)]
            term = dot(x, grads_ref[:, pl.ds(p * WIDE, WIDE)], ((0,), (0,)))
            for j in range(2):
                part = term[:, j * BLOCK : (j + 1) * BLOCK]
                if side == 0:
                    keep_ref[j, p] = part
                else:
                    send_ref[j, p] = part.astype(BF16)
        src, dst = ((keep_ref, keep_out), (send_ref, send_out))[side]
        stores.append(pltpu.make_async_copy(src, dst, out_sems.at[side]))
        stores[-1].start()
    for store in stores:
        store.wait()


def weight_terms(acts, own, other):
    shape = (2, 3, BLOCK, BLOCK)
    return pl.pallas_call(
        weight_kernel,
        out_shape=(jax.ShapeDtypeStruct(shape, F32), jax.ShapeDtypeStruct(shape, BF16)),
        in_specs=[ANYWHERE] * 3,
        out_specs=(ANYWHERE,) * 2,
        scratch_shapes=[
            pltpu.VMEM((2, 2 * HALF, WIDE), BF16),
            pltpu.VMEM((2 * HALF, GRADS), BF16),
            pltpu.VMEM(shape, F32),
            pltpu.VMEM(shape, BF16),
            pltpu.SemaphoreType.DMA((3,)),
            pltpu.SemaphoreType.DMA((2,)),
        ],
        compiler_params=params(),
        cost_estimate=pl.CostEstimate(flops=800000000, bytes_accessed=6000000, transcendentals=0),
        name="weight_terms",
    )(acts, own, other)


def exchange(pieces, axes):
    return lax.all_to_all(pieces, axes, split_axis=0, concat_axis=0, tiled=True)


def local(inputs, out_grad, codes, scales):
    place = jnp.stack([lax.axis_index("core"), lax.axis_index("x0")])
    there = turned()

    acts = lax.ppermute(jnp.stack([inputs, out_grad]), AXES, there)
    w = (codes.astype(F32) * scales.astype(F32)).astype(BF16)
    w_z = lax.ppermute(w, "zl", SWAP)
    w_x = lax.ppermute(jnp.stack([w, w_z]), "x0", SWAP)
    acts = exchange(jnp.broadcast_to(acts[None], (16,) + acts.shape), SPREAD)

    keep, send, acts = gates(place, acts, w, w_z, w_x)
    total = (keep + lax.ppermute(send, "core", SWAP).astype(F32)).astype(BF16)
    grads = hidden_grads(exchange(total.reshape(4, SHARE, GRADS), REST))
    own = exchange(grads, REST).reshape(HALF, GRADS)
    other = lax.ppermute(own, "core", SWAP)

    dx = exchange(input_terms(place, own, other, w, w_z, w_x), SPREAD)
    dx = jnp.sum(dx.astype(F32), axis=0).astype(BF16)
    input_grad = lax.ppermute(dx, AXES, [(b, a) for a, b in there])

    keep, send = weight_terms(acts, own, other)
    got = lax.ppermute(send, "x0", SWAP).astype(F32)
    send = (keep[1] + got[1]).astype(BF16)
    weight_grad = keep[0] + got[0] + lax.ppermute(send, "zl", SWAP).astype(F32)
    return input_grad, weight_grad


def solution(mesh):
    fine = Mesh(mesh.devices.reshape((2,) * len(AXES)), AXES)
    return jax.shard_map(
        local,
        mesh=fine,
        in_specs=(P(ROW, COL), P(ROW, COL), P(None, ROW, COL), P(None, ROW, COL)),
        out_specs=(P(ROW, COL), P(None, ROW, COL)),
        check_vma=False,
    )
```

time: 184 us -> 182 us (0.989)
  the two profiles are of different devices: /device:TPU:56 before, /device:TPU:48 now
where the time goes in v8:
time: 182 us
  waiting for transfers between devices  78.5 us (43%)
  starting transfers between devices  54.1 us (30%)
  blocking collectives  32.4 us (18%)
  other arithmetic  7.02 us (4%)
  Pallas kernels  6.88 us (4%)
  local copies, waits for them, and re-layouts  1.83 us (1%)
    all_to_all x2, blocking collectives, exchange(): return lax.all_to_all(pieces, axes, split_axis=0, concat_axis=0, tiled=True)  32.4 us
    all_to_all x2, starting transfers between devices, exchange(): return lax.all_to_all(pieces, axes, split_axis=0, concat_axis=0, tiled=True)  28.5 us
    ppermute x1, waiting for transfers between devices, local(): w_z = lax.ppermute(w, 'zl', SWAP)  28.1 us
    ppermute x1, waiting for transfers between devices, local(): w_x = lax.ppermute(jnp.stack([w, w_z]), 'x0', SWAP)  17.4 us
    ppermute x1, waiting for transfers between devices, local(): input_grad = lax.ppermute(dx, AXES, [(b, a) for a, b in there])  9.5 us
    all_to_all x2, waiting for transfers between devices, exchange(): return lax.all_to_all(pieces, axes, split_axis=0, concat_axis=0, tiled=True)  8.63 us
    ppermute x1, waiting for transfers between devices, local(): acts = lax.ppermute(jnp.stack([inputs, out_grad]), AXES, there)  6.3 us
    ppermute x1, starting transfers between devices, local(): acts = lax.ppermute(jnp.stack([inputs, out_grad]), AXES, there)  5.39 us
  transfers between devices with their start and end apart: 10, of which 8 were waited for; matrix products, arithmetic and copies ran while one was open for 3% of the time, Pallas kernels for 1%

profile of v8, /device:TPU:48, one launch (start us, length us, event | category | flops | bytes accessed | tf_op | source)
XLA Modules:
  0.0 181.6 jit_solution(10448259191610835263)
XLA Ops:
  0.6 0.8 pad_maximum_fusion.1
  1.4 0.0 copy-start.1
  1.4 0.0 copy-start
  1.4 5.4 %collective-permute-start = (bf16[2,128,128]{2,1,0:T(8,128)(2,1)S(1)}, bf16[2,128,128]{2,1,0:T(8,128)(2,1)S(1)}, u32[]{:S(2)}, u32[]{:S(2)}) collective-permute-start(bf16[2,128,128]{2,1,0:T(8,128)(2,1)S(1)} %pad_maximum_fusion.1), channel_id=1, source_target_pairs={{0,0},{1,2},{2,32},{3,34},{4,4},{5,6},{6,36},{7,38},{8,128},{9,130... | collective-permute-start | bytes 196616 | tf_op jit(solution)/shard_map/ppermute | solution.py:250
  6.8 6.3 %collective-permute-done = bf16[2,128,128]{2,1,0:T(8,128)(2,1)S(1)} collective-permute-done((bf16[2,128,128]{2,1,0:T(8,128)(2,1)S(1)}, bf16[2,128,128]{2,1,0:T(8,128)(2,1)S(1)}, u32[]{:S(2)}, u32[]{:S(2)}) %collective-permute-start) | collective-permute-done | bytes 65568 | tf_op jit(solution)/shard_map/ppermute | solution.py:250
  13.1 1.2 broadcast_in_dim.2
  14.3 16.2 %all-to-all-start = ((bf16[16,2,128,128]{3,2,1,0:T(8,128)(2,1)}), bf16[16,2,128,128]{3,2,1,0:T(8,128)(2,1)S(1)}, u32[]{:S(2)}, u32[]{:S(2)}) async-start(bf16[16,2,128,128]{3,2,1,0:T(8,128)(2,1)} %broadcast_in_dim.2), calls=%async_computation | async-start | bytes 2097152 | tf_op jit(solution)/shard_map/all_to_all | solution.py:243
  30.5 0.0 copy-done.1
  30.5 0.0 copy-done
  30.5 0.1 multiply_convert_fusion.w_in
  30.6 4.1 %collective-permute-start.1 = (bf16[3,256,256]{2,1,0:T(8,128)(2,1)S(1)}, bf16[3,256,256]{2,1,0:T(8,128)(2,1)S(1)}, u32[]{:S(2)}, u32[]{:S(2)}) collective-permute-start(bf16[3,256,256]{2,1,0:T(8,128)(2,1)S(1)} %multiply_convert_fusion.w_in), channel_id=1, source_target_pairs={{0,1},{1,0},{2,3},{3,2},{4,5},{5,4},{6,7},{7,6},{8,9},{9,8},{10,11... | collective-permute-start | bytes 1179656 | tf_op jit(solution)/shard_map/ppermute | solution.py:252
  34.7 0.1 fusion.4
  34.7 28.1 %collective-permute-done.1.w_z_in = bf16[3,256,256]{2,1,0:T(8,128)(2,1)S(1)} collective-permute-done((bf16[3,256,256]{2,1,0:T(8,128)(2,1)S(1)}, bf16[3,256,256]{2,1,0:T(8,128)(2,1)S(1)}, u32[]{:S(2)}, u32[]{:S(2)}) %collective-permute-start.1) | collective-permute-done | bytes 393248 | tf_op jit(solution)/shard_map/ppermute | solution.py:252
  62.8 0.9 pad_maximum_fusion
  63.8 3.1 %collective-permute-start.2 = (bf16[2,3,256,256]{3,2,1,0:T(8,128)(2,1)}, bf16[2,3,256,256]{3,2,1,0:T(8,128)(2,1)S(1)}, u32[]{:S(2)}, u32[]{:S(2)}) collective-permute-start(bf16[2,3,256,256]{3,2,1,0:T(8,128)(2,1)} %pad_maximum_fusion), channel_id=1, source_target_pairs={{0,64},{64,0},{1,65},{65,1},{2,66},{66,2},{3,67},{67,3},{4,68},{68... | collective-permute-start | bytes 2359304 | tf_op jit(solution)/shard_map/ppermute | solution.py:253
  66.9 0.1 pad_add_fusion.place_ref
  67.0 17.4 %collective-permute-done.2.w_x_in = bf16[2,3,256,256]{3,2,1,0:T(8,128)(2,1)S(1)} collective-permute-done((bf16[2,3,256,256]{3,2,1,0:T(8,128)(2,1)}, bf16[2,3,256,256]{3,2,1,0:T(8,128)(2,1)S(1)}, u32[]{:S(2)}, u32[]{:S(2)}) %collective-permute-start.2) | collective-permute-done | bytes 786464 | tf_op jit(solution)/shard_map/ppermute | solution.py:253
  84.4 0.0 all-to-all-done.acts_in
  84.4 2.6 %gates.1 = (f32[256,1536]{1,0:T(8,128)S(1)}, bf16[256,1536]{1,0:T(8,128)(2,1)S(1)}, bf16[2,512,512]{2,1,0:T(8,128)(2,1)S(1)}) custom-call(s32[2]{0:T(128)S(1)} %pad_add_fusion.place_ref, bf16[16,2,128,128]{3,2,1,0:T(8,128)(2,1)S(1)} %all-to-all-done.acts_in, bf16[3,256,256]{2,1,0:T(8,128)(2,1)S(1)} %multiply_convert_fusion.w_in, ...), custom_call_target="tpu_custom_call" | custom-call | flops 800000000 | bytes 6000000 | tf_op jit(solution)/shard_map/gates/pallas_call | solution.py:95
  87.0 1.9 %collective-permute-start.3 = (bf16[256,1536]{1,0:T(8,128)(2,1)S(1)}, bf16[256,1536]{1,0:T(8,128)(2,1)S(1)}, u32[]{:S(2)}, u32[]{:S(2)}) collective-permute-start(bf16[256,1536]{1,0:T(8,128)(2,1)S(1)} %get-tuple-element.8), channel_id=1, source_target_pairs={{0,32},{32,0},{1,33},{33,1},{2,34},{34,2},{3,35},{35,3},{4,36},{36... | collective-permute-start | bytes 2359304 | tf_op jit(solution)/shard_map/ppermute | solution.py:257
  89.0 2.3 %collective-permute-done.3 = bf16[256,1536]{1,0:T(8,128)(2,1)S(1)} collective-permute-done((bf16[256,1536]{1,0:T(8,128)(2,1)S(1)}, bf16[256,1536]{1,0:T(8,128)(2,1)S(1)}, u32[]{:S(2)}, u32[]{:S(2)}) %collective-permute-start.3) | collective-permute-done | bytes 786464 | tf_op jit(solution)/shard_map/ppermute | solution.py:257
  91.2 0.2 add_convert_fusion
  91.4 18.1 %all_to_all.20.parts_ref = bf16[4,64,1536]{2,1,0:T(8,128)(2,1)S(1)} all-to-all(bf16[4,64,1536]{2,1,0:T(8,128)(2,1)S(1)} %bitcast.22), channel_id=1, replica_groups=mesh['yl'=2,'x1'=2,'x0'=2,'core'=2,'yh1'=2,'yh0'=2,'zh1'=2,'zh0'=2,'zl'=..., dimensions={0} | all-to-all | bytes 1572864 | tf_op jit(solution)/shard_map/all_to_all | solution.py:243
  109.5 0.2 hidden_grads.1
  109.7 14.3 %all_to_all.21 = bf16[4,64,1536]{2,1,0:T(8,128)(2,1)S(1)} all-to-all(bf16[4,64,1536]{2,1,0:T(8,128)(2,1)S(1)} %hidden_grads.1), channel_id=1, replica_groups=mesh['yl'=2,'x1'=2,'x0'=2,'core'=2,'yh1'=2,'yh0'=2,'zh1'=2,'zh0'=2,'zl'=..., dimensions={0} | all-to-all | bytes 1572864 | tf_op jit(solution)/shard_map/all_to_all | solution.py:243
  124.0 1.9 %collective-permute-start.4 = (bf16[256,1536]{1,0:T(8,128)(2,1)S(1)}, bf16[256,1536]{1,0:T(8,128)(2,1)S(1)}, u32[]{:S(2)}, u32[]{:S(2)}) collective-permute-start(bf16[256,1536]{1,0:T(8,128)(2,1)S(1)} %bitcast.18), channel_id=1, source_target_pairs={{0,32},{32,0},{1,33},{33,1},{2,34},{34,2},{3,35},{35,3},{4,36},{36... | collective-permute-start | bytes 2359304 | tf_op jit(solution)/shard_map/ppermute | solution.py:260
  125.9 2.3 %collective-permute-done.4.other_in = bf16[256,1536]{1,0:T(8,128)(2,1)S(1)} collective-permute-done((bf16[256,1536]{1,0:T(8,128)(2,1)S(1)}, bf16[256,1536]{1,0:T(8,128)(2,1)S(1)}, u32[]{:S(2)}, u32[]{:S(2)}) %collective-permute-start.4) | collective-permute-done | bytes 786464 | tf_op jit(solution)/shard_map/ppermute | solution.py:260
  128.2 1.7 weight_terms.1
  129.9 3.0 %collective-permute-start.6 = (bf16[2,3,256,256]{3,2,1,0:T(8,128)(2,1)}, bf16[2,3,256,256]{3,2,1,0:T(8,128)(2,1)}, u32[]{:S(2)}, u32[]{:S(2)}) collective-permute-start(bf16[2,3,256,256]{3,2,1,0:T(8,128)(2,1)} %get-tuple-element.11), channel_id=1, source_target_pairs={{0,64},{64,0},{1,65},{65,1},{2,66},{66,2},{3,67},{67,3},{4,68},{68... | collective-permute-start | bytes 2359304 | tf_op jit(solution)/shard_map/ppermute | solution.py:267
  132.9 2.3 %input_terms.1 = bf16[16,128,128]{2,1,0:T(8,128)(2,1)} custom-call(s32[2]{0:T(128)S(1)} %pad_add_fusion.place_ref, bf16[256,1536]{1,0:T(8,128)(2,1)S(1)} %bitcast.20, bf16[256,1536]{1,0:T(8,128)(2,1)S(1)} %collective-permute-done.4.other_in, bf16[3,256,256]{2,1,0:T(8,128)(2,1)S(1)} %multiply_convert_fusion.w_in, ...), custom_call_target="tpu_custom_call" | custom-call | flops 540000000 | bytes 4000000 | tf_op jit(solution)/shard_map/input_terms/pallas_call | solution.py:175
  135.3 12.3 %all-to-all-start.3 = ((bf16[16,128,128]{2,1,0:T(8,128)(2,1)}), bf16[16,128,128]{2,1,0:T(8,128)(2,1)}, u32[]{:S(2)}, u32[]{:S(2)}) async-start(bf16[16,128,128]{2,1,0:T(8,128)(2,1)} %input_terms.1), calls=%async_computation.3 | async-start | bytes 1048576 | tf_op jit(solution)/shard_map/all_to_all | solution.py:243
  147.6 4.1 %collective-permute-done.6 = bf16[2,3,256,256]{3,2,1,0:T(8,128)(2,1)} collective-permute-done((bf16[2,3,256,256]{3,2,1,0:T(8,128)(2,1)}, bf16[2,3,256,256]{3,2,1,0:T(8,128)(2,1)}, u32[]{:S(2)}, u32[]{:S(2)}) %collective-permute-start.6) | collective-permute-done | bytes 786464 | tf_op jit(solution)/shard_map/ppermute | solution.py:267
  151.7 1.3 convert_element_type.31
  153.0 0.8 fusion.3
  153.8 4.4 %collective-permute-start.7 = (bf16[3,256,256]{2,1,0:T(8,128)(2,1)}, bf16[3,256,256]{2,1,0:T(8,128)(2,1)S(1)}, u32[]{:S(2)}, u32[]{:S(2)}) collective-permute-start(bf16[3,256,256]{2,1,0:T(8,128)(2,1)} %fusion.3), channel_id=1, source_target_pairs={{0,1},{1,0},{2,3},{3,2},{4,5},{5,4},{6,7},{7,6},{8,9},{9,8},{10,11... | collective-permute-start | bytes 1179656 | tf_op jit(solution)/shard_map/ppermute | solution.py:269
  158.2 8.6 %all-to-all-done.3 = bf16[16,128,128]{2,1,0:T(8,128)(2,1)} async-done(((bf16[16,128,128]{2,1,0:T(8,128)(2,1)}), bf16[16,128,128]{2,1,0:T(8,128)(2,1)}, u32[]{:S(2)}, u32[]{:S(2)}) %all-to-all-start.3) | async-done | bytes 524320 | tf_op jit(solution)/shard_map/all_to_all | solution.py:243
  166.8 1.7 reduce_sum.12
  168.5 1.9 %collective-permute-start.5 = (bf16[128,128]{1,0:T(8,128)(2,1)}, bf16[128,128]{1,0:T(8,128)(2,1)S(1)}, u32[]{:S(2)}, u32[]{:S(2)}) collective-permute-start(bf16[128,128]{1,0:T(8,128)(2,1)} %reduce_sum.12), channel_id=1, source_target_pairs={{0,0},{2,1},{32,2},{34,3},{4,4},{6,5},{36,6},{38,7},{128,8},{130,9... | collective-permute-start | bytes 98312 | tf_op jit(solution)/shard_map/ppermute | solution.py:264
  170.4 9.5 %collective-permute-done.5 = bf16[128,128]{1,0:T(8,128)(2,1)S(1)} collective-permute-done((bf16[128,128]{1,0:T(8,128)(2,1)}, bf16[128,128]{1,0:T(8,128)(2,1)S(1)}, u32[]{:S(2)}, u32[]{:S(2)}) %collective-permute-start.5) | collective-permute-done | bytes 32800 | tf_op jit(solution)/shard_map/ppermute | solution.py:264
  179.9 0.0 collective-permute-done.7
  180.0 1.0 fusion.2
  181.0 0.6 copy.7
  (1 shorter events, 0.0 us)
Async XLA Ops:
  1.4 29.1 %copy-start.1 = (bf16[3,1,256]{2,0,1:T(4,128)(2,1)S(1)}, bf16[3,1,256]{2,0,1:T(4,128)(2,1)}, u32[]{:S(2)}) copy-start(bf16[3,1,256]{2,0,1:T(4,128)(2,1)} %param.7) | copy-start | bytes 4612
  1.4 29.1 %copy-start = (bf16[3,256,256]{2,1,0:T(8,128)(2,1)S(1)}, bf16[3,256,256]{2,1,0:T(8,128)(2,1)}, u32[]{:S(2)}) copy-start(bf16[3,256,256]{2,1,0:T(8,128)(2,1)} %param.6) | copy-start | bytes 1179652
  1.4 11.7 %collective-permute-start = (bf16[2,128,128]{2,1,0:T(8,128)(2,1)S(1)}, bf16[2,128,128]{2,1,0:T(8,128)(2,1)S(1)}, u32[]{:S(2)}, u32[]{:S(2)}) collective-permute-start(bf16[2,128,128]{2,1,0:T(8,128)(2,1)S(1)} %pad_maximum_fusion.1), channel_id=1, source_target_pairs={{0,0},{1,2},{2,32},{3,34},{4,4},{5,6},{6,36},{7,38},{8,128},{9,130... | collective-permute-start | bytes 196616 | tf_op jit(solution)/shard_map/ppermute | solution.py:250
  14.3 70.0 %all-to-all-start = ((bf16[16,2,128,128]{3,2,1,0:T(8,128)(2,1)}), bf16[16,2,128,128]{3,2,1,0:T(8,128)(2,1)S(1)}, u32[]{:S(2)}, u32[]{:S(2)}) async-start(bf16[16,2,128,128]{3,2,1,0:T(8,128)(2,1)} %broadcast_in_dim.2), calls=%async_computation | async-start | bytes 2097152 | tf_op jit(solution)/shard_map/all_to_all | solution.py:243
  30.6 32.2 %collective-permute-start.1 = (bf16[3,256,256]{2,1,0:T(8,128)(2,1)S(1)}, bf16[3,256,256]{2,1,0:T(8,128)(2,1)S(1)}, u32[]{:S(2)}, u32[]{:S(2)}) collective-permute-start(bf16[3,256,256]{2,1,0:T(8,128)(2,1)S(1)} %multiply_convert_fusion.w_in), channel_id=1, source_target_pairs={{0,1},{1,0},{2,3},{3,2},{4,5},{5,4},{6,7},{7,6},{8,9},{9,8},{10,11... | collective-permute-start | bytes 1179656 | tf_op jit(solution)/shard_map/ppermute | solution.py:252
  63.8 20.6 %collective-permute-start.2 = (bf16[2,3,256,256]{3,2,1,0:T(8,128)(2,1)}, bf16[2,3,256,256]{3,2,1,0:T(8,128)(2,1)S(1)}, u32[]{:S(2)}, u32[]{:S(2)}) collective-permute-start(bf16[2,3,256,256]{3,2,1,0:T(8,128)(2,1)} %pad_maximum_fusion), channel_id=1, source_target_pairs={{0,64},{64,0},{1,65},{65,1},{2,66},{66,2},{3,67},{67,3},{4,68},{68... | collective-permute-start | bytes 2359304 | tf_op jit(solution)/shard_map/ppermute | solution.py:253
  87.0 4.2 %collective-permute-start.3 = (bf16[256,1536]{1,0:T(8,128)(2,1)S(1)}, bf16[256,1536]{1,0:T(8,128)(2,1)S(1)}, u32[]{:S(2)}, u32[]{:S(2)}) collective-permute-start(bf16[256,1536]{1,0:T(8,128)(2,1)S(1)} %get-tuple-element.8), channel_id=1, source_target_pairs={{0,32},{32,0},{1,33},{33,1},{2,34},{34,2},{3,35},{35,3},{4,36},{36... | collective-permute-start | bytes 2359304 | tf_op jit(solution)/shard_map/ppermute | solution.py:257
  124.0 4.2 %collective-permute-start.4 = (bf16[256,1536]{1,0:T(8,128)(2,1)S(1)}, bf16[256,1536]{1,0:T(8,128)(2,1)S(1)}, u32[]{:S(2)}, u32[]{:S(2)}) collective-permute-start(bf16[256,1536]{1,0:T(8,128)(2,1)S(1)} %bitcast.18), channel_id=1, source_target_pairs={{0,32},{32,0},{1,33},{33,1},{2,34},{34,2},{3,35},{35,3},{4,36},{36... | collective-permute-start | bytes 2359304 | tf_op jit(solution)/shard_map/ppermute | solution.py:260
  129.9 21.8 %collective-permute-start.6 = (bf16[2,3,256,256]{3,2,1,0:T(8,128)(2,1)}, bf16[2,3,256,256]{3,2,1,0:T(8,128)(2,1)}, u32[]{:S(2)}, u32[]{:S(2)}) collective-permute-start(bf16[2,3,256,256]{3,2,1,0:T(8,128)(2,1)} %get-tuple-element.11), channel_id=1, source_target_pairs={{0,64},{64,0},{1,65},{65,1},{2,66},{66,2},{3,67},{67,3},{4,68},{68... | collective-permute-start | bytes 2359304 | tf_op jit(solution)/shard_map/ppermute | solution.py:267
  135.3 31.5 %all-to-all-start.3 = ((bf16[16,128,128]{2,1,0:T(8,128)(2,1)}), bf16[16,128,128]{2,1,0:T(8,128)(2,1)}, u32[]{:S(2)}, u32[]{:S(2)}) async-start(bf16[16,128,128]{2,1,0:T(8,128)(2,1)} %input_terms.1), calls=%async_computation.3 | async-start | bytes 1048576 | tf_op jit(solution)/shard_map/all_to_all | solution.py:243
  153.8 26.2 %collective-permute-start.7 = (bf16[3,256,256]{2,1,0:T(8,128)(2,1)}, bf16[3,256,256]{2,1,0:T(8,128)(2,1)S(1)}, u32[]{:S(2)}, u32[]{:S(2)}) collective-permute-start(bf16[3,256,256]{2,1,0:T(8,128)(2,1)} %fusion.3), channel_id=1, source_target_pairs={{0,1},{1,0},{2,3},{3,2},{4,5},{5,4},{6,7},{7,6},{8,9},{9,8},{10,11... | collective-permute-start | bytes 1179656 | tf_op jit(solution)/shard_map/ppermute | solution.py:269
  168.5 11.4 %collective-permute-start.5 = (bf16[128,128]{1,0:T(8,128)(2,1)}, bf16[128,128]{1,0:T(8,128)(2,1)S(1)}, u32[]{:S(2)}, u32[]{:S(2)}) collective-permute-start(bf16[128,128]{1,0:T(8,128)(2,1)} %reduce_sum.12), channel_id=1, source_target_pairs={{0,0},{2,1},{32,2},{34,3},{4,4},{6,5},{36,6},{38,7},{128,8},{130,9... | collective-permute-start | bytes 98312 | tf_op jit(solution)/shard_map/ppermute | solution.py:264

commit v9 on v8

--- a/solution.py
+++ b/solution.py
@@ -250,6 +250,7 @@
     acts = lax.ppermute(jnp.stack([inputs, out_grad]), AXES, there)
     w = (codes.astype(F32) * scales.astype(F32)).astype(BF16)
     w_z = lax.ppermute(w, "zl", SWAP)
+    acts, w_z = lax.optimization_barrier((acts, w_z))
     w_x = lax.ppermute(jnp.stack([w, w_z]), "x0", SWAP)
     acts = exchange(jnp.broadcast_to(acts[None], (16,) + acts.shape), SPREAD)
 
@@ -259,7 +260,9 @@
     own = exchange(grads, REST).reshape(HALF, GRADS)
     other = lax.ppermute(own, "core", SWAP)
 
-    dx = exchange(input_terms(place, own, other, w, w_z, w_x), SPREAD)
+    dx = input_terms(place, own, other, w, w_z, w_x)
+    dx, acts = lax.optimization_barrier((dx, acts))
+    dx = exchange(dx, SPREAD)
     dx = jnp.sum(dx.astype(F32), axis=0).astype(BF16)
     input_grad = lax.ppermute(dx, AXES, [(b, a) for a, b in there])
 

time: 182 us -> 162 us (0.89)
  waiting for transfers between devices: 78.5 us -> 65.6 us
  starting transfers between devices: 54.1 us -> 47.8 us
    ppermute x1, waiting for transfers between devices: 28.1 us -> 0.01 us  [local(): w_z = lax.ppermute(w, 'zl', SWAP)]
    all_to_all x2, waiting for transfers between devices: 8.63 us -> 18 us  [exchange(): return lax.all_to_all(pieces, axes, split_axis=0, concat_axis=0, tiled=True)]
    ppermute x1, waiting for transfers between devices: 4.09 us -> 10.5 us  [local(): got = lax.ppermute(send, 'x0', SWAP).astype(F32)]
    all_to_all x2, starting transfers between devices: 28.5 us -> 22.8 us  [exchange(): return lax.all_to_all(pieces, axes, split_axis=0, concat_axis=0, tiled=True)]
    ppermute x1, starting transfers between devices: 4.37 us -> 1.91 us  [local(): weight_grad = keep[0] + got[0] + lax.ppermute(send, 'zl', SWAP).astype(F32)]
  transfers between devices with their start and end apart: 10 -> 10, of which waited for: 8 -> 8; matrix products, arithmetic and copies ran while one was open for 3% -> 3% of each run, Pallas kernels for 1% -> 0%
where the time goes in v9:
time: 162 us; the launch traced here: 161 us
  waiting for transfers between devices  65.6 us (40%)
  starting transfers between devices  47.8 us (30%)
  blocking collectives  30.8 us (19%)
  other arithmetic  7.81 us (5%)
  Pallas kernels  6.76 us (4%)
  local copies, waits for them, and re-layouts  1.83 us (1%)
    all_to_all x2, blocking collectives, exchange(): return lax.all_to_all(pieces, axes, split_axis=0, concat_axis=0, tiled=True)  30.8 us
    all_to_all x2, starting transfers between devices, exchange(): return lax.all_to_all(pieces, axes, split_axis=0, concat_axis=0, tiled=True)  22.8 us
    all_to_all x2, waiting for transfers between devices, exchange(): return lax.all_to_all(pieces, axes, split_axis=0, concat_axis=0, tiled=True)  18 us
    ppermute x1, waiting for transfers between devices, local(): w_x = lax.ppermute(jnp.stack([w, w_z]), 'x0', SWAP)  17.1 us
    ppermute x1, waiting for transfers between devices, local(): got = lax.ppermute(send, 'x0', SWAP).astype(F32)  10.5 us
    ppermute x1, waiting for transfers between devices, local(): input_grad = lax.ppermute(dx, AXES, [(b, a) for a, b in there])  9.2 us
    ppermute x1, waiting for transfers between devices, local(): acts = lax.ppermute(jnp.stack([inputs, out_grad]), AXES, there)  6.3 us
    ppermute x1, starting transfers between devices, local(): acts = lax.ppermute(jnp.stack([inputs, out_grad]), AXES, there)  5.39 us
  transfers between devices with their start and end apart: 10, of which 8 were waited for; matrix products, arithmetic and copies ran while one was open for 3% of the time, Pallas kernels for 0%

profile of v9, /device:TPU:48, one launch (start us, length us, event | category | flops | bytes accessed | tf_op | source)
XLA Modules:
  0.0 161.4 jit_solution(14589676731902660728)
XLA Ops:
  0.6 0.7 bitcast_convert_fusion
  1.3 1.1 multiply_convert_fusion.w_in
  2.4 4.3 %collective-permute-start.1 = (bf16[3,256,256]{2,1,0:T(8,128)(2,1)S(1)}, bf16[3,256,256]{2,1,0:T(8,128)(2,1)S(1)}, u32[]{:S(2)}, u32[]{:S(2)}) collective-permute-start(bf16[3,256,256]{2,1,0:T(8,128)(2,1)S(1)} %multiply_convert_fusion.w_in), channel_id=1, source_target_pairs={{0,1},{1,0},{2,3},{3,2},{4,5},{5,4},{6,7},{7,6},{8,9},{9,8},{10,11... | collective-permute-start | bytes 1179656 | tf_op jit(solution)/shard_map/ppermute | solution.py:252
  6.7 0.8 pad_maximum_fusion.1
  7.5 0.0 copy-start
  7.5 5.4 %collective-permute-start = (bf16[2,128,128]{2,1,0:T(8,128)(2,1)S(1)}, bf16[2,128,128]{2,1,0:T(8,128)(2,1)S(1)}, u32[]{:S(2)}, u32[]{:S(2)}) collective-permute-start(bf16[2,128,128]{2,1,0:T(8,128)(2,1)S(1)} %pad_maximum_fusion.1), channel_id=1, source_target_pairs={{0,0},{1,2},{2,32},{3,34},{4,4},{5,6},{6,36},{7,38},{8,128},{9,130... | collective-permute-start | bytes 196616 | tf_op jit(solution)/shard_map/ppermute | solution.py:250
  12.9 6.3 %collective-permute-done = bf16[2,128,128]{2,1,0:T(8,128)(2,1)S(1)} collective-permute-done((bf16[2,128,128]{2,1,0:T(8,128)(2,1)S(1)}, bf16[2,128,128]{2,1,0:T(8,128)(2,1)S(1)}, u32[]{:S(2)}, u32[]{:S(2)}) %collective-permute-start) | collective-permute-done | bytes 65568 | tf_op jit(solution)/shard_map/ppermute | solution.py:250
  19.2 0.0 collective-permute-done.1.w_z_in
  19.2 1.2 broadcast_in_dim.2
  20.4 15.4 %all-to-all-start = ((bf16[16,2,128,128]{3,2,1,0:T(8,128)(2,1)}), bf16[16,2,128,128]{3,2,1,0:T(8,128)(2,1)S(1)}, u32[]{:S(2)}, u32[]{:S(2)}) async-start(bf16[16,2,128,128]{3,2,1,0:T(8,128)(2,1)} %broadcast_in_dim.2), calls=%async_computation | async-start | bytes 2097152 | tf_op jit(solution)/shard_map/all_to_all | solution.py:243
  35.7 0.0 copy-done
  35.7 0.1 fusion.4
  35.8 0.1 pad_maximum_fusion
  35.9 2.6 %collective-permute-start.2 = (bf16[2,3,256,256]{3,2,1,0:T(8,128)(2,1)S(1)}, bf16[2,3,256,256]{3,2,1,0:T(8,128)(2,1)S(1)}, u32[]{:S(2)}, u32[]{:S(2)}) collective-permute-start(bf16[2,3,256,256]{3,2,1,0:T(8,128)(2,1)S(1)} %pad_maximum_fusion), channel_id=1, source_target_pairs={{0,64},{64,0},{1,65},{65,1},{2,66},{66,2},{3,67},{67,3},{4,68},{68... | collective-permute-start | bytes 2359304 | tf_op jit(solution)/shard_map/ppermute | solution.py:254
  38.5 0.1 pad_add_fusion.place_ref
  38.6 17.1 %collective-permute-done.2.w_x_in = bf16[2,3,256,256]{3,2,1,0:T(8,128)(2,1)S(1)} collective-permute-done((bf16[2,3,256,256]{3,2,1,0:T(8,128)(2,1)S(1)}, bf16[2,3,256,256]{3,2,1,0:T(8,128)(2,1)S(1)}, u32[]{:S(2)}, u32[]{:S(2)}) %collective-permute-start.2) | collective-permute-done | bytes 786464 | tf_op jit(solution)/shard_map/ppermute | solution.py:254
  55.7 13.8 %all-to-all-done.acts_in = bf16[16,2,128,128]{3,2,1,0:T(8,128)(2,1)S(1)} async-done(((bf16[16,2,128,128]{3,2,1,0:T(8,128)(2,1)}), bf16[16,2,128,128]{3,2,1,0:T(8,128)(2,1)S(1)}, u32[]{:S(2)}, u32[]{:S(2)}) %all-to-all-start) | async-done | bytes 1048608 | tf_op jit(solution)/shard_map/all_to_all | solution.py:243
  69.5 2.6 %gates.1 = (f32[256,1536]{1,0:T(8,128)S(1)}, bf16[256,1536]{1,0:T(8,128)(2,1)S(1)}, bf16[2,512,512]{2,1,0:T(8,128)(2,1)S(1)}) custom-call(s32[2]{0:T(128)S(1)} %pad_add_fusion.place_ref, bf16[16,2,128,128]{3,2,1,0:T(8,128)(2,1)S(1)} %all-to-all-done.acts_in, bf16[3,256,256]{2,1,0:T(8,128)(2,1)S(1)} %multiply_convert_fusion.w_in, ...), custom_call_target="tpu_custom_call" | custom-call | flops 800000000 | bytes 6000000 | tf_op jit(solution)/shard_map/gates/pallas_call | solution.py:95
  72.1 1.9 %collective-permute-start.3 = (bf16[256,1536]{1,0:T(8,128)(2,1)S(1)}, bf16[256,1536]{1,0:T(8,128)(2,1)S(1)}, u32[]{:S(2)}, u32[]{:S(2)}) collective-permute-start(bf16[256,1536]{1,0:T(8,128)(2,1)S(1)} %get-tuple-element.14), channel_id=1, source_target_pairs={{0,32},{32,0},{1,33},{33,1},{2,34},{34,2},{3,35},{35,3},{4,36},{36... | collective-permute-start | bytes 2359304 | tf_op jit(solution)/shard_map/ppermute | solution.py:258
  74.1 2.3 %collective-permute-done.3 = bf16[256,1536]{1,0:T(8,128)(2,1)S(1)} collective-permute-done((bf16[256,1536]{1,0:T(8,128)(2,1)S(1)}, bf16[256,1536]{1,0:T(8,128)(2,1)S(1)}, u32[]{:S(2)}, u32[]{:S(2)}) %collective-permute-start.3) | collective-permute-done | bytes 786464 | tf_op jit(solution)/shard_map/ppermute | solution.py:258
  76.3 0.2 add_convert_fusion
  76.5 16.5 %all_to_all.20.parts_ref = bf16[4,64,1536]{2,1,0:T(8,128)(2,1)S(1)} all-to-all(bf16[4,64,1536]{2,1,0:T(8,128)(2,1)S(1)} %bitcast.22), channel_id=1, replica_groups=mesh['yl'=2,'x1'=2,'x0'=2,'core'=2,'yh1'=2,'yh0'=2,'zh1'=2,'zh0'=2,'zl'=..., dimensions={0} | all-to-all | bytes 1572864 | tf_op jit(solution)/shard_map/all_to_all | solution.py:243
  93.1 0.2 hidden_grads.1
  93.2 14.3 %all_to_all.21 = bf16[4,64,1536]{2,1,0:T(8,128)(2,1)S(1)} all-to-all(bf16[4,64,1536]{2,1,0:T(8,128)(2,1)S(1)} %hidden_grads.1), channel_id=1, replica_groups=mesh['yl'=2,'x1'=2,'x0'=2,'core'=2,'yh1'=2,'yh0'=2,'zh1'=2,'zh0'=2,'zl'=..., dimensions={0} | all-to-all | bytes 1572864 | tf_op jit(solution)/shard_map/all_to_all | solution.py:243
  107.6 1.9 %collective-permute-start.4 = (bf16[256,1536]{1,0:T(8,128)(2,1)S(1)}, bf16[256,1536]{1,0:T(8,128)(2,1)S(1)}, u32[]{:S(2)}, u32[]{:S(2)}) collective-permute-start(bf16[256,1536]{1,0:T(8,128)(2,1)S(1)} %bitcast.18), channel_id=1, source_target_pairs={{0,32},{32,0},{1,33},{33,1},{2,34},{34,2},{3,35},{35,3},{4,36},{36... | collective-permute-start | bytes 2359304 | tf_op jit(solution)/shard_map/ppermute | solution.py:261
  109.5 2.3 %collective-permute-done.4.other_in = bf16[256,1536]{1,0:T(8,128)(2,1)S(1)} collective-permute-done((bf16[256,1536]{1,0:T(8,128)(2,1)S(1)}, bf16[256,1536]{1,0:T(8,128)(2,1)S(1)}, u32[]{:S(2)}, u32[]{:S(2)}) %collective-permute-start.4) | collective-permute-done | bytes 786464 | tf_op jit(solution)/shard_map/ppermute | solution.py:261
  111.7 2.3 %input_terms.1 = bf16[16,128,128]{2,1,0:T(8,128)(2,1)} custom-call(s32[2]{0:T(128)S(1)} %pad_add_fusion.place_ref, bf16[256,1536]{1,0:T(8,128)(2,1)S(1)} %bitcast.19, bf16[256,1536]{1,0:T(8,128)(2,1)S(1)} %collective-permute-done.4.other_in, bf16[3,256,256]{2,1,0:T(8,128)(2,1)S(1)} %multiply_convert_fusion.w_in, ...), custom_call_target="tpu_custom_call" | custom-call | flops 540000000 | bytes 4000000 | tf_op jit(solution)/shard_map/input_terms/pallas_call | solution.py:175
  114.1 1.6 weight_terms.1
  115.7 4.8 %collective-permute-start.6 = (bf16[2,3,256,256]{3,2,1,0:T(8,128)(2,1)S(1)}, bf16[2,3,256,256]{3,2,1,0:T(8,128)(2,1)}, u32[]{:S(2)}, u32[]{:S(2)}) collective-permute-start(bf16[2,3,256,256]{3,2,1,0:T(8,128)(2,1)S(1)} %get-tuple-element.19), channel_id=1, source_target_pairs={{0,64},{64,0},{1,65},{65,1},{2,66},{66,2},{3,67},{67,3},{4,68},{68... | collective-permute-start | bytes 2359304 | tf_op jit(solution)/shard_map/ppermute | solution.py:270
  120.5 7.5 %all-to-all-start.3 = ((bf16[16,128,128]{2,1,0:T(8,128)(2,1)}), bf16[16,128,128]{2,1,0:T(8,128)(2,1)}, u32[]{:S(2)}, u32[]{:S(2)}) async-start(bf16[16,128,128]{2,1,0:T(8,128)(2,1)} %input_terms.1), calls=%async_computation.3 | async-start | bytes 1048576 | tf_op jit(solution)/shard_map/all_to_all | solution.py:243
  127.9 10.5 %collective-permute-done.6 = bf16[2,3,256,256]{3,2,1,0:T(8,128)(2,1)} collective-permute-done((bf16[2,3,256,256]{3,2,1,0:T(8,128)(2,1)S(1)}, bf16[2,3,256,256]{3,2,1,0:T(8,128)(2,1)}, u32[]{:S(2)}, u32[]{:S(2)}) %collective-permute-start.6) | collective-permute-done | bytes 786464 | tf_op jit(solution)/shard_map/ppermute | solution.py:270
  138.4 1.3 convert_element_type.31
  139.7 0.8 fusion.3
  140.5 1.9 %collective-permute-start.7 = (bf16[3,256,256]{2,1,0:T(8,128)(2,1)}, bf16[3,256,256]{2,1,0:T(8,128)(2,1)S(1)}, u32[]{:S(2)}, u32[]{:S(2)}) collective-permute-start(bf16[3,256,256]{2,1,0:T(8,128)(2,1)} %fusion.3), channel_id=1, source_target_pairs={{0,1},{1,0},{2,3},{3,2},{4,5},{5,4},{6,7},{7,6},{8,9},{9,8},{10,11... | collective-permute-start | bytes 1179656 | tf_op jit(solution)/shard_map/ppermute | solution.py:272
  142.4 4.2 %all-to-all-done.3 = bf16[16,128,128]{2,1,0:T(8,128)(2,1)} async-done(((bf16[16,128,128]{2,1,0:T(8,128)(2,1)}), bf16[16,128,128]{2,1,0:T(8,128)(2,1)}, u32[]{:S(2)}, u32[]{:S(2)}) %all-to-all-start.3) | async-done | bytes 524320 | tf_op jit(solution)/shard_map/all_to_all | solution.py:243
  146.6 1.7 %reduce_sum.12 = bf16[128,128]{1,0:T(8,128)(2,1)} reduce(bf16[16,128,128]{2,1,0:T(8,128)(2,1)} %all-to-all-done.3, bf16[]{:T(256)} %constant.12.clone.1), dimensions={0}, to_apply=%region_0.0 | reduce | flops 245760 | bytes 557058 | tf_op jit(solution)/shard_map/reduce_sum | solution.py:266
  148.3 2.2 %collective-permute-start.5 = (bf16[128,128]{1,0:T(8,128)(2,1)}, bf16[128,128]{1,0:T(8,128)(2,1)S(1)}, u32[]{:S(2)}, u32[]{:S(2)}) collective-permute-start(bf16[128,128]{1,0:T(8,128)(2,1)} %reduce_sum.12), channel_id=1, source_target_pairs={{0,0},{2,1},{32,2},{34,3},{4,4},{6,5},{36,6},{38,7},{128,8},{130,9... | collective-permute-start | bytes 98312 | tf_op jit(solution)/shard_map/ppermute | solution.py:267
  150.6 9.2 %collective-permute-done.5 = bf16[128,128]{1,0:T(8,128)(2,1)S(1)} collective-permute-done((bf16[128,128]{1,0:T(8,128)(2,1)}, bf16[128,128]{1,0:T(8,128)(2,1)S(1)}, u32[]{:S(2)}, u32[]{:S(2)}) %collective-permute-start.5) | collective-permute-done | bytes 32800 | tf_op jit(solution)/shard_map/ppermute | solution.py:267
  159.8 0.0 collective-permute-done.7
  159.8 1.0 fusion.2
  160.8 0.6 copy.7
Async XLA Ops:
  2.4 16.8 %collective-permute-start.1 = (bf16[3,256,256]{2,1,0:T(8,128)(2,1)S(1)}, bf16[3,256,256]{2,1,0:T(8,128)(2,1)S(1)}, u32[]{:S(2)}, u32[]{:S(2)}) collective-permute-start(bf16[3,256,256]{2,1,0:T(8,128)(2,1)S(1)} %multiply_convert_fusion.w_in), channel_id=1, source_target_pairs={{0,1},{1,0},{2,3},{3,2},{4,5},{5,4},{6,7},{7,6},{8,9},{9,8},{10,11... | collective-permute-start | bytes 1179656 | tf_op jit(solution)/shard_map/ppermute | solution.py:252
  7.5 28.3 %copy-start = (bf16[3,256,256]{2,1,0:T(8,128)(2,1)S(1)}, bf16[3,256,256]{2,1,0:T(8,128)(2,1)}, u32[]{:S(2)}) copy-start(bf16[3,256,256]{2,1,0:T(8,128)(2,1)} %param.6) | copy-start | bytes 1179652
  7.5 11.7 %collective-permute-start = (bf16[2,128,128]{2,1,0:T(8,128)(2,1)S(1)}, bf16[2,128,128]{2,1,0:T(8,128)(2,1)S(1)}, u32[]{:S(2)}, u32[]{:S(2)}) collective-permute-start(bf16[2,128,128]{2,1,0:T(8,128)(2,1)S(1)} %pad_maximum_fusion.1), channel_id=1, source_target_pairs={{0,0},{1,2},{2,32},{3,34},{4,4},{5,6},{6,36},{7,38},{8,128},{9,130... | collective-permute-start | bytes 196616 | tf_op jit(solution)/shard_map/ppermute | solution.py:250
  20.4 49.1 %all-to-all-start = ((bf16[16,2,128,128]{3,2,1,0:T(8,128)(2,1)}), bf16[16,2,128,128]{3,2,1,0:T(8,128)(2,1)S(1)}, u32[]{:S(2)}, u32[]{:S(2)}) async-start(bf16[16,2,128,128]{3,2,1,0:T(8,128)(2,1)} %broadcast_in_dim.2), calls=%async_computation | async-start | bytes 2097152 | tf_op jit(solution)/shard_map/all_to_all | solution.py:243
  35.9 19.8 %collective-permute-start.2 = (bf16[2,3,256,256]{3,2,1,0:T(8,128)(2,1)S(1)}, bf16[2,3,256,256]{3,2,1,0:T(8,128)(2,1)S(1)}, u32[]{:S(2)}, u32[]{:S(2)}) collective-permute-start(bf16[2,3,256,256]{3,2,1,0:T(8,128)(2,1)S(1)} %pad_maximum_fusion), channel_id=1, source_target_pairs={{0,64},{64,0},{1,65},{65,1},{2,66},{66,2},{3,67},{67,3},{4,68},{68... | collective-permute-start | bytes 2359304 | tf_op jit(solution)/shard_map/ppermute | solution.py:254
  72.1 4.2 %collective-permute-start.3 = (bf16[256,1536]{1,0:T(8,128)(2,1)S(1)}, bf16[256,1536]{1,0:T(8,128)(2,1)S(1)}, u32[]{:S(2)}, u32[]{:S(2)}) collective-permute-start(bf16[256,1536]{1,0:T(8,128)(2,1)S(1)} %get-tuple-element.14), channel_id=1, source_target_pairs={{0,32},{32,0},{1,33},{33,1},{2,34},{34,2},{3,35},{35,3},{4,36},{36... | collective-permute-start | bytes 2359304 | tf_op jit(solution)/shard_map/ppermute | solution.py:258
  107.6 4.2 %collective-permute-start.4 = (bf16[256,1536]{1,0:T(8,128)(2,1)S(1)}, bf16[256,1536]{1,0:T(8,128)(2,1)S(1)}, u32[]{:S(2)}, u32[]{:S(2)}) collective-permute-start(bf16[256,1536]{1,0:T(8,128)(2,1)S(1)} %bitcast.18), channel_id=1, source_target_pairs={{0,32},{32,0},{1,33},{33,1},{2,34},{34,2},{3,35},{35,3},{4,36},{36... | collective-permute-start | bytes 2359304 | tf_op jit(solution)/shard_map/ppermute | solution.py:261
  115.7 22.7 %collective-permute-start.6 = (bf16[2,3,256,256]{3,2,1,0:T(8,128)(2,1)S(1)}, bf16[2,3,256,256]{3,2,1,0:T(8,128)(2,1)}, u32[]{:S(2)}, u32[]{:S(2)}) collective-permute-start(bf16[2,3,256,256]{3,2,1,0:T(8,128)(2,1)S(1)} %get-tuple-element.19), channel_id=1, source_target_pairs={{0,64},{64,0},{1,65},{65,1},{2,66},{66,2},{3,67},{67,3},{4,68},{68... | collective-permute-start | bytes 2359304 | tf_op jit(solution)/shard_map/ppermute | solution.py:270
  120.5 26.1 %all-to-all-start.3 = ((bf16[16,128,128]{2,1,0:T(8,128)(2,1)}), bf16[16,128,128]{2,1,0:T(8,128)(2,1)}, u32[]{:S(2)}, u32[]{:S(2)}) async-start(bf16[16,128,128]{2,1,0:T(8,128)(2,1)} %input_terms.1), calls=%async_computation.3 | async-start | bytes 1048576 | tf_op jit(solution)/shard_map/all_to_all | solution.py:243
  140.5 19.3 %collective-permute-start.7 = (bf16[3,256,256]{2,1,0:T(8,128)(2,1)}, bf16[3,256,256]{2,1,0:T(8,128)(2,1)S(1)}, u32[]{:S(2)}, u32[]{:S(2)}) collective-permute-start(bf16[3,256,256]{2,1,0:T(8,128)(2,1)} %fusion.3), channel_id=1, source_target_pairs={{0,1},{1,0},{2,3},{3,2},{4,5},{5,4},{6,7},{7,6},{8,9},{9,8},{10,11... | collective-permute-start | bytes 1179656 | tf_op jit(solution)/shard_map/ppermute | solution.py:272
  148.3 11.4 %collective-permute-start.5 = (bf16[128,128]{1,0:T(8,128)(2,1)}, bf16[128,128]{1,0:T(8,128)(2,1)S(1)}, u32[]{:S(2)}, u32[]{:S(2)}) collective-permute-start(bf16[128,128]{1,0:T(8,128)(2,1)} %reduce_sum.12), channel_id=1, source_target_pairs={{0,0},{2,1},{32,2},{34,3},{4,4},{6,5},{36,6},{38,7},{128,8},{130,9... | collective-permute-start | bytes 98312 | tf_op jit(solution)/shard_map/ppermute | solution.py:267

commit v10 on v8

v10 whole, which is shorter than its diff:
```python
import itertools

import jax
import jax.numpy as jnp
from jax import lax
from jax.experimental import pallas as pl
from jax.experimental.pallas import tpu as pltpu
from jax.sharding import Mesh, PartitionSpec as P

F32 = jnp.float32
BF16 = jnp.bfloat16
ROW = ("yl", "x1", "x0", "core")
COL = ("yh1", "yh0", "zh1", "zh0", "zl")
AXES = ROW + COL
YH = ("yh1", "yh0")
ZH = ("zh1", "zh0")
REST = ("yl", "x1")
SWAP = [(0, 1), (1, 0)]
TOK = 128
BLOCK = 256
WIDE = 2 * BLOCK
TOKENS = 2 * TOK
SHARE = TOKENS // 4
FEATURES = 4 * BLOCK
GRADS = 3 * WIDE
VMEM_LIMIT = 24 * 1024 * 1024
ANYWHERE = pl.BlockSpec(memory_space=pl.ANY)
SCALARS = pl.BlockSpec(memory_space=pltpu.SMEM)


def turned():
    pairs = []
    for bits in itertools.product(range(2), repeat=len(AXES)):
        yl, x1, x0, core, yh1, yh0, zh1, zh0, zl = bits
        there = (yh1, yh0, x0, core, yl, zl, zh1, zh0, x1)
        pairs.append(tuple(sum(b << (8 - i) for i, b in enumerate(at)) for at in (bits, there)))
    return pairs


def dot(a, b, dims):
    return lax.dot_general(a, b, (dims, ((), ())), preferred_element_type=F32)


def params():
    return pltpu.CompilerParams(vmem_limit_bytes=VMEM_LIMIT)


def chunk(place_ref, t, f):
    core, x0 = place_ref[0], place_ref[1]
    core = core if f < 4 else 1 - core
    x0 = x0 if f % 4 < 2 else 1 - x0
    return 8 * x0 + 4 * core + 2 * t + f % 2


def load_weights(w_ins, w_ref, sems):
    loads = []
    for i, src in enumerate(w_ins):
        rows, cols = pl.ds(i // 2 * BLOCK, BLOCK), pl.ds(i % 2 * BLOCK, BLOCK)
        src = src.at[pl.ds(0, w_ref.shape[0])]
        loads.append(pltpu.make_async_copy(src, w_ref.at[:, rows, cols], sems.at[i]))
        loads[-1].start()
    return loads


def gates_kernel(
    place_ref, acts_in, w0, w1, w2, w3, w4, w5, w6, w7, parts_out, keep_out, send_out,
    acts_ref, w_ref, parts_ref, act_sems, w_sems, out_sems,
):
    w_loads = load_weights((w0, w1, w2, w3, w4, w5, w6, w7), w_ref, w_sems)
    loads = []
    for p in range(2):
        for t in range(2):
            for f in range(8):
                src = acts_in.at[chunk(place_ref, t, f), p]
                dst = acts_ref.at[p, pl.ds(t * TOK, TOK), pl.ds(f * TOK, TOK)]
                loads.append(pltpu.make_async_copy(src, dst, act_sems.at[len(loads)]))
                loads[-1].start()
    for load in loads:
        load.wait()
    stores = []
    for side, out in enumerate((keep_out, send_out)):
        src = acts_ref.at[:, :, pl.ds(side * WIDE, WIDE)]
        stores.append(pltpu.make_async_copy(src, out, out_sems.at[side]))
        stores[-1].start()
    for load in w_loads:
        load.wait()
    for p in range(3):
        sums = dot(acts_ref[p // 2], w_ref[p], ((1,), (0,)))
        parts_ref[:, pl.ds(p * WIDE, WIDE)] = sums.astype(BF16)
    stores.append(pltpu.make_async_copy(parts_ref, parts_out, out_sems.at[2]))
    stores[-1].start()
    for store in stores:
        store.wait()


def gates(place, acts, *weights):
    return pl.pallas_call(
        gates_kernel,
        out_shape=(
            jax.ShapeDtypeStruct((TOKENS, GRADS), BF16),
            jax.ShapeDtypeStruct((2, TOKENS, WIDE), BF16),
            jax.ShapeDtypeStruct((2, TOKENS, WIDE), BF16),
        ),
        in_specs=[SCALARS] + [ANYWHERE] * 9,
        out_specs=(ANYWHERE,) * 3,
        scratch_shapes=[
            pltpu.VMEM((2, TOKENS, FEATURES), BF16),
            pltpu.VMEM((3, FEATURES, WIDE), BF16),
            pltpu.VMEM((TOKENS, GRADS), BF16),
            pltpu.SemaphoreType.DMA((32,)),
            pltpu.SemaphoreType.DMA((8,)),
            pltpu.SemaphoreType.DMA((3,)),
        ],
        compiler_params=params(),
        cost_estimate=pl.CostEstimate(flops=800000000, bytes_accessed=6000000, transcendentals=0),
        name="gates",
    )(place, acts, *weights)


def hidden_kernel(parts_ref, out_ref):
    total = parts_ref[0].astype(F32)
    for i in range(1, 4):
        total += parts_ref[i].astype(F32)
    gate, up, hidden_grad = (total[:, p * WIDE : (p + 1) * WIDE] for p in range(3))
    sig = 1.0 / (1.0 + jnp.exp(-gate))
    act = gate * sig
    gate_grad = (hidden_grad * up * sig * (1.0 + gate * (1.0 - sig))).astype(BF16)
    up_grad = (hidden_grad * act).astype(BF16)
    hidden = (act * up).astype(BF16)
    for i in range(4):
        for p, value in enumerate((gate_grad, up_grad, hidden)):
            out_ref[i, :, pl.ds(p * WIDE, WIDE)] = value


def hidden_grads(parts):
    whole = pl.BlockSpec(memory_space=pltpu.VMEM)
    return pl.pallas_call(
        hidden_kernel,
        out_shape=jax.ShapeDtypeStruct(parts.shape, BF16),
        in_specs=[whole],
        out_specs=whole,
        compiler_params=params(),
        cost_estimate=pl.CostEstimate(flops=2000000, bytes_accessed=1600000, transcendentals=32768),
        name="hidden_grads",
    )(parts)


def input_kernel(
    place_ref, grads_in, w0, w1, w2, w3, w4, w5, w6, w7, dx_out, grads_ref, w_ref, dx_ref, in_sem, w_sems, out_sem
):
    loads = load_weights((w0, w1, w2, w3, w4, w5, w6, w7), w_ref, w_sems)
    loads.append(pltpu.make_async_copy(grads_in, grads_ref, in_sem))
    loads[-1].start()
    for load in loads:
        load.wait()
    dx = dot(grads_ref[:, pl.ds(0, WIDE)], w_ref[0], ((1,), (1,)))
    dx = (dx + dot(grads_ref[:, pl.ds(WIDE, WIDE)], w_ref[1], ((1,), (1,)))).astype(BF16)
    for t in range(2):
        for f in range(8):
            dx_ref[chunk(place_ref, t, f)] = dx[t * TOK : (t + 1) * TOK, f * TOK : (f + 1) * TOK]
    store = pltpu.make_async_copy(dx_ref, dx_out, out_sem)
    store.start()
    store.wait()


def input_terms(place, grads, *weights):
    return pl.pallas_call(
        input_kernel,
        out_shape=jax.ShapeDtypeStruct((16, TOK, TOK), BF16),
        in_specs=[SCALARS] + [ANYWHERE] * 9,
        out_specs=ANYWHERE,
        scratch_shapes=[
            pltpu.VMEM((TOKENS, GRADS), BF16),
            pltpu.VMEM((2, FEATURES, WIDE), BF16),
            pltpu.VMEM((16, TOK, TOK), BF16),
            pltpu.SemaphoreType.DMA,
            pltpu.SemaphoreType.DMA((8,)),
            pltpu.SemaphoreType.DMA,
        ],
        compiler_params=params(),
        cost_estimate=pl.CostEstimate(flops=540000000, bytes_accessed=4000000, transcendentals=0),
        name="input_terms",
    )(place, grads, *weights)


def weight_kernel(
    acts_in, other_acts_in, grads_in, other_grads_in, keep_out, z_out, x_out, xz_out,
    acts_ref, grads_ref, keep_ref, send_ref, in_sems, out_sems,
):
    loads = []
    for i, (acts, grads) in enumerate(((acts_in, grads_in), (other_acts_in, other_grads_in))):
        rows = pl.ds(i * TOKENS, TOKENS)
        loads.append(pltpu.make_async_copy(acts, acts_ref.at[:, rows], in_sems.at[i]))
        loads.append(pltpu.make_async_copy(grads, grads_ref.at[rows], in_sems.at[2 + i]))
    for load in loads:
        load.start()
    for load in loads:
        load.wait()
    stores = []
    for side in (1, 0):
        for p in range(3):
            x = acts_ref[p // 2, :, pl.ds(side * BLOCK, BLOCK)]
            term = dot(x, grads_ref[:, pl.ds(p * WIDE, WIDE)], ((0,), (0,)))
            for j in range(2):
                part = term[:, j * BLOCK : (j + 1) * BLOCK]
                if side or j:
                    send_ref[2 * side + j - 1, p] = part.astype(BF16)
                else:
                    keep_ref[p] = part
        for j in range(2):
            out = ((keep_out, z_out), (x_out, xz_out))[side][j]
            src = send_ref.at[2 * side + j - 1] if side or j else keep_ref
            stores.append(pltpu.make_async_copy(src, out, out_sems.at[2 * side + j]))
            stores[-1].start()
    for store in stores:
        store.wait()


def weight_terms(acts, other_acts, grads, other_grads):
    shape = (3, BLOCK, BLOCK)
    send = jax.ShapeDtypeStruct(shape, BF16)
    return pl.pallas_call(
        weight_kernel,
        out_shape=(jax.ShapeDtypeStruct(shape, F32), send, send, send),
        in_specs=[ANYWHERE] * 4,
        out_specs=(ANYWHERE,) * 4,
        scratch_shapes=[
            pltpu.VMEM((2, 2 * TOKENS, WIDE), BF16),
            pltpu.VMEM((2 * TOKENS, GRADS), BF16),
            pltpu.VMEM(shape, F32),
            pltpu.VMEM((3,) + shape, BF16),
            pltpu.SemaphoreType.DMA((4,)),
            pltpu.SemaphoreType.DMA((4,)),
        ],
        compiler_params=params(),
        cost_estimate=pl.CostEstimate(flops=800000000, bytes_accessed=6000000, transcendentals=0),
        name="weight_terms",
    )(acts, other_acts, grads, other_grads)


def exchange(pieces, axes):
    return lax.all_to_all(pieces, axes, split_axis=0, concat_axis=0, tiled=True)


def local(inputs, out_grad, codes, scales):
    place = jnp.stack([lax.axis_index("core"), lax.axis_index("x0")])
    there = turned()

    acts = lax.ppermute(jnp.stack([inputs, out_grad]), AXES, there)
    acts = exchange(jnp.broadcast_to(acts[None], (4,) + acts.shape), YH)
    w = (codes.astype(F32) * scales.astype(F32)).astype(BF16)
    w_z = lax.ppermute(w, "zl", SWAP)
    w_x = lax.ppermute(w, "x0", SWAP)
    acts, w_z, w_x = lax.optimization_barrier((acts, w_z, w_x))
    weights = [w, w_z, w_x, lax.ppermute(w_z, "x0", SWAP)]
    weights += [lax.ppermute(block, "core", SWAP) for block in weights]
    acts = exchange(jnp.broadcast_to(acts[None], (4,) + acts.shape), ZH).reshape(16, 2, TOK, TOK)

    parts, acts, send = gates(place, acts, *weights)
    other_acts = lax.ppermute(send, "core", SWAP)
    parts = exchange(parts.reshape(4, SHARE, GRADS), REST)
    parts, other_acts = lax.optimization_barrier((parts, other_acts))
    grads = exchange(hidden_grads(parts), REST).reshape(TOKENS, GRADS)
    other_grads = lax.ppermute(grads, "core", SWAP)

    dx = exchange(input_terms(place, grads, *weights), ZH + YH)
    dx = jnp.sum(dx.astype(F32), axis=0).astype(BF16)
    input_grad = lax.ppermute(dx, AXES, [(b, a) for a, b in there])

    weight_grad, z, x, xz = weight_terms(acts, other_acts, grads, other_grads)
    weight_grad += lax.ppermute(z, "zl", SWAP).astype(F32)
    weight_grad += lax.ppermute(x, "x0", SWAP).astype(F32)
    weight_grad += lax.ppermute(xz, ("x0", "zl"), [(i, 3 - i) for i in range(4)]).astype(F32)
    return input_grad, weight_grad


def solution(mesh):
    fine = Mesh(mesh.devices.reshape((2,) * len(AXES)), AXES)
    return jax.shard_map(
        local,
        mesh=fine,
        in_specs=(P(ROW, COL), P(ROW, COL), P(None, ROW, COL), P(None, ROW, COL)),
        out_specs=(P(ROW, COL), P(None, ROW, COL)),
        check_vma=False,
    )
```

time: 182 us -> 152 us (0.84)
  the two profiles are of different devices: /device:TPU:48 before, /device:TPU:1 now
where the time goes in v10:
time: 152 us; the launch traced here: 151 us
  starting transfers between devices  78.7 us (52%)
  waiting for transfers between devices  34.8 us (23%)
  blocking collectives  14.8 us (10%)
  Pallas kernels  9.9 us (7%)
  local copies, waits for them, and re-layouts  7.99 us (5%)
  other arithmetic  4.09 us (3%)
    all_to_all x4, starting transfers between devices, exchange(): return lax.all_to_all(pieces, axes, split_axis=0, concat_axis=0, tiled=True)  35.4 us
    all_to_all x4, waiting for transfers between devices, exchange(): return lax.all_to_all(pieces, axes, split_axis=0, concat_axis=0, tiled=True)  18.1 us
    all_to_all x1, blocking collectives, exchange(): return lax.all_to_all(pieces, axes, split_axis=0, concat_axis=0, tiled=True)  14.8 us
    ppermute x4, starting transfers between devices, local(): weights += [lax.ppermute(block, 'core', SWAP) for block in weights]  12.2 us
    ppermute x1, waiting for transfers between devices, local(): lax.ppermute(xz, ('x0', 'zl'), [(i, 3 - i) for i in range(4)]).astype(F32)  8.48 us
    ppermute x1, starting transfers between devices, local(): w_z = lax.ppermute(w, 'zl', SWAP)  6.64 us
    unnamed x15, local copies, waits for them, and re-layouts  6 us
    ppermute x1, waiting for transfers between devices, local(): weight_grad += lax.ppermute(z, 'zl', SWAP).astype(F32)  4.23 us
  transfers between devices with their start and end apart: 18, of which 8 were waited for; matrix products, arithmetic and copies ran while one was open for 2% of the time, Pallas kernels for 4%

profile of v10, /device:TPU:1, one launch (start us, length us, event | category | flops | bytes accessed | tf_op | source)
XLA Modules:
  0.0 151.1 jit_solution(23920476610037268)
XLA Ops:
  0.6 0.0 copy-start.6
  0.6 0.8 pad_maximum_fusion
  1.4 0.7 collective-permute-start
  2.1 0.0 copy-done.6
  2.1 1.1 multiply_convert_fusion.w0
  3.2 3.9 %collective-permute-start.2 = (bf16[3,256,256]{2,1,0:T(8,128)(2,1)S(1)}, bf16[3,256,256]{2,1,0:T(8,128)(2,1)S(1)}, u32[]{:S(2)}, u32[]{:S(2)}) collective-permute-start(bf16[3,256,256]{2,1,0:T(8,128)(2,1)S(1)} %multiply_convert_fusion.w0), channel_id=1, source_target_pairs={{0,64},{64,0},{1,65},{65,1},{2,66},{66,2},{3,67},{67,3},{4,68},{68... | collective-permute-start | bytes 1179656 | tf_op jit(solution)/shard_map/ppermute | solution.py:253
  7.1 6.6 %collective-permute-start.1 = (bf16[3,256,256]{2,1,0:T(8,128)(2,1)S(1)}, bf16[3,256,256]{2,1,0:T(8,128)(2,1)S(1)}, u32[]{:S(2)}, u32[]{:S(2)}) collective-permute-start(bf16[3,256,256]{2,1,0:T(8,128)(2,1)S(1)} %multiply_convert_fusion.w0), channel_id=1, source_target_pairs={{0,1},{1,0},{2,3},{3,2},{4,5},{5,4},{6,7},{7,6},{8,9},{9,8},{10,11... | collective-permute-start | bytes 1179656 | tf_op jit(solution)/shard_map/ppermute | solution.py:252
  13.8 0.0 collective-permute-done
  13.8 0.7 broadcast_in_dim.4
  14.5 6.2 %all-to-all-start = ((bf16[4,2,128,128]{3,2,1,0:T(8,128)(2,1)}), bf16[4,2,128,128]{3,2,1,0:T(8,128)(2,1)S(1)}, u32[]{:S(2)}, u32[]{:S(2)}) async-start(bf16[4,2,128,128]{3,2,1,0:T(8,128)(2,1)} %broadcast_in_dim.4), calls=%async_computation | async-start | bytes 524288 | tf_op jit(solution)/shard_map/all_to_all | solution.py:242
  20.8 0.0 collective-permute-done.2.w2
  20.8 0.6 collective-permute-done.1.w1
  21.4 7.6 %all-to-all-done = bf16[4,2,128,128]{3,2,1,0:T(8,128)(2,1)S(1)} async-done(((bf16[4,2,128,128]{3,2,1,0:T(8,128)(2,1)}), bf16[4,2,128,128]{3,2,1,0:T(8,128)(2,1)S(1)}, u32[]{:S(2)}, u32[]{:S(2)}) %all-to-all-start) | async-done | bytes 262176 | tf_op jit(solution)/shard_map/all_to_all | solution.py:242
  28.9 1.3 broadcast_in_dim.5
  30.2 10.0 %all-to-all-start.1 = ((bf16[4,4,2,128,128]{4,3,2,1,0:T(8,128)(2,1)}), bf16[4,4,2,128,128]{4,3,2,1,0:T(8,128)(2,1)S(1)}, u32[]{:S(2)}, u32[]{:S(2)}) async-start(bf16[4,4,2,128,128]{4,3,2,1,0:T(8,128)(2,1)} %broadcast_in_dim.5), calls=%async_computation.1 | async-start | bytes 2097152 | tf_op jit(solution)/shard_map/all_to_all | solution.py:242
  40.2 3.0 %collective-permute-start.3 = (bf16[3,256,256]{2,1,0:T(8,128)(2,1)S(1)}, bf16[3,256,256]{2,1,0:T(8,128)(2,1)S(1)}, u32[]{:S(2)}, u32[]{:S(2)}) collective-permute-start(bf16[3,256,256]{2,1,0:T(8,128)(2,1)S(1)} %collective-permute-done.1.w1), channel_id=1, source_target_pairs={{0,64},{64,0},{1,65},{65,1},{2,66},{66,2},{3,67},{67,3},{4,68},{68... | collective-permute-start | bytes 1179656 | tf_op jit(solution)/shard_map/ppermute | solution.py:255
  43.3 5.8 %collective-permute-start.4 = (bf16[3,256,256]{2,1,0:T(8,128)(2,1)S(1)}, bf16[3,256,256]{2,1,0:T(8,128)(2,1)S(1)}, u32[]{:S(2)}, u32[]{:S(2)}) collective-permute-start(bf16[3,256,256]{2,1,0:T(8,128)(2,1)S(1)} %multiply_convert_fusion.w0), channel_id=1, source_target_pairs={{0,32},{32,0},{1,33},{33,1},{2,34},{34,2},{3,35},{35,3},{4,36},{36... | collective-permute-start | bytes 1179656 | tf_op jit(solution)/shard_map/ppermute | solution.py:256
  49.1 1.9 %collective-permute-start.5 = (bf16[3,256,256]{2,1,0:T(8,128)(2,1)S(1)}, bf16[3,256,256]{2,1,0:T(8,128)(2,1)S(1)}, u32[]{:S(2)}, u32[]{:S(2)}) collective-permute-start(bf16[3,256,256]{2,1,0:T(8,128)(2,1)S(1)} %collective-permute-done.1.w1), channel_id=1, source_target_pairs={{0,32},{32,0},{1,33},{33,1},{2,34},{34,2},{3,35},{35,3},{4,36},{36... | collective-permute-start | bytes 1179656 | tf_op jit(solution)/shard_map/ppermute | solution.py:256
  51.0 2.4 %collective-permute-start.6 = (bf16[3,256,256]{2,1,0:T(8,128)(2,1)S(1)}, bf16[3,256,256]{2,1,0:T(8,128)(2,1)}, u32[]{:S(2)}, u32[]{:S(2)}) collective-permute-start(bf16[3,256,256]{2,1,0:T(8,128)(2,1)S(1)} %collective-permute-done.2.w2), channel_id=1, source_target_pairs={{0,32},{32,0},{1,33},{33,1},{2,34},{34,2},{3,35},{35,3},{4,36},{36... | collective-permute-start | bytes 1179656 | tf_op jit(solution)/shard_map/ppermute | solution.py:256
  53.4 0.0 collective-permute-done.3.w3
  53.5 2.0 %collective-permute-start.7 = (bf16[3,256,256]{2,1,0:T(8,128)(2,1)S(1)}, bf16[3,256,256]{2,1,0:T(8,128)(2,1)}, u32[]{:S(2)}, u32[]{:S(2)}) collective-permute-start(bf16[3,256,256]{2,1,0:T(8,128)(2,1)S(1)} %collective-permute-done.3.w3), channel_id=1, source_target_pairs={{0,32},{32,0},{1,33},{33,1},{2,34},{34,2},{3,35},{35,3},{4,36},{36... | collective-permute-start | bytes 1179656 | tf_op jit(solution)/shard_map/ppermute | solution.py:256
  55.5 0.1 pad_add_fusion.place_ref
  55.6 0.0 collective-permute-done.4.w4
  55.6 0.0 collective-permute-done.6.w6
  55.6 0.0 collective-permute-done.5.w5
  55.6 1.6 %collective-permute-done.7.w7 = bf16[3,256,256]{2,1,0:T(8,128)(2,1)} collective-permute-done((bf16[3,256,256]{2,1,0:T(8,128)(2,1)S(1)}, bf16[3,256,256]{2,1,0:T(8,128)(2,1)}, u32[]{:S(2)}, u32[]{:S(2)}) %collective-permute-start.7) | collective-permute-done | bytes 393248 | tf_op jit(solution)/shard_map/ppermute | solution.py:256
  57.2 0.0 all-to-all-done.1
  57.2 3.3 %gates.1 = (bf16[256,1536]{1,0:T(8,128)(2,1)S(1)}, bf16[2,256,512]{2,1,0:T(8,128)(2,1)S(1)}, bf16[2,256,512]{2,1,0:T(8,128)(2,1)S(1)}) custom-call(s32[2]{0:T(128)S(1)} %pad_add_fusion.place_ref, bf16[16,2,128,128]{3,2,1,0:T(8,128)(2,1)S(1)} %bitcast.10, bf16[3,256,256]{2,1,0:T(8,128)(2,1)S(1)} %multiply_convert_fusion.w0, ...), custom_call_target="tpu_custom_call" | custom-call | flops 800000000 | bytes 6000000 | tf_op jit(solution)/shard_map/gates/pallas_call | solution.py:97
  60.5 0.0 copy-start
  60.5 0.9 copy-done
  61.4 0.0 copy-start.1
  61.4 0.8 copy-done.1
  62.2 0.0 copy-start.5
  62.2 0.8 copy-done.5
  63.0 10.6 %all-to-all-start.2 = ((bf16[4,64,1536]{2,1,0:T(8,128)(2,1)}), bf16[4,64,1536]{2,1,0:T(8,128)(2,1)S(1)}, u32[]{:S(2)}, u32[]{:S(2)}) async-start(bf16[4,64,1536]{2,1,0:T(8,128)(2,1)} %bitcast.14), calls=%async_computation.2 | async-start | bytes 1572864 | tf_op jit(solution)/shard_map/all_to_all | solution.py:242
  73.6 3.5 %collective-permute-start.8 = (bf16[2,256,512]{2,1,0:T(8,128)(2,1)}, bf16[2,256,512]{2,1,0:T(8,128)(2,1)S(1)}, u32[]{:S(2)}, u32[]{:S(2)}) collective-permute-start(bf16[2,256,512]{2,1,0:T(8,128)(2,1)} %copy-done.5), channel_id=1, source_target_pairs={{0,32},{32,0},{1,33},{33,1},{2,34},{34,2},{3,35},{35,3},{4,36},{36... | collective-permute-start | bytes 1572872 | tf_op jit(solution)/shard_map/ppermute | solution.py:260
  77.1 1.7 %collective-permute-done.8.other_acts_in = bf16[2,256,512]{2,1,0:T(8,128)(2,1)S(1)} collective-permute-done((bf16[2,256,512]{2,1,0:T(8,128)(2,1)}, bf16[2,256,512]{2,1,0:T(8,128)(2,1)S(1)}, u32[]{:S(2)}, u32[]{:S(2)}) %collective-permute-start.8) | collective-permute-done | bytes 524320 | tf_op jit(solution)/shard_map/ppermute | solution.py:260
  78.8 0.0 copy-start.3
  78.8 0.8 copy-done.3
  79.7 5.7 %all-to-all-done.2.parts_ref = bf16[4,64,1536]{2,1,0:T(8,128)(2,1)S(1)} async-done(((bf16[4,64,1536]{2,1,0:T(8,128)(2,1)}), bf16[4,64,1536]{2,1,0:T(8,128)(2,1)S(1)}, u32[]{:S(2)}, u32[]{:S(2)}) %all-to-all-start.2) | async-done | bytes 786464 | tf_op jit(solution)/shard_map/all_to_all | solution.py:242
  85.4 0.2 hidden_grads.1
  85.5 14.8 %all_to_all.25 = bf16[4,64,1536]{2,1,0:T(8,128)(2,1)S(1)} all-to-all(bf16[4,64,1536]{2,1,0:T(8,128)(2,1)S(1)} %hidden_grads.1), channel_id=1, replica_groups=mesh['yl'=2,'x1'=2,'x0'=2,'core'=2,'yh1'=2,'yh0'=2,'zh1'=2,'zh0'=2,'zl'=..., dimensions={0} | all-to-all | bytes 1572864 | tf_op jit(solution)/shard_map/all_to_all | solution.py:242
  100.3 4.1 %collective-permute-start.10 = (bf16[256,1536]{1,0:T(8,128)(2,1)S(1)}, bf16[256,1536]{1,0:T(8,128)(2,1)}, u32[]{:S(2)}, u32[]{:S(2)}) collective-permute-start(bf16[256,1536]{1,0:T(8,128)(2,1)S(1)} %bitcast.11), channel_id=1, source_target_pairs={{0,32},{32,0},{1,33},{33,1},{2,34},{34,2},{3,35},{35,3},{4,36},{36... | collective-permute-start | bytes 2359304 | tf_op jit(solution)/shard_map/ppermute | solution.py:264
  104.4 3.3 %input_terms.1 = bf16[16,128,128]{2,1,0:T(8,128)(2,1)} custom-call(s32[2]{0:T(128)S(1)} %pad_add_fusion.place_ref, bf16[256,1536]{1,0:T(8,128)(2,1)S(1)} %bitcast.12, bf16[3,256,256]{2,1,0:T(8,128)(2,1)S(1)} %multiply_convert_fusion.w0, bf16[3,256,256]{2,1,0:T(8,128)(2,1)S(1)} %collective-permute-done.1.w1, ...), custom_call_target="tpu_custom_call" | custom-call | flops 540000000 | bytes 4000000 | tf_op jit(solution)/shard_map/input_terms/pallas_call | solution.py:167
  107.8 8.6 %all-to-all-start.4 = ((bf16[16,128,128]{2,1,0:T(8,128)(2,1)}), bf16[16,128,128]{2,1,0:T(8,128)(2,1)}, u32[]{:S(2)}, u32[]{:S(2)}) async-start(bf16[16,128,128]{2,1,0:T(8,128)(2,1)} %input_terms.1), calls=%async_computation.4 | async-start | bytes 1048576 | tf_op jit(solution)/shard_map/all_to_all | solution.py:242
  116.3 0.0 collective-permute-done.10.other_grads_in
  116.4 0.0 copy-start.2
  116.4 1.0 copy-done.2
  117.4 0.0 copy-start.4
  117.4 1.0 copy-done.4
  118.4 3.1 %weight_terms.1 = (f32[3,256,256]{2,1,0:T(8,128)S(1)}, bf16[3,256,256]{2,1,0:T(8,128)(2,1)S(1)}, bf16[3,256,256]{2,1,0:T(8,128)(2,1)S(1)}, bf16[3,256,256]{2,1,0:T(8,128)(2,1)S(1)}) custom-call(bf16[2,256,512]{2,1,0:T(8,128)(2,1)S(1)} %copy-done.2, bf16[2,256,512]{2,1,0:T(8,128)(2,1)S(1)} %copy-done.4, bf16[256,1536]{1,0:T(8,128)(2,1)S(1)} %bitcast.13, ...), custom_call_target="tpu_custom_call" | custom-call | flops 800000000 | bytes 6000000 | tf_op jit(solution)/shard_map/weight_terms/pallas_call | solution.py:222
  121.6 3.5 %collective-permute-start.11 = (bf16[3,256,256]{2,1,0:T(8,128)(2,1)S(1)}, bf16[3,256,256]{2,1,0:T(8,128)(2,1)S(1)}, u32[]{:S(2)}, u32[]{:S(2)}) collective-permute-start(bf16[3,256,256]{2,1,0:T(8,128)(2,1)S(1)} %get-tuple-element.23), channel_id=1, source_target_pairs={{0,1},{1,0},{2,3},{3,2},{4,5},{5,4},{6,7},{7,6},{8,9},{9,8},{10,11... | collective-permute-start | bytes 1179656 | tf_op jit(solution)/shard_map/ppermute | solution.py:271
  125.1 1.9 %collective-permute-start.12 = (bf16[3,256,256]{2,1,0:T(8,128)(2,1)S(1)}, bf16[3,256,256]{2,1,0:T(8,128)(2,1)S(1)}, u32[]{:S(2)}, u32[]{:S(2)}) collective-permute-start(bf16[3,256,256]{2,1,0:T(8,128)(2,1)S(1)} %get-tuple-element.24), channel_id=1, source_target_pairs={{0,64},{64,0},{1,65},{65,1},{2,66},{66,2},{3,67},{67,3},{4,68},{68... | collective-permute-start | bytes 1179656 | tf_op jit(solution)/shard_map/ppermute | solution.py:272
  127.0 3.1 %collective-permute-start.13 = (bf16[3,256,256]{2,1,0:T(8,128)(2,1)S(1)}, bf16[3,256,256]{2,1,0:T(8,128)(2,1)S(1)}, u32[]{:S(2)}, u32[]{:S(2)}) collective-permute-start(bf16[3,256,256]{2,1,0:T(8,128)(2,1)S(1)} %get-tuple-element.25), channel_id=1, source_target_pairs={{0,65},{1,64},{64,1},{65,0},{2,67},{3,66},{66,3},{67,2},{4,69},{5,... | collective-permute-start | bytes 1179656 | tf_op jit(solution)/shard_map/ppermute | solution.py:273
  130.1 4.9 %all-to-all-done.4 = bf16[16,128,128]{2,1,0:T(8,128)(2,1)} async-done(((bf16[16,128,128]{2,1,0:T(8,128)(2,1)}), bf16[16,128,128]{2,1,0:T(8,128)(2,1)}, u32[]{:S(2)}, u32[]{:S(2)}) %all-to-all-start.4) | async-done | bytes 524320 | tf_op jit(solution)/shard_map/all_to_all | solution.py:242
  135.0 1.1 reduce_sum.12
  136.1 0.7 collective-permute-start.9
  136.8 0.0 collective-permute-done.9
  136.8 4.2 %collective-permute-done.11 = bf16[3,256,256]{2,1,0:T(8,128)(2,1)S(1)} collective-permute-done((bf16[3,256,256]{2,1,0:T(8,128)(2,1)S(1)}, bf16[3,256,256]{2,1,0:T(8,128)(2,1)S(1)}, u32[]{:S(2)}, u32[]{:S(2)}) %collective-permute-start.11) | collective-permute-done | bytes 393248 | tf_op jit(solution)/shard_map/ppermute | solution.py:271
  141.0 0.0 collective-permute-done.12
  141.0 8.5 %collective-permute-done.13 = bf16[3,256,256]{2,1,0:T(8,128)(2,1)S(1)} collective-permute-done((bf16[3,256,256]{2,1,0:T(8,128)(2,1)S(1)}, bf16[3,256,256]{2,1,0:T(8,128)(2,1)S(1)}, u32[]{:S(2)}, u32[]{:S(2)}) %collective-permute-start.13) | collective-permute-done | bytes 393248 | tf_op jit(solution)/shard_map/ppermute | solution.py:273
  149.5 1.0 convert_add_fusion
  150.5 0.6 copy.7
  (1 shorter events, 0.0 us)
Async XLA Ops:
  0.6 1.5 copy-start.6
  1.4 12.4 %collective-permute-start = (bf16[2,128,128]{2,1,0:T(8,128)(2,1)S(1)}, bf16[2,128,128]{2,1,0:T(8,128)(2,1)S(1)}, u32[]{:S(2)}, u32[]{:S(2)}) collective-permute-start(bf16[2,128,128]{2,1,0:T(8,128)(2,1)S(1)} %pad_maximum_fusion), channel_id=1, source_target_pairs={{0,0},{1,8},{2,2},{3,10},{4,4},{5,12},{6,6},{7,14},{8,128},{9,136}... | collective-permute-start | bytes 196616 | tf_op jit(solution)/shard_map/ppermute | solution.py:249
  3.2 17.6 %collective-permute-start.2 = (bf16[3,256,256]{2,1,0:T(8,128)(2,1)S(1)}, bf16[3,256,256]{2,1,0:T(8,128)(2,1)S(1)}, u32[]{:S(2)}, u32[]{:S(2)}) collective-permute-start(bf16[3,256,256]{2,1,0:T(8,128)(2,1)S(1)} %multiply_convert_fusion.w0), channel_id=1, source_target_pairs={{0,64},{64,0},{1,65},{65,1},{2,66},{66,2},{3,67},{67,3},{4,68},{68... | collective-permute-start | bytes 1179656 | tf_op jit(solution)/shard_map/ppermute | solution.py:253
  7.1 14.2 %collective-permute-start.1 = (bf16[3,256,256]{2,1,0:T(8,128)(2,1)S(1)}, bf16[3,256,256]{2,1,0:T(8,128)(2,1)S(1)}, u32[]{:S(2)}, u32[]{:S(2)}) collective-permute-start(bf16[3,256,256]{2,1,0:T(8,128)(2,1)S(1)} %multiply_convert_fusion.w0), channel_id=1, source_target_pairs={{0,1},{1,0},{2,3},{3,2},{4,5},{5,4},{6,7},{7,6},{8,9},{9,8},{10,11... | collective-permute-start | bytes 1179656 | tf_op jit(solution)/shard_map/ppermute | solution.py:252
  14.5 14.4 %all-to-all-start = ((bf16[4,2,128,128]{3,2,1,0:T(8,128)(2,1)}), bf16[4,2,128,128]{3,2,1,0:T(8,128)(2,1)S(1)}, u32[]{:S(2)}, u32[]{:S(2)}) async-start(bf16[4,2,128,128]{3,2,1,0:T(8,128)(2,1)} %broadcast_in_dim.4), calls=%async_computation | async-start | bytes 524288 | tf_op jit(solution)/shard_map/all_to_all | solution.py:242
  30.2 27.0 %all-to-all-start.1 = ((bf16[4,4,2,128,128]{4,3,2,1,0:T(8,128)(2,1)}), bf16[4,4,2,128,128]{4,3,2,1,0:T(8,128)(2,1)S(1)}, u32[]{:S(2)}, u32[]{:S(2)}) async-start(bf16[4,4,2,128,128]{4,3,2,1,0:T(8,128)(2,1)} %broadcast_in_dim.5), calls=%async_computation.1 | async-start | bytes 2097152 | tf_op jit(solution)/shard_map/all_to_all | solution.py:242
  40.2 13.3 %collective-permute-start.3 = (bf16[3,256,256]{2,1,0:T(8,128)(2,1)S(1)}, bf16[3,256,256]{2,1,0:T(8,128)(2,1)S(1)}, u32[]{:S(2)}, u32[]{:S(2)}) collective-permute-start(bf16[3,256,256]{2,1,0:T(8,128)(2,1)S(1)} %collective-permute-done.1.w1), channel_id=1, source_target_pairs={{0,64},{64,0},{1,65},{65,1},{2,66},{66,2},{3,67},{67,3},{4,68},{68... | collective-permute-start | bytes 1179656 | tf_op jit(solution)/shard_map/ppermute | solution.py:255
  43.3 12.3 %collective-permute-start.4 = (bf16[3,256,256]{2,1,0:T(8,128)(2,1)S(1)}, bf16[3,256,256]{2,1,0:T(8,128)(2,1)S(1)}, u32[]{:S(2)}, u32[]{:S(2)}) collective-permute-start(bf16[3,256,256]{2,1,0:T(8,128)(2,1)S(1)} %multiply_convert_fusion.w0), channel_id=1, source_target_pairs={{0,32},{32,0},{1,33},{33,1},{2,34},{34,2},{3,35},{35,3},{4,36},{36... | collective-permute-start | bytes 1179656 | tf_op jit(solution)/shard_map/ppermute | solution.py:256
  49.1 6.5 %collective-permute-start.5 = (bf16[3,256,256]{2,1,0:T(8,128)(2,1)S(1)}, bf16[3,256,256]{2,1,0:T(8,128)(2,1)S(1)}, u32[]{:S(2)}, u32[]{:S(2)}) collective-permute-start(bf16[3,256,256]{2,1,0:T(8,128)(2,1)S(1)} %collective-permute-done.1.w1), channel_id=1, source_target_pairs={{0,32},{32,0},{1,33},{33,1},{2,34},{34,2},{3,35},{35,3},{4,36},{36... | collective-permute-start | bytes 1179656 | tf_op jit(solution)/shard_map/ppermute | solution.py:256
  51.0 4.6 %collective-permute-start.6 = (bf16[3,256,256]{2,1,0:T(8,128)(2,1)S(1)}, bf16[3,256,256]{2,1,0:T(8,128)(2,1)}, u32[]{:S(2)}, u32[]{:S(2)}) collective-permute-start(bf16[3,256,256]{2,1,0:T(8,128)(2,1)S(1)} %collective-permute-done.2.w2), channel_id=1, source_target_pairs={{0,32},{32,0},{1,33},{33,1},{2,34},{34,2},{3,35},{35,3},{4,36},{36... | collective-permute-start | bytes 1179656 | tf_op jit(solution)/shard_map/ppermute | solution.py:256
  53.5 3.7 %collective-permute-start.7 = (bf16[3,256,256]{2,1,0:T(8,128)(2,1)S(1)}, bf16[3,256,256]{2,1,0:T(8,128)(2,1)}, u32[]{:S(2)}, u32[]{:S(2)}) collective-permute-start(bf16[3,256,256]{2,1,0:T(8,128)(2,1)S(1)} %collective-permute-done.3.w3), channel_id=1, source_target_pairs={{0,32},{32,0},{1,33},{33,1},{2,34},{34,2},{3,35},{35,3},{4,36},{36... | collective-permute-start | bytes 1179656 | tf_op jit(solution)/shard_map/ppermute | solution.py:256
  60.5 0.9 copy-start
  61.4 0.8 copy-start.1
  62.2 0.8 copy-start.5
  63.0 22.4 %all-to-all-start.2 = ((bf16[4,64,1536]{2,1,0:T(8,128)(2,1)}), bf16[4,64,1536]{2,1,0:T(8,128)(2,1)S(1)}, u32[]{:S(2)}, u32[]{:S(2)}) async-start(bf16[4,64,1536]{2,1,0:T(8,128)(2,1)} %bitcast.14), calls=%async_computation.2 | async-start | bytes 1572864 | tf_op jit(solution)/shard_map/all_to_all | solution.py:242
  73.6 5.3 %collective-permute-start.8 = (bf16[2,256,512]{2,1,0:T(8,128)(2,1)}, bf16[2,256,512]{2,1,0:T(8,128)(2,1)S(1)}, u32[]{:S(2)}, u32[]{:S(2)}) collective-permute-start(bf16[2,256,512]{2,1,0:T(8,128)(2,1)} %copy-done.5), channel_id=1, source_target_pairs={{0,32},{32,0},{1,33},{33,1},{2,34},{34,2},{3,35},{35,3},{4,36},{36... | collective-permute-start | bytes 1572872 | tf_op jit(solution)/shard_map/ppermute | solution.py:260
  78.8 0.8 copy-start.3
  100.3 16.1 %collective-permute-start.10 = (bf16[256,1536]{1,0:T(8,128)(2,1)S(1)}, bf16[256,1536]{1,0:T(8,128)(2,1)}, u32[]{:S(2)}, u32[]{:S(2)}) collective-permute-start(bf16[256,1536]{1,0:T(8,128)(2,1)S(1)} %bitcast.11), channel_id=1, source_target_pairs={{0,32},{32,0},{1,33},{33,1},{2,34},{34,2},{3,35},{35,3},{4,36},{36... | collective-permute-start | bytes 2359304 | tf_op jit(solution)/shard_map/ppermute | solution.py:264
  107.8 27.2 %all-to-all-start.4 = ((bf16[16,128,128]{2,1,0:T(8,128)(2,1)}), bf16[16,128,128]{2,1,0:T(8,128)(2,1)}, u32[]{:S(2)}, u32[]{:S(2)}) async-start(bf16[16,128,128]{2,1,0:T(8,128)(2,1)} %input_terms.1), calls=%async_computation.4 | async-start | bytes 1048576 | tf_op jit(solution)/shard_map/all_to_all | solution.py:242
  116.4 1.0 copy-start.2
  117.4 1.0 copy-start.4
  121.6 19.4 %collective-permute-start.11 = (bf16[3,256,256]{2,1,0:T(8,128)(2,1)S(1)}, bf16[3,256,256]{2,1,0:T(8,128)(2,1)S(1)}, u32[]{:S(2)}, u32[]{:S(2)}) collective-permute-start(bf16[3,256,256]{2,1,0:T(8,128)(2,1)S(1)} %get-tuple-element.23), channel_id=1, source_target_pairs={{0,1},{1,0},{2,3},{3,2},{4,5},{5,4},{6,7},{7,6},{8,9},{9,8},{10,11... | collective-permute-start | bytes 1179656 | tf_op jit(solution)/shard_map/ppermute | solution.py:271
  125.1 15.9 %collective-permute-start.12 = (bf16[3,256,256]{2,1,0:T(8,128)(2,1)S(1)}, bf16[3,256,256]{2,1,0:T(8,128)(2,1)S(1)}, u32[]{:S(2)}, u32[]{:S(2)}) collective-permute-start(bf16[3,256,256]{2,1,0:T(8,128)(2,1)S(1)} %get-tuple-element.24), channel_id=1, source_target_pairs={{0,64},{64,0},{1,65},{65,1},{2,66},{66,2},{3,67},{67,3},{4,68},{68... | collective-permute-start | bytes 1179656 | tf_op jit(solution)/shard_map/ppermute | solution.py:272
  127.0 22.5 %collective-permute-start.13 = (bf16[3,256,256]{2,1,0:T(8,128)(2,1)S(1)}, bf16[3,256,256]{2,1,0:T(8,128)(2,1)S(1)}, u32[]{:S(2)}, u32[]{:S(2)}) collective-permute-start(bf16[3,256,256]{2,1,0:T(8,128)(2,1)S(1)} %get-tuple-element.25), channel_id=1, source_target_pairs={{0,65},{1,64},{64,1},{65,0},{2,67},{3,66},{66,3},{67,2},{4,69},{5,... | collective-permute-start | bytes 1179656 | tf_op jit(solution)/shard_map/ppermute | solution.py:273
  136.1 0.7 collective-permute-start.9

commit v11 on v10

v11 whole, which is shorter than its diff:
```python
import itertools

import jax
import jax.numpy as jnp
from jax import lax
from jax.experimental import pallas as pl
from jax.experimental.pallas import tpu as pltpu
from jax.sharding import Mesh, PartitionSpec as P

F32 = jnp.float32
BF16 = jnp.bfloat16
ROW = ("yl", "x1", "x0", "core")
COL = ("yh1", "yh0", "zh1", "zh0", "zl")
AXES = ROW + COL
YH = ("yh1", "yh0")
ZH = ("zh1", "zh0")
REST = ("yl", "x1")
SWAP = [(0, 1), (1, 0)]
TOK = 128
BLOCK = 256
WIDE = 2 * BLOCK
TOKENS = 2 * TOK
SHARE = TOKENS // 4
FEATURES = 4 * BLOCK
GRADS = 3 * WIDE
VMEM_LIMIT = 24 * 1024 * 1024
WHOLE = pl.BlockSpec(memory_space=pltpu.VMEM)
SCALARS = pl.BlockSpec(memory_space=pltpu.SMEM)


def turned():
    pairs = []
    for bits in itertools.product(range(2), repeat=len(AXES)):
        yl, x1, x0, core, yh1, yh0, zh1, zh0, zl = bits
        there = (yh1, yh0, x0, core, yl, zl, zh1, zh0, x1)
        pairs.append(tuple(sum(b << (8 - i) for i, b in enumerate(at)) for at in (bits, there)))
    return pairs


def dot(a, b, dims):
    return lax.dot_general(a, b, (dims, ((), ())), preferred_element_type=F32)


def params():
    return pltpu.CompilerParams(vmem_limit_bytes=VMEM_LIMIT)


def chunk(place_ref, t, f):
    core, x0 = place_ref[0], place_ref[1]
    core = core if f < 4 else 1 - core
    x0 = x0 if f % 4 < 2 else 1 - x0
    return 8 * x0 + 4 * core + 2 * t + f % 2


def gates_kernel(place_ref, acts_ref, *refs):
    w_refs, parts_ref, wide_ref = refs[:8], refs[8], refs[9]
    for p in range(2):
        for t in range(2):
            for f in range(8):
                block = acts_ref[chunk(place_ref, t, f), p]
                wide_ref[p, pl.ds(t * TOK, TOK), pl.ds(f * TOK, TOK)] = block
    for p in range(3):
        for j in range(2):
            total = jnp.zeros((TOKENS, BLOCK), F32)
            for s in range(4):
                total += dot(wide_ref[p // 2, :, pl.ds(s * BLOCK, BLOCK)], w_refs[2 * s + j][p], ((1,), (0,)))
            parts_ref[:, pl.ds(p * WIDE + j * BLOCK, BLOCK)] = total.astype(BF16)


def gates(place, acts, *weights):
    return pl.pallas_call(
        gates_kernel,
        out_shape=jax.ShapeDtypeStruct((TOKENS, GRADS), BF16),
        in_specs=[SCALARS] + [WHOLE] * 9,
        out_specs=WHOLE,
        scratch_shapes=[pltpu.VMEM((2, TOKENS, FEATURES), BF16)],
        compiler_params=params(),
        cost_estimate=pl.CostEstimate(flops=800000000, bytes_accessed=6000000, transcendentals=0),
        name="gates",
    )(place, acts, *weights)


def hidden_kernel(parts_ref, out_ref):
    total = parts_ref[0].astype(F32)
    for i in range(1, 4):
        total += parts_ref[i].astype(F32)
    gate, up, hidden_grad = (total[:, p * WIDE : (p + 1) * WIDE] for p in range(3))
    sig = 1.0 / (1.0 + jnp.exp(-gate))
    act = gate * sig
    gate_grad = (hidden_grad * up * sig * (1.0 + gate * (1.0 - sig))).astype(BF16)
    up_grad = (hidden_grad * act).astype(BF16)
    hidden = (act * up).astype(BF16)
    for i in range(4):
        for p, value in enumerate((gate_grad, up_grad, hidden)):
            out_ref[i, :, pl.ds(p * WIDE, WIDE)] = value


def hidden_grads(parts):
    return pl.pallas_call(
        hidden_kernel,
        out_shape=jax.ShapeDtypeStruct(parts.shape, BF16),
        in_specs=[WHOLE],
        out_specs=WHOLE,
        compiler_params=params(),
        cost_estimate=pl.CostEstimate(flops=2000000, bytes_accessed=1600000, transcendentals=32768),
        name="hidden_grads",
    )(parts)


def input_kernel(place_ref, grads_ref, *refs):
    w_refs, dx_ref = refs[:8], refs[8]
    for s in range(4):
        dx = jnp.zeros((TOKENS, BLOCK), F32)
        for p in range(2):
            for j in range(2):
                grads = grads_ref[:, pl.ds(p * WIDE + j * BLOCK, BLOCK)]
                dx += dot(grads, w_refs[2 * s + j][p], ((1,), (1,)))
        dx = dx.astype(BF16)
        for t in range(2):
            for f in range(2):
                part = dx[t * TOK : (t + 1) * TOK, f * TOK : (f + 1) * TOK]
                dx_ref[chunk(place_ref, t, 2 * s + f)] = part


def input_terms(place, grads, *weights):
    return pl.pallas_call(
        input_kernel,
        out_shape=jax.ShapeDtypeStruct((16, TOK, TOK), BF16),
        in_specs=[SCALARS] + [WHOLE] * 9,
        out_specs=WHOLE,
        compiler_params=params(),
        cost_estimate=pl.CostEstimate(flops=540000000, bytes_accessed=4000000, transcendentals=0),
        name="input_terms",
    )(place, grads, *weights)


def weight_kernel(
    place_ref, acts_ref, other_acts_ref, grads_ref, other_grads_ref, keep_ref, z_ref, x_ref, xz_ref, wide_ref
):
    for p in range(2):
        for t in range(2):
            for f in range(4):
                x0 = place_ref[1] if f < 2 else 1 - place_ref[1]
                cols = pl.ds(f * TOK, TOK)
                mine = acts_ref[chunk(place_ref, t, f), p]
                wide_ref[p, pl.ds(t * TOK, TOK), cols] = mine
                wide_ref[p, pl.ds(TOKENS + t * TOK, TOK), cols] = other_acts_ref[x0, 2 * t + f % 2, p]
    for side in (1, 0):
        for p in range(3):
            for j in range(2):
                cols = pl.ds(p * WIDE + j * BLOCK, BLOCK)
                term = jnp.zeros((BLOCK, BLOCK), F32)
                for i, ref in enumerate((grads_ref, other_grads_ref)):
                    x = wide_ref[p // 2, pl.ds(i * TOKENS, TOKENS), pl.ds(side * BLOCK, BLOCK)]
                    term += dot(x, ref[:, cols], ((0,), (0,)))
                out_ref = ((keep_ref, z_ref), (x_ref, xz_ref))[side][j]
                out_ref[p] = term.astype(out_ref.dtype)


def weight_terms(place, acts, other_acts, grads, other_grads):
    shape = (3, BLOCK, BLOCK)
    send = jax.ShapeDtypeStruct(shape, BF16)
    return pl.pallas_call(
        weight_kernel,
        out_shape=(jax.ShapeDtypeStruct(shape, F32), send, send, send),
        in_specs=[SCALARS] + [WHOLE] * 4,
        out_specs=(WHOLE,) * 4,
        scratch_shapes=[pltpu.VMEM((2, 2 * TOKENS, WIDE), BF16)],
        compiler_params=params(),
        cost_estimate=pl.CostEstimate(flops=800000000, bytes_accessed=6000000, transcendentals=0),
        name="weight_terms",
    )(place, acts, other_acts, grads, other_grads)


def exchange(pieces, axes):
    return lax.all_to_all(pieces, axes, split_axis=0, concat_axis=0, tiled=True)


def local(inputs, out_grad, codes, scales):
    place = jnp.stack([lax.axis_index("core"), lax.axis_index("x0")])
    there = turned()

    acts = lax.ppermute(jnp.stack([inputs, out_grad]), AXES, there)
    acts = exchange(jnp.broadcast_to(acts[None], (4,) + acts.shape), YH)
    w = (codes.astype(F32) * scales.astype(F32)).astype(BF16)
    w_z = lax.ppermute(w, "zl", SWAP)
    w_x = lax.ppermute(w, "x0", SWAP)
    acts, w_z, w_x = lax.optimization_barrier((acts, w_z, w_x))
    weights = [w, w_z, w_x, lax.ppermute(w_z, "x0", SWAP)]
    weights += [lax.ppermute(block, "core", SWAP) for block in weights]
    acts = exchange(jnp.broadcast_to(acts[None], (4,) + acts.shape), ZH).reshape(16, 2, TOK, TOK)

    parts = gates(place, acts, *weights)
    other_acts = acts.reshape(2, 2, 4, 2, TOK, TOK)
    other_acts = lax.dynamic_index_in_dim(other_acts, 1 - place[0], axis=1, keepdims=False)
    other_acts = lax.ppermute(other_acts, "core", SWAP)
    parts = exchange(parts.reshape(4, SHARE, GRADS), REST)
    parts, other_acts = lax.optimization_barrier((parts, other_acts))
    grads = exchange(hidden_grads(parts), REST).reshape(TOKENS, GRADS)
    other_grads = lax.ppermute(grads, "core", SWAP)

    dx = exchange(input_terms(place, grads, *weights), ZH + YH)
    dx = jnp.sum(dx.astype(F32), axis=0).astype(BF16)
    input_grad = lax.ppermute(dx, AXES, [(b, a) for a, b in there])

    weight_grad, z, x, xz = weight_terms(place, acts, other_acts, grads, other_grads)
    weight_grad += lax.ppermute(z, "zl", SWAP).astype(F32)
    weight_grad += lax.ppermute(x, "x0", SWAP).astype(F32)
    weight_grad += lax.ppermute(xz, ("x0", "zl"), [(i, 3 - i) for i in range(4)]).astype(F32)
    return input_grad, weight_grad


def solution(mesh):
    fine = Mesh(mesh.devices.reshape((2,) * len(AXES)), AXES)
    return jax.shard_map(
        local,
        mesh=fine,
        in_specs=(P(ROW, COL), P(ROW, COL), P(None, ROW, COL), P(None, ROW, COL)),
        out_specs=(P(ROW, COL), P(None, ROW, COL)),
        check_vma=False,
    )
```

time: 152 us -> 149 us (0.980)
  the two profiles are of different devices: /device:TPU:1 before, /device:TPU:4 now
where the time goes in v11:
time: 149 us; the launch traced here: 147 us
  starting transfers between devices  73.6 us (49%)
  waiting for transfers between devices  41.4 us (28%)
  blocking collectives  15.1 us (10%)
  Pallas kernels  8.83 us (6%)
  other arithmetic  4.09 us (3%)
  local copies, waits for them, and re-layouts  3.49 us (2%)
    all_to_all x4, starting transfers between devices, exchange(): return lax.all_to_all(pieces, axes, split_axis=0, concat_axis=0, tiled=True)  30.6 us
    all_to_all x4, waiting for transfers between devices, exchange(): return lax.all_to_all(pieces, axes, split_axis=0, concat_axis=0, tiled=True)  26.2 us
    all_to_all x1, blocking collectives, exchange(): return lax.all_to_all(pieces, axes, split_axis=0, concat_axis=0, tiled=True)  15.1 us
    ppermute x1, waiting for transfers between devices, local(): input_grad = lax.ppermute(dx, AXES, [(b, a) for a, b in there])  8.37 us
    ppermute x4, starting transfers between devices, local(): weights += [lax.ppermute(block, 'core', SWAP) for block in weights]  8.2 us
    ppermute x1, starting transfers between devices, local(): input_grad = lax.ppermute(dx, AXES, [(b, a) for a, b in there])  5.71 us
    ppermute x1, starting transfers between devices, local(): w_z = lax.ppermute(w, 'zl', SWAP)  4.5 us
    ppermute x1, starting transfers between devices, local(): acts = lax.ppermute(jnp.stack([inputs, out_grad]), AXES, there)  4.21 us
  transfers between devices with their start and end apart: 18, of which 9 were waited for; matrix products, arithmetic and copies ran while one was open for 2% of the time, Pallas kernels for 4%

profile of v11, /device:TPU:4, one launch (start us, length us, event | category | flops | bytes accessed | tf_op | source)
XLA Modules:
  0.0 147.4 jit_solution(9491025834993123282)
XLA Ops:
  0.6 0.0 copy-start.6
  0.6 0.8 pad_maximum_fusion
  1.4 4.2 %collective-permute-start = (bf16[2,128,128]{2,1,0:T(8,128)(2,1)S(1)}, bf16[2,128,128]{2,1,0:T(8,128)(2,1)S(1)}, u32[]{:S(2)}, u32[]{:S(2)}) collective-permute-start(bf16[2,128,128]{2,1,0:T(8,128)(2,1)S(1)} %pad_maximum_fusion), channel_id=1, source_target_pairs={{0,0},{1,8},{2,2},{3,10},{4,4},{5,12},{6,6},{7,14},{8,128},{9,136}... | collective-permute-start | bytes 196616 | tf_op jit(solution)/shard_map/ppermute | solution.py:183
  5.6 0.0 copy-done.6
  5.7 1.1 multiply_convert_fusion.refs_0_
  6.7 4.0 %collective-permute-start.2 = (bf16[3,256,256]{2,1,0:T(8,128)(2,1)S(1)}, bf16[3,256,256]{2,1,0:T(8,128)(2,1)S(1)}, u32[]{:S(2)}, u32[]{:S(2)}) collective-permute-start(bf16[3,256,256]{2,1,0:T(8,128)(2,1)S(1)} %multiply_convert_fusion.refs_0_), channel_id=1, source_target_pairs={{0,64},{64,0},{1,65},{65,1},{2,66},{66,2},{3,67},{67,3},{4,68},{68... | collective-permute-start | bytes 1179656 | tf_op jit(solution)/shard_map/ppermute | solution.py:187
  10.8 4.5 %collective-permute-start.1 = (bf16[3,256,256]{2,1,0:T(8,128)(2,1)S(1)}, bf16[3,256,256]{2,1,0:T(8,128)(2,1)S(1)}, u32[]{:S(2)}, u32[]{:S(2)}) collective-permute-start(bf16[3,256,256]{2,1,0:T(8,128)(2,1)S(1)} %multiply_convert_fusion.refs_0_), channel_id=1, source_target_pairs={{0,1},{1,0},{2,3},{3,2},{4,5},{5,4},{6,7},{7,6},{8,9},{9,8},{10,11... | collective-permute-start | bytes 1179656 | tf_op jit(solution)/shard_map/ppermute | solution.py:186
  15.3 0.0 collective-permute-done
  15.3 0.7 broadcast_in_dim.4
  16.0 5.0 %all-to-all-start = ((bf16[4,2,128,128]{3,2,1,0:T(8,128)(2,1)}), bf16[4,2,128,128]{3,2,1,0:T(8,128)(2,1)S(1)}, u32[]{:S(2)}, u32[]{:S(2)}) async-start(bf16[4,2,128,128]{3,2,1,0:T(8,128)(2,1)} %broadcast_in_dim.4), calls=%async_computation | async-start | bytes 524288 | tf_op jit(solution)/shard_map/all_to_all | solution.py:176
  21.0 0.0 collective-permute-done.2.refs_2_
  21.0 2.8 %collective-permute-done.1.refs_1_ = bf16[3,256,256]{2,1,0:T(8,128)(2,1)S(1)} collective-permute-done((bf16[3,256,256]{2,1,0:T(8,128)(2,1)S(1)}, bf16[3,256,256]{2,1,0:T(8,128)(2,1)S(1)}, u32[]{:S(2)}, u32[]{:S(2)}) %collective-permute-start.1) | collective-permute-done | bytes 393248 | tf_op jit(solution)/shard_map/ppermute | solution.py:186
  23.8 7.5 %all-to-all-done = bf16[4,2,128,128]{3,2,1,0:T(8,128)(2,1)S(1)} async-done(((bf16[4,2,128,128]{3,2,1,0:T(8,128)(2,1)}), bf16[4,2,128,128]{3,2,1,0:T(8,128)(2,1)S(1)}, u32[]{:S(2)}, u32[]{:S(2)}) %all-to-all-start) | async-done | bytes 262176 | tf_op jit(solution)/shard_map/all_to_all | solution.py:176
  31.3 1.3 broadcast_in_dim.5
  32.6 9.4 %all-to-all-start.1 = ((bf16[4,4,2,128,128]{4,3,2,1,0:T(8,128)(2,1)}), bf16[4,4,2,128,128]{4,3,2,1,0:T(8,128)(2,1)S(1)}, u32[]{:S(2)}, u32[]{:S(2)}) async-start(bf16[4,4,2,128,128]{4,3,2,1,0:T(8,128)(2,1)} %broadcast_in_dim.5), calls=%async_computation.1 | async-start | bytes 2097152 | tf_op jit(solution)/shard_map/all_to_all | solution.py:176
  42.0 3.0 %collective-permute-start.3 = (bf16[3,256,256]{2,1,0:T(8,128)(2,1)S(1)}, bf16[3,256,256]{2,1,0:T(8,128)(2,1)S(1)}, u32[]{:S(2)}, u32[]{:S(2)}) collective-permute-start(bf16[3,256,256]{2,1,0:T(8,128)(2,1)S(1)} %collective-permute-done.1.refs_1_), channel_id=1, source_target_pairs={{0,64},{64,0},{1,65},{65,1},{2,66},{66,2},{3,67},{67,3},{4,68},{68... | collective-permute-start | bytes 1179656 | tf_op jit(solution)/shard_map/ppermute | solution.py:189
  45.0 1.9 %collective-permute-start.4 = (bf16[3,256,256]{2,1,0:T(8,128)(2,1)S(1)}, bf16[3,256,256]{2,1,0:T(8,128)(2,1)S(1)}, u32[]{:S(2)}, u32[]{:S(2)}) collective-permute-start(bf16[3,256,256]{2,1,0:T(8,128)(2,1)S(1)} %multiply_convert_fusion.refs_0_), channel_id=1, source_target_pairs={{0,32},{32,0},{1,33},{33,1},{2,34},{34,2},{3,35},{35,3},{4,36},{36... | collective-permute-start | bytes 1179656 | tf_op jit(solution)/shard_map/ppermute | solution.py:190
  46.9 2.4 %collective-permute-start.5 = (bf16[3,256,256]{2,1,0:T(8,128)(2,1)S(1)}, bf16[3,256,256]{2,1,0:T(8,128)(2,1)S(1)}, u32[]{:S(2)}, u32[]{:S(2)}) collective-permute-start(bf16[3,256,256]{2,1,0:T(8,128)(2,1)S(1)} %collective-permute-done.1.refs_1_), channel_id=1, source_target_pairs={{0,32},{32,0},{1,33},{33,1},{2,34},{34,2},{3,35},{35,3},{4,36},{36... | collective-permute-start | bytes 1179656 | tf_op jit(solution)/shard_map/ppermute | solution.py:190
  49.3 1.9 %collective-permute-start.6 = (bf16[3,256,256]{2,1,0:T(8,128)(2,1)S(1)}, bf16[3,256,256]{2,1,0:T(8,128)(2,1)}, u32[]{:S(2)}, u32[]{:S(2)}) collective-permute-start(bf16[3,256,256]{2,1,0:T(8,128)(2,1)S(1)} %collective-permute-done.2.refs_2_), channel_id=1, source_target_pairs={{0,32},{32,0},{1,33},{33,1},{2,34},{34,2},{3,35},{35,3},{4,36},{36... | collective-permute-start | bytes 1179656 | tf_op jit(solution)/shard_map/ppermute | solution.py:190
  51.2 0.5 collective-permute-done.3.refs_3_
  51.7 2.0 %collective-permute-start.7 = (bf16[3,256,256]{2,1,0:T(8,128)(2,1)S(1)}, bf16[3,256,256]{2,1,0:T(8,128)(2,1)}, u32[]{:S(2)}, u32[]{:S(2)}) collective-permute-start(bf16[3,256,256]{2,1,0:T(8,128)(2,1)S(1)} %collective-permute-done.3.refs_3_), channel_id=1, source_target_pairs={{0,32},{32,0},{1,33},{33,1},{2,34},{34,2},{3,35},{35,3},{4,36},{36... | collective-permute-start | bytes 1179656 | tf_op jit(solution)/shard_map/ppermute | solution.py:190
  53.7 0.1 pad_add_fusion.place_ref
  53.7 0.0 collective-permute-done.4.refs_4_
  53.7 0.0 copy-start
  53.7 0.0 collective-permute-done.6.refs_6_
  53.7 0.0 collective-permute-done.5.refs_5_
  53.8 0.0 copy-start.2
  53.8 1.7 %collective-permute-done.7.refs_7_ = bf16[3,256,256]{2,1,0:T(8,128)(2,1)} collective-permute-done((bf16[3,256,256]{2,1,0:T(8,128)(2,1)S(1)}, bf16[3,256,256]{2,1,0:T(8,128)(2,1)}, u32[]{:S(2)}, u32[]{:S(2)}) %collective-permute-start.7) | collective-permute-done | bytes 393248 | tf_op jit(solution)/shard_map/ppermute | solution.py:190
  55.4 5.7 %all-to-all-done.1 = bf16[4,4,2,128,128]{4,3,2,1,0:T(8,128)(2,1)S(1)} async-done(((bf16[4,4,2,128,128]{4,3,2,1,0:T(8,128)(2,1)}), bf16[4,4,2,128,128]{4,3,2,1,0:T(8,128)(2,1)S(1)}, u32[]{:S(2)}, u32[]{:S(2)}) %all-to-all-start.1) | async-done | bytes 1048608 | tf_op jit(solution)/shard_map/all_to_all | solution.py:176
  61.1 3.0 %gates.1 = bf16[256,1536]{1,0:T(8,128)(2,1)} custom-call(s32[2]{0:T(128)S(1)} %pad_add_fusion.place_ref, bf16[16,2,128,128]{3,2,1,0:T(8,128)(2,1)S(1)} %bitcast.13, bf16[3,256,256]{2,1,0:T(8,128)(2,1)S(1)} %multiply_convert_fusion.refs_0_, bf16[3,256,256]{2,1,0:T(8,128)(2,1)S(1)} %collective-permute-done.1.refs_1_, ...), custom_call_target="tpu_custom_call" | custom-call | flops 800000000 | bytes 6000000 | tf_op jit(solution)/shard_map/gates/pallas_call | solution.py:71
  64.1 0.0 copy-done
  64.1 0.0 copy-done.2
  64.1 7.3 %all-to-all-start.2 = ((bf16[4,64,1536]{2,1,0:T(8,128)(2,1)}), bf16[4,64,1536]{2,1,0:T(8,128)(2,1)S(1)}, u32[]{:S(2)}, u32[]{:S(2)}) async-start(bf16[4,64,1536]{2,1,0:T(8,128)(2,1)} %bitcast.6), calls=%async_computation.2 | async-start | bytes 1572864 | tf_op jit(solution)/shard_map/all_to_all | solution.py:176
  71.5 1.9 %collective-permute-start.8 = (bf16[2,4,2,128,128]{4,3,2,1,0:T(8,128)(2,1)S(1)}, bf16[2,4,2,128,128]{4,3,2,1,0:T(8,128)(2,1)S(1)}, u32[]{:S(2)}, u32[]{:S(2)}) collective-permute-start(bf16[2,4,2,128,128]{4,3,2,1,0:T(8,128)(2,1)S(1)} %dynamic-slice_bitcast_fusion), channel_id=1, source_target_pairs={{0,32},{32,0},{1,33},{33,1},{2,34},{34,2},{3,35},{35,3},{4,36},{36... | collective-permute-start | bytes 1572872 | tf_op jit(solution)/shard_map/ppermute | solution.py:196
  73.4 1.9 %collective-permute-done.8.other_acts_ref = bf16[2,4,2,128,128]{4,3,2,1,0:T(8,128)(2,1)S(1)} collective-permute-done((bf16[2,4,2,128,128]{4,3,2,1,0:T(8,128)(2,1)S(1)}, bf16[2,4,2,128,128]{4,3,2,1,0:T(8,128)(2,1)S(1)}, u32[]{:S(2)}, u32[]{:S(2)}) %collective-permute-start.8) | collective-permute-done | bytes 524320 | tf_op jit(solution)/shard_map/ppermute | solution.py:196
  75.3 0.0 copy-start.4
  75.3 0.8 copy-done.4
  76.1 4.9 %all-to-all-done.2.parts_ref = bf16[4,64,1536]{2,1,0:T(8,128)(2,1)S(1)} async-done(((bf16[4,64,1536]{2,1,0:T(8,128)(2,1)}), bf16[4,64,1536]{2,1,0:T(8,128)(2,1)S(1)}, u32[]{:S(2)}, u32[]{:S(2)}) %all-to-all-start.2) | async-done | bytes 786464 | tf_op jit(solution)/shard_map/all_to_all | solution.py:176
  81.0 0.2 hidden_grads.1
  81.2 0.0 copy-start.1
  81.2 0.0 copy-start.3
  81.2 15.1 %all_to_all.25 = bf16[4,64,1536]{2,1,0:T(8,128)(2,1)S(1)} all-to-all(bf16[4,64,1536]{2,1,0:T(8,128)(2,1)S(1)} %hidden_grads.1), channel_id=1, replica_groups=mesh['yl'=2,'x1'=2,'x0'=2,'core'=2,'yh1'=2,'yh0'=2,'zh1'=2,'zh0'=2,'zl'=..., dimensions={0} | all-to-all | bytes 1572864 | tf_op jit(solution)/shard_map/all_to_all | solution.py:176
  96.3 1.9 %collective-permute-start.10 = (bf16[256,1536]{1,0:T(8,128)(2,1)S(1)}, bf16[256,1536]{1,0:T(8,128)(2,1)}, u32[]{:S(2)}, u32[]{:S(2)}) collective-permute-start(bf16[256,1536]{1,0:T(8,128)(2,1)S(1)} %bitcast.16), channel_id=1, source_target_pairs={{0,32},{32,0},{1,33},{33,1},{2,34},{34,2},{3,35},{35,3},{4,36},{36... | collective-permute-start | bytes 2359304 | tf_op jit(solution)/shard_map/ppermute | solution.py:200
  98.2 0.0 copy-done.1
  98.2 0.0 copy-done.3
  98.2 2.7 %input_terms.1 = bf16[16,128,128]{2,1,0:T(8,128)(2,1)} custom-call(s32[2]{0:T(128)S(1)} %pad_add_fusion.place_ref, bf16[256,1536]{1,0:T(8,128)(2,1)S(1)} %bitcast.17, bf16[3,256,256]{2,1,0:T(8,128)(2,1)S(1)} %multiply_convert_fusion.refs_0_, bf16[3,256,256]{2,1,0:T(8,128)(2,1)S(1)} %collective-permute-done.1.refs_1_, ...), custom_call_target="tpu_custom_call" | custom-call | flops 540000000 | bytes 4000000 | tf_op jit(solution)/shard_map/input_terms/pallas_call | solution.py:126
  100.9 0.0 copy-start.5
  100.9 9.0 %all-to-all-start.4 = ((bf16[16,128,128]{2,1,0:T(8,128)(2,1)}), bf16[16,128,128]{2,1,0:T(8,128)(2,1)}, u32[]{:S(2)}, u32[]{:S(2)}) async-start(bf16[16,128,128]{2,1,0:T(8,128)(2,1)} %input_terms.1), calls=%async_computation.4 | async-start | bytes 1048576 | tf_op jit(solution)/shard_map/all_to_all | solution.py:176
  109.9 0.0 collective-permute-done.10.other_grads_ref
  109.9 0.0 copy-done.5
  109.9 3.0 %weight_terms.1 = (f32[3,256,256]{2,1,0:T(8,128)S(1)}, bf16[3,256,256]{2,1,0:T(8,128)(2,1)}, bf16[3,256,256]{2,1,0:T(8,128)(2,1)}, bf16[3,256,256]{2,1,0:T(8,128)(2,1)}) custom-call(s32[2]{0:T(128)S(1)} %pad_add_fusion.place_ref, bf16[16,2,128,128]{3,2,1,0:T(8,128)(2,1)S(1)} %bitcast.15, bf16[2,4,2,128,128]{4,3,2,1,0:T(8,128)(2,1)S(1)} %copy-done.5, ...), custom_call_target="tpu_custom_call" | custom-call | flops 800000000 | bytes 6000000 | tf_op jit(solution)/shard_map/weight_terms/pallas_call | solution.py:163
  112.9 3.4 %collective-permute-start.11 = (bf16[3,256,256]{2,1,0:T(8,128)(2,1)}, bf16[3,256,256]{2,1,0:T(8,128)(2,1)S(1)}, u32[]{:S(2)}, u32[]{:S(2)}) collective-permute-start(bf16[3,256,256]{2,1,0:T(8,128)(2,1)} %get-tuple-element.17), channel_id=1, source_target_pairs={{0,1},{1,0},{2,3},{3,2},{4,5},{5,4},{6,7},{7,6},{8,9},{9,8},{10,11... | collective-permute-start | bytes 1179656 | tf_op jit(solution)/shard_map/ppermute | solution.py:207
  116.4 2.7 %collective-permute-start.12 = (bf16[3,256,256]{2,1,0:T(8,128)(2,1)}, bf16[3,256,256]{2,1,0:T(8,128)(2,1)S(1)}, u32[]{:S(2)}, u32[]{:S(2)}) collective-permute-start(bf16[3,256,256]{2,1,0:T(8,128)(2,1)} %get-tuple-element.18), channel_id=1, source_target_pairs={{0,64},{64,0},{1,65},{65,1},{2,66},{66,2},{3,67},{67,3},{4,68},{68... | collective-permute-start | bytes 1179656 | tf_op jit(solution)/shard_map/ppermute | solution.py:208
  119.1 3.4 %collective-permute-start.13 = (bf16[3,256,256]{2,1,0:T(8,128)(2,1)}, bf16[3,256,256]{2,1,0:T(8,128)(2,1)S(1)}, u32[]{:S(2)}, u32[]{:S(2)}) collective-permute-start(bf16[3,256,256]{2,1,0:T(8,128)(2,1)} %get-tuple-element.19), channel_id=1, source_target_pairs={{0,65},{1,64},{64,1},{65,0},{2,67},{3,66},{66,3},{67,2},{4,69},{5,... | collective-permute-start | bytes 1179656 | tf_op jit(solution)/shard_map/ppermute | solution.py:209
  122.5 8.1 %all-to-all-done.4 = bf16[16,128,128]{2,1,0:T(8,128)(2,1)} async-done(((bf16[16,128,128]{2,1,0:T(8,128)(2,1)}), bf16[16,128,128]{2,1,0:T(8,128)(2,1)}, u32[]{:S(2)}, u32[]{:S(2)}) %all-to-all-start.4) | async-done | bytes 524320 | tf_op jit(solution)/shard_map/all_to_all | solution.py:176
  130.5 1.1 reduce_sum.12
  131.7 5.7 %collective-permute-start.9 = (bf16[128,128]{1,0:T(8,128)(2,1)S(1)}, bf16[128,128]{1,0:T(8,128)(2,1)S(1)}, u32[]{:S(2)}, u32[]{:S(2)}) collective-permute-start(bf16[128,128]{1,0:T(8,128)(2,1)S(1)} %reduce_sum.12), channel_id=1, source_target_pairs={{0,0},{8,1},{2,2},{10,3},{4,4},{12,5},{6,6},{14,7},{128,8},{136,9}... | collective-permute-start | bytes 98312 | tf_op jit(solution)/shard_map/ppermute | solution.py:204
  137.4 8.4 %collective-permute-done.9 = bf16[128,128]{1,0:T(8,128)(2,1)S(1)} collective-permute-done((bf16[128,128]{1,0:T(8,128)(2,1)S(1)}, bf16[128,128]{1,0:T(8,128)(2,1)S(1)}, u32[]{:S(2)}, u32[]{:S(2)}) %collective-permute-start.9) | collective-permute-done | bytes 32800 | tf_op jit(solution)/shard_map/ppermute | solution.py:204
  145.7 0.0 collective-permute-done.11
  145.7 0.0 collective-permute-done.12
  145.7 0.0 collective-permute-done.13
  145.8 1.0 convert_add_fusion
  146.8 0.6 copy.7
  (2 shorter events, 0.0 us)
Async XLA Ops:
  0.6 5.0 %copy-start.6 = (bf16[3,1,256]{2,0,1:T(4,128)(2,1)S(1)}, bf16[3,1,256]{2,0,1:T(4,128)(2,1)}, u32[]{:S(2)}) copy-start(bf16[3,1,256]{2,0,1:T(4,128)(2,1)} %param.7) | copy-start | bytes 4612
  1.4 13.8 %collective-permute-start = (bf16[2,128,128]{2,1,0:T(8,128)(2,1)S(1)}, bf16[2,128,128]{2,1,0:T(8,128)(2,1)S(1)}, u32[]{:S(2)}, u32[]{:S(2)}) collective-permute-start(bf16[2,128,128]{2,1,0:T(8,128)(2,1)S(1)} %pad_maximum_fusion), channel_id=1, source_target_pairs={{0,0},{1,8},{2,2},{3,10},{4,4},{5,12},{6,6},{7,14},{8,128},{9,136}... | collective-permute-start | bytes 196616 | tf_op jit(solution)/shard_map/ppermute | solution.py:183
  6.7 14.2 %collective-permute-start.2 = (bf16[3,256,256]{2,1,0:T(8,128)(2,1)S(1)}, bf16[3,256,256]{2,1,0:T(8,128)(2,1)S(1)}, u32[]{:S(2)}, u32[]{:S(2)}) collective-permute-start(bf16[3,256,256]{2,1,0:T(8,128)(2,1)S(1)} %multiply_convert_fusion.refs_0_), channel_id=1, source_target_pairs={{0,64},{64,0},{1,65},{65,1},{2,66},{66,2},{3,67},{67,3},{4,68},{68... | collective-permute-start | bytes 1179656 | tf_op jit(solution)/shard_map/ppermute | solution.py:187
  10.8 13.0 %collective-permute-start.1 = (bf16[3,256,256]{2,1,0:T(8,128)(2,1)S(1)}, bf16[3,256,256]{2,1,0:T(8,128)(2,1)S(1)}, u32[]{:S(2)}, u32[]{:S(2)}) collective-permute-start(bf16[3,256,256]{2,1,0:T(8,128)(2,1)S(1)} %multiply_convert_fusion.refs_0_), channel_id=1, source_target_pairs={{0,1},{1,0},{2,3},{3,2},{4,5},{5,4},{6,7},{7,6},{8,9},{9,8},{10,11... | collective-permute-start | bytes 1179656 | tf_op jit(solution)/shard_map/ppermute | solution.py:186
  16.0 15.3 %all-to-all-start = ((bf16[4,2,128,128]{3,2,1,0:T(8,128)(2,1)}), bf16[4,2,128,128]{3,2,1,0:T(8,128)(2,1)S(1)}, u32[]{:S(2)}, u32[]{:S(2)}) async-start(bf16[4,2,128,128]{3,2,1,0:T(8,128)(2,1)} %broadcast_in_dim.4), calls=%async_computation | async-start | bytes 524288 | tf_op jit(solution)/shard_map/all_to_all | solution.py:176
  32.6 28.6 %all-to-all-start.1 = ((bf16[4,4,2,128,128]{4,3,2,1,0:T(8,128)(2,1)}), bf16[4,4,2,128,128]{4,3,2,1,0:T(8,128)(2,1)S(1)}, u32[]{:S(2)}, u32[]{:S(2)}) async-start(bf16[4,4,2,128,128]{4,3,2,1,0:T(8,128)(2,1)} %broadcast_in_dim.5), calls=%async_computation.1 | async-start | bytes 2097152 | tf_op jit(solution)/shard_map/all_to_all | solution.py:176
  42.0 9.7 %collective-permute-start.3 = (bf16[3,256,256]{2,1,0:T(8,128)(2,1)S(1)}, bf16[3,256,256]{2,1,0:T(8,128)(2,1)S(1)}, u32[]{:S(2)}, u32[]{:S(2)}) collective-permute-start(bf16[3,256,256]{2,1,0:T(8,128)(2,1)S(1)} %collective-permute-done.1.refs_1_), channel_id=1, source_target_pairs={{0,64},{64,0},{1,65},{65,1},{2,66},{66,2},{3,67},{67,3},{4,68},{68... | collective-permute-start | bytes 1179656 | tf_op jit(solution)/shard_map/ppermute | solution.py:189
  45.0 8.8 %collective-permute-start.4 = (bf16[3,256,256]{2,1,0:T(8,128)(2,1)S(1)}, bf16[3,256,256]{2,1,0:T(8,128)(2,1)S(1)}, u32[]{:S(2)}, u32[]{:S(2)}) collective-permute-start(bf16[3,256,256]{2,1,0:T(8,128)(2,1)S(1)} %multiply_convert_fusion.refs_0_), channel_id=1, source_target_pairs={{0,32},{32,0},{1,33},{33,1},{2,34},{34,2},{3,35},{35,3},{4,36},{36... | collective-permute-start | bytes 1179656 | tf_op jit(solution)/shard_map/ppermute | solution.py:190
  46.9 6.9 %collective-permute-start.5 = (bf16[3,256,256]{2,1,0:T(8,128)(2,1)S(1)}, bf16[3,256,256]{2,1,0:T(8,128)(2,1)S(1)}, u32[]{:S(2)}, u32[]{:S(2)}) collective-permute-start(bf16[3,256,256]{2,1,0:T(8,128)(2,1)S(1)} %collective-permute-done.1.refs_1_), channel_id=1, source_target_pairs={{0,32},{32,0},{1,33},{33,1},{2,34},{34,2},{3,35},{35,3},{4,36},{36... | collective-permute-start | bytes 1179656 | tf_op jit(solution)/shard_map/ppermute | solution.py:190
  49.3 4.4 %collective-permute-start.6 = (bf16[3,256,256]{2,1,0:T(8,128)(2,1)S(1)}, bf16[3,256,256]{2,1,0:T(8,128)(2,1)}, u32[]{:S(2)}, u32[]{:S(2)}) collective-permute-start(bf16[3,256,256]{2,1,0:T(8,128)(2,1)S(1)} %collective-permute-done.2.refs_2_), channel_id=1, source_target_pairs={{0,32},{32,0},{1,33},{33,1},{2,34},{34,2},{3,35},{35,3},{4,36},{36... | collective-permute-start | bytes 1179656 | tf_op jit(solution)/shard_map/ppermute | solution.py:190
  51.7 3.7 %collective-permute-start.7 = (bf16[3,256,256]{2,1,0:T(8,128)(2,1)S(1)}, bf16[3,256,256]{2,1,0:T(8,128)(2,1)}, u32[]{:S(2)}, u32[]{:S(2)}) collective-permute-start(bf16[3,256,256]{2,1,0:T(8,128)(2,1)S(1)} %collective-permute-done.3.refs_3_), channel_id=1, source_target_pairs={{0,32},{32,0},{1,33},{33,1},{2,34},{34,2},{3,35},{35,3},{4,36},{36... | collective-permute-start | bytes 1179656 | tf_op jit(solution)/shard_map/ppermute | solution.py:190
  53.7 10.4 %copy-start = (bf16[3,256,256]{2,1,0:T(8,128)(2,1)}, bf16[3,256,256]{2,1,0:T(8,128)(2,1)S(1)}, u32[]{:S(2)}) copy-start(bf16[3,256,256]{2,1,0:T(8,128)(2,1)S(1)} %collective-permute-done.4.refs_4_) | copy-start | bytes 1179652
  53.8 10.4 %copy-start.2 = (bf16[3,256,256]{2,1,0:T(8,128)(2,1)}, bf16[3,256,256]{2,1,0:T(8,128)(2,1)S(1)}, u32[]{:S(2)}) copy-start(bf16[3,256,256]{2,1,0:T(8,128)(2,1)S(1)} %collective-permute-done.5.refs_5_) | copy-start | bytes 1179652
  64.1 16.9 %all-to-all-start.2 = ((bf16[4,64,1536]{2,1,0:T(8,128)(2,1)}), bf16[4,64,1536]{2,1,0:T(8,128)(2,1)S(1)}, u32[]{:S(2)}, u32[]{:S(2)}) async-start(bf16[4,64,1536]{2,1,0:T(8,128)(2,1)} %bitcast.6), calls=%async_computation.2 | async-start | bytes 1572864 | tf_op jit(solution)/shard_map/all_to_all | solution.py:176
  71.5 3.8 %collective-permute-start.8 = (bf16[2,4,2,128,128]{4,3,2,1,0:T(8,128)(2,1)S(1)}, bf16[2,4,2,128,128]{4,3,2,1,0:T(8,128)(2,1)S(1)}, u32[]{:S(2)}, u32[]{:S(2)}) collective-permute-start(bf16[2,4,2,128,128]{4,3,2,1,0:T(8,128)(2,1)S(1)} %dynamic-slice_bitcast_fusion), channel_id=1, source_target_pairs={{0,32},{32,0},{1,33},{33,1},{2,34},{34,2},{3,35},{35,3},{4,36},{36... | collective-permute-start | bytes 1572872 | tf_op jit(solution)/shard_map/ppermute | solution.py:196
  75.3 0.8 copy-start.4
  81.2 17.0 %copy-start.1 = (bf16[3,256,256]{2,1,0:T(8,128)(2,1)S(1)}, bf16[3,256,256]{2,1,0:T(8,128)(2,1)}, u32[]{:S(2)}) copy-start(bf16[3,256,256]{2,1,0:T(8,128)(2,1)} %copy-done) | copy-start | bytes 1179652
  81.2 17.0 %copy-start.3 = (bf16[3,256,256]{2,1,0:T(8,128)(2,1)S(1)}, bf16[3,256,256]{2,1,0:T(8,128)(2,1)}, u32[]{:S(2)}) copy-start(bf16[3,256,256]{2,1,0:T(8,128)(2,1)} %copy-done.2) | copy-start | bytes 1179652
  96.3 13.6 %collective-permute-start.10 = (bf16[256,1536]{1,0:T(8,128)(2,1)S(1)}, bf16[256,1536]{1,0:T(8,128)(2,1)}, u32[]{:S(2)}, u32[]{:S(2)}) collective-permute-start(bf16[256,1536]{1,0:T(8,128)(2,1)S(1)} %bitcast.16), channel_id=1, source_target_pairs={{0,32},{32,0},{1,33},{33,1},{2,34},{34,2},{3,35},{35,3},{4,36},{36... | collective-permute-start | bytes 2359304 | tf_op jit(solution)/shard_map/ppermute | solution.py:200
  100.9 9.0 %copy-start.5 = (bf16[2,4,2,128,128]{4,3,2,1,0:T(8,128)(2,1)S(1)}, bf16[2,4,2,128,128]{4,3,2,1,0:T(8,128)(2,1)}, u32[]{:S(2)}) copy-start(bf16[2,4,2,128,128]{4,3,2,1,0:T(8,128)(2,1)} %copy-done.4) | copy-start | bytes 1572868
  100.9 29.6 %all-to-all-start.4 = ((bf16[16,128,128]{2,1,0:T(8,128)(2,1)}), bf16[16,128,128]{2,1,0:T(8,128)(2,1)}, u32[]{:S(2)}, u32[]{:S(2)}) async-start(bf16[16,128,128]{2,1,0:T(8,128)(2,1)} %input_terms.1), calls=%async_computation.4 | async-start | bytes 1048576 | tf_op jit(solution)/shard_map/all_to_all | solution.py:176
  112.9 32.8 %collective-permute-start.11 = (bf16[3,256,256]{2,1,0:T(8,128)(2,1)}, bf16[3,256,256]{2,1,0:T(8,128)(2,1)S(1)}, u32[]{:S(2)}, u32[]{:S(2)}) collective-permute-start(bf16[3,256,256]{2,1,0:T(8,128)(2,1)} %get-tuple-element.17), channel_id=1, source_target_pairs={{0,1},{1,0},{2,3},{3,2},{4,5},{5,4},{6,7},{7,6},{8,9},{9,8},{10,11... | collective-permute-start | bytes 1179656 | tf_op jit(solution)/shard_map/ppermute | solution.py:207
  116.4 29.4 %collective-permute-start.12 = (bf16[3,256,256]{2,1,0:T(8,128)(2,1)}, bf16[3,256,256]{2,1,0:T(8,128)(2,1)S(1)}, u32[]{:S(2)}, u32[]{:S(2)}) collective-permute-start(bf16[3,256,256]{2,1,0:T(8,128)(2,1)} %get-tuple-element.18), channel_id=1, source_target_pairs={{0,64},{64,0},{1,65},{65,1},{2,66},{66,2},{3,67},{67,3},{4,68},{68... | collective-permute-start | bytes 1179656 | tf_op jit(solution)/shard_map/ppermute | solution.py:208
  119.1 26.7 %collective-permute-start.13 = (bf16[3,256,256]{2,1,0:T(8,128)(2,1)}, bf16[3,256,256]{2,1,0:T(8,128)(2,1)S(1)}, u32[]{:S(2)}, u32[]{:S(2)}) collective-permute-start(bf16[3,256,256]{2,1,0:T(8,128)(2,1)} %get-tuple-element.19), channel_id=1, source_target_pairs={{0,65},{1,64},{64,1},{65,0},{2,67},{3,66},{66,3},{67,2},{4,69},{5,... | collective-permute-start | bytes 1179656 | tf_op jit(solution)/shard_map/ppermute | solution.py:209
  131.7 14.1 %collective-permute-start.9 = (bf16[128,128]{1,0:T(8,128)(2,1)S(1)}, bf16[128,128]{1,0:T(8,128)(2,1)S(1)}, u32[]{:S(2)}, u32[]{:S(2)}) collective-permute-start(bf16[128,128]{1,0:T(8,128)(2,1)S(1)} %reduce_sum.12), channel_id=1, source_target_pairs={{0,0},{8,1},{2,2},{10,3},{4,4},{12,5},{6,6},{14,7},{128,8},{136,9}... | collective-permute-start | bytes 98312 | tf_op jit(solution)/shard_map/ppermute | solution.py:204

commit v12 on v11

--- a/solution.py
+++ b/solution.py
@@ -181,14 +181,12 @@
     there = turned()
 
     acts = lax.ppermute(jnp.stack([inputs, out_grad]), AXES, there)
-    acts = exchange(jnp.broadcast_to(acts[None], (4,) + acts.shape), YH)
     w = (codes.astype(F32) * scales.astype(F32)).astype(BF16)
     w_z = lax.ppermute(w, "zl", SWAP)
-    w_x = lax.ppermute(w, "x0", SWAP)
-    acts, w_z, w_x = lax.optimization_barrier((acts, w_z, w_x))
-    weights = [w, w_z, w_x, lax.ppermute(w_z, "x0", SWAP)]
+    acts, w_z = lax.optimization_barrier((acts, w_z))
+    weights = [w, w_z] + [lax.ppermute(block, "x0", SWAP) for block in (w, w_z)]
     weights += [lax.ppermute(block, "core", SWAP) for block in weights]
-    acts = exchange(jnp.broadcast_to(acts[None], (4,) + acts.shape), ZH).reshape(16, 2, TOK, TOK)
+    acts = exchange(jnp.broadcast_to(acts[None], (16,) + acts.shape), ZH + YH)
 
     parts = gates(place, acts, *weights)
     other_acts = acts.reshape(2, 2, 4, 2, TOK, TOK)

time: 149 us -> 149 us (level)
  the two profiles are of different devices: /device:TPU:4 before, /device:TPU:1 now
where the time goes in v12:
time: 149 us; the launch traced here: 148 us
  starting transfers between devices  84.9 us (57%)
  waiting for transfers between devices  32.5 us (22%)
  blocking collectives  14 us (9%)
  Pallas kernels  8.84 us (6%)
  other arithmetic  4 us (3%)
  local copies, waits for them, and re-layouts  2.77 us (2%)
    all_to_all x3, starting transfers between devices, exchange(): return lax.all_to_all(pieces, axes, split_axis=0, concat_axis=0, tiled=True)  35.1 us
    ppermute x4, starting transfers between devices, local(): weights += [lax.ppermute(block, 'core', SWAP) for block in weights]  18.4 us
    all_to_all x1, blocking collectives, exchange(): return lax.all_to_all(pieces, axes, split_axis=0, concat_axis=0, tiled=True)  14 us
    all_to_all x3, waiting for transfers between devices, exchange(): return lax.all_to_all(pieces, axes, split_axis=0, concat_axis=0, tiled=True)  11.4 us
    ppermute x1, waiting for transfers between devices, local(): lax.ppermute(xz, ('x0', 'zl'), [(i, 3 - i) for i in range(4)]).astype(F32)  8.66 us
    ppermute x1, starting transfers between devices, local(): other_grads = lax.ppermute(grads, 'core', SWAP)  5.59 us
    ppermute x2, starting transfers between devices, local(): weights = [w, w_z] + [lax.ppermute(block, 'x0', SWAP) for block in (w, w_z)]  5.28 us
    ppermute x1, waiting for transfers between devices, local(): weight_grad += lax.ppermute(z, 'zl', SWAP).astype(F32)  5.15 us
  transfers between devices with their start and end apart: 17, of which 8 were waited for; matrix products, arithmetic and copies ran while one was open for 1% of the time, Pallas kernels for 4%

profile of v12, /device:TPU:1, one launch (start us, length us, event | category | flops | bytes accessed | tf_op | source)
XLA Modules:
  0.0 148.0 jit_solution(9148659652378522516)
XLA Ops:
  0.6 0.7 bitcast_convert_fusion
  1.3 0.0 copy-start.6
  1.3 0.0 copy-start.7
  1.3 1.1 multiply_convert_fusion.refs_0_
  2.4 4.8 %collective-permute-start.1 = (bf16[3,256,256]{2,1,0:T(8,128)(2,1)S(1)}, bf16[3,256,256]{2,1,0:T(8,128)(2,1)S(1)}, u32[]{:S(2)}, u32[]{:S(2)}) collective-permute-start(bf16[3,256,256]{2,1,0:T(8,128)(2,1)S(1)} %multiply_convert_fusion.refs_0_), channel_id=1, source_target_pairs={{0,1},{1,0},{2,3},{3,2},{4,5},{5,4},{6,7},{7,6},{8,9},{9,8},{10,11... | collective-permute-start | bytes 1179656 | tf_op jit(solution)/shard_map/ppermute | solution.py:185
  7.2 0.0 copy-done.6
  7.2 0.0 copy-done.7
  7.3 0.7 collective-permute-start
  7.9 0.0 collective-permute-done
  8.0 4.4 %collective-permute-done.1.refs_1_ = bf16[3,256,256]{2,1,0:T(8,128)(2,1)S(1)} collective-permute-done((bf16[3,256,256]{2,1,0:T(8,128)(2,1)S(1)}, bf16[3,256,256]{2,1,0:T(8,128)(2,1)S(1)}, u32[]{:S(2)}, u32[]{:S(2)}) %collective-permute-start.1) | collective-permute-done | bytes 393248 | tf_op jit(solution)/shard_map/ppermute | solution.py:185
  12.4 1.3 broadcast_in_dim.2
  13.6 18.1 %all-to-all-start = ((bf16[16,2,128,128]{3,2,1,0:T(8,128)(2,1)}), bf16[16,2,128,128]{3,2,1,0:T(8,128)(2,1)S(1)}, u32[]{:S(2)}, u32[]{:S(2)}) async-start(bf16[16,2,128,128]{3,2,1,0:T(8,128)(2,1)} %broadcast_in_dim.2), calls=%async_computation | async-start | bytes 2097152 | tf_op jit(solution)/shard_map/all_to_all | solution.py:176
  31.8 3.1 %collective-permute-start.2 = (bf16[3,256,256]{2,1,0:T(8,128)(2,1)S(1)}, bf16[3,256,256]{2,1,0:T(8,128)(2,1)S(1)}, u32[]{:S(2)}, u32[]{:S(2)}) collective-permute-start(bf16[3,256,256]{2,1,0:T(8,128)(2,1)S(1)} %multiply_convert_fusion.refs_0_), channel_id=1, source_target_pairs={{0,64},{64,0},{1,65},{65,1},{2,66},{66,2},{3,67},{67,3},{4,68},{68... | collective-permute-start | bytes 1179656 | tf_op jit(solution)/shard_map/ppermute | solution.py:187
  34.9 2.2 %collective-permute-start.3 = (bf16[3,256,256]{2,1,0:T(8,128)(2,1)S(1)}, bf16[3,256,256]{2,1,0:T(8,128)(2,1)S(1)}, u32[]{:S(2)}, u32[]{:S(2)}) collective-permute-start(bf16[3,256,256]{2,1,0:T(8,128)(2,1)S(1)} %collective-permute-done.1.refs_1_), channel_id=1, source_target_pairs={{0,64},{64,0},{1,65},{65,1},{2,66},{66,2},{3,67},{67,3},{4,68},{68... | collective-permute-start | bytes 1179656 | tf_op jit(solution)/shard_map/ppermute | solution.py:187
  37.1 5.0 %collective-permute-start.4 = (bf16[3,256,256]{2,1,0:T(8,128)(2,1)S(1)}, bf16[3,256,256]{2,1,0:T(8,128)(2,1)S(1)}, u32[]{:S(2)}, u32[]{:S(2)}) collective-permute-start(bf16[3,256,256]{2,1,0:T(8,128)(2,1)S(1)} %multiply_convert_fusion.refs_0_), channel_id=1, source_target_pairs={{0,32},{32,0},{1,33},{33,1},{2,34},{34,2},{3,35},{35,3},{4,36},{36... | collective-permute-start | bytes 1179656 | tf_op jit(solution)/shard_map/ppermute | solution.py:188
  42.1 1.9 %collective-permute-start.5 = (bf16[3,256,256]{2,1,0:T(8,128)(2,1)S(1)}, bf16[3,256,256]{2,1,0:T(8,128)(2,1)S(1)}, u32[]{:S(2)}, u32[]{:S(2)}) collective-permute-start(bf16[3,256,256]{2,1,0:T(8,128)(2,1)S(1)} %collective-permute-done.1.refs_1_), channel_id=1, source_target_pairs={{0,32},{32,0},{1,33},{33,1},{2,34},{34,2},{3,35},{35,3},{4,36},{36... | collective-permute-start | bytes 1179656 | tf_op jit(solution)/shard_map/ppermute | solution.py:188
  44.0 0.0 collective-permute-done.2.refs_2_
  44.0 6.1 %collective-permute-start.6 = (bf16[3,256,256]{2,1,0:T(8,128)(2,1)S(1)}, bf16[3,256,256]{2,1,0:T(8,128)(2,1)}, u32[]{:S(2)}, u32[]{:S(2)}) collective-permute-start(bf16[3,256,256]{2,1,0:T(8,128)(2,1)S(1)} %collective-permute-done.2.refs_2_), channel_id=1, source_target_pairs={{0,32},{32,0},{1,33},{33,1},{2,34},{34,2},{3,35},{35,3},{4,36},{36... | collective-permute-start | bytes 1179656 | tf_op jit(solution)/shard_map/ppermute | solution.py:188
  50.2 0.0 collective-permute-done.3.refs_3_
  50.2 5.3 %collective-permute-start.7 = (bf16[3,256,256]{2,1,0:T(8,128)(2,1)S(1)}, bf16[3,256,256]{2,1,0:T(8,128)(2,1)}, u32[]{:S(2)}, u32[]{:S(2)}) collective-permute-start(bf16[3,256,256]{2,1,0:T(8,128)(2,1)S(1)} %collective-permute-done.3.refs_3_), channel_id=1, source_target_pairs={{0,32},{32,0},{1,33},{33,1},{2,34},{34,2},{3,35},{35,3},{4,36},{36... | collective-permute-start | bytes 1179656 | tf_op jit(solution)/shard_map/ppermute | solution.py:188
  55.5 0.1 pad_add_fusion.place_ref
  55.6 0.0 collective-permute-done.4.refs_4_
  55.6 0.0 copy-start
  55.6 0.0 collective-permute-done.6.refs_6_
  55.6 0.0 collective-permute-done.5.refs_5_
  55.6 0.0 copy-start.2
  55.6 1.3 collective-permute-done.7.refs_7_
  57.0 2.7 %all-to-all-done.acts_ref = bf16[16,2,128,128]{3,2,1,0:T(8,128)(2,1)S(1)} async-done(((bf16[16,2,128,128]{3,2,1,0:T(8,128)(2,1)}), bf16[16,2,128,128]{3,2,1,0:T(8,128)(2,1)S(1)}, u32[]{:S(2)}, u32[]{:S(2)}) %all-to-all-start) | async-done | bytes 1048608 | tf_op jit(solution)/shard_map/all_to_all | solution.py:176
  59.7 3.0 %gates.1 = bf16[256,1536]{1,0:T(8,128)(2,1)} custom-call(s32[2]{0:T(128)S(1)} %pad_add_fusion.place_ref, bf16[16,2,128,128]{3,2,1,0:T(8,128)(2,1)S(1)} %all-to-all-done.acts_ref, bf16[3,256,256]{2,1,0:T(8,128)(2,1)S(1)} %multiply_convert_fusion.refs_0_, bf16[3,256,256]{2,1,0:T(8,128)(2,1)S(1)} %collective-permute-done.1.refs_1_, ...), custom_call_target="tpu_custom_call" | custom-call | flops 800000000 | bytes 6000000 | tf_op jit(solution)/shard_map/gates/pallas_call | solution.py:71
  62.7 0.0 copy-done
  62.7 0.0 copy-done.2
  62.7 8.3 %all-to-all-start.1 = ((bf16[4,64,1536]{2,1,0:T(8,128)(2,1)}), bf16[4,64,1536]{2,1,0:T(8,128)(2,1)S(1)}, u32[]{:S(2)}, u32[]{:S(2)}) async-start(bf16[4,64,1536]{2,1,0:T(8,128)(2,1)} %bitcast.5), calls=%async_computation.1 | async-start | bytes 1572864 | tf_op jit(solution)/shard_map/all_to_all | solution.py:176
  71.1 4.8 %collective-permute-start.8 = (bf16[2,4,2,128,128]{4,3,2,1,0:T(8,128)(2,1)S(1)}, bf16[2,4,2,128,128]{4,3,2,1,0:T(8,128)(2,1)S(1)}, u32[]{:S(2)}, u32[]{:S(2)}) collective-permute-start(bf16[2,4,2,128,128]{4,3,2,1,0:T(8,128)(2,1)S(1)} %dynamic-slice_bitcast_fusion), channel_id=1, source_target_pairs={{0,32},{32,0},{1,33},{33,1},{2,34},{34,2},{3,35},{35,3},{4,36},{36... | collective-permute-start | bytes 1572872 | tf_op jit(solution)/shard_map/ppermute | solution.py:194
  75.9 1.5 %collective-permute-done.8.other_acts_ref = bf16[2,4,2,128,128]{4,3,2,1,0:T(8,128)(2,1)S(1)} collective-permute-done((bf16[2,4,2,128,128]{4,3,2,1,0:T(8,128)(2,1)S(1)}, bf16[2,4,2,128,128]{4,3,2,1,0:T(8,128)(2,1)S(1)}, u32[]{:S(2)}, u32[]{:S(2)}) %collective-permute-start.8) | collective-permute-done | bytes 524320 | tf_op jit(solution)/shard_map/ppermute | solution.py:194
  77.4 0.0 copy-start.4
  77.4 0.8 copy-done.4
  78.3 2.7 %all-to-all-done.1.parts_ref = bf16[4,64,1536]{2,1,0:T(8,128)(2,1)S(1)} async-done(((bf16[4,64,1536]{2,1,0:T(8,128)(2,1)}), bf16[4,64,1536]{2,1,0:T(8,128)(2,1)S(1)}, u32[]{:S(2)}, u32[]{:S(2)}) %all-to-all-start.1) | async-done | bytes 786464 | tf_op jit(solution)/shard_map/all_to_all | solution.py:176
  81.0 0.2 hidden_grads.1
  81.2 0.0 copy-start.1
  81.2 0.0 copy-start.3
  81.2 14.0 %all_to_all.20 = bf16[4,64,1536]{2,1,0:T(8,128)(2,1)S(1)} all-to-all(bf16[4,64,1536]{2,1,0:T(8,128)(2,1)S(1)} %hidden_grads.1), channel_id=1, replica_groups=mesh['yl'=2,'x1'=2,'x0'=2,'core'=2,'yh1'=2,'yh0'=2,'zh1'=2,'zh0'=2,'zl'=..., dimensions={0} | all-to-all | bytes 1572864 | tf_op jit(solution)/shard_map/all_to_all | solution.py:176
  95.2 5.6 %collective-permute-start.10 = (bf16[256,1536]{1,0:T(8,128)(2,1)S(1)}, bf16[256,1536]{1,0:T(8,128)(2,1)}, u32[]{:S(2)}, u32[]{:S(2)}) collective-permute-start(bf16[256,1536]{1,0:T(8,128)(2,1)S(1)} %bitcast.15), channel_id=1, source_target_pairs={{0,32},{32,0},{1,33},{33,1},{2,34},{34,2},{3,35},{35,3},{4,36},{36... | collective-permute-start | bytes 2359304 | tf_op jit(solution)/shard_map/ppermute | solution.py:198
  100.8 0.0 copy-done.1
  100.8 0.0 copy-done.3
  100.8 2.7 %input_terms.1 = bf16[16,128,128]{2,1,0:T(8,128)(2,1)} custom-call(s32[2]{0:T(128)S(1)} %pad_add_fusion.place_ref, bf16[256,1536]{1,0:T(8,128)(2,1)S(1)} %bitcast.16, bf16[3,256,256]{2,1,0:T(8,128)(2,1)S(1)} %multiply_convert_fusion.refs_0_, bf16[3,256,256]{2,1,0:T(8,128)(2,1)S(1)} %collective-permute-done.1.refs_1_, ...), custom_call_target="tpu_custom_call" | custom-call | flops 540000000 | bytes 4000000 | tf_op jit(solution)/shard_map/input_terms/pallas_call | solution.py:126
  103.5 0.0 copy-start.5
  103.5 8.6 %all-to-all-start.3 = ((bf16[16,128,128]{2,1,0:T(8,128)(2,1)}), bf16[16,128,128]{2,1,0:T(8,128)(2,1)}, u32[]{:S(2)}, u32[]{:S(2)}) async-start(bf16[16,128,128]{2,1,0:T(8,128)(2,1)} %input_terms.1), calls=%async_computation.3 | async-start | bytes 1048576 | tf_op jit(solution)/shard_map/all_to_all | solution.py:176
  112.1 0.0 collective-permute-done.10.other_grads_ref
  112.1 0.0 copy-done.5
  112.1 3.0 %weight_terms.1 = (f32[3,256,256]{2,1,0:T(8,128)S(1)}, bf16[3,256,256]{2,1,0:T(8,128)(2,1)}, bf16[3,256,256]{2,1,0:T(8,128)(2,1)}, bf16[3,256,256]{2,1,0:T(8,128)(2,1)}) custom-call(s32[2]{0:T(128)S(1)} %pad_add_fusion.place_ref, bf16[16,2,128,128]{3,2,1,0:T(8,128)(2,1)S(1)} %all-to-all-done.acts_ref, bf16[2,4,2,128,128]{4,3,2,1,0:T(8,128)(2,1)S(1)} %copy-done.5, ...), custom_call_target="tpu_custom_call" | custom-call | flops 800000000 | bytes 6000000 | tf_op jit(solution)/shard_map/weight_terms/pallas_call | solution.py:163
  115.1 4.6 %collective-permute-start.11 = (bf16[3,256,256]{2,1,0:T(8,128)(2,1)}, bf16[3,256,256]{2,1,0:T(8,128)(2,1)S(1)}, u32[]{:S(2)}, u32[]{:S(2)}) collective-permute-start(bf16[3,256,256]{2,1,0:T(8,128)(2,1)} %get-tuple-element.15), channel_id=1, source_target_pairs={{0,1},{1,0},{2,3},{3,2},{4,5},{5,4},{6,7},{7,6},{8,9},{9,8},{10,11... | collective-permute-start | bytes 1179656 | tf_op jit(solution)/shard_map/ppermute | solution.py:205
  119.7 2.9 %collective-permute-start.12 = (bf16[3,256,256]{2,1,0:T(8,128)(2,1)}, bf16[3,256,256]{2,1,0:T(8,128)(2,1)S(1)}, u32[]{:S(2)}, u32[]{:S(2)}) collective-permute-start(bf16[3,256,256]{2,1,0:T(8,128)(2,1)} %get-tuple-element.16), channel_id=1, source_target_pairs={{0,64},{64,0},{1,65},{65,1},{2,66},{66,2},{3,67},{67,3},{4,68},{68... | collective-permute-start | bytes 1179656 | tf_op jit(solution)/shard_map/ppermute | solution.py:206
  122.6 2.1 %collective-permute-start.13 = (bf16[3,256,256]{2,1,0:T(8,128)(2,1)}, bf16[3,256,256]{2,1,0:T(8,128)(2,1)S(1)}, u32[]{:S(2)}, u32[]{:S(2)}) collective-permute-start(bf16[3,256,256]{2,1,0:T(8,128)(2,1)} %get-tuple-element.17), channel_id=1, source_target_pairs={{0,65},{1,64},{64,1},{65,0},{2,67},{3,66},{66,3},{67,2},{4,69},{5,... | collective-permute-start | bytes 1179656 | tf_op jit(solution)/shard_map/ppermute | solution.py:207
  124.7 6.0 %all-to-all-done.3 = bf16[16,128,128]{2,1,0:T(8,128)(2,1)} async-done(((bf16[16,128,128]{2,1,0:T(8,128)(2,1)}), bf16[16,128,128]{2,1,0:T(8,128)(2,1)}, u32[]{:S(2)}, u32[]{:S(2)}) %all-to-all-start.3) | async-done | bytes 524320 | tf_op jit(solution)/shard_map/all_to_all | solution.py:176
  130.7 1.1 reduce_sum.12
  131.8 0.7 collective-permute-start.9
  132.5 0.0 collective-permute-done.9
  132.5 5.1 %collective-permute-done.11 = bf16[3,256,256]{2,1,0:T(8,128)(2,1)S(1)} collective-permute-done((bf16[3,256,256]{2,1,0:T(8,128)(2,1)}, bf16[3,256,256]{2,1,0:T(8,128)(2,1)S(1)}, u32[]{:S(2)}, u32[]{:S(2)}) %collective-permute-start.11) | collective-permute-done | bytes 393248 | tf_op jit(solution)/shard_map/ppermute | solution.py:205
  137.7 0.0 collective-permute-done.12
  137.7 8.7 %collective-permute-done.13 = bf16[3,256,256]{2,1,0:T(8,128)(2,1)S(1)} collective-permute-done((bf16[3,256,256]{2,1,0:T(8,128)(2,1)}, bf16[3,256,256]{2,1,0:T(8,128)(2,1)S(1)}, u32[]{:S(2)}, u32[]{:S(2)}) %collective-permute-start.13) | collective-permute-done | bytes 393248 | tf_op jit(solution)/shard_map/ppermute | solution.py:207
  146.3 1.0 convert_add_fusion
  147.4 0.6 copy.9
  (2 shorter events, 0.0 us)
Async XLA Ops:
  1.3 5.9 %copy-start.6 = (bf16[128,128]{1,0:T(8,128)(2,1)S(1)}, bf16[128,128]{1,0:T(8,128)(2,1)}, u32[]{:S(2)}) copy-start(bf16[128,128]{1,0:T(8,128)(2,1)} %param.5) | copy-start | bytes 98308
  1.3 5.9 %copy-start.7 = (bf16[128,128]{1,0:T(8,128)(2,1)S(1)}, bf16[128,128]{1,0:T(8,128)(2,1)}, u32[]{:S(2)}) copy-start(bf16[128,128]{1,0:T(8,128)(2,1)} %param.4) | copy-start | bytes 98308
  2.4 10.0 %collective-permute-start.1 = (bf16[3,256,256]{2,1,0:T(8,128)(2,1)S(1)}, bf16[3,256,256]{2,1,0:T(8,128)(2,1)S(1)}, u32[]{:S(2)}, u32[]{:S(2)}) collective-permute-start(bf16[3,256,256]{2,1,0:T(8,128)(2,1)S(1)} %multiply_convert_fusion.refs_0_), channel_id=1, source_target_pairs={{0,1},{1,0},{2,3},{3,2},{4,5},{5,4},{6,7},{7,6},{8,9},{9,8},{10,11... | collective-permute-start | bytes 1179656 | tf_op jit(solution)/shard_map/ppermute | solution.py:185
  7.3 0.7 collective-permute-start
  13.6 46.0 %all-to-all-start = ((bf16[16,2,128,128]{3,2,1,0:T(8,128)(2,1)}), bf16[16,2,128,128]{3,2,1,0:T(8,128)(2,1)S(1)}, u32[]{:S(2)}, u32[]{:S(2)}) async-start(bf16[16,2,128,128]{3,2,1,0:T(8,128)(2,1)} %broadcast_in_dim.2), calls=%async_computation | async-start | bytes 2097152 | tf_op jit(solution)/shard_map/all_to_all | solution.py:176
  31.8 12.2 %collective-permute-start.2 = (bf16[3,256,256]{2,1,0:T(8,128)(2,1)S(1)}, bf16[3,256,256]{2,1,0:T(8,128)(2,1)S(1)}, u32[]{:S(2)}, u32[]{:S(2)}) collective-permute-start(bf16[3,256,256]{2,1,0:T(8,128)(2,1)S(1)} %multiply_convert_fusion.refs_0_), channel_id=1, source_target_pairs={{0,64},{64,0},{1,65},{65,1},{2,66},{66,2},{3,67},{67,3},{4,68},{68... | collective-permute-start | bytes 1179656 | tf_op jit(solution)/shard_map/ppermute | solution.py:187
  34.9 15.3 %collective-permute-start.3 = (bf16[3,256,256]{2,1,0:T(8,128)(2,1)S(1)}, bf16[3,256,256]{2,1,0:T(8,128)(2,1)S(1)}, u32[]{:S(2)}, u32[]{:S(2)}) collective-permute-start(bf16[3,256,256]{2,1,0:T(8,128)(2,1)S(1)} %collective-permute-done.1.refs_1_), channel_id=1, source_target_pairs={{0,64},{64,0},{1,65},{65,1},{2,66},{66,2},{3,67},{67,3},{4,68},{68... | collective-permute-start | bytes 1179656 | tf_op jit(solution)/shard_map/ppermute | solution.py:187
  37.1 18.5 %collective-permute-start.4 = (bf16[3,256,256]{2,1,0:T(8,128)(2,1)S(1)}, bf16[3,256,256]{2,1,0:T(8,128)(2,1)S(1)}, u32[]{:S(2)}, u32[]{:S(2)}) collective-permute-start(bf16[3,256,256]{2,1,0:T(8,128)(2,1)S(1)} %multiply_convert_fusion.refs_0_), channel_id=1, source_target_pairs={{0,32},{32,0},{1,33},{33,1},{2,34},{34,2},{3,35},{35,3},{4,36},{36... | collective-permute-start | bytes 1179656 | tf_op jit(solution)/shard_map/ppermute | solution.py:188
  42.1 13.5 %collective-permute-start.5 = (bf16[3,256,256]{2,1,0:T(8,128)(2,1)S(1)}, bf16[3,256,256]{2,1,0:T(8,128)(2,1)S(1)}, u32[]{:S(2)}, u32[]{:S(2)}) collective-permute-start(bf16[3,256,256]{2,1,0:T(8,128)(2,1)S(1)} %collective-permute-done.1.refs_1_), channel_id=1, source_target_pairs={{0,32},{32,0},{1,33},{33,1},{2,34},{34,2},{3,35},{35,3},{4,36},{36... | collective-permute-start | bytes 1179656 | tf_op jit(solution)/shard_map/ppermute | solution.py:188
  44.0 11.6 %collective-permute-start.6 = (bf16[3,256,256]{2,1,0:T(8,128)(2,1)S(1)}, bf16[3,256,256]{2,1,0:T(8,128)(2,1)}, u32[]{:S(2)}, u32[]{:S(2)}) collective-permute-start(bf16[3,256,256]{2,1,0:T(8,128)(2,1)S(1)} %collective-permute-done.2.refs_2_), channel_id=1, source_target_pairs={{0,32},{32,0},{1,33},{33,1},{2,34},{34,2},{3,35},{35,3},{4,36},{36... | collective-permute-start | bytes 1179656 | tf_op jit(solution)/shard_map/ppermute | solution.py:188
  50.2 6.8 %collective-permute-start.7 = (bf16[3,256,256]{2,1,0:T(8,128)(2,1)S(1)}, bf16[3,256,256]{2,1,0:T(8,128)(2,1)}, u32[]{:S(2)}, u32[]{:S(2)}) collective-permute-start(bf16[3,256,256]{2,1,0:T(8,128)(2,1)S(1)} %collective-permute-done.3.refs_3_), channel_id=1, source_target_pairs={{0,32},{32,0},{1,33},{33,1},{2,34},{34,2},{3,35},{35,3},{4,36},{36... | collective-permute-start | bytes 1179656 | tf_op jit(solution)/shard_map/ppermute | solution.py:188
  55.6 7.1 %copy-start = (bf16[3,256,256]{2,1,0:T(8,128)(2,1)}, bf16[3,256,256]{2,1,0:T(8,128)(2,1)S(1)}, u32[]{:S(2)}) copy-start(bf16[3,256,256]{2,1,0:T(8,128)(2,1)S(1)} %collective-permute-done.4.refs_4_) | copy-start | bytes 1179652
  55.6 7.1 %copy-start.2 = (bf16[3,256,256]{2,1,0:T(8,128)(2,1)}, bf16[3,256,256]{2,1,0:T(8,128)(2,1)S(1)}, u32[]{:S(2)}) copy-start(bf16[3,256,256]{2,1,0:T(8,128)(2,1)S(1)} %collective-permute-done.5.refs_5_) | copy-start | bytes 1179652
  62.7 18.3 %all-to-all-start.1 = ((bf16[4,64,1536]{2,1,0:T(8,128)(2,1)}), bf16[4,64,1536]{2,1,0:T(8,128)(2,1)S(1)}, u32[]{:S(2)}, u32[]{:S(2)}) async-start(bf16[4,64,1536]{2,1,0:T(8,128)(2,1)} %bitcast.5), calls=%async_computation.1 | async-start | bytes 1572864 | tf_op jit(solution)/shard_map/all_to_all | solution.py:176
  71.1 6.4 %collective-permute-start.8 = (bf16[2,4,2,128,128]{4,3,2,1,0:T(8,128)(2,1)S(1)}, bf16[2,4,2,128,128]{4,3,2,1,0:T(8,128)(2,1)S(1)}, u32[]{:S(2)}, u32[]{:S(2)}) collective-permute-start(bf16[2,4,2,128,128]{4,3,2,1,0:T(8,128)(2,1)S(1)} %dynamic-slice_bitcast_fusion), channel_id=1, source_target_pairs={{0,32},{32,0},{1,33},{33,1},{2,34},{34,2},{3,35},{35,3},{4,36},{36... | collective-permute-start | bytes 1572872 | tf_op jit(solution)/shard_map/ppermute | solution.py:194
  77.4 0.8 copy-start.4
  81.2 19.6 %copy-start.1 = (bf16[3,256,256]{2,1,0:T(8,128)(2,1)S(1)}, bf16[3,256,256]{2,1,0:T(8,128)(2,1)}, u32[]{:S(2)}) copy-start(bf16[3,256,256]{2,1,0:T(8,128)(2,1)} %copy-done) | copy-start | bytes 1179652
  81.2 19.6 %copy-start.3 = (bf16[3,256,256]{2,1,0:T(8,128)(2,1)S(1)}, bf16[3,256,256]{2,1,0:T(8,128)(2,1)}, u32[]{:S(2)}) copy-start(bf16[3,256,256]{2,1,0:T(8,128)(2,1)} %copy-done.2) | copy-start | bytes 1179652
  95.2 16.9 %collective-permute-start.10 = (bf16[256,1536]{1,0:T(8,128)(2,1)S(1)}, bf16[256,1536]{1,0:T(8,128)(2,1)}, u32[]{:S(2)}, u32[]{:S(2)}) collective-permute-start(bf16[256,1536]{1,0:T(8,128)(2,1)S(1)} %bitcast.15), channel_id=1, source_target_pairs={{0,32},{32,0},{1,33},{33,1},{2,34},{34,2},{3,35},{35,3},{4,36},{36... | collective-permute-start | bytes 2359304 | tf_op jit(solution)/shard_map/ppermute | solution.py:198
  103.5 8.6 %copy-start.5 = (bf16[2,4,2,128,128]{4,3,2,1,0:T(8,128)(2,1)S(1)}, bf16[2,4,2,128,128]{4,3,2,1,0:T(8,128)(2,1)}, u32[]{:S(2)}) copy-start(bf16[2,4,2,128,128]{4,3,2,1,0:T(8,128)(2,1)} %copy-done.4) | copy-start | bytes 1572868
  103.5 27.2 %all-to-all-start.3 = ((bf16[16,128,128]{2,1,0:T(8,128)(2,1)}), bf16[16,128,128]{2,1,0:T(8,128)(2,1)}, u32[]{:S(2)}, u32[]{:S(2)}) async-start(bf16[16,128,128]{2,1,0:T(8,128)(2,1)} %input_terms.1), calls=%async_computation.3 | async-start | bytes 1048576 | tf_op jit(solution)/shard_map/all_to_all | solution.py:176
  115.1 22.6 %collective-permute-start.11 = (bf16[3,256,256]{2,1,0:T(8,128)(2,1)}, bf16[3,256,256]{2,1,0:T(8,128)(2,1)S(1)}, u32[]{:S(2)}, u32[]{:S(2)}) collective-permute-start(bf16[3,256,256]{2,1,0:T(8,128)(2,1)} %get-tuple-element.15), channel_id=1, source_target_pairs={{0,1},{1,0},{2,3},{3,2},{4,5},{5,4},{6,7},{7,6},{8,9},{9,8},{10,11... | collective-permute-start | bytes 1179656 | tf_op jit(solution)/shard_map/ppermute | solution.py:205
  119.7 18.0 %collective-permute-start.12 = (bf16[3,256,256]{2,1,0:T(8,128)(2,1)}, bf16[3,256,256]{2,1,0:T(8,128)(2,1)S(1)}, u32[]{:S(2)}, u32[]{:S(2)}) collective-permute-start(bf16[3,256,256]{2,1,0:T(8,128)(2,1)} %get-tuple-element.16), channel_id=1, source_target_pairs={{0,64},{64,0},{1,65},{65,1},{2,66},{66,2},{3,67},{67,3},{4,68},{68... | collective-permute-start | bytes 1179656 | tf_op jit(solution)/shard_map/ppermute | solution.py:206
  122.6 23.8 %collective-permute-start.13 = (bf16[3,256,256]{2,1,0:T(8,128)(2,1)}, bf16[3,256,256]{2,1,0:T(8,128)(2,1)S(1)}, u32[]{:S(2)}, u32[]{:S(2)}) collective-permute-start(bf16[3,256,256]{2,1,0:T(8,128)(2,1)} %get-tuple-element.17), channel_id=1, source_target_pairs={{0,65},{1,64},{64,1},{65,0},{2,67},{3,66},{66,3},{67,2},{4,69},{5,... | collective-permute-start | bytes 1179656 | tf_op jit(solution)/shard_map/ppermute | solution.py:207
  131.8 0.7 collective-permute-start.9

commit v13 on v12

--- a/solution.py
+++ b/solution.py
@@ -25,6 +25,7 @@
 GRADS = 3 * WIDE
 VMEM_LIMIT = 24 * 1024 * 1024
 WHOLE = pl.BlockSpec(memory_space=pltpu.VMEM)
+ANYWHERE = pl.BlockSpec(memory_space=pl.ANY)
 SCALARS = pl.BlockSpec(memory_space=pltpu.SMEM)
 
 
@@ -52,28 +53,54 @@
     return 8 * x0 + 4 * core + 2 * t + f % 2
 
 
+def load_last(refs, last_ref, sems):
+    loads = []
+    for i, src in enumerate(refs[6:8]):
+        src = src.at[pl.ds(0, last_ref.shape[1])]
+        loads.append(pltpu.make_async_copy(src, last_ref.at[i], sems.at[i]))
+        loads[-1].start()
+    return list(refs[:6]) + [last_ref.at[0], last_ref.at[1]], loads
+
+
 def gates_kernel(place_ref, acts_ref, *refs):
-    w_refs, parts_ref, wide_ref = refs[:8], refs[8], refs[9]
+    parts_out, wide_ref, last_ref, parts_ref, in_sems, out_sems = refs[8:]
+    w_refs, loads = load_last(refs, last_ref, in_sems)
     for p in range(2):
         for t in range(2):
             for f in range(8):
                 block = acts_ref[chunk(place_ref, t, f), p]
                 wide_ref[p, pl.ds(t * TOK, TOK), pl.ds(f * TOK, TOK)] = block
+    stores = []
     for p in range(3):
         for j in range(2):
             total = jnp.zeros((TOKENS, BLOCK), F32)
             for s in range(4):
+                if s == 3 and p == 0:
+                    loads[j].wait()
                 total += dot(wide_ref[p // 2, :, pl.ds(s * BLOCK, BLOCK)], w_refs[2 * s + j][p], ((1,), (0,)))
             parts_ref[:, pl.ds(p * WIDE + j * BLOCK, BLOCK)] = total.astype(BF16)
+        cols = pl.ds(p * WIDE, WIDE)
+        stores.append(
+            pltpu.make_async_copy(parts_ref.at[:, cols], parts_out.at[:, cols], out_sems.at[p])
+        )
+        stores[-1].start()
+    for store in stores:
+        store.wait()
 
 
 def gates(place, acts, *weights):
     return pl.pallas_call(
         gates_kernel,
         out_shape=jax.ShapeDtypeStruct((TOKENS, GRADS), BF16),
-        in_specs=[SCALARS] + [WHOLE] * 9,
-        out_specs=WHOLE,
-        scratch_shapes=[pltpu.VMEM((2, TOKENS, FEATURES), BF16)],
+        in_specs=[SCALARS] + [WHOLE] * 7 + [ANYWHERE] * 2,
+        out_specs=ANYWHERE,
+        scratch_shapes=[
+            pltpu.VMEM((2, TOKENS, FEATURES), BF16),
+            pltpu.VMEM((2, 3, BLOCK, BLOCK), BF16),
+            pltpu.VMEM((TOKENS, GRADS), BF16),
+            pltpu.SemaphoreType.DMA((2,)),
+            pltpu.SemaphoreType.DMA((3,)),
+        ],
         compiler_params=params(),
         cost_estimate=pl.CostEstimate(flops=800000000, bytes_accessed=6000000, transcendentals=0),
         name="gates",
@@ -108,8 +135,13 @@
 
 
 def input_kernel(place_ref, grads_ref, *refs):
-    w_refs, dx_ref = refs[:8], refs[8]
+    dx_out, last_ref, dx_ref, in_sems, out_sems = refs[8:]
+    w_refs, loads = load_last(refs, last_ref, in_sems)
+    stores = []
     for s in range(4):
+        if s == 3:
+            for load in loads:
+                load.wait()
         dx = jnp.zeros((TOKENS, BLOCK), F32)
         for p in range(2):
             for j in range(2):
@@ -118,16 +150,28 @@
         dx = dx.astype(BF16)
         for t in range(2):
             for f in range(2):
-                part = dx[t * TOK : (t + 1) * TOK, f * TOK : (f + 1) * TOK]
-                dx_ref[chunk(place_ref, t, 2 * s + f)] = part
+                at = chunk(place_ref, t, 2 * s + f)
+                dx_ref[at] = dx[t * TOK : (t + 1) * TOK, f * TOK : (f + 1) * TOK]
+                stores.append(
+                    pltpu.make_async_copy(dx_ref.at[at], dx_out.at[at], out_sems.at[len(stores)])
+                )
+                stores[-1].start()
+    for store in stores:
+        store.wait()
 
 
 def input_terms(place, grads, *weights):
     return pl.pallas_call(
         input_kernel,
         out_shape=jax.ShapeDtypeStruct((16, TOK, TOK), BF16),
-        in_specs=[SCALARS] + [WHOLE] * 9,
-        out_specs=WHOLE,
+        in_specs=[SCALARS] + [WHOLE] * 7 + [ANYWHERE] * 2,
+        out_specs=ANYWHERE,
+        scratch_shapes=[
+            pltpu.VMEM((2, 2, BLOCK, BLOCK), BF16),
+            pltpu.VMEM((16, TOK, TOK), BF16),
+            pltpu.SemaphoreType.DMA((2,)),
+            pltpu.SemaphoreType.DMA((16,)),
+        ],
         compiler_params=params(),
         cost_estimate=pl.CostEstimate(flops=540000000, bytes_accessed=4000000, transcendentals=0),
         name="input_terms",
@@ -135,8 +179,11 @@
 
 
 def weight_kernel(
-    place_ref, acts_ref, other_acts_ref, grads_ref, other_grads_ref, keep_ref, z_ref, x_ref, xz_ref, wide_ref
+    place_ref, acts_ref, other_acts_ref, grads_ref, other_grads_in, keep_ref, z_out, x_out, xz_out,
+    wide_ref, other_grads_ref, send_ref, in_sem, out_sems,
 ):
+    load = pltpu.make_async_copy(other_grads_in, other_grads_ref, in_sem)
+    load.start()
     for p in range(2):
         for t in range(2):
             for f in range(4):
@@ -145,16 +192,26 @@
                 mine = acts_ref[chunk(place_ref, t, f), p]
                 wide_ref[p, pl.ds(t * TOK, TOK), cols] = mine
                 wide_ref[p, pl.ds(TOKENS + t * TOK, TOK), cols] = other_acts_ref[x0, 2 * t + f % 2, p]
-    for side in (1, 0):
+    load.wait()
+    stores = []
+    for side, j in ((1, 1), (0, 1), (1, 0), (0, 0)):
         for p in range(3):
-            for j in range(2):
-                cols = pl.ds(p * WIDE + j * BLOCK, BLOCK)
-                term = jnp.zeros((BLOCK, BLOCK), F32)
-                for i, ref in enumerate((grads_ref, other_grads_ref)):
-                    x = wide_ref[p // 2, pl.ds(i * TOKENS, TOKENS), pl.ds(side * BLOCK, BLOCK)]
-                    term += dot(x, ref[:, cols], ((0,), (0,)))
-                out_ref = ((keep_ref, z_ref), (x_ref, xz_ref))[side][j]
-                out_ref[p] = term.astype(out_ref.dtype)
+            cols = pl.ds(p * WIDE + j * BLOCK, BLOCK)
+            term = jnp.zeros((BLOCK, BLOCK), F32)
+            for i, ref in enumerate((grads_ref, other_grads_ref)):
+                x = wide_ref[p // 2, pl.ds(i * TOKENS, TOKENS), pl.ds(side * BLOCK, BLOCK)]
+                term += dot(x, ref[:, cols], ((0,), (0,)))
+            if side or j:
+                send_ref[2 * side + j - 1, p] = term.astype(BF16)
+            else:
+                keep_ref[p] = term
+        if side or j:
+            at = 2 * side + j - 1
+            out = (z_out, x_out, xz_out)[at]
+            stores.append(pltpu.make_async_copy(send_ref.at[at], out, out_sems.at[at]))
+            stores[-1].start()
+    for store in stores:
+        store.wait()
 
 
 def weight_terms(place, acts, other_acts, grads, other_grads):
@@ -163,9 +220,15 @@
     return pl.pallas_call(
         weight_kernel,
         out_shape=(jax.ShapeDtypeStruct(shape, F32), send, send, send),
-        in_specs=[SCALARS] + [WHOLE] * 4,
-        out_specs=(WHOLE,) * 4,
-        scratch_shapes=[pltpu.VMEM((2, 2 * TOKENS, WIDE), BF16)],
+        in_specs=[SCALARS] + [WHOLE] * 3 + [ANYWHERE],
+        out_specs=(WHOLE,) + (ANYWHERE,) * 3,
+        scratch_shapes=[
+            pltpu.VMEM((2, 2 * TOKENS, WIDE), BF16),
+            pltpu.VMEM((TOKENS, GRADS), BF16),
+            pltpu.VMEM((3,) + shape, BF16),
+            pltpu.SemaphoreType.DMA,
+            pltpu.SemaphoreType.DMA((3,)),
+        ],
         compiler_params=params(),
         cost_estimate=pl.CostEstimate(flops=800000000, bytes_accessed=6000000, transcendentals=0),
         name="weight_terms",

time: 149 us -> 151 us (1.013)
  Pallas kernels: 8.84 us -> 10.5 us
where the time goes in v13:
time: 151 us; the launch traced here: 150 us
  starting transfers between devices  85 us (56%)
  waiting for transfers between devices  32.4 us (21%)
  blocking collectives  14 us (9%)
  Pallas kernels  10.5 us (7%)
  other arithmetic  4 us (3%)
  local copies, waits for them, and re-layouts  2.77 us (2%)
    all_to_all x3, starting transfers between devices, exchange(): return lax.all_to_all(pieces, axes, split_axis=0, concat_axis=0, tiled=True)  35.1 us
    ppermute x4, starting transfers between devices, local(): weights += [lax.ppermute(block, 'core', SWAP) for block in weights]  18.4 us
    all_to_all x1, blocking collectives, exchange(): return lax.all_to_all(pieces, axes, split_axis=0, concat_axis=0, tiled=True)  14 us
    all_to_all x3, waiting for transfers between devices, exchange(): return lax.all_to_all(pieces, axes, split_axis=0, concat_axis=0, tiled=True)  11 us
    ppermute x1, waiting for transfers between devices, local(): lax.ppermute(xz, ('x0', 'zl'), [(i, 3 - i) for i in range(4)]).astype(F32)  8.79 us
    ppermute x1, starting transfers between devices, local(): other_grads = lax.ppermute(grads, 'core', SWAP)  5.59 us
    ppermute x1, waiting for transfers between devices, local(): weight_grad += lax.ppermute(z, 'zl', SWAP).astype(F32)  5.3 us
    ppermute x2, starting transfers between devices, local(): weights = [w, w_z] + [lax.ppermute(block, 'x0', SWAP) for block in (w, w_z)]  5.28 us
  transfers between devices with their start and end apart: 17, of which 8 were waited for; matrix products, arithmetic and copies ran while one was open for 1% of the time, Pallas kernels for 4%

profile of v13, /device:TPU:1, one launch (start us, length us, event | category | flops | bytes accessed | tf_op | source)
XLA Modules:
  0.0 149.6 jit_solution(4624469526937068119)
XLA Ops:
  0.6 0.7 bitcast_convert_fusion
  1.3 0.0 copy-start.6
  1.3 0.0 copy-start.7
  1.3 1.1 multiply_convert_fusion.refs_0_
  2.4 4.8 %collective-permute-start.1 = (bf16[3,256,256]{2,1,0:T(8,128)(2,1)S(1)}, bf16[3,256,256]{2,1,0:T(8,128)(2,1)S(1)}, u32[]{:S(2)}, u32[]{:S(2)}) collective-permute-start(bf16[3,256,256]{2,1,0:T(8,128)(2,1)S(1)} %multiply_convert_fusion.refs_0_), channel_id=1, source_target_pairs={{0,1},{1,0},{2,3},{3,2},{4,5},{5,4},{6,7},{7,6},{8,9},{9,8},{10,11... | collective-permute-start | bytes 1179656 | tf_op jit(solution)/shard_map/ppermute | solution.py:248
  7.2 0.0 copy-done.6
  7.2 0.0 copy-done.7
  7.3 0.7 collective-permute-start
  7.9 0.0 collective-permute-done
  8.0 4.4 %collective-permute-done.1.refs_1_ = bf16[3,256,256]{2,1,0:T(8,128)(2,1)S(1)} collective-permute-done((bf16[3,256,256]{2,1,0:T(8,128)(2,1)S(1)}, bf16[3,256,256]{2,1,0:T(8,128)(2,1)S(1)}, u32[]{:S(2)}, u32[]{:S(2)}) %collective-permute-start.1) | collective-permute-done | bytes 393248 | tf_op jit(solution)/shard_map/ppermute | solution.py:248
  12.4 1.3 broadcast_in_dim.2
  13.6 18.1 %all-to-all-start = ((bf16[16,2,128,128]{3,2,1,0:T(8,128)(2,1)}), bf16[16,2,128,128]{3,2,1,0:T(8,128)(2,1)S(1)}, u32[]{:S(2)}, u32[]{:S(2)}) async-start(bf16[16,2,128,128]{3,2,1,0:T(8,128)(2,1)} %broadcast_in_dim.2), calls=%async_computation | async-start | bytes 2097152 | tf_op jit(solution)/shard_map/all_to_all | solution.py:239
  31.8 3.1 %collective-permute-start.2 = (bf16[3,256,256]{2,1,0:T(8,128)(2,1)S(1)}, bf16[3,256,256]{2,1,0:T(8,128)(2,1)S(1)}, u32[]{:S(2)}, u32[]{:S(2)}) collective-permute-start(bf16[3,256,256]{2,1,0:T(8,128)(2,1)S(1)} %multiply_convert_fusion.refs_0_), channel_id=1, source_target_pairs={{0,64},{64,0},{1,65},{65,1},{2,66},{66,2},{3,67},{67,3},{4,68},{68... | collective-permute-start | bytes 1179656 | tf_op jit(solution)/shard_map/ppermute | solution.py:250
  34.9 2.2 %collective-permute-start.3 = (bf16[3,256,256]{2,1,0:T(8,128)(2,1)S(1)}, bf16[3,256,256]{2,1,0:T(8,128)(2,1)S(1)}, u32[]{:S(2)}, u32[]{:S(2)}) collective-permute-start(bf16[3,256,256]{2,1,0:T(8,128)(2,1)S(1)} %collective-permute-done.1.refs_1_), channel_id=1, source_target_pairs={{0,64},{64,0},{1,65},{65,1},{2,66},{66,2},{3,67},{67,3},{4,68},{68... | collective-permute-start | bytes 1179656 | tf_op jit(solution)/shard_map/ppermute | solution.py:250
  37.1 5.0 %collective-permute-start.4 = (bf16[3,256,256]{2,1,0:T(8,128)(2,1)S(1)}, bf16[3,256,256]{2,1,0:T(8,128)(2,1)S(1)}, u32[]{:S(2)}, u32[]{:S(2)}) collective-permute-start(bf16[3,256,256]{2,1,0:T(8,128)(2,1)S(1)} %multiply_convert_fusion.refs_0_), channel_id=1, source_target_pairs={{0,32},{32,0},{1,33},{33,1},{2,34},{34,2},{3,35},{35,3},{4,36},{36... | collective-permute-start | bytes 1179656 | tf_op jit(solution)/shard_map/ppermute | solution.py:251
  42.1 1.9 %collective-permute-start.5 = (bf16[3,256,256]{2,1,0:T(8,128)(2,1)S(1)}, bf16[3,256,256]{2,1,0:T(8,128)(2,1)S(1)}, u32[]{:S(2)}, u32[]{:S(2)}) collective-permute-start(bf16[3,256,256]{2,1,0:T(8,128)(2,1)S(1)} %collective-permute-done.1.refs_1_), channel_id=1, source_target_pairs={{0,32},{32,0},{1,33},{33,1},{2,34},{34,2},{3,35},{35,3},{4,36},{36... | collective-permute-start | bytes 1179656 | tf_op jit(solution)/shard_map/ppermute | solution.py:251
  44.0 0.0 collective-permute-done.2.refs_2_
  44.0 6.1 %collective-permute-start.6 = (bf16[3,256,256]{2,1,0:T(8,128)(2,1)S(1)}, bf16[3,256,256]{2,1,0:T(8,128)(2,1)}, u32[]{:S(2)}, u32[]{:S(2)}) collective-permute-start(bf16[3,256,256]{2,1,0:T(8,128)(2,1)S(1)} %collective-permute-done.2.refs_2_), channel_id=1, source_target_pairs={{0,32},{32,0},{1,33},{33,1},{2,34},{34,2},{3,35},{35,3},{4,36},{36... | collective-permute-start | bytes 1179656 | tf_op jit(solution)/shard_map/ppermute | solution.py:251
  50.2 0.0 collective-permute-done.3.refs_3_
  50.2 5.3 %collective-permute-start.7 = (bf16[3,256,256]{2,1,0:T(8,128)(2,1)S(1)}, bf16[3,256,256]{2,1,0:T(8,128)(2,1)}, u32[]{:S(2)}, u32[]{:S(2)}) collective-permute-start(bf16[3,256,256]{2,1,0:T(8,128)(2,1)S(1)} %collective-permute-done.3.refs_3_), channel_id=1, source_target_pairs={{0,32},{32,0},{1,33},{33,1},{2,34},{34,2},{3,35},{35,3},{4,36},{36... | collective-permute-start | bytes 1179656 | tf_op jit(solution)/shard_map/ppermute | solution.py:251
  55.5 0.1 pad_add_fusion.place_ref
  55.6 0.0 collective-permute-done.4.refs_4_
  55.6 0.0 copy-start
  55.6 0.0 collective-permute-done.6.refs_6_
  55.6 0.0 collective-permute-done.5.refs_5_
  55.6 0.0 copy-start.2
  55.6 1.3 collective-permute-done.7.refs_7_
  57.0 2.7 %all-to-all-done.acts_ref = bf16[16,2,128,128]{3,2,1,0:T(8,128)(2,1)S(1)} async-done(((bf16[16,2,128,128]{3,2,1,0:T(8,128)(2,1)}), bf16[16,2,128,128]{3,2,1,0:T(8,128)(2,1)S(1)}, u32[]{:S(2)}, u32[]{:S(2)}) %all-to-all-start) | async-done | bytes 1048608 | tf_op jit(solution)/shard_map/all_to_all | solution.py:239
  59.7 3.6 %gates.1 = bf16[256,1536]{1,0:T(8,128)(2,1)} custom-call(s32[2]{0:T(128)S(1)} %pad_add_fusion.place_ref, bf16[16,2,128,128]{3,2,1,0:T(8,128)(2,1)S(1)} %all-to-all-done.acts_ref, bf16[3,256,256]{2,1,0:T(8,128)(2,1)S(1)} %multiply_convert_fusion.refs_0_, bf16[3,256,256]{2,1,0:T(8,128)(2,1)S(1)} %collective-permute-done.1.refs_1_, ...), custom_call_target="tpu_custom_call" | custom-call | flops 800000000 | bytes 6000000 | tf_op jit(solution)/shard_map/gates/pallas_call | solution.py:92
  63.3 0.0 copy-done
  63.3 0.0 copy-done.2
  63.3 8.4 %all-to-all-start.1 = ((bf16[4,64,1536]{2,1,0:T(8,128)(2,1)}), bf16[4,64,1536]{2,1,0:T(8,128)(2,1)S(1)}, u32[]{:S(2)}, u32[]{:S(2)}) async-start(bf16[4,64,1536]{2,1,0:T(8,128)(2,1)} %bitcast.5), calls=%async_computation.1 | async-start | bytes 1572864 | tf_op jit(solution)/shard_map/all_to_all | solution.py:239
  71.7 4.8 %collective-permute-start.8 = (bf16[2,4,2,128,128]{4,3,2,1,0:T(8,128)(2,1)S(1)}, bf16[2,4,2,128,128]{4,3,2,1,0:T(8,128)(2,1)S(1)}, u32[]{:S(2)}, u32[]{:S(2)}) collective-permute-start(bf16[2,4,2,128,128]{4,3,2,1,0:T(8,128)(2,1)S(1)} %dynamic-slice_bitcast_fusion), channel_id=1, source_target_pairs={{0,32},{32,0},{1,33},{33,1},{2,34},{34,2},{3,35},{35,3},{4,36},{36... | collective-permute-start | bytes 1572872 | tf_op jit(solution)/shard_map/ppermute | solution.py:257
  76.5 1.5 %collective-permute-done.8.other_acts_ref = bf16[2,4,2,128,128]{4,3,2,1,0:T(8,128)(2,1)S(1)} collective-permute-done((bf16[2,4,2,128,128]{4,3,2,1,0:T(8,128)(2,1)S(1)}, bf16[2,4,2,128,128]{4,3,2,1,0:T(8,128)(2,1)S(1)}, u32[]{:S(2)}, u32[]{:S(2)}) %collective-permute-start.8) | collective-permute-done | bytes 524320 | tf_op jit(solution)/shard_map/ppermute | solution.py:257
  78.0 0.0 copy-start.4
  78.0 0.8 copy-done.4
  78.9 2.7 %all-to-all-done.1.parts_ref = bf16[4,64,1536]{2,1,0:T(8,128)(2,1)S(1)} async-done(((bf16[4,64,1536]{2,1,0:T(8,128)(2,1)}), bf16[4,64,1536]{2,1,0:T(8,128)(2,1)S(1)}, u32[]{:S(2)}, u32[]{:S(2)}) %all-to-all-start.1) | async-done | bytes 786464 | tf_op jit(solution)/shard_map/all_to_all | solution.py:239
  81.6 0.2 hidden_grads.1
  81.8 0.0 copy-start.1
  81.8 0.0 copy-start.3
  81.8 14.0 %all_to_all.20 = bf16[4,64,1536]{2,1,0:T(8,128)(2,1)S(1)} all-to-all(bf16[4,64,1536]{2,1,0:T(8,128)(2,1)S(1)} %hidden_grads.1), channel_id=1, replica_groups=mesh['yl'=2,'x1'=2,'x0'=2,'core'=2,'yh1'=2,'yh0'=2,'zh1'=2,'zh0'=2,'zl'=..., dimensions={0} | all-to-all | bytes 1572864 | tf_op jit(solution)/shard_map/all_to_all | solution.py:239
  95.8 5.6 %collective-permute-start.10 = (bf16[256,1536]{1,0:T(8,128)(2,1)S(1)}, bf16[256,1536]{1,0:T(8,128)(2,1)}, u32[]{:S(2)}, u32[]{:S(2)}) collective-permute-start(bf16[256,1536]{1,0:T(8,128)(2,1)S(1)} %bitcast.15), channel_id=1, source_target_pairs={{0,32},{32,0},{1,33},{33,1},{2,34},{34,2},{3,35},{35,3},{4,36},{36... | collective-permute-start | bytes 2359304 | tf_op jit(solution)/shard_map/ppermute | solution.py:261
  101.4 0.0 copy-done.1
  101.4 0.0 copy-done.3
  101.4 3.3 %input_terms.1 = bf16[16,128,128]{2,1,0:T(8,128)(2,1)} custom-call(s32[2]{0:T(128)S(1)} %pad_add_fusion.place_ref, bf16[256,1536]{1,0:T(8,128)(2,1)S(1)} %bitcast.16, bf16[3,256,256]{2,1,0:T(8,128)(2,1)S(1)} %multiply_convert_fusion.refs_0_, bf16[3,256,256]{2,1,0:T(8,128)(2,1)S(1)} %collective-permute-done.1.refs_1_, ...), custom_call_target="tpu_custom_call" | custom-call | flops 540000000 | bytes 4000000 | tf_op jit(solution)/shard_map/input_terms/pallas_call | solution.py:164
  104.8 0.0 copy-start.5
  104.8 8.6 %all-to-all-start.3 = ((bf16[16,128,128]{2,1,0:T(8,128)(2,1)}), bf16[16,128,128]{2,1,0:T(8,128)(2,1)}, u32[]{:S(2)}, u32[]{:S(2)}) async-start(bf16[16,128,128]{2,1,0:T(8,128)(2,1)} %input_terms.1), calls=%async_computation.3 | async-start | bytes 1048576 | tf_op jit(solution)/shard_map/all_to_all | solution.py:239
  113.4 0.0 collective-permute-done.10.other_grads_in
  113.4 0.0 copy-done.5
  113.4 3.4 %weight_terms.1 = (f32[3,256,256]{2,1,0:T(8,128)S(1)}, bf16[3,256,256]{2,1,0:T(8,128)(2,1)}, bf16[3,256,256]{2,1,0:T(8,128)(2,1)}, bf16[3,256,256]{2,1,0:T(8,128)(2,1)}) custom-call(s32[2]{0:T(128)S(1)} %pad_add_fusion.place_ref, bf16[16,2,128,128]{3,2,1,0:T(8,128)(2,1)S(1)} %all-to-all-done.acts_ref, bf16[2,4,2,128,128]{4,3,2,1,0:T(8,128)(2,1)S(1)} %copy-done.5, ...), custom_call_target="tpu_custom_call" | custom-call | flops 800000000 | bytes 6000000 | tf_op jit(solution)/shard_map/weight_terms/pallas_call | solution.py:220
  116.8 4.6 %collective-permute-start.11 = (bf16[3,256,256]{2,1,0:T(8,128)(2,1)}, bf16[3,256,256]{2,1,0:T(8,128)(2,1)S(1)}, u32[]{:S(2)}, u32[]{:S(2)}) collective-permute-start(bf16[3,256,256]{2,1,0:T(8,128)(2,1)} %get-tuple-element.15), channel_id=1, source_target_pairs={{0,1},{1,0},{2,3},{3,2},{4,5},{5,4},{6,7},{7,6},{8,9},{9,8},{10,11... | collective-permute-start | bytes 1179656 | tf_op jit(solution)/shard_map/ppermute | solution.py:268
  121.4 2.9 %collective-permute-start.12 = (bf16[3,256,256]{2,1,0:T(8,128)(2,1)}, bf16[3,256,256]{2,1,0:T(8,128)(2,1)S(1)}, u32[]{:S(2)}, u32[]{:S(2)}) collective-permute-start(bf16[3,256,256]{2,1,0:T(8,128)(2,1)} %get-tuple-element.16), channel_id=1, source_target_pairs={{0,64},{64,0},{1,65},{65,1},{2,66},{66,2},{3,67},{67,3},{4,68},{68... | collective-permute-start | bytes 1179656 | tf_op jit(solution)/shard_map/ppermute | solution.py:269
  124.3 2.1 %collective-permute-start.13 = (bf16[3,256,256]{2,1,0:T(8,128)(2,1)}, bf16[3,256,256]{2,1,0:T(8,128)(2,1)S(1)}, u32[]{:S(2)}, u32[]{:S(2)}) collective-permute-start(bf16[3,256,256]{2,1,0:T(8,128)(2,1)} %get-tuple-element.17), channel_id=1, source_target_pairs={{0,65},{1,64},{64,1},{65,0},{2,67},{3,66},{66,3},{67,2},{4,69},{5,... | collective-permute-start | bytes 1179656 | tf_op jit(solution)/shard_map/ppermute | solution.py:270
  126.4 5.6 %all-to-all-done.3 = bf16[16,128,128]{2,1,0:T(8,128)(2,1)} async-done(((bf16[16,128,128]{2,1,0:T(8,128)(2,1)}), bf16[16,128,128]{2,1,0:T(8,128)(2,1)}, u32[]{:S(2)}, u32[]{:S(2)}) %all-to-all-start.3) | async-done | bytes 524320 | tf_op jit(solution)/shard_map/all_to_all | solution.py:239
  132.0 1.1 reduce_sum.12
  133.2 0.7 collective-permute-start.9
  133.8 0.0 collective-permute-done.9
  133.8 5.3 %collective-permute-done.11 = bf16[3,256,256]{2,1,0:T(8,128)(2,1)S(1)} collective-permute-done((bf16[3,256,256]{2,1,0:T(8,128)(2,1)}, bf16[3,256,256]{2,1,0:T(8,128)(2,1)S(1)}, u32[]{:S(2)}, u32[]{:S(2)}) %collective-permute-start.11) | collective-permute-done | bytes 393248 | tf_op jit(solution)/shard_map/ppermute | solution.py:268
  139.1 0.0 collective-permute-done.12
  139.1 8.8 %collective-permute-done.13 = bf16[3,256,256]{2,1,0:T(8,128)(2,1)S(1)} collective-permute-done((bf16[3,256,256]{2,1,0:T(8,128)(2,1)}, bf16[3,256,256]{2,1,0:T(8,128)(2,1)S(1)}, u32[]{:S(2)}, u32[]{:S(2)}) %collective-permute-start.13) | collective-permute-done | bytes 393248 | tf_op jit(solution)/shard_map/ppermute | solution.py:270
  147.9 1.0 convert_add_fusion
  149.0 0.6 copy.9
  (2 shorter events, 0.0 us)
Async XLA Ops:
  1.3 5.9 %copy-start.6 = (bf16[128,128]{1,0:T(8,128)(2,1)S(1)}, bf16[128,128]{1,0:T(8,128)(2,1)}, u32[]{:S(2)}) copy-start(bf16[128,128]{1,0:T(8,128)(2,1)} %param.5) | copy-start | bytes 98308
  1.3 5.9 %copy-start.7 = (bf16[128,128]{1,0:T(8,128)(2,1)S(1)}, bf16[128,128]{1,0:T(8,128)(2,1)}, u32[]{:S(2)}) copy-start(bf16[128,128]{1,0:T(8,128)(2,1)} %param.4) | copy-start | bytes 98308
  2.4 10.0 %collective-permute-start.1 = (bf16[3,256,256]{2,1,0:T(8,128)(2,1)S(1)}, bf16[3,256,256]{2,1,0:T(8,128)(2,1)S(1)}, u32[]{:S(2)}, u32[]{:S(2)}) collective-permute-start(bf16[3,256,256]{2,1,0:T(8,128)(2,1)S(1)} %multiply_convert_fusion.refs_0_), channel_id=1, source_target_pairs={{0,1},{1,0},{2,3},{3,2},{4,5},{5,4},{6,7},{7,6},{8,9},{9,8},{10,11... | collective-permute-start | bytes 1179656 | tf_op jit(solution)/shard_map/ppermute | solution.py:248
  7.3 0.7 collective-permute-start
  13.6 46.0 %all-to-all-start = ((bf16[16,2,128,128]{3,2,1,0:T(8,128)(2,1)}), bf16[16,2,128,128]{3,2,1,0:T(8,128)(2,1)S(1)}, u32[]{:S(2)}, u32[]{:S(2)}) async-start(bf16[16,2,128,128]{3,2,1,0:T(8,128)(2,1)} %broadcast_in_dim.2), calls=%async_computation | async-start | bytes 2097152 | tf_op jit(solution)/shard_map/all_to_all | solution.py:239
  31.8 12.2 %collective-permute-start.2 = (bf16[3,256,256]{2,1,0:T(8,128)(2,1)S(1)}, bf16[3,256,256]{2,1,0:T(8,128)(2,1)S(1)}, u32[]{:S(2)}, u32[]{:S(2)}) collective-permute-start(bf16[3,256,256]{2,1,0:T(8,128)(2,1)S(1)} %multiply_convert_fusion.refs_0_), channel_id=1, source_target_pairs={{0,64},{64,0},{1,65},{65,1},{2,66},{66,2},{3,67},{67,3},{4,68},{68... | collective-permute-start | bytes 1179656 | tf_op jit(solution)/shard_map/ppermute | solution.py:250
  34.9 15.3 %collective-permute-start.3 = (bf16[3,256,256]{2,1,0:T(8,128)(2,1)S(1)}, bf16[3,256,256]{2,1,0:T(8,128)(2,1)S(1)}, u32[]{:S(2)}, u32[]{:S(2)}) collective-permute-start(bf16[3,256,256]{2,1,0:T(8,128)(2,1)S(1)} %collective-permute-done.1.refs_1_), channel_id=1, source_target_pairs={{0,64},{64,0},{1,65},{65,1},{2,66},{66,2},{3,67},{67,3},{4,68},{68... | collective-permute-start | bytes 1179656 | tf_op jit(solution)/shard_map/ppermute | solution.py:250
  37.1 18.5 %collective-permute-start.4 = (bf16[3,256,256]{2,1,0:T(8,128)(2,1)S(1)}, bf16[3,256,256]{2,1,0:T(8,128)(2,1)S(1)}, u32[]{:S(2)}, u32[]{:S(2)}) collective-permute-start(bf16[3,256,256]{2,1,0:T(8,128)(2,1)S(1)} %multiply_convert_fusion.refs_0_), channel_id=1, source_target_pairs={{0,32},{32,0},{1,33},{33,1},{2,34},{34,2},{3,35},{35,3},{4,36},{36... | collective-permute-start | bytes 1179656 | tf_op jit(solution)/shard_map/ppermute | solution.py:251
  42.1 13.5 %collective-permute-start.5 = (bf16[3,256,256]{2,1,0:T(8,128)(2,1)S(1)}, bf16[3,256,256]{2,1,0:T(8,128)(2,1)S(1)}, u32[]{:S(2)}, u32[]{:S(2)}) collective-permute-start(bf16[3,256,256]{2,1,0:T(8,128)(2,1)S(1)} %collective-permute-done.1.refs_1_), channel_id=1, source_target_pairs={{0,32},{32,0},{1,33},{33,1},{2,34},{34,2},{3,35},{35,3},{4,36},{36... | collective-permute-start | bytes 1179656 | tf_op jit(solution)/shard_map/ppermute | solution.py:251
  44.0 11.6 %collective-permute-start.6 = (bf16[3,256,256]{2,1,0:T(8,128)(2,1)S(1)}, bf16[3,256,256]{2,1,0:T(8,128)(2,1)}, u32[]{:S(2)}, u32[]{:S(2)}) collective-permute-start(bf16[3,256,256]{2,1,0:T(8,128)(2,1)S(1)} %collective-permute-done.2.refs_2_), channel_id=1, source_target_pairs={{0,32},{32,0},{1,33},{33,1},{2,34},{34,2},{3,35},{35,3},{4,36},{36... | collective-permute-start | bytes 1179656 | tf_op jit(solution)/shard_map/ppermute | solution.py:251
  50.2 6.8 %collective-permute-start.7 = (bf16[3,256,256]{2,1,0:T(8,128)(2,1)S(1)}, bf16[3,256,256]{2,1,0:T(8,128)(2,1)}, u32[]{:S(2)}, u32[]{:S(2)}) collective-permute-start(bf16[3,256,256]{2,1,0:T(8,128)(2,1)S(1)} %collective-permute-done.3.refs_3_), channel_id=1, source_target_pairs={{0,32},{32,0},{1,33},{33,1},{2,34},{34,2},{3,35},{35,3},{4,36},{36... | collective-permute-start | bytes 1179656 | tf_op jit(solution)/shard_map/ppermute | solution.py:251
  55.6 7.7 %copy-start = (bf16[3,256,256]{2,1,0:T(8,128)(2,1)}, bf16[3,256,256]{2,1,0:T(8,128)(2,1)S(1)}, u32[]{:S(2)}) copy-start(bf16[3,256,256]{2,1,0:T(8,128)(2,1)S(1)} %collective-permute-done.4.refs_4_) | copy-start | bytes 1179652
  55.6 7.7 %copy-start.2 = (bf16[3,256,256]{2,1,0:T(8,128)(2,1)}, bf16[3,256,256]{2,1,0:T(8,128)(2,1)S(1)}, u32[]{:S(2)}) copy-start(bf16[3,256,256]{2,1,0:T(8,128)(2,1)S(1)} %collective-permute-done.5.refs_5_) | copy-start | bytes 1179652
  63.3 18.3 %all-to-all-start.1 = ((bf16[4,64,1536]{2,1,0:T(8,128)(2,1)}), bf16[4,64,1536]{2,1,0:T(8,128)(2,1)S(1)}, u32[]{:S(2)}, u32[]{:S(2)}) async-start(bf16[4,64,1536]{2,1,0:T(8,128)(2,1)} %bitcast.5), calls=%async_computation.1 | async-start | bytes 1572864 | tf_op jit(solution)/shard_map/all_to_all | solution.py:239
  71.7 6.4 %collective-permute-start.8 = (bf16[2,4,2,128,128]{4,3,2,1,0:T(8,128)(2,1)S(1)}, bf16[2,4,2,128,128]{4,3,2,1,0:T(8,128)(2,1)S(1)}, u32[]{:S(2)}, u32[]{:S(2)}) collective-permute-start(bf16[2,4,2,128,128]{4,3,2,1,0:T(8,128)(2,1)S(1)} %dynamic-slice_bitcast_fusion), channel_id=1, source_target_pairs={{0,32},{32,0},{1,33},{33,1},{2,34},{34,2},{3,35},{35,3},{4,36},{36... | collective-permute-start | bytes 1572872 | tf_op jit(solution)/shard_map/ppermute | solution.py:257
  78.0 0.8 copy-start.4
  81.8 19.6 %copy-start.1 = (bf16[3,256,256]{2,1,0:T(8,128)(2,1)S(1)}, bf16[3,256,256]{2,1,0:T(8,128)(2,1)}, u32[]{:S(2)}) copy-start(bf16[3,256,256]{2,1,0:T(8,128)(2,1)} %copy-done) | copy-start | bytes 1179652
  81.8 19.6 %copy-start.3 = (bf16[3,256,256]{2,1,0:T(8,128)(2,1)S(1)}, bf16[3,256,256]{2,1,0:T(8,128)(2,1)}, u32[]{:S(2)}) copy-start(bf16[3,256,256]{2,1,0:T(8,128)(2,1)} %copy-done.2) | copy-start | bytes 1179652
  95.8 17.6 %collective-permute-start.10 = (bf16[256,1536]{1,0:T(8,128)(2,1)S(1)}, bf16[256,1536]{1,0:T(8,128)(2,1)}, u32[]{:S(2)}, u32[]{:S(2)}) collective-permute-start(bf16[256,1536]{1,0:T(8,128)(2,1)S(1)} %bitcast.15), channel_id=1, source_target_pairs={{0,32},{32,0},{1,33},{33,1},{2,34},{34,2},{3,35},{35,3},{4,36},{36... | collective-permute-start | bytes 2359304 | tf_op jit(solution)/shard_map/ppermute | solution.py:261
  104.8 8.7 %copy-start.5 = (bf16[2,4,2,128,128]{4,3,2,1,0:T(8,128)(2,1)S(1)}, bf16[2,4,2,128,128]{4,3,2,1,0:T(8,128)(2,1)}, u32[]{:S(2)}) copy-start(bf16[2,4,2,128,128]{4,3,2,1,0:T(8,128)(2,1)} %copy-done.4) | copy-start | bytes 1572868
  104.8 27.3 %all-to-all-start.3 = ((bf16[16,128,128]{2,1,0:T(8,128)(2,1)}), bf16[16,128,128]{2,1,0:T(8,128)(2,1)}, u32[]{:S(2)}, u32[]{:S(2)}) async-start(bf16[16,128,128]{2,1,0:T(8,128)(2,1)} %input_terms.1), calls=%async_computation.3 | async-start | bytes 1048576 | tf_op jit(solution)/shard_map/all_to_all | solution.py:239
  116.8 22.3 %collective-permute-start.11 = (bf16[3,256,256]{2,1,0:T(8,128)(2,1)}, bf16[3,256,256]{2,1,0:T(8,128)(2,1)S(1)}, u32[]{:S(2)}, u32[]{:S(2)}) collective-permute-start(bf16[3,256,256]{2,1,0:T(8,128)(2,1)} %get-tuple-element.15), channel_id=1, source_target_pairs={{0,1},{1,0},{2,3},{3,2},{4,5},{5,4},{6,7},{7,6},{8,9},{9,8},{10,11... | collective-permute-start | bytes 1179656 | tf_op jit(solution)/shard_map/ppermute | solution.py:268
  121.4 17.7 %collective-permute-start.12 = (bf16[3,256,256]{2,1,0:T(8,128)(2,1)}, bf16[3,256,256]{2,1,0:T(8,128)(2,1)S(1)}, u32[]{:S(2)}, u32[]{:S(2)}) collective-permute-start(bf16[3,256,256]{2,1,0:T(8,128)(2,1)} %get-tuple-element.16), channel_id=1, source_target_pairs={{0,64},{64,0},{1,65},{65,1},{2,66},{66,2},{3,67},{67,3},{4,68},{68... | collective-permute-start | bytes 1179656 | tf_op jit(solution)/shard_map/ppermute | solution.py:269
  124.3 23.6 %collective-permute-start.13 = (bf16[3,256,256]{2,1,0:T(8,128)(2,1)}, bf16[3,256,256]{2,1,0:T(8,128)(2,1)S(1)}, u32[]{:S(2)}, u32[]{:S(2)}) collective-permute-start(bf16[3,256,256]{2,1,0:T(8,128)(2,1)} %get-tuple-element.17), channel_id=1, source_target_pairs={{0,65},{1,64},{64,1},{65,0},{2,67},{3,66},{66,3},{67,2},{4,69},{5,... | collective-permute-start | bytes 1179656 | tf_op jit(solution)/shard_map/ppermute | solution.py:270
  133.2 0.7 collective-permute-start.9

commit v14 on v12

--- a/solution.py
+++ b/solution.py
@@ -12,8 +12,7 @@
 ROW = ("yl", "x1", "x0", "core")
 COL = ("yh1", "yh0", "zh1", "zh0", "zl")
 AXES = ROW + COL
-YH = ("yh1", "yh0")
-ZH = ("zh1", "zh0")
+SPREAD = ("zh1", "zh0", "yh0")
 REST = ("yl", "x1")
 SWAP = [(0, 1), (1, 0)]
 TOK = 128
@@ -28,11 +27,11 @@
 SCALARS = pl.BlockSpec(memory_space=pltpu.SMEM)
 
 
-def turned():
+def turned(flip):
     pairs = []
     for bits in itertools.product(range(2), repeat=len(AXES)):
         yl, x1, x0, core, yh1, yh0, zh1, zh0, zl = bits
-        there = (yh1, yh0, x0, core, yl, zl, zh1, zh0, x1)
+        there = (yh1, yh0, x0, core, yl ^ flip, zl, zh1, zh0, x1)
         pairs.append(tuple(sum(b << (8 - i) for i, b in enumerate(at)) for at in (bits, there)))
     return pairs
 
@@ -45,11 +44,11 @@
     return pltpu.CompilerParams(vmem_limit_bytes=VMEM_LIMIT)
 
 
-def chunk(place_ref, t, f):
+def chunk(place_ref, f):
     core, x0 = place_ref[0], place_ref[1]
     core = core if f < 4 else 1 - core
     x0 = x0 if f % 4 < 2 else 1 - x0
-    return 8 * x0 + 4 * core + 2 * t + f % 2
+    return 4 * x0 + 2 * core + f % 2
 
 
 def gates_kernel(place_ref, acts_ref, *refs):
@@ -57,7 +56,7 @@
     for p in range(2):
         for t in range(2):
             for f in range(8):
-                block = acts_ref[chunk(place_ref, t, f), p]
+                block = acts_ref[chunk(place_ref, f), t, p]
                 wide_ref[p, pl.ds(t * TOK, TOK), pl.ds(f * TOK, TOK)] = block
     for p in range(3):
         for j in range(2):
@@ -119,13 +118,13 @@
         for t in range(2):
             for f in range(2):
                 part = dx[t * TOK : (t + 1) * TOK, f * TOK : (f + 1) * TOK]
-                dx_ref[chunk(place_ref, t, 2 * s + f)] = part
+                dx_ref[chunk(place_ref, 2 * s + f), t] = part
 
 
 def input_terms(place, grads, *weights):
     return pl.pallas_call(
         input_kernel,
-        out_shape=jax.ShapeDtypeStruct((16, TOK, TOK), BF16),
+        out_shape=jax.ShapeDtypeStruct((8, 2, TOK, TOK), BF16),
         in_specs=[SCALARS] + [WHOLE] * 9,
         out_specs=WHOLE,
         compiler_params=params(),
@@ -142,9 +141,9 @@
             for f in range(4):
                 x0 = place_ref[1] if f < 2 else 1 - place_ref[1]
                 cols = pl.ds(f * TOK, TOK)
-                mine = acts_ref[chunk(place_ref, t, f), p]
+                mine = acts_ref[chunk(place_ref, f), t, p]
                 wide_ref[p, pl.ds(t * TOK, TOK), cols] = mine
-                wide_ref[p, pl.ds(TOKENS + t * TOK, TOK), cols] = other_acts_ref[x0, 2 * t + f % 2, p]
+                wide_ref[p, pl.ds(TOKENS + t * TOK, TOK), cols] = other_acts_ref[x0, f % 2, t, p]
     for side in (1, 0):
         for p in range(3):
             for j in range(2):
@@ -178,18 +177,19 @@
 
 def local(inputs, out_grad, codes, scales):
     place = jnp.stack([lax.axis_index("core"), lax.axis_index("x0")])
-    there = turned()
-
-    acts = lax.ppermute(jnp.stack([inputs, out_grad]), AXES, there)
+    there = [turned(flip) for flip in range(2)]
+
+    acts = jnp.stack([inputs, out_grad])
+    acts = jnp.stack([lax.ppermute(acts, AXES, pairs) for pairs in there])
     w = (codes.astype(F32) * scales.astype(F32)).astype(BF16)
     w_z = lax.ppermute(w, "zl", SWAP)
     acts, w_z = lax.optimization_barrier((acts, w_z))
     weights = [w, w_z] + [lax.ppermute(block, "x0", SWAP) for block in (w, w_z)]
     weights += [lax.ppermute(block, "core", SWAP) for block in weights]
-    acts = exchange(jnp.broadcast_to(acts[None], (16,) + acts.shape), ZH + YH)
+    acts = exchange(jnp.broadcast_to(acts[None], (8,) + acts.shape), SPREAD)
 
     parts = gates(place, acts, *weights)
-    other_acts = acts.reshape(2, 2, 4, 2, TOK, TOK)
+    other_acts = acts.reshape(2, 2, 2, 2, 2, TOK, TOK)
     other_acts = lax.dynamic_index_in_dim(other_acts, 1 - place[0], axis=1, keepdims=False)
     other_acts = lax.ppermute(other_acts, "core", SWAP)
     parts = exchange(parts.reshape(4, SHARE, GRADS), REST)
@@ -197,9 +197,10 @@
     grads = exchange(hidden_grads(parts), REST).reshape(TOKENS, GRADS)
     other_grads = lax.ppermute(grads, "core", SWAP)
 
-    dx = exchange(input_terms(place, grads, *weights), ZH + YH)
+    dx = exchange(input_terms(place, grads, *weights), SPREAD)
     dx = jnp.sum(dx.astype(F32), axis=0).astype(BF16)
-    input_grad = lax.ppermute(dx, AXES, [(b, a) for a, b in there])
+    back = [lax.ppermute(dx[i], AXES, [(b, a) for a, b in there[i]]) for i in range(2)]
+    input_grad = (back[0].astype(F32) + back[1].astype(F32)).astype(BF16)
 
     weight_grad, z, x, xz = weight_terms(place, acts, other_acts, grads, other_grads)
     weight_grad += lax.ppermute(z, "zl", SWAP).astype(F32)

time: 149 us -> 150 us (level)
  the two profiles are of different devices: /device:TPU:1 before, /device:TPU:4 now
where the time goes in v14:
time: 150 us; the launch traced here: 149 us
  starting transfers between devices  76 us (51%)
  waiting for transfers between devices  42 us (28%)
  blocking collectives  15 us (10%)
  Pallas kernels  8.22 us (5%)
  other arithmetic  4.64 us (3%)
  local copies, waits for them, and re-layouts  2.11 us (1%)
    all_to_all x3, starting transfers between devices, exchange(): return lax.all_to_all(pieces, axes, split_axis=0, concat_axis=0, tiled=True)  26.2 us
    all_to_all x1, blocking collectives, exchange(): return lax.all_to_all(pieces, axes, split_axis=0, concat_axis=0, tiled=True)  15 us
    all_to_all x3, waiting for transfers between devices, exchange(): return lax.all_to_all(pieces, axes, split_axis=0, concat_axis=0, tiled=True)  12.4 us
    ppermute x2, starting transfers between devices, local(): acts = jnp.stack([lax.ppermute(acts, AXES, pairs) for pairs in there])  9.48 us
    ppermute x2, waiting for transfers between devices, local(): lax.ppermute(dx[i], AXES, [(b, a) for a, b in there[i]])  9.23 us
    ppermute x2, starting transfers between devices, local(): lax.ppermute(dx[i], AXES, [(b, a) for a, b in there[i]])  8.9 us
    ppermute x4, starting transfers between devices, local(): weights += [lax.ppermute(block, 'core', SWAP) for block in weights]  8.15 us
    ppermute x2, waiting for transfers between devices, local(): weights = [w, w_z] + [lax.ppermute(block, 'x0', SWAP) for block in (w, w_z)]  7.35 us
  transfers between devices with their start and end apart: 19, of which 12 were waited for; matrix products, arithmetic and copies ran while one was open for 1% of the time, Pallas kernels for 2%

profile of v14, /device:TPU:4, one launch (start us, length us, event | category | flops | bytes accessed | tf_op | source)
XLA Modules:
  0.0 148.9 jit_solution(3778090737560423150)
XLA Ops:
  0.6 0.7 bitcast_convert_fusion
  1.3 0.0 copy-start.6
  1.3 0.0 copy-start.7
  1.3 1.1 multiply_convert_fusion.refs_0_
  2.4 4.3 %collective-permute-start.2 = (bf16[3,256,256]{2,1,0:T(8,128)(2,1)S(1)}, bf16[3,256,256]{2,1,0:T(8,128)(2,1)S(1)}, u32[]{:S(2)}, u32[]{:S(2)}) collective-permute-start(bf16[3,256,256]{2,1,0:T(8,128)(2,1)S(1)} %multiply_convert_fusion.refs_0_), channel_id=1, source_target_pairs={{0,1},{1,0},{2,3},{3,2},{4,5},{5,4},{6,7},{7,6},{8,9},{9,8},{10,11... | collective-permute-start | bytes 1179656 | tf_op jit(solution)/shard_map/ppermute | solution.py:185
  6.7 0.0 copy-done.6
  6.7 0.0 copy-done.7
  6.7 7.1 %collective-permute-start.1 = (bf16[2,128,128]{2,1,0:T(8,128)(2,1)S(1)}, bf16[2,128,128]{2,1,0:T(8,128)(2,1)S(1)}, u32[]{:S(2)}, u32[]{:S(2)}) collective-permute-start(bf16[2,128,128]{2,1,0:T(8,128)(2,1)S(1)} %pad_maximum_fusion.1), channel_id=1, source_target_pairs={{0,16},{1,24},{2,18},{3,26},{4,20},{5,28},{6,22},{7,30},{8,144},{9... | collective-permute-start | bytes 196616 | tf_op jit(solution)/shard_map/ppermute | solution.py:183
  13.9 2.4 %collective-permute-start = (bf16[2,128,128]{2,1,0:T(8,128)(2,1)S(1)}, bf16[2,128,128]{2,1,0:T(8,128)(2,1)S(1)}, u32[]{:S(2)}, u32[]{:S(2)}) collective-permute-start(bf16[2,128,128]{2,1,0:T(8,128)(2,1)S(1)} %pad_maximum_fusion.1), channel_id=1, source_target_pairs={{0,0},{1,8},{2,2},{3,10},{4,4},{5,12},{6,6},{7,14},{8,128},{9,136}... | collective-permute-start | bytes 196616 | tf_op jit(solution)/shard_map/ppermute | solution.py:183
  16.2 0.9 collective-permute-done.1
  17.1 6.2 %collective-permute-done = bf16[2,128,128]{2,1,0:T(8,128)(2,1)S(1)} collective-permute-done((bf16[2,128,128]{2,1,0:T(8,128)(2,1)S(1)}, bf16[2,128,128]{2,1,0:T(8,128)(2,1)S(1)}, u32[]{:S(2)}, u32[]{:S(2)}) %collective-permute-start) | collective-permute-done | bytes 65568 | tf_op jit(solution)/shard_map/ppermute | solution.py:183
  23.3 0.0 collective-permute-done.2.refs_1_
  23.3 1.2 broadcast_in_dim.2
  24.6 9.9 %all-to-all-start = ((bf16[8,2,2,128,128]{4,3,2,1,0:T(8,128)(2,1)}), bf16[8,2,2,128,128]{4,3,2,1,0:T(8,128)(2,1)S(1)}, u32[]{:S(2)}, u32[]{:S(2)}) async-start(bf16[8,2,2,128,128]{4,3,2,1,0:T(8,128)(2,1)} %broadcast_in_dim.2), calls=%async_computation | async-start | bytes 2097152 | tf_op jit(solution)/shard_map/all_to_all | solution.py:175
  34.5 4.0 %collective-permute-start.3 = (bf16[3,256,256]{2,1,0:T(8,128)(2,1)S(1)}, bf16[3,256,256]{2,1,0:T(8,128)(2,1)S(1)}, u32[]{:S(2)}, u32[]{:S(2)}) collective-permute-start(bf16[3,256,256]{2,1,0:T(8,128)(2,1)S(1)} %multiply_convert_fusion.refs_0_), channel_id=1, source_target_pairs={{0,64},{64,0},{1,65},{65,1},{2,66},{66,2},{3,67},{67,3},{4,68},{68... | collective-permute-start | bytes 1179656 | tf_op jit(solution)/shard_map/ppermute | solution.py:187
  38.5 1.9 %collective-permute-start.4 = (bf16[3,256,256]{2,1,0:T(8,128)(2,1)S(1)}, bf16[3,256,256]{2,1,0:T(8,128)(2,1)S(1)}, u32[]{:S(2)}, u32[]{:S(2)}) collective-permute-start(bf16[3,256,256]{2,1,0:T(8,128)(2,1)S(1)} %collective-permute-done.2.refs_1_), channel_id=1, source_target_pairs={{0,64},{64,0},{1,65},{65,1},{2,66},{66,2},{3,67},{67,3},{4,68},{68... | collective-permute-start | bytes 1179656 | tf_op jit(solution)/shard_map/ppermute | solution.py:187
  40.4 1.9 %collective-permute-start.5 = (bf16[3,256,256]{2,1,0:T(8,128)(2,1)S(1)}, bf16[3,256,256]{2,1,0:T(8,128)(2,1)S(1)}, u32[]{:S(2)}, u32[]{:S(2)}) collective-permute-start(bf16[3,256,256]{2,1,0:T(8,128)(2,1)S(1)} %multiply_convert_fusion.refs_0_), channel_id=1, source_target_pairs={{0,32},{32,0},{1,33},{33,1},{2,34},{34,2},{3,35},{35,3},{4,36},{36... | collective-permute-start | bytes 1179656 | tf_op jit(solution)/shard_map/ppermute | solution.py:188
  42.4 2.4 %collective-permute-start.6 = (bf16[3,256,256]{2,1,0:T(8,128)(2,1)S(1)}, bf16[3,256,256]{2,1,0:T(8,128)(2,1)S(1)}, u32[]{:S(2)}, u32[]{:S(2)}) collective-permute-start(bf16[3,256,256]{2,1,0:T(8,128)(2,1)S(1)} %collective-permute-done.2.refs_1_), channel_id=1, source_target_pairs={{0,32},{32,0},{1,33},{33,1},{2,34},{34,2},{3,35},{35,3},{4,36},{36... | collective-permute-start | bytes 1179656 | tf_op jit(solution)/shard_map/ppermute | solution.py:188
  44.8 3.7 %collective-permute-done.3.refs_2_ = bf16[3,256,256]{2,1,0:T(8,128)(2,1)S(1)} collective-permute-done((bf16[3,256,256]{2,1,0:T(8,128)(2,1)S(1)}, bf16[3,256,256]{2,1,0:T(8,128)(2,1)S(1)}, u32[]{:S(2)}, u32[]{:S(2)}) %collective-permute-start.3) | collective-permute-done | bytes 393248 | tf_op jit(solution)/shard_map/ppermute | solution.py:187
  48.5 1.9 %collective-permute-start.7 = (bf16[3,256,256]{2,1,0:T(8,128)(2,1)S(1)}, bf16[3,256,256]{2,1,0:T(8,128)(2,1)}, u32[]{:S(2)}, u32[]{:S(2)}) collective-permute-start(bf16[3,256,256]{2,1,0:T(8,128)(2,1)S(1)} %collective-permute-done.3.refs_2_), channel_id=1, source_target_pairs={{0,32},{32,0},{1,33},{33,1},{2,34},{34,2},{3,35},{35,3},{4,36},{36... | collective-permute-start | bytes 1179656 | tf_op jit(solution)/shard_map/ppermute | solution.py:188
  50.5 3.6 %collective-permute-done.4.refs_3_ = bf16[3,256,256]{2,1,0:T(8,128)(2,1)S(1)} collective-permute-done((bf16[3,256,256]{2,1,0:T(8,128)(2,1)S(1)}, bf16[3,256,256]{2,1,0:T(8,128)(2,1)S(1)}, u32[]{:S(2)}, u32[]{:S(2)}) %collective-permute-start.4) | collective-permute-done | bytes 393248 | tf_op jit(solution)/shard_map/ppermute | solution.py:187
  54.1 1.9 %collective-permute-start.8 = (bf16[3,256,256]{2,1,0:T(8,128)(2,1)S(1)}, bf16[3,256,256]{2,1,0:T(8,128)(2,1)}, u32[]{:S(2)}, u32[]{:S(2)}) collective-permute-start(bf16[3,256,256]{2,1,0:T(8,128)(2,1)S(1)} %collective-permute-done.4.refs_3_), channel_id=1, source_target_pairs={{0,32},{32,0},{1,33},{33,1},{2,34},{34,2},{3,35},{35,3},{4,36},{36... | collective-permute-start | bytes 1179656 | tf_op jit(solution)/shard_map/ppermute | solution.py:188
  56.0 0.1 pad_add_fusion.place_ref
  56.1 0.0 collective-permute-done.5.refs_4_
  56.1 0.0 copy-start
  56.1 0.0 collective-permute-done.7.refs_6_
  56.1 0.0 collective-permute-done.6.refs_5_
  56.1 0.0 copy-start.2
  56.1 1.7 %collective-permute-done.8.refs_7_ = bf16[3,256,256]{2,1,0:T(8,128)(2,1)} collective-permute-done((bf16[3,256,256]{2,1,0:T(8,128)(2,1)S(1)}, bf16[3,256,256]{2,1,0:T(8,128)(2,1)}, u32[]{:S(2)}, u32[]{:S(2)}) %collective-permute-start.8) | collective-permute-done | bytes 393248 | tf_op jit(solution)/shard_map/ppermute | solution.py:188
  57.8 5.9 %all-to-all-done.acts_ref = bf16[8,2,2,128,128]{4,3,2,1,0:T(8,128)(2,1)S(1)} async-done(((bf16[8,2,2,128,128]{4,3,2,1,0:T(8,128)(2,1)}), bf16[8,2,2,128,128]{4,3,2,1,0:T(8,128)(2,1)S(1)}, u32[]{:S(2)}, u32[]{:S(2)}) %all-to-all-start) | async-done | bytes 1048608 | tf_op jit(solution)/shard_map/all_to_all | solution.py:175
  63.7 3.0 %gates.1 = bf16[256,1536]{1,0:T(8,128)(2,1)} custom-call(s32[2]{0:T(128)S(1)} %pad_add_fusion.place_ref, bf16[8,2,2,128,128]{4,3,2,1,0:T(8,128)(2,1)S(1)} %all-to-all-done.acts_ref, bf16[3,256,256]{2,1,0:T(8,128)(2,1)S(1)} %multiply_convert_fusion.refs_0_, bf16[3,256,256]{2,1,0:T(8,128)(2,1)S(1)} %collective-permute-done.2.refs_1_, ...), custom_call_target="tpu_custom_call" | custom-call | flops 800000000 | bytes 6000000 | tf_op jit(solution)/shard_map/gates/pallas_call | solution.py:70
  66.7 0.0 copy-done
  66.7 0.0 copy-done.2
  66.7 7.5 %all-to-all-start.1 = ((bf16[4,64,1536]{2,1,0:T(8,128)(2,1)}), bf16[4,64,1536]{2,1,0:T(8,128)(2,1)S(1)}, u32[]{:S(2)}, u32[]{:S(2)}) async-start(bf16[4,64,1536]{2,1,0:T(8,128)(2,1)} %bitcast.7), calls=%async_computation.1 | async-start | bytes 1572864 | tf_op jit(solution)/shard_map/all_to_all | solution.py:175
  74.2 1.9 %collective-permute-start.9 = (bf16[2,2,2,2,128,128]{5,4,3,2,1,0:T(8,128)(2,1)S(1)}, bf16[2,2,2,2,128,128]{5,4,3,2,1,0:T(8,128)(2,1)S(1)}, u32[]{:S(2)}, u32[]{:S(2)}) collective-permute-start(bf16[2,2,2,2,128,128]{5,4,3,2,1,0:T(8,128)(2,1)S(1)} %dynamic-slice_bitcast_fusion), channel_id=1, source_target_pairs={{0,32},{32,0},{1,33},{33,1},{2,34},{34,2},{3,35},{35,3},{4,36},{36... | collective-permute-start | bytes 1572872 | tf_op jit(solution)/shard_map/ppermute | solution.py:194
  76.2 1.9 %collective-permute-done.9.other_acts_ref = bf16[2,2,2,2,128,128]{5,4,3,2,1,0:T(8,128)(2,1)S(1)} collective-permute-done((bf16[2,2,2,2,128,128]{5,4,3,2,1,0:T(8,128)(2,1)S(1)}, bf16[2,2,2,2,128,128]{5,4,3,2,1,0:T(8,128)(2,1)S(1)}, u32[]{:S(2)}, u32[]{:S(2)}) %collective-permute-start.9) | collective-permute-done | bytes 524320 | tf_op jit(solution)/shard_map/ppermute | solution.py:194
  78.1 0.8 copy-done.4
  78.9 4.8 %all-to-all-done.1.parts_ref = bf16[4,64,1536]{2,1,0:T(8,128)(2,1)S(1)} async-done(((bf16[4,64,1536]{2,1,0:T(8,128)(2,1)}), bf16[4,64,1536]{2,1,0:T(8,128)(2,1)S(1)}, u32[]{:S(2)}, u32[]{:S(2)}) %all-to-all-start.1) | async-done | bytes 786464 | tf_op jit(solution)/shard_map/all_to_all | solution.py:175
  83.6 0.2 hidden_grads.1
  83.8 0.0 copy-start.1
  83.8 0.0 copy-start.3
  83.8 15.0 %all_to_all.20 = bf16[4,64,1536]{2,1,0:T(8,128)(2,1)S(1)} all-to-all(bf16[4,64,1536]{2,1,0:T(8,128)(2,1)S(1)} %hidden_grads.1), channel_id=1, replica_groups=mesh['yl'=2,'x1'=2,'x0'=2,'core'=2,'yh1'=2,'yh0'=2,'zh1'=2,'zh0'=2,'zl'=..., dimensions={0} | all-to-all | bytes 1572864 | tf_op jit(solution)/shard_map/all_to_all | solution.py:175
  98.9 0.0 copy-done.1
  98.9 0.0 copy-done.3
  98.9 2.7 %input_terms.1 = bf16[8,2,128,128]{3,2,1,0:T(8,128)(2,1)} custom-call(s32[2]{0:T(128)S(1)} %pad_add_fusion.place_ref, bf16[256,1536]{1,0:T(8,128)(2,1)S(1)} %bitcast.21, bf16[3,256,256]{2,1,0:T(8,128)(2,1)S(1)} %multiply_convert_fusion.refs_0_, bf16[3,256,256]{2,1,0:T(8,128)(2,1)S(1)} %collective-permute-done.2.refs_1_, ...), custom_call_target="tpu_custom_call" | custom-call | flops 540000000 | bytes 4000000 | tf_op jit(solution)/shard_map/input_terms/pallas_call | solution.py:125
  101.6 8.7 %all-to-all-start.3 = ((bf16[8,2,128,128]{3,2,1,0:T(8,128)(2,1)}), bf16[8,2,128,128]{3,2,1,0:T(8,128)(2,1)}, u32[]{:S(2)}, u32[]{:S(2)}) async-start(bf16[8,2,128,128]{3,2,1,0:T(8,128)(2,1)} %input_terms.1), calls=%async_computation.3 | async-start | bytes 1048576 | tf_op jit(solution)/shard_map/all_to_all | solution.py:175
  110.3 1.9 %collective-permute-start.12 = (bf16[256,1536]{1,0:T(8,128)(2,1)S(1)}, bf16[256,1536]{1,0:T(8,128)(2,1)S(1)}, u32[]{:S(2)}, u32[]{:S(2)}) collective-permute-start(bf16[256,1536]{1,0:T(8,128)(2,1)S(1)} %bitcast.22), channel_id=1, source_target_pairs={{0,32},{32,0},{1,33},{33,1},{2,34},{34,2},{3,35},{35,3},{4,36},{36... | collective-permute-start | bytes 2359304 | tf_op jit(solution)/shard_map/ppermute | solution.py:198
  112.2 2.3 %collective-permute-done.12.other_grads_ref = bf16[256,1536]{1,0:T(8,128)(2,1)S(1)} collective-permute-done((bf16[256,1536]{1,0:T(8,128)(2,1)S(1)}, bf16[256,1536]{1,0:T(8,128)(2,1)S(1)}, u32[]{:S(2)}, u32[]{:S(2)}) %collective-permute-start.12) | collective-permute-done | bytes 786464 | tf_op jit(solution)/shard_map/ppermute | solution.py:198
  114.5 0.0 copy-done.5
  114.5 2.4 %weight_terms.1 = (f32[3,256,256]{2,1,0:T(8,128)S(1)}, bf16[3,256,256]{2,1,0:T(8,128)(2,1)}, bf16[3,256,256]{2,1,0:T(8,128)(2,1)}, bf16[3,256,256]{2,1,0:T(8,128)(2,1)}) custom-call(s32[2]{0:T(128)S(1)} %pad_add_fusion.place_ref, bf16[8,2,2,128,128]{4,3,2,1,0:T(8,128)(2,1)S(1)} %all-to-all-done.acts_ref, bf16[2,2,2,2,128,128]{5,4,3,2,1,0:T(8,128)(2,1)S(1)} %copy-done.5, ...), custom_call_target="tpu_custom_call" | custom-call | flops 800000000 | bytes 6000000 | tf_op jit(solution)/shard_map/weight_terms/pallas_call | solution.py:162
  116.8 4.0 %collective-permute-start.13 = (bf16[3,256,256]{2,1,0:T(8,128)(2,1)}, bf16[3,256,256]{2,1,0:T(8,128)(2,1)S(1)}, u32[]{:S(2)}, u32[]{:S(2)}) collective-permute-start(bf16[3,256,256]{2,1,0:T(8,128)(2,1)} %get-tuple-element.15), channel_id=1, source_target_pairs={{0,1},{1,0},{2,3},{3,2},{4,5},{5,4},{6,7},{7,6},{8,9},{9,8},{10,11... | collective-permute-start | bytes 1179656 | tf_op jit(solution)/shard_map/ppermute | solution.py:206
  120.8 2.8 %collective-permute-start.14 = (bf16[3,256,256]{2,1,0:T(8,128)(2,1)}, bf16[3,256,256]{2,1,0:T(8,128)(2,1)S(1)}, u32[]{:S(2)}, u32[]{:S(2)}) collective-permute-start(bf16[3,256,256]{2,1,0:T(8,128)(2,1)} %get-tuple-element.16), channel_id=1, source_target_pairs={{0,64},{64,0},{1,65},{65,1},{2,66},{66,2},{3,67},{67,3},{4,68},{68... | collective-permute-start | bytes 1179656 | tf_op jit(solution)/shard_map/ppermute | solution.py:207
  123.6 2.5 %collective-permute-start.15 = (bf16[3,256,256]{2,1,0:T(8,128)(2,1)}, bf16[3,256,256]{2,1,0:T(8,128)(2,1)S(1)}, u32[]{:S(2)}, u32[]{:S(2)}) collective-permute-start(bf16[3,256,256]{2,1,0:T(8,128)(2,1)} %get-tuple-element.17), channel_id=1, source_target_pairs={{0,65},{1,64},{64,1},{65,0},{2,67},{3,66},{66,3},{67,2},{4,69},{5,... | collective-permute-start | bytes 1179656 | tf_op jit(solution)/shard_map/ppermute | solution.py:208
  126.1 1.8 %all-to-all-done.3 = bf16[8,2,128,128]{3,2,1,0:T(8,128)(2,1)} async-done(((bf16[8,2,128,128]{3,2,1,0:T(8,128)(2,1)}), bf16[8,2,128,128]{3,2,1,0:T(8,128)(2,1)}, u32[]{:S(2)}, u32[]{:S(2)}) %all-to-all-start.3) | async-done | bytes 524320 | tf_op jit(solution)/shard_map/all_to_all | solution.py:175
  127.9 1.1 reduce_sum.12
  129.0 5.1 %collective-permute-start.10 = (bf16[128,128]{1,0:T(8,128)(2,1)S(1)}, bf16[128,128]{1,0:T(8,128)(2,1)S(1)}, u32[]{:S(2)}, u32[]{:S(2)}) collective-permute-start(bf16[128,128]{1,0:T(8,128)(2,1)S(1)} %get-tuple-element.18), channel_id=1, source_target_pairs={{0,0},{8,1},{2,2},{10,3},{4,4},{12,5},{6,6},{14,7},{128,8},{136,9}... | collective-permute-start | bytes 98312 | tf_op jit(solution)/shard_map/ppermute | solution.py:202
  134.2 3.8 %collective-permute-start.11 = (bf16[128,128]{1,0:T(8,128)(2,1)S(1)}, bf16[128,128]{1,0:T(8,128)(2,1)S(1)}, u32[]{:S(2)}, u32[]{:S(2)}) collective-permute-start(bf16[128,128]{1,0:T(8,128)(2,1)S(1)} %get-tuple-element.19), channel_id=1, source_target_pairs={{16,0},{24,1},{18,2},{26,3},{20,4},{28,5},{22,6},{30,7},{144,8},{1... | collective-permute-start | bytes 98312 | tf_op jit(solution)/shard_map/ppermute | solution.py:202
  137.9 6.8 %collective-permute-done.10 = bf16[128,128]{1,0:T(8,128)(2,1)S(1)} collective-permute-done((bf16[128,128]{1,0:T(8,128)(2,1)S(1)}, bf16[128,128]{1,0:T(8,128)(2,1)S(1)}, u32[]{:S(2)}, u32[]{:S(2)}) %collective-permute-start.10) | collective-permute-done | bytes 32800 | tf_op jit(solution)/shard_map/ppermute | solution.py:202
  144.8 2.4 %collective-permute-done.11 = bf16[128,128]{1,0:T(8,128)(2,1)S(1)} collective-permute-done((bf16[128,128]{1,0:T(8,128)(2,1)S(1)}, bf16[128,128]{1,0:T(8,128)(2,1)S(1)}, u32[]{:S(2)}, u32[]{:S(2)}) %collective-permute-start.11) | collective-permute-done | bytes 32800 | tf_op jit(solution)/shard_map/ppermute | solution.py:202
  147.2 0.6 add_convert_fusion
  147.8 0.0 collective-permute-done.13
  147.8 0.0 collective-permute-done.14
  147.8 0.0 collective-permute-done.15
  147.8 1.0 convert_add_fusion
  (6 shorter events, 0.1 us)
Async XLA Ops:
  1.3 5.4 %copy-start.6 = (bf16[128,128]{1,0:T(8,128)(2,1)S(1)}, bf16[128,128]{1,0:T(8,128)(2,1)}, u32[]{:S(2)}) copy-start(bf16[128,128]{1,0:T(8,128)(2,1)} %param.5) | copy-start | bytes 98308
  1.3 5.4 %copy-start.7 = (bf16[128,128]{1,0:T(8,128)(2,1)S(1)}, bf16[128,128]{1,0:T(8,128)(2,1)}, u32[]{:S(2)}) copy-start(bf16[128,128]{1,0:T(8,128)(2,1)} %param.4) | copy-start | bytes 98308
  2.4 20.9 %collective-permute-start.2 = (bf16[3,256,256]{2,1,0:T(8,128)(2,1)S(1)}, bf16[3,256,256]{2,1,0:T(8,128)(2,1)S(1)}, u32[]{:S(2)}, u32[]{:S(2)}) collective-permute-start(bf16[3,256,256]{2,1,0:T(8,128)(2,1)S(1)} %multiply_convert_fusion.refs_0_), channel_id=1, source_target_pairs={{0,1},{1,0},{2,3},{3,2},{4,5},{5,4},{6,7},{7,6},{8,9},{9,8},{10,11... | collective-permute-start | bytes 1179656 | tf_op jit(solution)/shard_map/ppermute | solution.py:185
  6.7 10.4 %collective-permute-start.1 = (bf16[2,128,128]{2,1,0:T(8,128)(2,1)S(1)}, bf16[2,128,128]{2,1,0:T(8,128)(2,1)S(1)}, u32[]{:S(2)}, u32[]{:S(2)}) collective-permute-start(bf16[2,128,128]{2,1,0:T(8,128)(2,1)S(1)} %pad_maximum_fusion.1), channel_id=1, source_target_pairs={{0,16},{1,24},{2,18},{3,26},{4,20},{5,28},{6,22},{7,30},{8,144},{9... | collective-permute-start | bytes 196616 | tf_op jit(solution)/shard_map/ppermute | solution.py:183
  13.9 9.5 %collective-permute-start = (bf16[2,128,128]{2,1,0:T(8,128)(2,1)S(1)}, bf16[2,128,128]{2,1,0:T(8,128)(2,1)S(1)}, u32[]{:S(2)}, u32[]{:S(2)}) collective-permute-start(bf16[2,128,128]{2,1,0:T(8,128)(2,1)S(1)} %pad_maximum_fusion.1), channel_id=1, source_target_pairs={{0,0},{1,8},{2,2},{3,10},{4,4},{5,12},{6,6},{7,14},{8,128},{9,136}... | collective-permute-start | bytes 196616 | tf_op jit(solution)/shard_map/ppermute | solution.py:183
  24.6 39.1 %all-to-all-start = ((bf16[8,2,2,128,128]{4,3,2,1,0:T(8,128)(2,1)}), bf16[8,2,2,128,128]{4,3,2,1,0:T(8,128)(2,1)S(1)}, u32[]{:S(2)}, u32[]{:S(2)}) async-start(bf16[8,2,2,128,128]{4,3,2,1,0:T(8,128)(2,1)} %broadcast_in_dim.2), calls=%async_computation | async-start | bytes 2097152 | tf_op jit(solution)/shard_map/all_to_all | solution.py:175
  34.5 14.0 %collective-permute-start.3 = (bf16[3,256,256]{2,1,0:T(8,128)(2,1)S(1)}, bf16[3,256,256]{2,1,0:T(8,128)(2,1)S(1)}, u32[]{:S(2)}, u32[]{:S(2)}) collective-permute-start(bf16[3,256,256]{2,1,0:T(8,128)(2,1)S(1)} %multiply_convert_fusion.refs_0_), channel_id=1, source_target_pairs={{0,64},{64,0},{1,65},{65,1},{2,66},{66,2},{3,67},{67,3},{4,68},{68... | collective-permute-start | bytes 1179656 | tf_op jit(solution)/shard_map/ppermute | solution.py:187
  38.5 15.5 %collective-permute-start.4 = (bf16[3,256,256]{2,1,0:T(8,128)(2,1)S(1)}, bf16[3,256,256]{2,1,0:T(8,128)(2,1)S(1)}, u32[]{:S(2)}, u32[]{:S(2)}) collective-permute-start(bf16[3,256,256]{2,1,0:T(8,128)(2,1)S(1)} %collective-permute-done.2.refs_1_), channel_id=1, source_target_pairs={{0,64},{64,0},{1,65},{65,1},{2,66},{66,2},{3,67},{67,3},{4,68},{68... | collective-permute-start | bytes 1179656 | tf_op jit(solution)/shard_map/ppermute | solution.py:187
  40.4 15.6 %collective-permute-start.5 = (bf16[3,256,256]{2,1,0:T(8,128)(2,1)S(1)}, bf16[3,256,256]{2,1,0:T(8,128)(2,1)S(1)}, u32[]{:S(2)}, u32[]{:S(2)}) collective-permute-start(bf16[3,256,256]{2,1,0:T(8,128)(2,1)S(1)} %multiply_convert_fusion.refs_0_), channel_id=1, source_target_pairs={{0,32},{32,0},{1,33},{33,1},{2,34},{34,2},{3,35},{35,3},{4,36},{36... | collective-permute-start | bytes 1179656 | tf_op jit(solution)/shard_map/ppermute | solution.py:188
  42.4 13.7 %collective-permute-start.6 = (bf16[3,256,256]{2,1,0:T(8,128)(2,1)S(1)}, bf16[3,256,256]{2,1,0:T(8,128)(2,1)S(1)}, u32[]{:S(2)}, u32[]{:S(2)}) collective-permute-start(bf16[3,256,256]{2,1,0:T(8,128)(2,1)S(1)} %collective-permute-done.2.refs_1_), channel_id=1, source_target_pairs={{0,32},{32,0},{1,33},{33,1},{2,34},{34,2},{3,35},{35,3},{4,36},{36... | collective-permute-start | bytes 1179656 | tf_op jit(solution)/shard_map/ppermute | solution.py:188
  48.5 7.5 %collective-permute-start.7 = (bf16[3,256,256]{2,1,0:T(8,128)(2,1)S(1)}, bf16[3,256,256]{2,1,0:T(8,128)(2,1)}, u32[]{:S(2)}, u32[]{:S(2)}) collective-permute-start(bf16[3,256,256]{2,1,0:T(8,128)(2,1)S(1)} %collective-permute-done.3.refs_2_), channel_id=1, source_target_pairs={{0,32},{32,0},{1,33},{33,1},{2,34},{34,2},{3,35},{35,3},{4,36},{36... | collective-permute-start | bytes 1179656 | tf_op jit(solution)/shard_map/ppermute | solution.py:188
  54.1 3.7 %collective-permute-start.8 = (bf16[3,256,256]{2,1,0:T(8,128)(2,1)S(1)}, bf16[3,256,256]{2,1,0:T(8,128)(2,1)}, u32[]{:S(2)}, u32[]{:S(2)}) collective-permute-start(bf16[3,256,256]{2,1,0:T(8,128)(2,1)S(1)} %collective-permute-done.4.refs_3_), channel_id=1, source_target_pairs={{0,32},{32,0},{1,33},{33,1},{2,34},{34,2},{3,35},{35,3},{4,36},{36... | collective-permute-start | bytes 1179656 | tf_op jit(solution)/shard_map/ppermute | solution.py:188
  56.1 10.6 %copy-start = (bf16[3,256,256]{2,1,0:T(8,128)(2,1)}, bf16[3,256,256]{2,1,0:T(8,128)(2,1)S(1)}, u32[]{:S(2)}) copy-start(bf16[3,256,256]{2,1,0:T(8,128)(2,1)S(1)} %collective-permute-done.5.refs_4_) | copy-start | bytes 1179652
  56.1 10.6 %copy-start.2 = (bf16[3,256,256]{2,1,0:T(8,128)(2,1)}, bf16[3,256,256]{2,1,0:T(8,128)(2,1)S(1)}, u32[]{:S(2)}) copy-start(bf16[3,256,256]{2,1,0:T(8,128)(2,1)S(1)} %collective-permute-done.6.refs_5_) | copy-start | bytes 1179652
  66.7 17.0 %all-to-all-start.1 = ((bf16[4,64,1536]{2,1,0:T(8,128)(2,1)}), bf16[4,64,1536]{2,1,0:T(8,128)(2,1)S(1)}, u32[]{:S(2)}, u32[]{:S(2)}) async-start(bf16[4,64,1536]{2,1,0:T(8,128)(2,1)} %bitcast.7), calls=%async_computation.1 | async-start | bytes 1572864 | tf_op jit(solution)/shard_map/all_to_all | solution.py:175
  74.2 3.8 %collective-permute-start.9 = (bf16[2,2,2,2,128,128]{5,4,3,2,1,0:T(8,128)(2,1)S(1)}, bf16[2,2,2,2,128,128]{5,4,3,2,1,0:T(8,128)(2,1)S(1)}, u32[]{:S(2)}, u32[]{:S(2)}) collective-permute-start(bf16[2,2,2,2,128,128]{5,4,3,2,1,0:T(8,128)(2,1)S(1)} %dynamic-slice_bitcast_fusion), channel_id=1, source_target_pairs={{0,32},{32,0},{1,33},{33,1},{2,34},{34,2},{3,35},{35,3},{4,36},{36... | collective-permute-start | bytes 1572872 | tf_op jit(solution)/shard_map/ppermute | solution.py:194
  78.1 0.8 copy-start.4
  83.8 15.1 %copy-start.1 = (bf16[3,256,256]{2,1,0:T(8,128)(2,1)S(1)}, bf16[3,256,256]{2,1,0:T(8,128)(2,1)}, u32[]{:S(2)}) copy-start(bf16[3,256,256]{2,1,0:T(8,128)(2,1)} %copy-done) | copy-start | bytes 1179652
  83.8 15.1 %copy-start.3 = (bf16[3,256,256]{2,1,0:T(8,128)(2,1)S(1)}, bf16[3,256,256]{2,1,0:T(8,128)(2,1)}, u32[]{:S(2)}) copy-start(bf16[3,256,256]{2,1,0:T(8,128)(2,1)} %copy-done.2) | copy-start | bytes 1179652
  101.6 12.9 %copy-start.5 = (bf16[2,2,2,2,128,128]{5,4,3,2,1,0:T(8,128)(2,1)S(1)}, bf16[2,2,2,2,128,128]{5,4,3,2,1,0:T(8,128)(2,1)}, u32[]{:S(2)}) copy-start(bf16[2,2,2,2,128,128]{5,4,3,2,1,0:T(8,128)(2,1)} %copy-done.4) | copy-start | bytes 1572868
  101.6 26.3 %all-to-all-start.3 = ((bf16[8,2,128,128]{3,2,1,0:T(8,128)(2,1)}), bf16[8,2,128,128]{3,2,1,0:T(8,128)(2,1)}, u32[]{:S(2)}, u32[]{:S(2)}) async-start(bf16[8,2,128,128]{3,2,1,0:T(8,128)(2,1)} %input_terms.1), calls=%async_computation.3 | async-start | bytes 1048576 | tf_op jit(solution)/shard_map/all_to_all | solution.py:175
  110.3 4.2 %collective-permute-start.12 = (bf16[256,1536]{1,0:T(8,128)(2,1)S(1)}, bf16[256,1536]{1,0:T(8,128)(2,1)S(1)}, u32[]{:S(2)}, u32[]{:S(2)}) collective-permute-start(bf16[256,1536]{1,0:T(8,128)(2,1)S(1)} %bitcast.22), channel_id=1, source_target_pairs={{0,32},{32,0},{1,33},{33,1},{2,34},{34,2},{3,35},{35,3},{4,36},{36... | collective-permute-start | bytes 2359304 | tf_op jit(solution)/shard_map/ppermute | solution.py:198
  116.8 31.0 %collective-permute-start.13 = (bf16[3,256,256]{2,1,0:T(8,128)(2,1)}, bf16[3,256,256]{2,1,0:T(8,128)(2,1)S(1)}, u32[]{:S(2)}, u32[]{:S(2)}) collective-permute-start(bf16[3,256,256]{2,1,0:T(8,128)(2,1)} %get-tuple-element.15), channel_id=1, source_target_pairs={{0,1},{1,0},{2,3},{3,2},{4,5},{5,4},{6,7},{7,6},{8,9},{9,8},{10,11... | collective-permute-start | bytes 1179656 | tf_op jit(solution)/shard_map/ppermute | solution.py:206
  120.8 27.0 %collective-permute-start.14 = (bf16[3,256,256]{2,1,0:T(8,128)(2,1)}, bf16[3,256,256]{2,1,0:T(8,128)(2,1)S(1)}, u32[]{:S(2)}, u32[]{:S(2)}) collective-permute-start(bf16[3,256,256]{2,1,0:T(8,128)(2,1)} %get-tuple-element.16), channel_id=1, source_target_pairs={{0,64},{64,0},{1,65},{65,1},{2,66},{66,2},{3,67},{67,3},{4,68},{68... | collective-permute-start | bytes 1179656 | tf_op jit(solution)/shard_map/ppermute | solution.py:207
  123.6 24.2 %collective-permute-start.15 = (bf16[3,256,256]{2,1,0:T(8,128)(2,1)}, bf16[3,256,256]{2,1,0:T(8,128)(2,1)S(1)}, u32[]{:S(2)}, u32[]{:S(2)}) collective-permute-start(bf16[3,256,256]{2,1,0:T(8,128)(2,1)} %get-tuple-element.17), channel_id=1, source_target_pairs={{0,65},{1,64},{64,1},{65,0},{2,67},{3,66},{66,3},{67,2},{4,69},{5,... | collective-permute-start | bytes 1179656 | tf_op jit(solution)/shard_map/ppermute | solution.py:208
  129.0 15.7 %collective-permute-start.10 = (bf16[128,128]{1,0:T(8,128)(2,1)S(1)}, bf16[128,128]{1,0:T(8,128)(2,1)S(1)}, u32[]{:S(2)}, u32[]{:S(2)}) collective-permute-start(bf16[128,128]{1,0:T(8,128)(2,1)S(1)} %get-tuple-element.18), channel_id=1, source_target_pairs={{0,0},{8,1},{2,2},{10,3},{4,4},{12,5},{6,6},{14,7},{128,8},{136,9}... | collective-permute-start | bytes 98312 | tf_op jit(solution)/shard_map/ppermute | solution.py:202
  134.2 13.0 %collective-permute-start.11 = (bf16[128,128]{1,0:T(8,128)(2,1)S(1)}, bf16[128,128]{1,0:T(8,128)(2,1)S(1)}, u32[]{:S(2)}, u32[]{:S(2)}) collective-permute-start(bf16[128,128]{1,0:T(8,128)(2,1)S(1)} %get-tuple-element.19), channel_id=1, source_target_pairs={{16,0},{24,1},{18,2},{26,3},{20,4},{28,5},{22,6},{30,7},{144,8},{1... | collective-permute-start | bytes 98312 | tf_op jit(solution)/shard_map/ppermute | solution.py:202

commit v15 on v14

--- a/solution.py
+++ b/solution.py
@@ -13,6 +13,7 @@
 COL = ("yh1", "yh0", "zh1", "zh0", "zl")
 AXES = ROW + COL
 SPREAD = ("zh1", "zh0", "yh0")
+GATHER = SPREAD + ("yh1",)
 REST = ("yl", "x1")
 SWAP = [(0, 1), (1, 0)]
 TOK = 128
@@ -51,12 +52,37 @@
     return 4 * x0 + 2 * core + f % 2
 
 
+def half(place_ref, t):
+    return place_ref[2] if t == 0 else 1 - place_ref[2]
+
+
+def spread_kernel(acts_ref, copies_out, sems):
+    copies = [pltpu.make_async_copy(acts_ref, copies_out.at[i], sems.at[i]) for i in range(16)]
+    for copy in copies:
+        copy.start()
+    for copy in copies:
+        copy.wait()
+
+
+def spread(acts):
+    return pl.pallas_call(
+        spread_kernel,
+        out_shape=jax.ShapeDtypeStruct((16,) + acts.shape, BF16),
+        in_specs=[WHOLE],
+        out_specs=pl.BlockSpec(memory_space=pl.ANY),
+        scratch_shapes=[pltpu.SemaphoreType.DMA((16,))],
+        compiler_params=params(),
+        cost_estimate=pl.CostEstimate(flops=0, bytes_accessed=1100000, transcendentals=0),
+        name="spread",
+    )(acts)
+
+
 def gates_kernel(place_ref, acts_ref, *refs):
     w_refs, parts_ref, wide_ref = refs[:8], refs[8], refs[9]
     for p in range(2):
         for t in range(2):
             for f in range(8):
-                block = acts_ref[chunk(place_ref, f), t, p]
+                block = acts_ref[chunk(place_ref, f), half(place_ref, t), p]
                 wide_ref[p, pl.ds(t * TOK, TOK), pl.ds(f * TOK, TOK)] = block
     for p in range(3):
         for j in range(2):
@@ -141,9 +167,9 @@
             for f in range(4):
                 x0 = place_ref[1] if f < 2 else 1 - place_ref[1]
                 cols = pl.ds(f * TOK, TOK)
-                mine = acts_ref[chunk(place_ref, f), t, p]
+                mine = acts_ref[chunk(place_ref, f), half(place_ref, t), p]
                 wide_ref[p, pl.ds(t * TOK, TOK), cols] = mine
-                wide_ref[p, pl.ds(TOKENS + t * TOK, TOK), cols] = other_acts_ref[x0, f % 2, t, p]
+                wide_ref[p, pl.ds(TOKENS + t * TOK, TOK), cols] = other_acts_ref[x0, f % 2, half(place_ref, t), p]
     for side in (1, 0):
         for p in range(3):
             for j in range(2):
@@ -176,17 +202,16 @@
 
 
 def local(inputs, out_grad, codes, scales):
-    place = jnp.stack([lax.axis_index("core"), lax.axis_index("x0")])
+    place = jnp.stack([lax.axis_index("core"), lax.axis_index("x0"), lax.axis_index("yh1")])
     there = [turned(flip) for flip in range(2)]
 
-    acts = jnp.stack([inputs, out_grad])
-    acts = jnp.stack([lax.ppermute(acts, AXES, pairs) for pairs in there])
+    acts = spread(lax.ppermute(jnp.stack([inputs, out_grad]), AXES, there[0]))
     w = (codes.astype(F32) * scales.astype(F32)).astype(BF16)
     w_z = lax.ppermute(w, "zl", SWAP)
     acts, w_z = lax.optimization_barrier((acts, w_z))
     weights = [w, w_z] + [lax.ppermute(block, "x0", SWAP) for block in (w, w_z)]
     weights += [lax.ppermute(block, "core", SWAP) for block in weights]
-    acts = exchange(jnp.broadcast_to(acts[None], (8,) + acts.shape), SPREAD)
+    acts = exchange(acts, GATHER).reshape(8, 2, 2, TOK, TOK)
 
     parts = gates(place, acts, *weights)
     other_acts = acts.reshape(2, 2, 2, 2, 2, TOK, TOK)

time: 150 us -> 147 us (0.980)
  the two profiles are of different devices: /device:TPU:4 before, /device:TPU:44 now
where the time goes in v15:
time: 147 us; the launch traced here: 146 us
  starting transfers between devices  74 us (50%)
  waiting for transfers between devices  42.6 us (29%)
  blocking collectives  13.4 us (9%)
  Pallas kernels  9.38 us (6%)
  other arithmetic  4.62 us (3%)
    all_to_all x3, starting transfers between devices, exchange(): return lax.all_to_all(pieces, axes, split_axis=0, concat_axis=0, tiled=True)  30.7 us
    all_to_all x1, blocking collectives, exchange(): return lax.all_to_all(pieces, axes, split_axis=0, concat_axis=0, tiled=True)  13.4 us
    ppermute x2, waiting for transfers between devices, local(): lax.ppermute(dx[i], AXES, [(b, a) for a, b in there[i]])  11.1 us
    ppermute x2, starting transfers between devices, local(): lax.ppermute(dx[i], AXES, [(b, a) for a, b in there[i]])  10.1 us
    ppermute x1, waiting for transfers between devices, local(): acts = spread(lax.ppermute(jnp.stack([inputs, out_grad]), AXES, there[0]))  9.19 us
    all_to_all x3, waiting for transfers between devices, exchange(): return lax.all_to_all(pieces, axes, split_axis=0, concat_axis=0, tiled=True)  8.84 us
    ppermute x4, starting transfers between devices, local(): weights += [lax.ppermute(block, 'core', SWAP) for block in weights]  8.15 us
    ppermute x2, waiting for transfers between devices, local(): weights = [w, w_z] + [lax.ppermute(block, 'x0', SWAP) for block in (w, w_z)]  7.62 us
  transfers between devices with their start and end apart: 18, of which 11 were waited for; matrix products, arithmetic and copies ran while one was open for 1% of the time, Pallas kernels for 2%

profile of v15, /device:TPU:44, one launch (start us, length us, event | category | flops | bytes accessed | tf_op | source)
XLA Modules:
  0.0 145.7 jit_solution(18015194753629434434)
XLA Ops:
  0.6 0.7 bitcast_convert_fusion
  1.3 0.0 copy-start.6
  1.3 0.0 copy-start.7
  1.3 1.1 multiply_convert_fusion.refs_0_
  2.4 4.3 %collective-permute-start.1 = (bf16[3,256,256]{2,1,0:T(8,128)(2,1)S(1)}, bf16[3,256,256]{2,1,0:T(8,128)(2,1)S(1)}, u32[]{:S(2)}, u32[]{:S(2)}) collective-permute-start(bf16[3,256,256]{2,1,0:T(8,128)(2,1)S(1)} %multiply_convert_fusion.refs_0_), channel_id=1, source_target_pairs={{0,1},{1,0},{2,3},{3,2},{4,5},{5,4},{6,7},{7,6},{8,9},{9,8},{10,11... | collective-permute-start | bytes 1179656 | tf_op jit(solution)/shard_map/ppermute | solution.py:210
  6.7 0.0 copy-done.6
  6.7 0.0 copy-done.7
  6.7 1.9 %collective-permute-start = (bf16[2,128,128]{2,1,0:T(8,128)(2,1)S(1)}, bf16[2,128,128]{2,1,0:T(8,128)(2,1)S(1)}, u32[]{:S(2)}, u32[]{:S(2)}) collective-permute-start(bf16[2,128,128]{2,1,0:T(8,128)(2,1)S(1)} %pad_maximum_fusion), channel_id=1, source_target_pairs={{0,0},{1,8},{2,2},{3,10},{4,4},{5,12},{6,6},{7,14},{8,128},{9,136}... | collective-permute-start | bytes 196616 | tf_op jit(solution)/shard_map/ppermute | solution.py:208
  8.6 9.2 %collective-permute-done.acts_ref = bf16[2,128,128]{2,1,0:T(8,128)(2,1)S(1)} collective-permute-done((bf16[2,128,128]{2,1,0:T(8,128)(2,1)S(1)}, bf16[2,128,128]{2,1,0:T(8,128)(2,1)S(1)}, u32[]{:S(2)}, u32[]{:S(2)}) %collective-permute-start) | collective-permute-done | bytes 65568 | tf_op jit(solution)/shard_map/ppermute | solution.py:208
  17.8 1.2 spread.1
  19.0 0.0 collective-permute-done.1.refs_1_
  19.0 14.8 %all-to-all-start = ((bf16[16,2,128,128]{3,2,1,0:T(8,128)(2,1)}), bf16[16,2,128,128]{3,2,1,0:T(8,128)(2,1)S(1)}, u32[]{:S(2)}, u32[]{:S(2)}) async-start(bf16[16,2,128,128]{3,2,1,0:T(8,128)(2,1)} %spread.1), calls=%async_computation | async-start | bytes 2097152 | tf_op jit(solution)/shard_map/all_to_all | solution.py:201
  33.8 3.4 %collective-permute-start.2 = (bf16[3,256,256]{2,1,0:T(8,128)(2,1)S(1)}, bf16[3,256,256]{2,1,0:T(8,128)(2,1)S(1)}, u32[]{:S(2)}, u32[]{:S(2)}) collective-permute-start(bf16[3,256,256]{2,1,0:T(8,128)(2,1)S(1)} %multiply_convert_fusion.refs_0_), channel_id=1, source_target_pairs={{0,64},{64,0},{1,65},{65,1},{2,66},{66,2},{3,67},{67,3},{4,68},{68... | collective-permute-start | bytes 1179656 | tf_op jit(solution)/shard_map/ppermute | solution.py:212
  37.2 2.5 %collective-permute-start.3 = (bf16[3,256,256]{2,1,0:T(8,128)(2,1)S(1)}, bf16[3,256,256]{2,1,0:T(8,128)(2,1)S(1)}, u32[]{:S(2)}, u32[]{:S(2)}) collective-permute-start(bf16[3,256,256]{2,1,0:T(8,128)(2,1)S(1)} %collective-permute-done.1.refs_1_), channel_id=1, source_target_pairs={{0,64},{64,0},{1,65},{65,1},{2,66},{66,2},{3,67},{67,3},{4,68},{68... | collective-permute-start | bytes 1179656 | tf_op jit(solution)/shard_map/ppermute | solution.py:212
  39.7 1.9 %collective-permute-start.4 = (bf16[3,256,256]{2,1,0:T(8,128)(2,1)S(1)}, bf16[3,256,256]{2,1,0:T(8,128)(2,1)S(1)}, u32[]{:S(2)}, u32[]{:S(2)}) collective-permute-start(bf16[3,256,256]{2,1,0:T(8,128)(2,1)S(1)} %multiply_convert_fusion.refs_0_), channel_id=1, source_target_pairs={{0,32},{32,0},{1,33},{33,1},{2,34},{34,2},{3,35},{35,3},{4,36},{36... | collective-permute-start | bytes 1179656 | tf_op jit(solution)/shard_map/ppermute | solution.py:213
  41.6 2.4 %collective-permute-start.5 = (bf16[3,256,256]{2,1,0:T(8,128)(2,1)S(1)}, bf16[3,256,256]{2,1,0:T(8,128)(2,1)S(1)}, u32[]{:S(2)}, u32[]{:S(2)}) collective-permute-start(bf16[3,256,256]{2,1,0:T(8,128)(2,1)S(1)} %collective-permute-done.1.refs_1_), channel_id=1, source_target_pairs={{0,32},{32,0},{1,33},{33,1},{2,34},{34,2},{3,35},{35,3},{4,36},{36... | collective-permute-start | bytes 1179656 | tf_op jit(solution)/shard_map/ppermute | solution.py:213
  44.0 3.7 %collective-permute-done.2.refs_2_ = bf16[3,256,256]{2,1,0:T(8,128)(2,1)S(1)} collective-permute-done((bf16[3,256,256]{2,1,0:T(8,128)(2,1)S(1)}, bf16[3,256,256]{2,1,0:T(8,128)(2,1)S(1)}, u32[]{:S(2)}, u32[]{:S(2)}) %collective-permute-start.2) | collective-permute-done | bytes 393248 | tf_op jit(solution)/shard_map/ppermute | solution.py:212
  47.7 1.9 %collective-permute-start.6 = (bf16[3,256,256]{2,1,0:T(8,128)(2,1)S(1)}, bf16[3,256,256]{2,1,0:T(8,128)(2,1)}, u32[]{:S(2)}, u32[]{:S(2)}) collective-permute-start(bf16[3,256,256]{2,1,0:T(8,128)(2,1)S(1)} %collective-permute-done.2.refs_2_), channel_id=1, source_target_pairs={{0,32},{32,0},{1,33},{33,1},{2,34},{34,2},{3,35},{35,3},{4,36},{36... | collective-permute-start | bytes 1179656 | tf_op jit(solution)/shard_map/ppermute | solution.py:213
  49.7 3.9 %collective-permute-done.3.refs_3_ = bf16[3,256,256]{2,1,0:T(8,128)(2,1)S(1)} collective-permute-done((bf16[3,256,256]{2,1,0:T(8,128)(2,1)S(1)}, bf16[3,256,256]{2,1,0:T(8,128)(2,1)S(1)}, u32[]{:S(2)}, u32[]{:S(2)}) %collective-permute-start.3) | collective-permute-done | bytes 393248 | tf_op jit(solution)/shard_map/ppermute | solution.py:212
  53.5 1.9 %collective-permute-start.7 = (bf16[3,256,256]{2,1,0:T(8,128)(2,1)S(1)}, bf16[3,256,256]{2,1,0:T(8,128)(2,1)}, u32[]{:S(2)}, u32[]{:S(2)}) collective-permute-start(bf16[3,256,256]{2,1,0:T(8,128)(2,1)S(1)} %collective-permute-done.3.refs_3_), channel_id=1, source_target_pairs={{0,32},{32,0},{1,33},{33,1},{2,34},{34,2},{3,35},{35,3},{4,36},{36... | collective-permute-start | bytes 1179656 | tf_op jit(solution)/shard_map/ppermute | solution.py:213
  55.5 0.1 pad_add_fusion.place_ref
  55.5 0.0 collective-permute-done.4.refs_4_
  55.6 0.0 copy-start
  55.6 0.0 collective-permute-done.6.refs_6_
  55.6 0.0 collective-permute-done.5.refs_5_
  55.6 0.0 copy-start.2
  55.6 1.7 %collective-permute-done.7.refs_7_ = bf16[3,256,256]{2,1,0:T(8,128)(2,1)} collective-permute-done((bf16[3,256,256]{2,1,0:T(8,128)(2,1)S(1)}, bf16[3,256,256]{2,1,0:T(8,128)(2,1)}, u32[]{:S(2)}, u32[]{:S(2)}) %collective-permute-start.7) | collective-permute-done | bytes 393248 | tf_op jit(solution)/shard_map/ppermute | solution.py:213
  57.3 6.8 %all-to-all-done = bf16[16,2,128,128]{3,2,1,0:T(8,128)(2,1)S(1)} async-done(((bf16[16,2,128,128]{3,2,1,0:T(8,128)(2,1)}), bf16[16,2,128,128]{3,2,1,0:T(8,128)(2,1)S(1)}, u32[]{:S(2)}, u32[]{:S(2)}) %all-to-all-start) | async-done | bytes 1048608 | tf_op jit(solution)/shard_map/all_to_all | solution.py:201
  64.0 3.0 %gates.1 = bf16[256,1536]{1,0:T(8,128)(2,1)} custom-call(s32[3]{0:T(128)S(1)} %pad_add_fusion.place_ref, bf16[8,2,2,128,128]{4,3,2,1,0:T(8,128)(2,1)S(1)} %bitcast.20, bf16[3,256,256]{2,1,0:T(8,128)(2,1)S(1)} %multiply_convert_fusion.refs_0_, bf16[3,256,256]{2,1,0:T(8,128)(2,1)S(1)} %collective-permute-done.1.refs_1_, ...), custom_call_target="tpu_custom_call" | custom-call | flops 800000000 | bytes 6000000 | tf_op jit(solution)/shard_map/gates/pallas_call | solution.py:96
  67.0 0.0 copy-done
  67.0 0.0 copy-done.2
  67.0 5.7 %all-to-all-start.1 = ((bf16[4,64,1536]{2,1,0:T(8,128)(2,1)}), bf16[4,64,1536]{2,1,0:T(8,128)(2,1)S(1)}, u32[]{:S(2)}, u32[]{:S(2)}) async-start(bf16[4,64,1536]{2,1,0:T(8,128)(2,1)} %bitcast.7), calls=%async_computation.1 | async-start | bytes 1572864 | tf_op jit(solution)/shard_map/all_to_all | solution.py:201
  72.8 1.9 %collective-permute-start.8 = (bf16[2,2,2,2,128,128]{5,4,3,2,1,0:T(8,128)(2,1)S(1)}, bf16[2,2,2,2,128,128]{5,4,3,2,1,0:T(8,128)(2,1)S(1)}, u32[]{:S(2)}, u32[]{:S(2)}) collective-permute-start(bf16[2,2,2,2,128,128]{5,4,3,2,1,0:T(8,128)(2,1)S(1)} %dynamic-slice_bitcast_fusion), channel_id=1, source_target_pairs={{0,32},{32,0},{1,33},{33,1},{2,34},{34,2},{3,35},{35,3},{4,36},{36... | collective-permute-start | bytes 1572872 | tf_op jit(solution)/shard_map/ppermute | solution.py:219
  74.7 1.9 %collective-permute-done.8.other_acts_ref = bf16[2,2,2,2,128,128]{5,4,3,2,1,0:T(8,128)(2,1)S(1)} collective-permute-done((bf16[2,2,2,2,128,128]{5,4,3,2,1,0:T(8,128)(2,1)S(1)}, bf16[2,2,2,2,128,128]{5,4,3,2,1,0:T(8,128)(2,1)S(1)}, u32[]{:S(2)}, u32[]{:S(2)}) %collective-permute-start.8) | collective-permute-done | bytes 524320 | tf_op jit(solution)/shard_map/ppermute | solution.py:219
  76.6 0.0 copy-start.4
  76.6 0.8 copy-done.4
  77.4 1.9 %all-to-all-done.1.parts_ref = bf16[4,64,1536]{2,1,0:T(8,128)(2,1)S(1)} async-done(((bf16[4,64,1536]{2,1,0:T(8,128)(2,1)}), bf16[4,64,1536]{2,1,0:T(8,128)(2,1)S(1)}, u32[]{:S(2)}, u32[]{:S(2)}) %all-to-all-start.1) | async-done | bytes 786464 | tf_op jit(solution)/shard_map/all_to_all | solution.py:201
  79.3 0.2 hidden_grads.1
  79.5 0.0 copy-start.1
  79.5 0.0 copy-start.3
  79.5 13.4 %all_to_all.20 = bf16[4,64,1536]{2,1,0:T(8,128)(2,1)S(1)} all-to-all(bf16[4,64,1536]{2,1,0:T(8,128)(2,1)S(1)} %hidden_grads.1), channel_id=1, replica_groups=mesh['yl'=2,'x1'=2,'x0'=2,'core'=2,'yh1'=2,'yh0'=2,'zh1'=2,'zh0'=2,'zl'=..., dimensions={0} | all-to-all | bytes 1572864 | tf_op jit(solution)/shard_map/all_to_all | solution.py:201
  92.9 0.0 copy-done.1
  92.9 0.0 copy-done.3
  92.9 2.7 %input_terms.1 = bf16[8,2,128,128]{3,2,1,0:T(8,128)(2,1)} custom-call(s32[3]{0:T(128)S(1)} %pad_add_fusion.place_ref, bf16[256,1536]{1,0:T(8,128)(2,1)S(1)} %bitcast.23, bf16[3,256,256]{2,1,0:T(8,128)(2,1)S(1)} %multiply_convert_fusion.refs_0_, bf16[3,256,256]{2,1,0:T(8,128)(2,1)S(1)} %collective-permute-done.1.refs_1_, ...), custom_call_target="tpu_custom_call" | custom-call | flops 540000000 | bytes 4000000 | tf_op jit(solution)/shard_map/input_terms/pallas_call | solution.py:151
  95.6 0.0 copy-start.5
  95.6 10.2 %all-to-all-start.3 = ((bf16[8,2,128,128]{3,2,1,0:T(8,128)(2,1)}), bf16[8,2,128,128]{3,2,1,0:T(8,128)(2,1)}, u32[]{:S(2)}, u32[]{:S(2)}) async-start(bf16[8,2,128,128]{3,2,1,0:T(8,128)(2,1)} %input_terms.1), calls=%async_computation.3 | async-start | bytes 1048576 | tf_op jit(solution)/shard_map/all_to_all | solution.py:201
  105.7 1.9 %collective-permute-start.11 = (bf16[256,1536]{1,0:T(8,128)(2,1)S(1)}, bf16[256,1536]{1,0:T(8,128)(2,1)S(1)}, u32[]{:S(2)}, u32[]{:S(2)}) collective-permute-start(bf16[256,1536]{1,0:T(8,128)(2,1)S(1)} %bitcast.24), channel_id=1, source_target_pairs={{0,32},{32,0},{1,33},{33,1},{2,34},{34,2},{3,35},{35,3},{4,36},{36... | collective-permute-start | bytes 2359304 | tf_op jit(solution)/shard_map/ppermute | solution.py:223
  107.7 2.3 %collective-permute-done.11.other_grads_ref = bf16[256,1536]{1,0:T(8,128)(2,1)S(1)} collective-permute-done((bf16[256,1536]{1,0:T(8,128)(2,1)S(1)}, bf16[256,1536]{1,0:T(8,128)(2,1)S(1)}, u32[]{:S(2)}, u32[]{:S(2)}) %collective-permute-start.11) | collective-permute-done | bytes 786464 | tf_op jit(solution)/shard_map/ppermute | solution.py:223
  109.9 0.0 copy-done.5
  109.9 2.4 %weight_terms.1 = (f32[3,256,256]{2,1,0:T(8,128)S(1)}, bf16[3,256,256]{2,1,0:T(8,128)(2,1)}, bf16[3,256,256]{2,1,0:T(8,128)(2,1)}, bf16[3,256,256]{2,1,0:T(8,128)(2,1)}) custom-call(s32[3]{0:T(128)S(1)} %pad_add_fusion.place_ref, bf16[8,2,2,128,128]{4,3,2,1,0:T(8,128)(2,1)S(1)} %bitcast.22, bf16[2,2,2,2,128,128]{5,4,3,2,1,0:T(8,128)(2,1)S(1)} %copy-done.5, ...), custom_call_target="tpu_custom_call" | custom-call | flops 800000000 | bytes 6000000 | tf_op jit(solution)/shard_map/weight_terms/pallas_call | solution.py:188
  112.3 3.6 %collective-permute-start.12 = (bf16[3,256,256]{2,1,0:T(8,128)(2,1)}, bf16[3,256,256]{2,1,0:T(8,128)(2,1)S(1)}, u32[]{:S(2)}, u32[]{:S(2)}) collective-permute-start(bf16[3,256,256]{2,1,0:T(8,128)(2,1)} %get-tuple-element.15), channel_id=1, source_target_pairs={{0,1},{1,0},{2,3},{3,2},{4,5},{5,4},{6,7},{7,6},{8,9},{9,8},{10,11... | collective-permute-start | bytes 1179656 | tf_op jit(solution)/shard_map/ppermute | solution.py:231
  115.9 1.9 %collective-permute-start.13 = (bf16[3,256,256]{2,1,0:T(8,128)(2,1)}, bf16[3,256,256]{2,1,0:T(8,128)(2,1)S(1)}, u32[]{:S(2)}, u32[]{:S(2)}) collective-permute-start(bf16[3,256,256]{2,1,0:T(8,128)(2,1)} %get-tuple-element.16), channel_id=1, source_target_pairs={{0,64},{64,0},{1,65},{65,1},{2,66},{66,2},{3,67},{67,3},{4,68},{68... | collective-permute-start | bytes 1179656 | tf_op jit(solution)/shard_map/ppermute | solution.py:232
  117.8 3.7 %collective-permute-start.14 = (bf16[3,256,256]{2,1,0:T(8,128)(2,1)}, bf16[3,256,256]{2,1,0:T(8,128)(2,1)S(1)}, u32[]{:S(2)}, u32[]{:S(2)}) collective-permute-start(bf16[3,256,256]{2,1,0:T(8,128)(2,1)} %get-tuple-element.17), channel_id=1, source_target_pairs={{0,65},{1,64},{64,1},{65,0},{2,67},{3,66},{66,3},{67,2},{4,69},{5,... | collective-permute-start | bytes 1179656 | tf_op jit(solution)/shard_map/ppermute | solution.py:233
  121.5 0.2 all-to-all-done.3
  121.7 1.1 reduce_sum.12
  122.8 8.2 %collective-permute-start.9 = (bf16[128,128]{1,0:T(8,128)(2,1)S(1)}, bf16[128,128]{1,0:T(8,128)(2,1)S(1)}, u32[]{:S(2)}, u32[]{:S(2)}) collective-permute-start(bf16[128,128]{1,0:T(8,128)(2,1)S(1)} %get-tuple-element.18), channel_id=1, source_target_pairs={{0,0},{8,1},{2,2},{10,3},{4,4},{12,5},{6,6},{14,7},{128,8},{136,9}... | collective-permute-start | bytes 98312 | tf_op jit(solution)/shard_map/ppermute | solution.py:227
  131.0 1.9 %collective-permute-start.10 = (bf16[128,128]{1,0:T(8,128)(2,1)S(1)}, bf16[128,128]{1,0:T(8,128)(2,1)S(1)}, u32[]{:S(2)}, u32[]{:S(2)}) collective-permute-start(bf16[128,128]{1,0:T(8,128)(2,1)S(1)} %get-tuple-element.19), channel_id=1, source_target_pairs={{16,0},{24,1},{18,2},{26,3},{20,4},{28,5},{22,6},{30,7},{144,8},{1... | collective-permute-start | bytes 98312 | tf_op jit(solution)/shard_map/ppermute | solution.py:227
  133.0 6.2 %collective-permute-done.9 = bf16[128,128]{1,0:T(8,128)(2,1)S(1)} collective-permute-done((bf16[128,128]{1,0:T(8,128)(2,1)S(1)}, bf16[128,128]{1,0:T(8,128)(2,1)S(1)}, u32[]{:S(2)}, u32[]{:S(2)}) %collective-permute-start.9) | collective-permute-done | bytes 32800 | tf_op jit(solution)/shard_map/ppermute | solution.py:227
  139.2 4.9 %collective-permute-done.10 = bf16[128,128]{1,0:T(8,128)(2,1)S(1)} collective-permute-done((bf16[128,128]{1,0:T(8,128)(2,1)S(1)}, bf16[128,128]{1,0:T(8,128)(2,1)S(1)}, u32[]{:S(2)}, u32[]{:S(2)}) %collective-permute-start.10) | collective-permute-done | bytes 32800 | tf_op jit(solution)/shard_map/ppermute | solution.py:227
  144.0 0.6 add_convert_fusion
  144.7 0.0 collective-permute-done.12
  144.7 0.0 collective-permute-done.13
  144.7 0.0 collective-permute-done.14
  144.7 1.0 convert_add_fusion
  (3 shorter events, 0.1 us)
Async XLA Ops:
  1.3 5.4 %copy-start.6 = (bf16[128,128]{1,0:T(8,128)(2,1)S(1)}, bf16[128,128]{1,0:T(8,128)(2,1)}, u32[]{:S(2)}) copy-start(bf16[128,128]{1,0:T(8,128)(2,1)} %param.5) | copy-start | bytes 98308
  1.3 5.4 %copy-start.7 = (bf16[128,128]{1,0:T(8,128)(2,1)S(1)}, bf16[128,128]{1,0:T(8,128)(2,1)}, u32[]{:S(2)}) copy-start(bf16[128,128]{1,0:T(8,128)(2,1)} %param.4) | copy-start | bytes 98308
  2.4 16.6 %collective-permute-start.1 = (bf16[3,256,256]{2,1,0:T(8,128)(2,1)S(1)}, bf16[3,256,256]{2,1,0:T(8,128)(2,1)S(1)}, u32[]{:S(2)}, u32[]{:S(2)}) collective-permute-start(bf16[3,256,256]{2,1,0:T(8,128)(2,1)S(1)} %multiply_convert_fusion.refs_0_), channel_id=1, source_target_pairs={{0,1},{1,0},{2,3},{3,2},{4,5},{5,4},{6,7},{7,6},{8,9},{9,8},{10,11... | collective-permute-start | bytes 1179656 | tf_op jit(solution)/shard_map/ppermute | solution.py:210
  6.7 11.1 %collective-permute-start = (bf16[2,128,128]{2,1,0:T(8,128)(2,1)S(1)}, bf16[2,128,128]{2,1,0:T(8,128)(2,1)S(1)}, u32[]{:S(2)}, u32[]{:S(2)}) collective-permute-start(bf16[2,128,128]{2,1,0:T(8,128)(2,1)S(1)} %pad_maximum_fusion), channel_id=1, source_target_pairs={{0,0},{1,8},{2,2},{3,10},{4,4},{5,12},{6,6},{7,14},{8,128},{9,136}... | collective-permute-start | bytes 196616 | tf_op jit(solution)/shard_map/ppermute | solution.py:208
  19.0 45.0 %all-to-all-start = ((bf16[16,2,128,128]{3,2,1,0:T(8,128)(2,1)}), bf16[16,2,128,128]{3,2,1,0:T(8,128)(2,1)S(1)}, u32[]{:S(2)}, u32[]{:S(2)}) async-start(bf16[16,2,128,128]{3,2,1,0:T(8,128)(2,1)} %spread.1), calls=%async_computation | async-start | bytes 2097152 | tf_op jit(solution)/shard_map/all_to_all | solution.py:201
  33.8 13.9 %collective-permute-start.2 = (bf16[3,256,256]{2,1,0:T(8,128)(2,1)S(1)}, bf16[3,256,256]{2,1,0:T(8,128)(2,1)S(1)}, u32[]{:S(2)}, u32[]{:S(2)}) collective-permute-start(bf16[3,256,256]{2,1,0:T(8,128)(2,1)S(1)} %multiply_convert_fusion.refs_0_), channel_id=1, source_target_pairs={{0,64},{64,0},{1,65},{65,1},{2,66},{66,2},{3,67},{67,3},{4,68},{68... | collective-permute-start | bytes 1179656 | tf_op jit(solution)/shard_map/ppermute | solution.py:212
  37.2 16.4 %collective-permute-start.3 = (bf16[3,256,256]{2,1,0:T(8,128)(2,1)S(1)}, bf16[3,256,256]{2,1,0:T(8,128)(2,1)S(1)}, u32[]{:S(2)}, u32[]{:S(2)}) collective-permute-start(bf16[3,256,256]{2,1,0:T(8,128)(2,1)S(1)} %collective-permute-done.1.refs_1_), channel_id=1, source_target_pairs={{0,64},{64,0},{1,65},{65,1},{2,66},{66,2},{3,67},{67,3},{4,68},{68... | collective-permute-start | bytes 1179656 | tf_op jit(solution)/shard_map/ppermute | solution.py:212
  39.7 15.9 %collective-permute-start.4 = (bf16[3,256,256]{2,1,0:T(8,128)(2,1)S(1)}, bf16[3,256,256]{2,1,0:T(8,128)(2,1)S(1)}, u32[]{:S(2)}, u32[]{:S(2)}) collective-permute-start(bf16[3,256,256]{2,1,0:T(8,128)(2,1)S(1)} %multiply_convert_fusion.refs_0_), channel_id=1, source_target_pairs={{0,32},{32,0},{1,33},{33,1},{2,34},{34,2},{3,35},{35,3},{4,36},{36... | collective-permute-start | bytes 1179656 | tf_op jit(solution)/shard_map/ppermute | solution.py:213
  41.6 14.0 %collective-permute-start.5 = (bf16[3,256,256]{2,1,0:T(8,128)(2,1)S(1)}, bf16[3,256,256]{2,1,0:T(8,128)(2,1)S(1)}, u32[]{:S(2)}, u32[]{:S(2)}) collective-permute-start(bf16[3,256,256]{2,1,0:T(8,128)(2,1)S(1)} %collective-permute-done.1.refs_1_), channel_id=1, source_target_pairs={{0,32},{32,0},{1,33},{33,1},{2,34},{34,2},{3,35},{35,3},{4,36},{36... | collective-permute-start | bytes 1179656 | tf_op jit(solution)/shard_map/ppermute | solution.py:213
  47.7 7.8 %collective-permute-start.6 = (bf16[3,256,256]{2,1,0:T(8,128)(2,1)S(1)}, bf16[3,256,256]{2,1,0:T(8,128)(2,1)}, u32[]{:S(2)}, u32[]{:S(2)}) collective-permute-start(bf16[3,256,256]{2,1,0:T(8,128)(2,1)S(1)} %collective-permute-done.2.refs_2_), channel_id=1, source_target_pairs={{0,32},{32,0},{1,33},{33,1},{2,34},{34,2},{3,35},{35,3},{4,36},{36... | collective-permute-start | bytes 1179656 | tf_op jit(solution)/shard_map/ppermute | solution.py:213
  53.5 3.7 %collective-permute-start.7 = (bf16[3,256,256]{2,1,0:T(8,128)(2,1)S(1)}, bf16[3,256,256]{2,1,0:T(8,128)(2,1)}, u32[]{:S(2)}, u32[]{:S(2)}) collective-permute-start(bf16[3,256,256]{2,1,0:T(8,128)(2,1)S(1)} %collective-permute-done.3.refs_3_), channel_id=1, source_target_pairs={{0,32},{32,0},{1,33},{33,1},{2,34},{34,2},{3,35},{35,3},{4,36},{36... | collective-permute-start | bytes 1179656 | tf_op jit(solution)/shard_map/ppermute | solution.py:213
  55.6 11.5 %copy-start = (bf16[3,256,256]{2,1,0:T(8,128)(2,1)}, bf16[3,256,256]{2,1,0:T(8,128)(2,1)S(1)}, u32[]{:S(2)}) copy-start(bf16[3,256,256]{2,1,0:T(8,128)(2,1)S(1)} %collective-permute-done.4.refs_4_) | copy-start | bytes 1179652
  55.6 11.5 %copy-start.2 = (bf16[3,256,256]{2,1,0:T(8,128)(2,1)}, bf16[3,256,256]{2,1,0:T(8,128)(2,1)S(1)}, u32[]{:S(2)}) copy-start(bf16[3,256,256]{2,1,0:T(8,128)(2,1)S(1)} %collective-permute-done.5.refs_5_) | copy-start | bytes 1179652
  67.0 12.3 %all-to-all-start.1 = ((bf16[4,64,1536]{2,1,0:T(8,128)(2,1)}), bf16[4,64,1536]{2,1,0:T(8,128)(2,1)S(1)}, u32[]{:S(2)}, u32[]{:S(2)}) async-start(bf16[4,64,1536]{2,1,0:T(8,128)(2,1)} %bitcast.7), calls=%async_computation.1 | async-start | bytes 1572864 | tf_op jit(solution)/shard_map/all_to_all | solution.py:201
  72.8 3.8 %collective-permute-start.8 = (bf16[2,2,2,2,128,128]{5,4,3,2,1,0:T(8,128)(2,1)S(1)}, bf16[2,2,2,2,128,128]{5,4,3,2,1,0:T(8,128)(2,1)S(1)}, u32[]{:S(2)}, u32[]{:S(2)}) collective-permute-start(bf16[2,2,2,2,128,128]{5,4,3,2,1,0:T(8,128)(2,1)S(1)} %dynamic-slice_bitcast_fusion), channel_id=1, source_target_pairs={{0,32},{32,0},{1,33},{33,1},{2,34},{34,2},{3,35},{35,3},{4,36},{36... | collective-permute-start | bytes 1572872 | tf_op jit(solution)/shard_map/ppermute | solution.py:219
  76.6 0.8 copy-start.4
  79.5 13.4 %copy-start.1 = (bf16[3,256,256]{2,1,0:T(8,128)(2,1)S(1)}, bf16[3,256,256]{2,1,0:T(8,128)(2,1)}, u32[]{:S(2)}) copy-start(bf16[3,256,256]{2,1,0:T(8,128)(2,1)} %copy-done) | copy-start | bytes 1179652
  79.5 13.4 %copy-start.3 = (bf16[3,256,256]{2,1,0:T(8,128)(2,1)S(1)}, bf16[3,256,256]{2,1,0:T(8,128)(2,1)}, u32[]{:S(2)}) copy-start(bf16[3,256,256]{2,1,0:T(8,128)(2,1)} %copy-done.2) | copy-start | bytes 1179652
  95.6 14.3 %copy-start.5 = (bf16[2,2,2,2,128,128]{5,4,3,2,1,0:T(8,128)(2,1)S(1)}, bf16[2,2,2,2,128,128]{5,4,3,2,1,0:T(8,128)(2,1)}, u32[]{:S(2)}) copy-start(bf16[2,2,2,2,128,128]{5,4,3,2,1,0:T(8,128)(2,1)} %copy-done.4) | copy-start | bytes 1572868
  95.6 26.1 %all-to-all-start.3 = ((bf16[8,2,128,128]{3,2,1,0:T(8,128)(2,1)}), bf16[8,2,128,128]{3,2,1,0:T(8,128)(2,1)}, u32[]{:S(2)}, u32[]{:S(2)}) async-start(bf16[8,2,128,128]{3,2,1,0:T(8,128)(2,1)} %input_terms.1), calls=%async_computation.3 | async-start | bytes 1048576 | tf_op jit(solution)/shard_map/all_to_all | solution.py:201
  105.7 4.2 %collective-permute-start.11 = (bf16[256,1536]{1,0:T(8,128)(2,1)S(1)}, bf16[256,1536]{1,0:T(8,128)(2,1)S(1)}, u32[]{:S(2)}, u32[]{:S(2)}) collective-permute-start(bf16[256,1536]{1,0:T(8,128)(2,1)S(1)} %bitcast.24), channel_id=1, source_target_pairs={{0,32},{32,0},{1,33},{33,1},{2,34},{34,2},{3,35},{35,3},{4,36},{36... | collective-permute-start | bytes 2359304 | tf_op jit(solution)/shard_map/ppermute | solution.py:223
  112.3 32.4 %collective-permute-start.12 = (bf16[3,256,256]{2,1,0:T(8,128)(2,1)}, bf16[3,256,256]{2,1,0:T(8,128)(2,1)S(1)}, u32[]{:S(2)}, u32[]{:S(2)}) collective-permute-start(bf16[3,256,256]{2,1,0:T(8,128)(2,1)} %get-tuple-element.15), channel_id=1, source_target_pairs={{0,1},{1,0},{2,3},{3,2},{4,5},{5,4},{6,7},{7,6},{8,9},{9,8},{10,11... | collective-permute-start | bytes 1179656 | tf_op jit(solution)/shard_map/ppermute | solution.py:231
  115.9 28.8 %collective-permute-start.13 = (bf16[3,256,256]{2,1,0:T(8,128)(2,1)}, bf16[3,256,256]{2,1,0:T(8,128)(2,1)S(1)}, u32[]{:S(2)}, u32[]{:S(2)}) collective-permute-start(bf16[3,256,256]{2,1,0:T(8,128)(2,1)} %get-tuple-element.16), channel_id=1, source_target_pairs={{0,64},{64,0},{1,65},{65,1},{2,66},{66,2},{3,67},{67,3},{4,68},{68... | collective-permute-start | bytes 1179656 | tf_op jit(solution)/shard_map/ppermute | solution.py:232
  117.8 26.8 %collective-permute-start.14 = (bf16[3,256,256]{2,1,0:T(8,128)(2,1)}, bf16[3,256,256]{2,1,0:T(8,128)(2,1)S(1)}, u32[]{:S(2)}, u32[]{:S(2)}) collective-permute-start(bf16[3,256,256]{2,1,0:T(8,128)(2,1)} %get-tuple-element.17), channel_id=1, source_target_pairs={{0,65},{1,64},{64,1},{65,0},{2,67},{3,66},{66,3},{67,2},{4,69},{5,... | collective-permute-start | bytes 1179656 | tf_op jit(solution)/shard_map/ppermute | solution.py:233
  122.8 16.4 %collective-permute-start.9 = (bf16[128,128]{1,0:T(8,128)(2,1)S(1)}, bf16[128,128]{1,0:T(8,128)(2,1)S(1)}, u32[]{:S(2)}, u32[]{:S(2)}) collective-permute-start(bf16[128,128]{1,0:T(8,128)(2,1)S(1)} %get-tuple-element.18), channel_id=1, source_target_pairs={{0,0},{8,1},{2,2},{10,3},{4,4},{12,5},{6,6},{14,7},{128,8},{136,9}... | collective-permute-start | bytes 98312 | tf_op jit(solution)/shard_map/ppermute | solution.py:227
  131.0 13.0 %collective-permute-start.10 = (bf16[128,128]{1,0:T(8,128)(2,1)S(1)}, bf16[128,128]{1,0:T(8,128)(2,1)S(1)}, u32[]{:S(2)}, u32[]{:S(2)}) collective-permute-start(bf16[128,128]{1,0:T(8,128)(2,1)S(1)} %get-tuple-element.19), channel_id=1, source_target_pairs={{16,0},{24,1},{18,2},{26,3},{20,4},{28,5},{22,6},{30,7},{144,8},{1... | collective-permute-start | bytes 98312 | tf_op jit(solution)/shard_map/ppermute | solution.py:227

commit v16 on v15

--- a/solution.py
+++ b/solution.py
@@ -23,6 +23,7 @@
 SHARE = TOKENS // 4
 FEATURES = 4 * BLOCK
 GRADS = 3 * WIDE
+EARLY = 2
 VMEM_LIMIT = 24 * 1024 * 1024
 WHOLE = pl.BlockSpec(memory_space=pltpu.VMEM)
 SCALARS = pl.BlockSpec(memory_space=pltpu.SMEM)
@@ -77,8 +78,18 @@
     )(acts)
 
 
+def block_of(w_refs, s, j, p):
+    if s < 2:
+        return w_refs[2 * s + j][p]
+    if s == 3:
+        return w_refs[4][3 * j + p]
+    if j == 0:
+        return w_refs[5][p]
+    return w_refs[4][6 + p] if p < EARLY else w_refs[5][3 + p - EARLY]
+
+
 def gates_kernel(place_ref, acts_ref, *refs):
-    w_refs, parts_ref, wide_ref = refs[:8], refs[8], refs[9]
+    w_refs, parts_ref, wide_ref = refs[:6], refs[6], refs[7]
     for p in range(2):
         for t in range(2):
             for f in range(8):
@@ -88,7 +99,7 @@
         for j in range(2):
             total = jnp.zeros((TOKENS, BLOCK), F32)
             for s in range(4):
-                total += dot(wide_ref[p // 2, :, pl.ds(s * BLOCK, BLOCK)], w_refs[2 * s + j][p], ((1,), (0,)))
+                total += dot(wide_ref[p // 2, :, pl.ds(s * BLOCK, BLOCK)], block_of(w_refs, s, j, p), ((1,), (0,)))
             parts_ref[:, pl.ds(p * WIDE + j * BLOCK, BLOCK)] = total.astype(BF16)
 
 
@@ -96,7 +107,7 @@
     return pl.pallas_call(
         gates_kernel,
         out_shape=jax.ShapeDtypeStruct((TOKENS, GRADS), BF16),
-        in_specs=[SCALARS] + [WHOLE] * 9,
+        in_specs=[SCALARS] + [WHOLE] * 7,
         out_specs=WHOLE,
         scratch_shapes=[pltpu.VMEM((2, TOKENS, FEATURES), BF16)],
         compiler_params=params(),
@@ -133,13 +144,13 @@
 
 
 def input_kernel(place_ref, grads_ref, *refs):
-    w_refs, dx_ref = refs[:8], refs[8]
+    w_refs, dx_ref = refs[:6], refs[6]
     for s in range(4):
         dx = jnp.zeros((TOKENS, BLOCK), F32)
         for p in range(2):
             for j in range(2):
                 grads = grads_ref[:, pl.ds(p * WIDE + j * BLOCK, BLOCK)]
-                dx += dot(grads, w_refs[2 * s + j][p], ((1,), (1,)))
+                dx += dot(grads, block_of(w_refs, s, j, p), ((1,), (1,)))
         dx = dx.astype(BF16)
         for t in range(2):
             for f in range(2):
@@ -151,7 +162,7 @@
     return pl.pallas_call(
         input_kernel,
         out_shape=jax.ShapeDtypeStruct((8, 2, TOK, TOK), BF16),
-        in_specs=[SCALARS] + [WHOLE] * 9,
+        in_specs=[SCALARS] + [WHOLE] * 7,
         out_specs=WHOLE,
         compiler_params=params(),
         cost_estimate=pl.CostEstimate(flops=540000000, bytes_accessed=4000000, transcendentals=0),
@@ -208,9 +219,9 @@
     acts = spread(lax.ppermute(jnp.stack([inputs, out_grad]), AXES, there[0]))
     w = (codes.astype(F32) * scales.astype(F32)).astype(BF16)
     w_z = lax.ppermute(w, "zl", SWAP)
-    acts, w_z = lax.optimization_barrier((acts, w_z))
     weights = [w, w_z] + [lax.ppermute(block, "x0", SWAP) for block in (w, w_z)]
-    weights += [lax.ppermute(block, "core", SWAP) for block in weights]
+    blocks = (weights[2], weights[3], w_z[:EARLY]), (w, w_z[EARLY:])
+    weights += [lax.ppermute(jnp.concatenate(part), "core", SWAP) for part in blocks]
     acts = exchange(acts, GATHER).reshape(8, 2, 2, TOK, TOK)
 
     parts = gates(place, acts, *weights)

time: 147 us -> 153 us (1.041)
  the two profiles are of different devices: /device:TPU:44 before, /device:TPU:4 now
where the time goes in v16:
time: 153 us; the launch traced here: 152 us
  starting transfers between devices  76.7 us (50%)
  waiting for transfers between devices  39.7 us (26%)
  blocking collectives  15.1 us (10%)
  Pallas kernels  7.33 us (5%)
  other arithmetic  6.67 us (4%)
  local copies, waits for them, and re-layouts  5.52 us (4%)
    all_to_all x3, starting transfers between devices, exchange(): return lax.all_to_all(pieces, axes, split_axis=0, concat_axis=0, tiled=True)  37.9 us
    all_to_all x1, blocking collectives, exchange(): return lax.all_to_all(pieces, axes, split_axis=0, concat_axis=0, tiled=True)  15.1 us
    ppermute x2, waiting for transfers between devices, local(): weights = [w, w_z] + [lax.ppermute(block, 'x0', SWAP) for block in (w, w_z)]  14.1 us
    ppermute x2, waiting for transfers between devices, local(): lax.ppermute(dx[i], AXES, [(b, a) for a, b in there[i]])  10.7 us
    all_to_all x3, waiting for transfers between devices, exchange(): return lax.all_to_all(pieces, axes, split_axis=0, concat_axis=0, tiled=True)  8.32 us
    ppermute x2, starting transfers between devices, local(): lax.ppermute(dx[i], AXES, [(b, a) for a, b in there[i]])  6.97 us
    ppermute x2, starting transfers between devices, local(): weights = [w, w_z] + [lax.ppermute(block, 'x0', SWAP) for block in (w, w_z)]  5.84 us
    ppermute x1, starting transfers between devices, local(): lax.ppermute(xz, ('x0', 'zl'), [(i, 3 - i) for i in range(4)]).astype(F32)  4.98 us
  transfers between devices with their start and end apart: 16, of which 10 were waited for; matrix products, arithmetic and copies ran while one was open for 4% of the time, Pallas kernels for 2%

profile of v16, /device:TPU:4, one launch (start us, length us, event | category | flops | bytes accessed | tf_op | source)
XLA Modules:
  0.0 151.9 jit_solution(6080520904632318861)
XLA Ops:
  0.6 0.0 copy-start.11
  0.6 0.8 pad_maximum_fusion.2
  1.4 4.2 %collective-permute-start = (bf16[2,128,128]{2,1,0:T(8,128)(2,1)S(1)}, bf16[2,128,128]{2,1,0:T(8,128)(2,1)S(1)}, u32[]{:S(2)}, u32[]{:S(2)}) collective-permute-start(bf16[2,128,128]{2,1,0:T(8,128)(2,1)S(1)} %pad_maximum_fusion.2), channel_id=1, source_target_pairs={{0,0},{1,8},{2,2},{3,10},{4,4},{5,12},{6,6},{7,14},{8,128},{9,136}... | collective-permute-start | bytes 196616 | tf_op jit(solution)/shard_map/ppermute | solution.py:219
  5.6 0.0 copy-done.11
  5.7 1.1 multiply_convert_fusion.refs_0_
  6.7 4.5 %collective-permute-start.1 = (bf16[3,256,256]{2,1,0:T(8,128)(2,1)S(1)}, bf16[3,256,256]{2,1,0:T(8,128)(2,1)S(1)}, u32[]{:S(2)}, u32[]{:S(2)}) collective-permute-start(bf16[3,256,256]{2,1,0:T(8,128)(2,1)S(1)} %multiply_convert_fusion.refs_0_), channel_id=1, source_target_pairs={{0,1},{1,0},{2,3},{3,2},{4,5},{5,4},{6,7},{7,6},{8,9},{9,8},{10,11... | collective-permute-start | bytes 1179656 | tf_op jit(solution)/shard_map/ppermute | solution.py:221
  11.2 0.6 collective-permute-done.acts_ref
  11.9 1.1 spread.1
  13.0 16.2 %all-to-all-start = ((bf16[16,2,128,128]{3,2,1,0:T(8,128)(2,1)}), bf16[16,2,128,128]{3,2,1,0:T(8,128)(2,1)S(1)}, u32[]{:S(2)}, u32[]{:S(2)}) async-start(bf16[16,2,128,128]{3,2,1,0:T(8,128)(2,1)} %spread.1), calls=%async_computation | async-start | bytes 2097152 | tf_op jit(solution)/shard_map/all_to_all | solution.py:212
  29.2 3.1 %collective-permute-start.2 = (bf16[3,256,256]{2,1,0:T(8,128)(2,1)S(1)}, bf16[3,256,256]{2,1,0:T(8,128)(2,1)S(1)}, u32[]{:S(2)}, u32[]{:S(2)}) collective-permute-start(bf16[3,256,256]{2,1,0:T(8,128)(2,1)S(1)} %multiply_convert_fusion.refs_0_), channel_id=1, source_target_pairs={{0,64},{64,0},{1,65},{65,1},{2,66},{66,2},{3,67},{67,3},{4,68},{68... | collective-permute-start | bytes 1179656 | tf_op jit(solution)/shard_map/ppermute | solution.py:222
  32.3 0.0 collective-permute-done.1.refs_1_
  32.3 0.0 copy-start.4
  32.3 2.7 %collective-permute-start.3 = (bf16[3,256,256]{2,1,0:T(8,128)(2,1)S(1)}, bf16[3,256,256]{2,1,0:T(8,128)(2,1)S(1)}, u32[]{:S(2)}, u32[]{:S(2)}) collective-permute-start(bf16[3,256,256]{2,1,0:T(8,128)(2,1)S(1)} %collective-permute-done.1.refs_1_), channel_id=1, source_target_pairs={{0,64},{64,0},{1,65},{65,1},{2,66},{66,2},{3,67},{67,3},{4,68},{68... | collective-permute-start | bytes 1179656 | tf_op jit(solution)/shard_map/ppermute | solution.py:222
  35.1 8.0 %collective-permute-done.2.refs_2_ = bf16[3,256,256]{2,1,0:T(8,128)(2,1)S(1)} collective-permute-done((bf16[3,256,256]{2,1,0:T(8,128)(2,1)S(1)}, bf16[3,256,256]{2,1,0:T(8,128)(2,1)S(1)}, u32[]{:S(2)}, u32[]{:S(2)}) %collective-permute-start.2) | collective-permute-done | bytes 393248 | tf_op jit(solution)/shard_map/ppermute | solution.py:222
  43.1 6.0 %collective-permute-done.3.refs_3_ = bf16[3,256,256]{2,1,0:T(8,128)(2,1)S(1)} collective-permute-done((bf16[3,256,256]{2,1,0:T(8,128)(2,1)S(1)}, bf16[3,256,256]{2,1,0:T(8,128)(2,1)S(1)}, u32[]{:S(2)}, u32[]{:S(2)}) %collective-permute-start.3) | collective-permute-done | bytes 393248 | tf_op jit(solution)/shard_map/ppermute | solution.py:222
  49.2 0.0 copy-done.4
  49.2 1.1 pad_maximum_fusion
  50.3 1.9 %collective-permute-start.4 = (bf16[8,256,256]{2,1,0:T(8,128)(2,1)}, bf16[8,256,256]{2,1,0:T(8,128)(2,1)S(1)}, u32[]{:S(2)}, u32[]{:S(2)}) collective-permute-start(bf16[8,256,256]{2,1,0:T(8,128)(2,1)} %pad_maximum_fusion), channel_id=1, source_target_pairs={{0,32},{32,0},{1,33},{33,1},{2,34},{34,2},{3,35},{35,3},{4,36},{36... | collective-permute-start | bytes 3145736 | tf_op jit(solution)/shard_map/ppermute | solution.py:224
  52.2 0.9 slice.17
  53.1 0.8 pad_maximum_fusion.1
  54.0 2.4 %collective-permute-start.5 = (bf16[4,256,256]{2,1,0:T(8,128)(2,1)}, bf16[4,256,256]{2,1,0:T(8,128)(2,1)}, u32[]{:S(2)}, u32[]{:S(2)}) collective-permute-start(bf16[4,256,256]{2,1,0:T(8,128)(2,1)} %pad_maximum_fusion.1), channel_id=1, source_target_pairs={{0,32},{32,0},{1,33},{33,1},{2,34},{34,2},{3,35},{35,3},{4,36},{36... | collective-permute-start | bytes 1572872 | tf_op jit(solution)/shard_map/ppermute | solution.py:224
  56.4 0.1 pad_add_fusion.place_ref
  56.5 1.8 %collective-permute-done.5.refs_5_ = bf16[4,256,256]{2,1,0:T(8,128)(2,1)} collective-permute-done((bf16[4,256,256]{2,1,0:T(8,128)(2,1)}, bf16[4,256,256]{2,1,0:T(8,128)(2,1)}, u32[]{:S(2)}, u32[]{:S(2)}) %collective-permute-start.5) | collective-permute-done | bytes 524320 | tf_op jit(solution)/shard_map/ppermute | solution.py:224
  58.2 0.0 collective-permute-done.4.refs_4_
  58.2 0.0 all-to-all-done
  58.2 0.0 copy-done
  58.2 0.0 copy-done.2
  58.3 0.0 copy-start.5
  58.3 1.0 copy-done.5
  59.2 2.0 %gates.1 = bf16[256,1536]{1,0:T(8,128)(2,1)S(1)} custom-call(s32[3]{0:T(128)S(1)} %pad_add_fusion.place_ref, bf16[8,2,2,128,128]{4,3,2,1,0:T(8,128)(2,1)S(1)} %bitcast.20, bf16[3,256,256]{2,1,0:T(8,128)(2,1)S(1)} %multiply_convert_fusion.refs_0_, bf16[3,256,256]{2,1,0:T(8,128)(2,1)S(1)} %copy-done.5, ...), custom_call_target="tpu_custom_call" | custom-call | flops 800000000 | bytes 6000000 | tf_op jit(solution)/shard_map/gates/pallas_call | solution.py:107
  61.3 0.0 copy-start.7
  61.3 0.9 copy-done.7
  62.2 4.8 %all-to-all-start.1 = ((bf16[4,64,1536]{2,1,0:T(8,128)(2,1)}), bf16[4,64,1536]{2,1,0:T(8,128)(2,1)S(1)}, u32[]{:S(2)}, u32[]{:S(2)}) async-start(bf16[4,64,1536]{2,1,0:T(8,128)(2,1)} %bitcast.26), calls=%async_computation.1 | async-start | bytes 1572864 | tf_op jit(solution)/shard_map/all_to_all | solution.py:212
  67.0 1.9 %collective-permute-start.6 = (bf16[2,2,2,2,128,128]{5,4,3,2,1,0:T(8,128)(2,1)S(1)}, bf16[2,2,2,2,128,128]{5,4,3,2,1,0:T(8,128)(2,1)S(1)}, u32[]{:S(2)}, u32[]{:S(2)}) collective-permute-start(bf16[2,2,2,2,128,128]{5,4,3,2,1,0:T(8,128)(2,1)S(1)} %dynamic-slice_bitcast_fusion), channel_id=1, source_target_pairs={{0,32},{32,0},{1,33},{33,1},{2,34},{34,2},{3,35},{35,3},{4,36},{36... | collective-permute-start | bytes 1572872 | tf_op jit(solution)/shard_map/ppermute | solution.py:230
  69.0 1.9 %collective-permute-done.6.other_acts_ref = bf16[2,2,2,2,128,128]{5,4,3,2,1,0:T(8,128)(2,1)S(1)} collective-permute-done((bf16[2,2,2,2,128,128]{5,4,3,2,1,0:T(8,128)(2,1)S(1)}, bf16[2,2,2,2,128,128]{5,4,3,2,1,0:T(8,128)(2,1)S(1)}, u32[]{:S(2)}, u32[]{:S(2)}) %collective-permute-start.6) | collective-permute-done | bytes 524320 | tf_op jit(solution)/shard_map/ppermute | solution.py:230
  70.8 0.8 copy-done.9
  71.7 6.1 %all-to-all-done.1.parts_ref = bf16[4,64,1536]{2,1,0:T(8,128)(2,1)S(1)} async-done(((bf16[4,64,1536]{2,1,0:T(8,128)(2,1)}), bf16[4,64,1536]{2,1,0:T(8,128)(2,1)S(1)}, u32[]{:S(2)}, u32[]{:S(2)}) %all-to-all-start.1) | async-done | bytes 786464 | tf_op jit(solution)/shard_map/all_to_all | solution.py:212
  77.8 0.2 hidden_grads.1
  78.0 0.0 copy-start.1
  78.0 0.0 copy-start.3
  78.0 0.0 copy-start.6
  78.0 15.1 %all_to_all.20 = bf16[4,64,1536]{2,1,0:T(8,128)(2,1)S(1)} all-to-all(bf16[4,64,1536]{2,1,0:T(8,128)(2,1)S(1)} %hidden_grads.1), channel_id=1, replica_groups=mesh['yl'=2,'x1'=2,'x0'=2,'core'=2,'yh1'=2,'yh0'=2,'zh1'=2,'zh0'=2,'zl'=..., dimensions={0} | all-to-all | bytes 1572864 | tf_op jit(solution)/shard_map/all_to_all | solution.py:212
  93.1 1.8 %input_terms.1 = bf16[8,2,128,128]{3,2,1,0:T(8,128)(2,1)S(1)} custom-call(s32[3]{0:T(128)S(1)} %pad_add_fusion.place_ref, bf16[256,1536]{1,0:T(8,128)(2,1)S(1)} %bitcast.23, bf16[3,256,256]{2,1,0:T(8,128)(2,1)S(1)} %multiply_convert_fusion.refs_0_, bf16[3,256,256]{2,1,0:T(8,128)(2,1)S(1)} %copy-done.6, bf16[3,256,256]{2,1,0:T(8,128)(2,1)S(1)} %copy-done.1, ...), custom_call_target="tpu_custom_call" | custom-call | flops 540000000 | bytes 4000000 | tf_op jit(solution)/shard_map/input_terms/pallas_call | solution.py:162
  94.9 0.0 copy-start.8
  94.9 0.8 copy-done.8
  95.7 16.9 %all-to-all-start.3 = ((bf16[8,2,128,128]{3,2,1,0:T(8,128)(2,1)}), bf16[8,2,128,128]{3,2,1,0:T(8,128)(2,1)}, u32[]{:S(2)}, u32[]{:S(2)}) async-start(bf16[8,2,128,128]{3,2,1,0:T(8,128)(2,1)} %copy-done.8), calls=%async_computation.3 | async-start | bytes 1048576 | tf_op jit(solution)/shard_map/all_to_all | solution.py:212
  112.6 1.9 %collective-permute-start.9 = (bf16[256,1536]{1,0:T(8,128)(2,1)S(1)}, bf16[256,1536]{1,0:T(8,128)(2,1)S(1)}, u32[]{:S(2)}, u32[]{:S(2)}) collective-permute-start(bf16[256,1536]{1,0:T(8,128)(2,1)S(1)} %bitcast.24), channel_id=1, source_target_pairs={{0,32},{32,0},{1,33},{33,1},{2,34},{34,2},{3,35},{35,3},{4,36},{36... | collective-permute-start | bytes 2359304 | tf_op jit(solution)/shard_map/ppermute | solution.py:234
  114.5 2.3 %collective-permute-done.9.other_grads_ref = bf16[256,1536]{1,0:T(8,128)(2,1)S(1)} collective-permute-done((bf16[256,1536]{1,0:T(8,128)(2,1)S(1)}, bf16[256,1536]{1,0:T(8,128)(2,1)S(1)}, u32[]{:S(2)}, u32[]{:S(2)}) %collective-permute-start.9) | collective-permute-done | bytes 786464 | tf_op jit(solution)/shard_map/ppermute | solution.py:234
  116.8 1.0 copy-done.10
  117.8 2.2 %weight_terms.1 = (f32[3,256,256]{2,1,0:T(8,128)S(1)}, bf16[3,256,256]{2,1,0:T(8,128)(2,1)S(1)}, bf16[3,256,256]{2,1,0:T(8,128)(2,1)}, bf16[3,256,256]{2,1,0:T(8,128)(2,1)}) custom-call(s32[3]{0:T(128)S(1)} %pad_add_fusion.place_ref, bf16[8,2,2,128,128]{4,3,2,1,0:T(8,128)(2,1)S(1)} %bitcast.22, bf16[2,2,2,2,128,128]{5,4,3,2,1,0:T(8,128)(2,1)S(1)} %copy-done.10, ...), custom_call_target="tpu_custom_call" | custom-call | flops 800000000 | bytes 6000000 | tf_op jit(solution)/shard_map/weight_terms/pallas_call | solution.py:199
  120.0 1.9 %collective-permute-start.10 = (bf16[3,256,256]{2,1,0:T(8,128)(2,1)S(1)}, bf16[3,256,256]{2,1,0:T(8,128)(2,1)S(1)}, u32[]{:S(2)}, u32[]{:S(2)}) collective-permute-start(bf16[3,256,256]{2,1,0:T(8,128)(2,1)S(1)} %get-tuple-element.11), channel_id=1, source_target_pairs={{0,1},{1,0},{2,3},{3,2},{4,5},{5,4},{6,7},{7,6},{8,9},{9,8},{10,11... | collective-permute-start | bytes 1179656 | tf_op jit(solution)/shard_map/ppermute | solution.py:242
  121.9 2.3 %collective-permute-start.11 = (bf16[3,256,256]{2,1,0:T(8,128)(2,1)}, bf16[3,256,256]{2,1,0:T(8,128)(2,1)S(1)}, u32[]{:S(2)}, u32[]{:S(2)}) collective-permute-start(bf16[3,256,256]{2,1,0:T(8,128)(2,1)} %get-tuple-element.12), channel_id=1, source_target_pairs={{0,64},{64,0},{1,65},{65,1},{2,66},{66,2},{3,67},{67,3},{4,68},{68... | collective-permute-start | bytes 1179656 | tf_op jit(solution)/shard_map/ppermute | solution.py:243
  124.2 5.0 %collective-permute-start.12 = (bf16[3,256,256]{2,1,0:T(8,128)(2,1)}, bf16[3,256,256]{2,1,0:T(8,128)(2,1)S(1)}, u32[]{:S(2)}, u32[]{:S(2)}) collective-permute-start(bf16[3,256,256]{2,1,0:T(8,128)(2,1)} %get-tuple-element.13), channel_id=1, source_target_pairs={{0,65},{1,64},{64,1},{65,0},{2,67},{3,66},{66,3},{67,2},{4,69},{5,... | collective-permute-start | bytes 1179656 | tf_op jit(solution)/shard_map/ppermute | solution.py:244
  129.2 2.2 %all-to-all-done.3 = bf16[8,2,128,128]{3,2,1,0:T(8,128)(2,1)} async-done(((bf16[8,2,128,128]{3,2,1,0:T(8,128)(2,1)}), bf16[8,2,128,128]{3,2,1,0:T(8,128)(2,1)}, u32[]{:S(2)}, u32[]{:S(2)}) %all-to-all-start.3) | async-done | bytes 524320 | tf_op jit(solution)/shard_map/all_to_all | solution.py:212
  131.4 1.1 reduce_sum.12
  132.5 4.7 %collective-permute-start.7 = (bf16[128,128]{1,0:T(8,128)(2,1)S(1)}, bf16[128,128]{1,0:T(8,128)(2,1)S(1)}, u32[]{:S(2)}, u32[]{:S(2)}) collective-permute-start(bf16[128,128]{1,0:T(8,128)(2,1)S(1)} %get-tuple-element.14), channel_id=1, source_target_pairs={{0,0},{8,1},{2,2},{10,3},{4,4},{12,5},{6,6},{14,7},{128,8},{136,9}... | collective-permute-start | bytes 98312 | tf_op jit(solution)/shard_map/ppermute | solution.py:238
  137.2 2.3 %collective-permute-start.8 = (bf16[128,128]{1,0:T(8,128)(2,1)S(1)}, bf16[128,128]{1,0:T(8,128)(2,1)S(1)}, u32[]{:S(2)}, u32[]{:S(2)}) collective-permute-start(bf16[128,128]{1,0:T(8,128)(2,1)S(1)} %get-tuple-element.15), channel_id=1, source_target_pairs={{16,0},{24,1},{18,2},{26,3},{20,4},{28,5},{22,6},{30,7},{144,8},{1... | collective-permute-start | bytes 98312 | tf_op jit(solution)/shard_map/ppermute | solution.py:238
  139.5 5.9 %collective-permute-done.7 = bf16[128,128]{1,0:T(8,128)(2,1)S(1)} collective-permute-done((bf16[128,128]{1,0:T(8,128)(2,1)S(1)}, bf16[128,128]{1,0:T(8,128)(2,1)S(1)}, u32[]{:S(2)}, u32[]{:S(2)}) %collective-permute-start.7) | collective-permute-done | bytes 32800 | tf_op jit(solution)/shard_map/ppermute | solution.py:238
  145.4 4.9 %collective-permute-done.8 = bf16[128,128]{1,0:T(8,128)(2,1)S(1)} collective-permute-done((bf16[128,128]{1,0:T(8,128)(2,1)S(1)}, bf16[128,128]{1,0:T(8,128)(2,1)S(1)}, u32[]{:S(2)}, u32[]{:S(2)}) %collective-permute-start.8) | collective-permute-done | bytes 32800 | tf_op jit(solution)/shard_map/ppermute | solution.py:238
  150.3 0.6 add_convert_fusion
  150.9 0.0 collective-permute-done.10
  150.9 0.0 collective-permute-done.11
  150.9 0.0 collective-permute-done.12
  150.9 1.0 convert_add_fusion
  (11 shorter events, 0.1 us)
Async XLA Ops:
  0.6 5.0 %copy-start.11 = (bf16[3,1,256]{2,0,1:T(4,128)(2,1)S(1)}, bf16[3,1,256]{2,0,1:T(4,128)(2,1)}, u32[]{:S(2)}) copy-start(bf16[3,1,256]{2,0,1:T(4,128)(2,1)} %param.7) | copy-start | bytes 4612
  1.4 10.5 %collective-permute-start = (bf16[2,128,128]{2,1,0:T(8,128)(2,1)S(1)}, bf16[2,128,128]{2,1,0:T(8,128)(2,1)S(1)}, u32[]{:S(2)}, u32[]{:S(2)}) collective-permute-start(bf16[2,128,128]{2,1,0:T(8,128)(2,1)S(1)} %pad_maximum_fusion.2), channel_id=1, source_target_pairs={{0,0},{1,8},{2,2},{3,10},{4,4},{5,12},{6,6},{7,14},{8,128},{9,136}... | collective-permute-start | bytes 196616 | tf_op jit(solution)/shard_map/ppermute | solution.py:219
  6.7 25.6 %collective-permute-start.1 = (bf16[3,256,256]{2,1,0:T(8,128)(2,1)S(1)}, bf16[3,256,256]{2,1,0:T(8,128)(2,1)S(1)}, u32[]{:S(2)}, u32[]{:S(2)}) collective-permute-start(bf16[3,256,256]{2,1,0:T(8,128)(2,1)S(1)} %multiply_convert_fusion.refs_0_), channel_id=1, source_target_pairs={{0,1},{1,0},{2,3},{3,2},{4,5},{5,4},{6,7},{7,6},{8,9},{9,8},{10,11... | collective-permute-start | bytes 1179656 | tf_op jit(solution)/shard_map/ppermute | solution.py:221
  13.0 45.2 %all-to-all-start = ((bf16[16,2,128,128]{3,2,1,0:T(8,128)(2,1)}), bf16[16,2,128,128]{3,2,1,0:T(8,128)(2,1)S(1)}, u32[]{:S(2)}, u32[]{:S(2)}) async-start(bf16[16,2,128,128]{3,2,1,0:T(8,128)(2,1)} %spread.1), calls=%async_computation | async-start | bytes 2097152 | tf_op jit(solution)/shard_map/all_to_all | solution.py:212
  29.2 13.9 %collective-permute-start.2 = (bf16[3,256,256]{2,1,0:T(8,128)(2,1)S(1)}, bf16[3,256,256]{2,1,0:T(8,128)(2,1)S(1)}, u32[]{:S(2)}, u32[]{:S(2)}) collective-permute-start(bf16[3,256,256]{2,1,0:T(8,128)(2,1)S(1)} %multiply_convert_fusion.refs_0_), channel_id=1, source_target_pairs={{0,64},{64,0},{1,65},{65,1},{2,66},{66,2},{3,67},{67,3},{4,68},{68... | collective-permute-start | bytes 1179656 | tf_op jit(solution)/shard_map/ppermute | solution.py:222
  32.3 16.9 %copy-start.4 = (bf16[3,256,256]{2,1,0:T(8,128)(2,1)}, bf16[3,256,256]{2,1,0:T(8,128)(2,1)S(1)}, u32[]{:S(2)}) copy-start(bf16[3,256,256]{2,1,0:T(8,128)(2,1)S(1)} %collective-permute-done.1.refs_1_) | copy-start | bytes 1179652
  32.3 16.8 %collective-permute-start.3 = (bf16[3,256,256]{2,1,0:T(8,128)(2,1)S(1)}, bf16[3,256,256]{2,1,0:T(8,128)(2,1)S(1)}, u32[]{:S(2)}, u32[]{:S(2)}) collective-permute-start(bf16[3,256,256]{2,1,0:T(8,128)(2,1)S(1)} %collective-permute-done.1.refs_1_), channel_id=1, source_target_pairs={{0,64},{64,0},{1,65},{65,1},{2,66},{66,2},{3,67},{67,3},{4,68},{68... | collective-permute-start | bytes 1179656 | tf_op jit(solution)/shard_map/ppermute | solution.py:222
  43.1 15.1 %copy-start = (bf16[3,256,256]{2,1,0:T(8,128)(2,1)}, bf16[3,256,256]{2,1,0:T(8,128)(2,1)S(1)}, u32[]{:S(2)}) copy-start(bf16[3,256,256]{2,1,0:T(8,128)(2,1)S(1)} %collective-permute-done.2.refs_2_) | copy-start | bytes 1179652
  49.2 9.1 %copy-start.2 = (bf16[3,256,256]{2,1,0:T(8,128)(2,1)}, bf16[3,256,256]{2,1,0:T(8,128)(2,1)S(1)}, u32[]{:S(2)}) copy-start(bf16[3,256,256]{2,1,0:T(8,128)(2,1)S(1)} %collective-permute-done.3.refs_3_) | copy-start | bytes 1179652
  50.3 7.9 %collective-permute-start.4 = (bf16[8,256,256]{2,1,0:T(8,128)(2,1)}, bf16[8,256,256]{2,1,0:T(8,128)(2,1)S(1)}, u32[]{:S(2)}, u32[]{:S(2)}) collective-permute-start(bf16[8,256,256]{2,1,0:T(8,128)(2,1)} %pad_maximum_fusion), channel_id=1, source_target_pairs={{0,32},{32,0},{1,33},{33,1},{2,34},{34,2},{3,35},{35,3},{4,36},{36... | collective-permute-start | bytes 3145736 | tf_op jit(solution)/shard_map/ppermute | solution.py:224
  54.0 4.3 %collective-permute-start.5 = (bf16[4,256,256]{2,1,0:T(8,128)(2,1)}, bf16[4,256,256]{2,1,0:T(8,128)(2,1)}, u32[]{:S(2)}, u32[]{:S(2)}) collective-permute-start(bf16[4,256,256]{2,1,0:T(8,128)(2,1)} %pad_maximum_fusion.1), channel_id=1, source_target_pairs={{0,32},{32,0},{1,33},{33,1},{2,34},{34,2},{3,35},{35,3},{4,36},{36... | collective-permute-start | bytes 1572872 | tf_op jit(solution)/shard_map/ppermute | solution.py:224
  58.3 1.0 copy-start.5
  61.3 0.9 copy-start.7
  62.2 15.6 %all-to-all-start.1 = ((bf16[4,64,1536]{2,1,0:T(8,128)(2,1)}), bf16[4,64,1536]{2,1,0:T(8,128)(2,1)S(1)}, u32[]{:S(2)}, u32[]{:S(2)}) async-start(bf16[4,64,1536]{2,1,0:T(8,128)(2,1)} %bitcast.26), calls=%async_computation.1 | async-start | bytes 1572864 | tf_op jit(solution)/shard_map/all_to_all | solution.py:212
  67.0 3.8 %collective-permute-start.6 = (bf16[2,2,2,2,128,128]{5,4,3,2,1,0:T(8,128)(2,1)S(1)}, bf16[2,2,2,2,128,128]{5,4,3,2,1,0:T(8,128)(2,1)S(1)}, u32[]{:S(2)}, u32[]{:S(2)}) collective-permute-start(bf16[2,2,2,2,128,128]{5,4,3,2,1,0:T(8,128)(2,1)S(1)} %dynamic-slice_bitcast_fusion), channel_id=1, source_target_pairs={{0,32},{32,0},{1,33},{33,1},{2,34},{34,2},{3,35},{35,3},{4,36},{36... | collective-permute-start | bytes 1572872 | tf_op jit(solution)/shard_map/ppermute | solution.py:230
  70.8 0.8 copy-start.9
  78.0 15.1 %copy-start.1 = (bf16[3,256,256]{2,1,0:T(8,128)(2,1)S(1)}, bf16[3,256,256]{2,1,0:T(8,128)(2,1)}, u32[]{:S(2)}) copy-start(bf16[3,256,256]{2,1,0:T(8,128)(2,1)} %copy-done) | copy-start | bytes 1179652
  78.0 15.1 %copy-start.3 = (bf16[3,256,256]{2,1,0:T(8,128)(2,1)S(1)}, bf16[3,256,256]{2,1,0:T(8,128)(2,1)}, u32[]{:S(2)}) copy-start(bf16[3,256,256]{2,1,0:T(8,128)(2,1)} %copy-done.2) | copy-start | bytes 1179652
  78.0 15.1 %copy-start.6 = (bf16[3,256,256]{2,1,0:T(8,128)(2,1)S(1)}, bf16[3,256,256]{2,1,0:T(8,128)(2,1)}, u32[]{:S(2)}) copy-start(bf16[3,256,256]{2,1,0:T(8,128)(2,1)} %copy-done.4) | copy-start | bytes 1179652
  94.9 0.8 copy-start.8
  95.7 35.7 %all-to-all-start.3 = ((bf16[8,2,128,128]{3,2,1,0:T(8,128)(2,1)}), bf16[8,2,128,128]{3,2,1,0:T(8,128)(2,1)}, u32[]{:S(2)}, u32[]{:S(2)}) async-start(bf16[8,2,128,128]{3,2,1,0:T(8,128)(2,1)} %copy-done.8), calls=%async_computation.3 | async-start | bytes 1048576 | tf_op jit(solution)/shard_map/all_to_all | solution.py:212
  112.6 4.2 %collective-permute-start.9 = (bf16[256,1536]{1,0:T(8,128)(2,1)S(1)}, bf16[256,1536]{1,0:T(8,128)(2,1)S(1)}, u32[]{:S(2)}, u32[]{:S(2)}) collective-permute-start(bf16[256,1536]{1,0:T(8,128)(2,1)S(1)} %bitcast.24), channel_id=1, source_target_pairs={{0,32},{32,0},{1,33},{33,1},{2,34},{34,2},{3,35},{35,3},{4,36},{36... | collective-permute-start | bytes 2359304 | tf_op jit(solution)/shard_map/ppermute | solution.py:234
  116.8 1.0 copy-start.10
  120.0 30.9 %collective-permute-start.10 = (bf16[3,256,256]{2,1,0:T(8,128)(2,1)S(1)}, bf16[3,256,256]{2,1,0:T(8,128)(2,1)S(1)}, u32[]{:S(2)}, u32[]{:S(2)}) collective-permute-start(bf16[3,256,256]{2,1,0:T(8,128)(2,1)S(1)} %get-tuple-element.11), channel_id=1, source_target_pairs={{0,1},{1,0},{2,3},{3,2},{4,5},{5,4},{6,7},{7,6},{8,9},{9,8},{10,11... | collective-permute-start | bytes 1179656 | tf_op jit(solution)/shard_map/ppermute | solution.py:242
  121.9 29.0 %collective-permute-start.11 = (bf16[3,256,256]{2,1,0:T(8,128)(2,1)}, bf16[3,256,256]{2,1,0:T(8,128)(2,1)S(1)}, u32[]{:S(2)}, u32[]{:S(2)}) collective-permute-start(bf16[3,256,256]{2,1,0:T(8,128)(2,1)} %get-tuple-element.12), channel_id=1, source_target_pairs={{0,64},{64,0},{1,65},{65,1},{2,66},{66,2},{3,67},{67,3},{4,68},{68... | collective-permute-start | bytes 1179656 | tf_op jit(solution)/shard_map/ppermute | solution.py:243
  124.2 26.7 %collective-permute-start.12 = (bf16[3,256,256]{2,1,0:T(8,128)(2,1)}, bf16[3,256,256]{2,1,0:T(8,128)(2,1)S(1)}, u32[]{:S(2)}, u32[]{:S(2)}) collective-permute-start(bf16[3,256,256]{2,1,0:T(8,128)(2,1)} %get-tuple-element.13), channel_id=1, source_target_pairs={{0,65},{1,64},{64,1},{65,0},{2,67},{3,66},{66,3},{67,2},{4,69},{5,... | collective-permute-start | bytes 1179656 | tf_op jit(solution)/shard_map/ppermute | solution.py:244
  132.5 12.9 %collective-permute-start.7 = (bf16[128,128]{1,0:T(8,128)(2,1)S(1)}, bf16[128,128]{1,0:T(8,128)(2,1)S(1)}, u32[]{:S(2)}, u32[]{:S(2)}) collective-permute-start(bf16[128,128]{1,0:T(8,128)(2,1)S(1)} %get-tuple-element.14), channel_id=1, source_target_pairs={{0,0},{8,1},{2,2},{10,3},{4,4},{12,5},{6,6},{14,7},{128,8},{136,9}... | collective-permute-start | bytes 98312 | tf_op jit(solution)/shard_map/ppermute | solution.py:238
  137.2 13.0 %collective-permute-start.8 = (bf16[128,128]{1,0:T(8,128)(2,1)S(1)}, bf16[128,128]{1,0:T(8,128)(2,1)S(1)}, u32[]{:S(2)}, u32[]{:S(2)}) collective-permute-start(bf16[128,128]{1,0:T(8,128)(2,1)S(1)} %get-tuple-element.15), channel_id=1, source_target_pairs={{16,0},{24,1},{18,2},{26,3},{20,4},{28,5},{22,6},{30,7},{144,8},{1... | collective-permute-start | bytes 98312 | tf_op jit(solution)/shard_map/ppermute | solution.py:238

commit v17 on v15

--- a/solution.py
+++ b/solution.py
@@ -12,8 +12,8 @@
 ROW = ("yl", "x1", "x0", "core")
 COL = ("yh1", "yh0", "zh1", "zh0", "zl")
 AXES = ROW + COL
-SPREAD = ("zh1", "zh0", "yh0")
-GATHER = SPREAD + ("yh1",)
+SPREAD = ("yh0", "zh1", "zh0")
+GATHER = ("yh1",) + SPREAD
 REST = ("yl", "x1")
 SWAP = [(0, 1), (1, 0)]
 TOK = 128
@@ -49,7 +49,7 @@
     core, x0 = place_ref[0], place_ref[1]
     core = core if f < 4 else 1 - core
     x0 = x0 if f % 4 < 2 else 1 - x0
-    return 4 * x0 + 2 * core + f % 2
+    return 4 * (f % 2) + 2 * x0 + core
 
 
 def half(place_ref, t):
@@ -82,7 +82,7 @@
     for p in range(2):
         for t in range(2):
             for f in range(8):
-                block = acts_ref[chunk(place_ref, f), half(place_ref, t), p]
+                block = acts_ref[half(place_ref, t), chunk(place_ref, f), p]
                 wide_ref[p, pl.ds(t * TOK, TOK), pl.ds(f * TOK, TOK)] = block
     for p in range(3):
         for j in range(2):
@@ -167,9 +167,9 @@
             for f in range(4):
                 x0 = place_ref[1] if f < 2 else 1 - place_ref[1]
                 cols = pl.ds(f * TOK, TOK)
-                mine = acts_ref[chunk(place_ref, f), half(place_ref, t), p]
+                mine = acts_ref[half(place_ref, t), chunk(place_ref, f), p]
                 wide_ref[p, pl.ds(t * TOK, TOK), cols] = mine
-                wide_ref[p, pl.ds(TOKENS + t * TOK, TOK), cols] = other_acts_ref[x0, f % 2, half(place_ref, t), p]
+                wide_ref[p, pl.ds(TOKENS + t * TOK, TOK), cols] = other_acts_ref[half(place_ref, t), f % 2, x0, p]
     for side in (1, 0):
         for p in range(3):
             for j in range(2):
@@ -211,11 +211,11 @@
     acts, w_z = lax.optimization_barrier((acts, w_z))
     weights = [w, w_z] + [lax.ppermute(block, "x0", SWAP) for block in (w, w_z)]
     weights += [lax.ppermute(block, "core", SWAP) for block in weights]
-    acts = exchange(acts, GATHER).reshape(8, 2, 2, TOK, TOK)
+    acts = exchange(acts, GATHER).reshape(2, 8, 2, TOK, TOK)
 
     parts = gates(place, acts, *weights)
     other_acts = acts.reshape(2, 2, 2, 2, 2, TOK, TOK)
-    other_acts = lax.dynamic_index_in_dim(other_acts, 1 - place[0], axis=1, keepdims=False)
+    other_acts = lax.dynamic_index_in_dim(other_acts, 1 - place[0], axis=3, keepdims=False)
     other_acts = lax.ppermute(other_acts, "core", SWAP)
     parts = exchange(parts.reshape(4, SHARE, GRADS), REST)
     parts, other_acts = lax.optimization_barrier((parts, other_acts))

time: 147 us -> 146 us (level)
  the two profiles are of different devices: /device:TPU:44 before, /device:TPU:4 now
where the time goes in v17:
time: 146 us; the launch traced here: 145 us
  starting transfers between devices  71 us (49%)
  waiting for transfers between devices  43.2 us (30%)
  blocking collectives  15.1 us (10%)
  Pallas kernels  9.38 us (6%)
  other arithmetic  4.62 us (3%)
    all_to_all x3, starting transfers between devices, exchange(): return lax.all_to_all(pieces, axes, split_axis=0, concat_axis=0, tiled=True)  27.1 us
    all_to_all x3, waiting for transfers between devices, exchange(): return lax.all_to_all(pieces, axes, split_axis=0, concat_axis=0, tiled=True)  16.5 us
    all_to_all x1, blocking collectives, exchange(): return lax.all_to_all(pieces, axes, split_axis=0, concat_axis=0, tiled=True)  15.1 us
    ppermute x2, waiting for transfers between devices, local(): lax.ppermute(dx[i], AXES, [(b, a) for a, b in there[i]])  9.16 us
    ppermute x4, starting transfers between devices, local(): weights += [lax.ppermute(block, 'core', SWAP) for block in weights]  8.15 us
    ppermute x2, waiting for transfers between devices, local(): weights = [w, w_z] + [lax.ppermute(block, 'x0', SWAP) for block in (w, w_z)]  7.47 us
    ppermute x1, starting transfers between devices, local(): acts = spread(lax.ppermute(jnp.stack([inputs, out_grad]), AXES, there[0]))  6.88 us
    ppermute x2, starting transfers between devices, local(): weights = [w, w_z] + [lax.ppermute(block, 'x0', SWAP) for block in (w, w_z)]  5.84 us
  transfers between devices with their start and end apart: 18, of which 11 were waited for; matrix products, arithmetic and copies ran while one was open for 1% of the time, Pallas kernels for 2%

profile of v17, /device:TPU:4, one launch (start us, length us, event | category | flops | bytes accessed | tf_op | source)
XLA Modules:
  0.0 145.1 jit_solution(18129536502348695120)
XLA Ops:
  0.6 0.7 bitcast_convert_fusion
  1.3 0.0 copy-start.6
  1.3 0.0 copy-start.7
  1.3 1.1 multiply_convert_fusion.refs_0_
  2.4 4.3 %collective-permute-start.1 = (bf16[3,256,256]{2,1,0:T(8,128)(2,1)S(1)}, bf16[3,256,256]{2,1,0:T(8,128)(2,1)S(1)}, u32[]{:S(2)}, u32[]{:S(2)}) collective-permute-start(bf16[3,256,256]{2,1,0:T(8,128)(2,1)S(1)} %multiply_convert_fusion.refs_0_), channel_id=1, source_target_pairs={{0,1},{1,0},{2,3},{3,2},{4,5},{5,4},{6,7},{7,6},{8,9},{9,8},{10,11... | collective-permute-start | bytes 1179656 | tf_op jit(solution)/shard_map/ppermute | solution.py:210
  6.7 0.0 copy-done.6
  6.7 0.0 copy-done.7
  6.7 6.9 %collective-permute-start = (bf16[2,128,128]{2,1,0:T(8,128)(2,1)S(1)}, bf16[2,128,128]{2,1,0:T(8,128)(2,1)S(1)}, u32[]{:S(2)}, u32[]{:S(2)}) collective-permute-start(bf16[2,128,128]{2,1,0:T(8,128)(2,1)S(1)} %pad_maximum_fusion), channel_id=1, source_target_pairs={{0,0},{1,8},{2,2},{3,10},{4,4},{5,12},{6,6},{7,14},{8,128},{9,136}... | collective-permute-start | bytes 196616 | tf_op jit(solution)/shard_map/ppermute | solution.py:208
  13.6 4.2 %collective-permute-done.acts_ref = bf16[2,128,128]{2,1,0:T(8,128)(2,1)S(1)} collective-permute-done((bf16[2,128,128]{2,1,0:T(8,128)(2,1)S(1)}, bf16[2,128,128]{2,1,0:T(8,128)(2,1)S(1)}, u32[]{:S(2)}, u32[]{:S(2)}) %collective-permute-start) | collective-permute-done | bytes 65568 | tf_op jit(solution)/shard_map/ppermute | solution.py:208
  17.8 1.2 spread.1
  19.0 0.0 collective-permute-done.1.refs_1_
  19.0 14.6 %all-to-all-start = ((bf16[16,2,128,128]{3,2,1,0:T(8,128)(2,1)}), bf16[16,2,128,128]{3,2,1,0:T(8,128)(2,1)S(1)}, u32[]{:S(2)}, u32[]{:S(2)}) async-start(bf16[16,2,128,128]{3,2,1,0:T(8,128)(2,1)} %spread.1), calls=%async_computation | async-start | bytes 2097152 | tf_op jit(solution)/shard_map/all_to_all | solution.py:201
  33.6 3.2 %collective-permute-start.2 = (bf16[3,256,256]{2,1,0:T(8,128)(2,1)S(1)}, bf16[3,256,256]{2,1,0:T(8,128)(2,1)S(1)}, u32[]{:S(2)}, u32[]{:S(2)}) collective-permute-start(bf16[3,256,256]{2,1,0:T(8,128)(2,1)S(1)} %multiply_convert_fusion.refs_0_), channel_id=1, source_target_pairs={{0,64},{64,0},{1,65},{65,1},{2,66},{66,2},{3,67},{67,3},{4,68},{68... | collective-permute-start | bytes 1179656 | tf_op jit(solution)/shard_map/ppermute | solution.py:212
  36.8 2.7 %collective-permute-start.3 = (bf16[3,256,256]{2,1,0:T(8,128)(2,1)S(1)}, bf16[3,256,256]{2,1,0:T(8,128)(2,1)S(1)}, u32[]{:S(2)}, u32[]{:S(2)}) collective-permute-start(bf16[3,256,256]{2,1,0:T(8,128)(2,1)S(1)} %collective-permute-done.1.refs_1_), channel_id=1, source_target_pairs={{0,64},{64,0},{1,65},{65,1},{2,66},{66,2},{3,67},{67,3},{4,68},{68... | collective-permute-start | bytes 1179656 | tf_op jit(solution)/shard_map/ppermute | solution.py:212
  39.4 1.9 %collective-permute-start.4 = (bf16[3,256,256]{2,1,0:T(8,128)(2,1)S(1)}, bf16[3,256,256]{2,1,0:T(8,128)(2,1)S(1)}, u32[]{:S(2)}, u32[]{:S(2)}) collective-permute-start(bf16[3,256,256]{2,1,0:T(8,128)(2,1)S(1)} %multiply_convert_fusion.refs_0_), channel_id=1, source_target_pairs={{0,32},{32,0},{1,33},{33,1},{2,34},{34,2},{3,35},{35,3},{4,36},{36... | collective-permute-start | bytes 1179656 | tf_op jit(solution)/shard_map/ppermute | solution.py:213
  41.4 2.4 %collective-permute-start.5 = (bf16[3,256,256]{2,1,0:T(8,128)(2,1)S(1)}, bf16[3,256,256]{2,1,0:T(8,128)(2,1)S(1)}, u32[]{:S(2)}, u32[]{:S(2)}) collective-permute-start(bf16[3,256,256]{2,1,0:T(8,128)(2,1)S(1)} %collective-permute-done.1.refs_1_), channel_id=1, source_target_pairs={{0,32},{32,0},{1,33},{33,1},{2,34},{34,2},{3,35},{35,3},{4,36},{36... | collective-permute-start | bytes 1179656 | tf_op jit(solution)/shard_map/ppermute | solution.py:213
  43.8 3.7 %collective-permute-done.2.refs_2_ = bf16[3,256,256]{2,1,0:T(8,128)(2,1)S(1)} collective-permute-done((bf16[3,256,256]{2,1,0:T(8,128)(2,1)S(1)}, bf16[3,256,256]{2,1,0:T(8,128)(2,1)S(1)}, u32[]{:S(2)}, u32[]{:S(2)}) %collective-permute-start.2) | collective-permute-done | bytes 393248 | tf_op jit(solution)/shard_map/ppermute | solution.py:212
  47.5 1.9 %collective-permute-start.6 = (bf16[3,256,256]{2,1,0:T(8,128)(2,1)S(1)}, bf16[3,256,256]{2,1,0:T(8,128)(2,1)}, u32[]{:S(2)}, u32[]{:S(2)}) collective-permute-start(bf16[3,256,256]{2,1,0:T(8,128)(2,1)S(1)} %collective-permute-done.2.refs_2_), channel_id=1, source_target_pairs={{0,32},{32,0},{1,33},{33,1},{2,34},{34,2},{3,35},{35,3},{4,36},{36... | collective-permute-start | bytes 1179656 | tf_op jit(solution)/shard_map/ppermute | solution.py:213
  49.4 3.7 %collective-permute-done.3.refs_3_ = bf16[3,256,256]{2,1,0:T(8,128)(2,1)S(1)} collective-permute-done((bf16[3,256,256]{2,1,0:T(8,128)(2,1)S(1)}, bf16[3,256,256]{2,1,0:T(8,128)(2,1)S(1)}, u32[]{:S(2)}, u32[]{:S(2)}) %collective-permute-start.3) | collective-permute-done | bytes 393248 | tf_op jit(solution)/shard_map/ppermute | solution.py:212
  53.2 1.9 %collective-permute-start.7 = (bf16[3,256,256]{2,1,0:T(8,128)(2,1)S(1)}, bf16[3,256,256]{2,1,0:T(8,128)(2,1)}, u32[]{:S(2)}, u32[]{:S(2)}) collective-permute-start(bf16[3,256,256]{2,1,0:T(8,128)(2,1)S(1)} %collective-permute-done.3.refs_3_), channel_id=1, source_target_pairs={{0,32},{32,0},{1,33},{33,1},{2,34},{34,2},{3,35},{35,3},{4,36},{36... | collective-permute-start | bytes 1179656 | tf_op jit(solution)/shard_map/ppermute | solution.py:213
  55.1 0.1 pad_add_fusion.place_ref
  55.2 0.0 collective-permute-done.4.refs_4_
  55.2 0.0 copy-start
  55.2 0.0 collective-permute-done.6.refs_6_
  55.2 0.0 collective-permute-done.5.refs_5_
  55.2 0.0 copy-start.2
  55.2 1.7 %collective-permute-done.7.refs_7_ = bf16[3,256,256]{2,1,0:T(8,128)(2,1)} collective-permute-done((bf16[3,256,256]{2,1,0:T(8,128)(2,1)S(1)}, bf16[3,256,256]{2,1,0:T(8,128)(2,1)}, u32[]{:S(2)}, u32[]{:S(2)}) %collective-permute-start.7) | collective-permute-done | bytes 393248 | tf_op jit(solution)/shard_map/ppermute | solution.py:213
  56.9 5.7 %all-to-all-done = bf16[16,2,128,128]{3,2,1,0:T(8,128)(2,1)S(1)} async-done(((bf16[16,2,128,128]{3,2,1,0:T(8,128)(2,1)}), bf16[16,2,128,128]{3,2,1,0:T(8,128)(2,1)S(1)}, u32[]{:S(2)}, u32[]{:S(2)}) %all-to-all-start) | async-done | bytes 1048608 | tf_op jit(solution)/shard_map/all_to_all | solution.py:201
  62.6 3.0 %gates.1 = bf16[256,1536]{1,0:T(8,128)(2,1)} custom-call(s32[3]{0:T(128)S(1)} %pad_add_fusion.place_ref, bf16[2,8,2,128,128]{4,3,2,1,0:T(8,128)(2,1)S(1)} %bitcast.20, bf16[3,256,256]{2,1,0:T(8,128)(2,1)S(1)} %multiply_convert_fusion.refs_0_, bf16[3,256,256]{2,1,0:T(8,128)(2,1)S(1)} %collective-permute-done.1.refs_1_, ...), custom_call_target="tpu_custom_call" | custom-call | flops 800000000 | bytes 6000000 | tf_op jit(solution)/shard_map/gates/pallas_call | solution.py:96
  65.6 0.0 copy-done
  65.6 0.0 copy-done.2
  65.6 8.2 %all-to-all-start.1 = ((bf16[4,64,1536]{2,1,0:T(8,128)(2,1)}), bf16[4,64,1536]{2,1,0:T(8,128)(2,1)S(1)}, u32[]{:S(2)}, u32[]{:S(2)}) async-start(bf16[4,64,1536]{2,1,0:T(8,128)(2,1)} %bitcast.7), calls=%async_computation.1 | async-start | bytes 1572864 | tf_op jit(solution)/shard_map/all_to_all | solution.py:201
  73.9 1.9 %collective-permute-start.8 = (bf16[2,2,2,2,128,128]{5,4,3,2,1,0:T(8,128)(2,1)S(1)}, bf16[2,2,2,2,128,128]{5,4,3,2,1,0:T(8,128)(2,1)S(1)}, u32[]{:S(2)}, u32[]{:S(2)}) collective-permute-start(bf16[2,2,2,2,128,128]{5,4,3,2,1,0:T(8,128)(2,1)S(1)} %dynamic-slice_bitcast_fusion), channel_id=1, source_target_pairs={{0,32},{32,0},{1,33},{33,1},{2,34},{34,2},{3,35},{35,3},{4,36},{36... | collective-permute-start | bytes 1572872 | tf_op jit(solution)/shard_map/ppermute | solution.py:219
  75.8 1.9 %collective-permute-done.8.other_acts_ref = bf16[2,2,2,2,128,128]{5,4,3,2,1,0:T(8,128)(2,1)S(1)} collective-permute-done((bf16[2,2,2,2,128,128]{5,4,3,2,1,0:T(8,128)(2,1)S(1)}, bf16[2,2,2,2,128,128]{5,4,3,2,1,0:T(8,128)(2,1)S(1)}, u32[]{:S(2)}, u32[]{:S(2)}) %collective-permute-start.8) | collective-permute-done | bytes 524320 | tf_op jit(solution)/shard_map/ppermute | solution.py:219
  77.7 0.0 copy-start.4
  77.7 0.8 copy-done.4
  78.5 5.3 %all-to-all-done.1.parts_ref = bf16[4,64,1536]{2,1,0:T(8,128)(2,1)S(1)} async-done(((bf16[4,64,1536]{2,1,0:T(8,128)(2,1)}), bf16[4,64,1536]{2,1,0:T(8,128)(2,1)S(1)}, u32[]{:S(2)}, u32[]{:S(2)}) %all-to-all-start.1) | async-done | bytes 786464 | tf_op jit(solution)/shard_map/all_to_all | solution.py:201
  83.8 0.2 hidden_grads.1
  84.0 0.0 copy-start.1
  84.0 0.0 copy-start.3
  84.0 15.1 %all_to_all.20 = bf16[4,64,1536]{2,1,0:T(8,128)(2,1)S(1)} all-to-all(bf16[4,64,1536]{2,1,0:T(8,128)(2,1)S(1)} %hidden_grads.1), channel_id=1, replica_groups=mesh['yl'=2,'x1'=2,'x0'=2,'core'=2,'yh1'=2,'yh0'=2,'zh1'=2,'zh0'=2,'zl'=..., dimensions={0} | all-to-all | bytes 1572864 | tf_op jit(solution)/shard_map/all_to_all | solution.py:201
  99.1 0.0 copy-done.1
  99.1 0.0 copy-done.3
  99.1 2.7 %input_terms.1 = bf16[8,2,128,128]{3,2,1,0:T(8,128)(2,1)} custom-call(s32[3]{0:T(128)S(1)} %pad_add_fusion.place_ref, bf16[256,1536]{1,0:T(8,128)(2,1)S(1)} %bitcast.23, bf16[3,256,256]{2,1,0:T(8,128)(2,1)S(1)} %multiply_convert_fusion.refs_0_, bf16[3,256,256]{2,1,0:T(8,128)(2,1)S(1)} %collective-permute-done.1.refs_1_, ...), custom_call_target="tpu_custom_call" | custom-call | flops 540000000 | bytes 4000000 | tf_op jit(solution)/shard_map/input_terms/pallas_call | solution.py:151
  101.8 0.0 copy-start.5
  101.8 4.3 %all-to-all-start.3 = ((bf16[8,2,128,128]{3,2,1,0:T(8,128)(2,1)}), bf16[8,2,128,128]{3,2,1,0:T(8,128)(2,1)}, u32[]{:S(2)}, u32[]{:S(2)}) async-start(bf16[8,2,128,128]{3,2,1,0:T(8,128)(2,1)} %input_terms.1), calls=%async_computation.3 | async-start | bytes 1048576 | tf_op jit(solution)/shard_map/all_to_all | solution.py:201
  106.1 1.9 %collective-permute-start.11 = (bf16[256,1536]{1,0:T(8,128)(2,1)S(1)}, bf16[256,1536]{1,0:T(8,128)(2,1)S(1)}, u32[]{:S(2)}, u32[]{:S(2)}) collective-permute-start(bf16[256,1536]{1,0:T(8,128)(2,1)S(1)} %bitcast.24), channel_id=1, source_target_pairs={{0,32},{32,0},{1,33},{33,1},{2,34},{34,2},{3,35},{35,3},{4,36},{36... | collective-permute-start | bytes 2359304 | tf_op jit(solution)/shard_map/ppermute | solution.py:223
  108.0 2.3 %collective-permute-done.11.other_grads_ref = bf16[256,1536]{1,0:T(8,128)(2,1)S(1)} collective-permute-done((bf16[256,1536]{1,0:T(8,128)(2,1)S(1)}, bf16[256,1536]{1,0:T(8,128)(2,1)S(1)}, u32[]{:S(2)}, u32[]{:S(2)}) %collective-permute-start.11) | collective-permute-done | bytes 786464 | tf_op jit(solution)/shard_map/ppermute | solution.py:223
  110.3 0.0 copy-done.5
  110.3 2.4 %weight_terms.1 = (f32[3,256,256]{2,1,0:T(8,128)S(1)}, bf16[3,256,256]{2,1,0:T(8,128)(2,1)}, bf16[3,256,256]{2,1,0:T(8,128)(2,1)}, bf16[3,256,256]{2,1,0:T(8,128)(2,1)}) custom-call(s32[3]{0:T(128)S(1)} %pad_add_fusion.place_ref, bf16[2,8,2,128,128]{4,3,2,1,0:T(8,128)(2,1)S(1)} %bitcast.22, bf16[2,2,2,2,128,128]{5,4,3,2,1,0:T(8,128)(2,1)S(1)} %copy-done.5, ...), custom_call_target="tpu_custom_call" | custom-call | flops 800000000 | bytes 6000000 | tf_op jit(solution)/shard_map/weight_terms/pallas_call | solution.py:188
  112.6 2.2 %collective-permute-start.12 = (bf16[3,256,256]{2,1,0:T(8,128)(2,1)}, bf16[3,256,256]{2,1,0:T(8,128)(2,1)S(1)}, u32[]{:S(2)}, u32[]{:S(2)}) collective-permute-start(bf16[3,256,256]{2,1,0:T(8,128)(2,1)} %get-tuple-element.15), channel_id=1, source_target_pairs={{0,1},{1,0},{2,3},{3,2},{4,5},{5,4},{6,7},{7,6},{8,9},{9,8},{10,11... | collective-permute-start | bytes 1179656 | tf_op jit(solution)/shard_map/ppermute | solution.py:231
  114.9 4.0 %collective-permute-start.13 = (bf16[3,256,256]{2,1,0:T(8,128)(2,1)}, bf16[3,256,256]{2,1,0:T(8,128)(2,1)S(1)}, u32[]{:S(2)}, u32[]{:S(2)}) collective-permute-start(bf16[3,256,256]{2,1,0:T(8,128)(2,1)} %get-tuple-element.16), channel_id=1, source_target_pairs={{0,64},{64,0},{1,65},{65,1},{2,66},{66,2},{3,67},{67,3},{4,68},{68... | collective-permute-start | bytes 1179656 | tf_op jit(solution)/shard_map/ppermute | solution.py:232
  118.9 3.0 %collective-permute-start.14 = (bf16[3,256,256]{2,1,0:T(8,128)(2,1)}, bf16[3,256,256]{2,1,0:T(8,128)(2,1)S(1)}, u32[]{:S(2)}, u32[]{:S(2)}) collective-permute-start(bf16[3,256,256]{2,1,0:T(8,128)(2,1)} %get-tuple-element.17), channel_id=1, source_target_pairs={{0,65},{1,64},{64,1},{65,0},{2,67},{3,66},{66,3},{67,2},{4,69},{5,... | collective-permute-start | bytes 1179656 | tf_op jit(solution)/shard_map/ppermute | solution.py:233
  121.9 5.5 %all-to-all-done.3 = bf16[8,2,128,128]{3,2,1,0:T(8,128)(2,1)} async-done(((bf16[8,2,128,128]{3,2,1,0:T(8,128)(2,1)}), bf16[8,2,128,128]{3,2,1,0:T(8,128)(2,1)}, u32[]{:S(2)}, u32[]{:S(2)}) %all-to-all-start.3) | async-done | bytes 524320 | tf_op jit(solution)/shard_map/all_to_all | solution.py:201
  127.4 1.1 reduce_sum.12
  128.5 1.9 %collective-permute-start.9 = (bf16[128,128]{1,0:T(8,128)(2,1)S(1)}, bf16[128,128]{1,0:T(8,128)(2,1)S(1)}, u32[]{:S(2)}, u32[]{:S(2)}) collective-permute-start(bf16[128,128]{1,0:T(8,128)(2,1)S(1)} %get-tuple-element.18), channel_id=1, source_target_pairs={{0,0},{8,1},{2,2},{10,3},{4,4},{12,5},{6,6},{14,7},{128,8},{136,9}... | collective-permute-start | bytes 98312 | tf_op jit(solution)/shard_map/ppermute | solution.py:227
  130.4 3.8 %collective-permute-start.10 = (bf16[128,128]{1,0:T(8,128)(2,1)S(1)}, bf16[128,128]{1,0:T(8,128)(2,1)S(1)}, u32[]{:S(2)}, u32[]{:S(2)}) collective-permute-start(bf16[128,128]{1,0:T(8,128)(2,1)S(1)} %get-tuple-element.19), channel_id=1, source_target_pairs={{16,0},{24,1},{18,2},{26,3},{20,4},{28,5},{22,6},{30,7},{144,8},{1... | collective-permute-start | bytes 98312 | tf_op jit(solution)/shard_map/ppermute | solution.py:227
  134.3 3.7 %collective-permute-done.9 = bf16[128,128]{1,0:T(8,128)(2,1)S(1)} collective-permute-done((bf16[128,128]{1,0:T(8,128)(2,1)S(1)}, bf16[128,128]{1,0:T(8,128)(2,1)S(1)}, u32[]{:S(2)}, u32[]{:S(2)}) %collective-permute-start.9) | collective-permute-done | bytes 32800 | tf_op jit(solution)/shard_map/ppermute | solution.py:227
  138.0 5.5 %collective-permute-done.10 = bf16[128,128]{1,0:T(8,128)(2,1)S(1)} collective-permute-done((bf16[128,128]{1,0:T(8,128)(2,1)S(1)}, bf16[128,128]{1,0:T(8,128)(2,1)S(1)}, u32[]{:S(2)}, u32[]{:S(2)}) %collective-permute-start.10) | collective-permute-done | bytes 32800 | tf_op jit(solution)/shard_map/ppermute | solution.py:227
  143.5 0.6 add_convert_fusion
  144.1 0.0 collective-permute-done.12
  144.1 0.0 collective-permute-done.13
  144.1 0.0 collective-permute-done.14
  144.1 1.0 convert_add_fusion
  (3 shorter events, 0.1 us)
Async XLA Ops:
  1.3 5.4 %copy-start.6 = (bf16[128,128]{1,0:T(8,128)(2,1)S(1)}, bf16[128,128]{1,0:T(8,128)(2,1)}, u32[]{:S(2)}) copy-start(bf16[128,128]{1,0:T(8,128)(2,1)} %param.5) | copy-start | bytes 98308
  1.3 5.4 %copy-start.7 = (bf16[128,128]{1,0:T(8,128)(2,1)S(1)}, bf16[128,128]{1,0:T(8,128)(2,1)}, u32[]{:S(2)}) copy-start(bf16[128,128]{1,0:T(8,128)(2,1)} %param.4) | copy-start | bytes 98308
  2.4 16.6 %collective-permute-start.1 = (bf16[3,256,256]{2,1,0:T(8,128)(2,1)S(1)}, bf16[3,256,256]{2,1,0:T(8,128)(2,1)S(1)}, u32[]{:S(2)}, u32[]{:S(2)}) collective-permute-start(bf16[3,256,256]{2,1,0:T(8,128)(2,1)S(1)} %multiply_convert_fusion.refs_0_), channel_id=1, source_target_pairs={{0,1},{1,0},{2,3},{3,2},{4,5},{5,4},{6,7},{7,6},{8,9},{9,8},{10,11... | collective-permute-start | bytes 1179656 | tf_op jit(solution)/shard_map/ppermute | solution.py:210
  6.7 11.1 %collective-permute-start = (bf16[2,128,128]{2,1,0:T(8,128)(2,1)S(1)}, bf16[2,128,128]{2,1,0:T(8,128)(2,1)S(1)}, u32[]{:S(2)}, u32[]{:S(2)}) collective-permute-start(bf16[2,128,128]{2,1,0:T(8,128)(2,1)S(1)} %pad_maximum_fusion), channel_id=1, source_target_pairs={{0,0},{1,8},{2,2},{3,10},{4,4},{5,12},{6,6},{7,14},{8,128},{9,136}... | collective-permute-start | bytes 196616 | tf_op jit(solution)/shard_map/ppermute | solution.py:208
  19.0 43.6 %all-to-all-start = ((bf16[16,2,128,128]{3,2,1,0:T(8,128)(2,1)}), bf16[16,2,128,128]{3,2,1,0:T(8,128)(2,1)S(1)}, u32[]{:S(2)}, u32[]{:S(2)}) async-start(bf16[16,2,128,128]{3,2,1,0:T(8,128)(2,1)} %spread.1), calls=%async_computation | async-start | bytes 2097152 | tf_op jit(solution)/shard_map/all_to_all | solution.py:201
  33.6 13.9 %collective-permute-start.2 = (bf16[3,256,256]{2,1,0:T(8,128)(2,1)S(1)}, bf16[3,256,256]{2,1,0:T(8,128)(2,1)S(1)}, u32[]{:S(2)}, u32[]{:S(2)}) collective-permute-start(bf16[3,256,256]{2,1,0:T(8,128)(2,1)S(1)} %multiply_convert_fusion.refs_0_), channel_id=1, source_target_pairs={{0,64},{64,0},{1,65},{65,1},{2,66},{66,2},{3,67},{67,3},{4,68},{68... | collective-permute-start | bytes 1179656 | tf_op jit(solution)/shard_map/ppermute | solution.py:212
  36.8 16.4 %collective-permute-start.3 = (bf16[3,256,256]{2,1,0:T(8,128)(2,1)S(1)}, bf16[3,256,256]{2,1,0:T(8,128)(2,1)S(1)}, u32[]{:S(2)}, u32[]{:S(2)}) collective-permute-start(bf16[3,256,256]{2,1,0:T(8,128)(2,1)S(1)} %collective-permute-done.1.refs_1_), channel_id=1, source_target_pairs={{0,64},{64,0},{1,65},{65,1},{2,66},{66,2},{3,67},{67,3},{4,68},{68... | collective-permute-start | bytes 1179656 | tf_op jit(solution)/shard_map/ppermute | solution.py:212
  39.4 15.7 %collective-permute-start.4 = (bf16[3,256,256]{2,1,0:T(8,128)(2,1)S(1)}, bf16[3,256,256]{2,1,0:T(8,128)(2,1)S(1)}, u32[]{:S(2)}, u32[]{:S(2)}) collective-permute-start(bf16[3,256,256]{2,1,0:T(8,128)(2,1)S(1)} %multiply_convert_fusion.refs_0_), channel_id=1, source_target_pairs={{0,32},{32,0},{1,33},{33,1},{2,34},{34,2},{3,35},{35,3},{4,36},{36... | collective-permute-start | bytes 1179656 | tf_op jit(solution)/shard_map/ppermute | solution.py:213
  41.4 13.8 %collective-permute-start.5 = (bf16[3,256,256]{2,1,0:T(8,128)(2,1)S(1)}, bf16[3,256,256]{2,1,0:T(8,128)(2,1)S(1)}, u32[]{:S(2)}, u32[]{:S(2)}) collective-permute-start(bf16[3,256,256]{2,1,0:T(8,128)(2,1)S(1)} %collective-permute-done.1.refs_1_), channel_id=1, source_target_pairs={{0,32},{32,0},{1,33},{33,1},{2,34},{34,2},{3,35},{35,3},{4,36},{36... | collective-permute-start | bytes 1179656 | tf_op jit(solution)/shard_map/ppermute | solution.py:213
  47.5 7.7 %collective-permute-start.6 = (bf16[3,256,256]{2,1,0:T(8,128)(2,1)S(1)}, bf16[3,256,256]{2,1,0:T(8,128)(2,1)}, u32[]{:S(2)}, u32[]{:S(2)}) collective-permute-start(bf16[3,256,256]{2,1,0:T(8,128)(2,1)S(1)} %collective-permute-done.2.refs_2_), channel_id=1, source_target_pairs={{0,32},{32,0},{1,33},{33,1},{2,34},{34,2},{3,35},{35,3},{4,36},{36... | collective-permute-start | bytes 1179656 | tf_op jit(solution)/shard_map/ppermute | solution.py:213
  53.2 3.7 %collective-permute-start.7 = (bf16[3,256,256]{2,1,0:T(8,128)(2,1)S(1)}, bf16[3,256,256]{2,1,0:T(8,128)(2,1)}, u32[]{:S(2)}, u32[]{:S(2)}) collective-permute-start(bf16[3,256,256]{2,1,0:T(8,128)(2,1)S(1)} %collective-permute-done.3.refs_3_), channel_id=1, source_target_pairs={{0,32},{32,0},{1,33},{33,1},{2,34},{34,2},{3,35},{35,3},{4,36},{36... | collective-permute-start | bytes 1179656 | tf_op jit(solution)/shard_map/ppermute | solution.py:213
  55.2 10.4 %copy-start = (bf16[3,256,256]{2,1,0:T(8,128)(2,1)}, bf16[3,256,256]{2,1,0:T(8,128)(2,1)S(1)}, u32[]{:S(2)}) copy-start(bf16[3,256,256]{2,1,0:T(8,128)(2,1)S(1)} %collective-permute-done.4.refs_4_) | copy-start | bytes 1179652
  55.2 10.4 %copy-start.2 = (bf16[3,256,256]{2,1,0:T(8,128)(2,1)}, bf16[3,256,256]{2,1,0:T(8,128)(2,1)S(1)}, u32[]{:S(2)}) copy-start(bf16[3,256,256]{2,1,0:T(8,128)(2,1)S(1)} %collective-permute-done.5.refs_5_) | copy-start | bytes 1179652
  65.6 18.2 %all-to-all-start.1 = ((bf16[4,64,1536]{2,1,0:T(8,128)(2,1)}), bf16[4,64,1536]{2,1,0:T(8,128)(2,1)S(1)}, u32[]{:S(2)}, u32[]{:S(2)}) async-start(bf16[4,64,1536]{2,1,0:T(8,128)(2,1)} %bitcast.7), calls=%async_computation.1 | async-start | bytes 1572864 | tf_op jit(solution)/shard_map/all_to_all | solution.py:201
  73.9 3.8 %collective-permute-start.8 = (bf16[2,2,2,2,128,128]{5,4,3,2,1,0:T(8,128)(2,1)S(1)}, bf16[2,2,2,2,128,128]{5,4,3,2,1,0:T(8,128)(2,1)S(1)}, u32[]{:S(2)}, u32[]{:S(2)}) collective-permute-start(bf16[2,2,2,2,128,128]{5,4,3,2,1,0:T(8,128)(2,1)S(1)} %dynamic-slice_bitcast_fusion), channel_id=1, source_target_pairs={{0,32},{32,0},{1,33},{33,1},{2,34},{34,2},{3,35},{35,3},{4,36},{36... | collective-permute-start | bytes 1572872 | tf_op jit(solution)/shard_map/ppermute | solution.py:219
  77.7 0.8 copy-start.4
  84.0 15.1 %copy-start.1 = (bf16[3,256,256]{2,1,0:T(8,128)(2,1)S(1)}, bf16[3,256,256]{2,1,0:T(8,128)(2,1)}, u32[]{:S(2)}) copy-start(bf16[3,256,256]{2,1,0:T(8,128)(2,1)} %copy-done) | copy-start | bytes 1179652
  84.0 15.1 %copy-start.3 = (bf16[3,256,256]{2,1,0:T(8,128)(2,1)S(1)}, bf16[3,256,256]{2,1,0:T(8,128)(2,1)}, u32[]{:S(2)}) copy-start(bf16[3,256,256]{2,1,0:T(8,128)(2,1)} %copy-done.2) | copy-start | bytes 1179652
  101.8 8.5 %copy-start.5 = (bf16[2,2,2,2,128,128]{5,4,3,2,1,0:T(8,128)(2,1)S(1)}, bf16[2,2,2,2,128,128]{5,4,3,2,1,0:T(8,128)(2,1)}, u32[]{:S(2)}) copy-start(bf16[2,2,2,2,128,128]{5,4,3,2,1,0:T(8,128)(2,1)} %copy-done.4) | copy-start | bytes 1572868
  101.8 25.6 %all-to-all-start.3 = ((bf16[8,2,128,128]{3,2,1,0:T(8,128)(2,1)}), bf16[8,2,128,128]{3,2,1,0:T(8,128)(2,1)}, u32[]{:S(2)}, u32[]{:S(2)}) async-start(bf16[8,2,128,128]{3,2,1,0:T(8,128)(2,1)} %input_terms.1), calls=%async_computation.3 | async-start | bytes 1048576 | tf_op jit(solution)/shard_map/all_to_all | solution.py:201
  106.1 4.2 %collective-permute-start.11 = (bf16[256,1536]{1,0:T(8,128)(2,1)S(1)}, bf16[256,1536]{1,0:T(8,128)(2,1)S(1)}, u32[]{:S(2)}, u32[]{:S(2)}) collective-permute-start(bf16[256,1536]{1,0:T(8,128)(2,1)S(1)} %bitcast.24), channel_id=1, source_target_pairs={{0,32},{32,0},{1,33},{33,1},{2,34},{34,2},{3,35},{35,3},{4,36},{36... | collective-permute-start | bytes 2359304 | tf_op jit(solution)/shard_map/ppermute | solution.py:223
  112.6 31.4 %collective-permute-start.12 = (bf16[3,256,256]{2,1,0:T(8,128)(2,1)}, bf16[3,256,256]{2,1,0:T(8,128)(2,1)S(1)}, u32[]{:S(2)}, u32[]{:S(2)}) collective-permute-start(bf16[3,256,256]{2,1,0:T(8,128)(2,1)} %get-tuple-element.15), channel_id=1, source_target_pairs={{0,1},{1,0},{2,3},{3,2},{4,5},{5,4},{6,7},{7,6},{8,9},{9,8},{10,11... | collective-permute-start | bytes 1179656 | tf_op jit(solution)/shard_map/ppermute | solution.py:231
  114.9 29.2 %collective-permute-start.13 = (bf16[3,256,256]{2,1,0:T(8,128)(2,1)}, bf16[3,256,256]{2,1,0:T(8,128)(2,1)S(1)}, u32[]{:S(2)}, u32[]{:S(2)}) collective-permute-start(bf16[3,256,256]{2,1,0:T(8,128)(2,1)} %get-tuple-element.16), channel_id=1, source_target_pairs={{0,64},{64,0},{1,65},{65,1},{2,66},{66,2},{3,67},{67,3},{4,68},{68... | collective-permute-start | bytes 1179656 | tf_op jit(solution)/shard_map/ppermute | solution.py:232
  118.9 25.2 %collective-permute-start.14 = (bf16[3,256,256]{2,1,0:T(8,128)(2,1)}, bf16[3,256,256]{2,1,0:T(8,128)(2,1)S(1)}, u32[]{:S(2)}, u32[]{:S(2)}) collective-permute-start(bf16[3,256,256]{2,1,0:T(8,128)(2,1)} %get-tuple-element.17), channel_id=1, source_target_pairs={{0,65},{1,64},{64,1},{65,0},{2,67},{3,66},{66,3},{67,2},{4,69},{5,... | collective-permute-start | bytes 1179656 | tf_op jit(solution)/shard_map/ppermute | solution.py:233
  128.5 9.4 %collective-permute-start.9 = (bf16[128,128]{1,0:T(8,128)(2,1)S(1)}, bf16[128,128]{1,0:T(8,128)(2,1)S(1)}, u32[]{:S(2)}, u32[]{:S(2)}) collective-permute-start(bf16[128,128]{1,0:T(8,128)(2,1)S(1)} %get-tuple-element.18), channel_id=1, source_target_pairs={{0,0},{8,1},{2,2},{10,3},{4,4},{12,5},{6,6},{14,7},{128,8},{136,9}... | collective-permute-start | bytes 98312 | tf_op jit(solution)/shard_map/ppermute | solution.py:227
  130.4 13.0 %collective-permute-start.10 = (bf16[128,128]{1,0:T(8,128)(2,1)S(1)}, bf16[128,128]{1,0:T(8,128)(2,1)S(1)}, u32[]{:S(2)}, u32[]{:S(2)}) collective-permute-start(bf16[128,128]{1,0:T(8,128)(2,1)S(1)} %get-tuple-element.19), channel_id=1, source_target_pairs={{16,0},{24,1},{18,2},{26,3},{20,4},{28,5},{22,6},{30,7},{144,8},{1... | collective-permute-start | bytes 98312 | tf_op jit(solution)/shard_map/ppermute | solution.py:227

commit v18 on v17

--- a/solution.py
+++ b/solution.py
@@ -14,7 +14,7 @@
 AXES = ROW + COL
 SPREAD = ("yh0", "zh1", "zh0")
 GATHER = ("yh1",) + SPREAD
-REST = ("yl", "x1")
+REST = ("x1", "yl")
 SWAP = [(0, 1), (1, 0)]
 TOK = 128
 BLOCK = 256

time: 146 us -> 145 us (level)
  waiting for transfers between devices: 43.2 us -> 40 us
  starting transfers between devices: 71 us -> 73.6 us
    all_to_all x3, waiting for transfers between devices: 16.5 us -> 12.5 us  [exchange(): return lax.all_to_all(pieces, axes, split_axis=0, concat_axis=0, tiled=True)]
    ppermute x2, starting transfers between devices: 5.77 us -> 8.32 us  [local(): lax.ppermute(dx[i], AXES, [(b, a) for a, b in there[i]])]
where the time goes in v18:
time: 145 us; the launch traced here: 144 us
  starting transfers between devices  73.6 us (51%)
  waiting for transfers between devices  40 us (28%)
  blocking collectives  14.3 us (10%)
  Pallas kernels  9.38 us (6%)
  other arithmetic  4.62 us (3%)
    all_to_all x3, starting transfers between devices, exchange(): return lax.all_to_all(pieces, axes, split_axis=0, concat_axis=0, tiled=True)  27.1 us
    all_to_all x1, blocking collectives, exchange(): return lax.all_to_all(pieces, axes, split_axis=0, concat_axis=0, tiled=True)  14.3 us
    all_to_all x3, waiting for transfers between devices, exchange(): return lax.all_to_all(pieces, axes, split_axis=0, concat_axis=0, tiled=True)  12.5 us
    ppermute x2, waiting for transfers between devices, local(): lax.ppermute(dx[i], AXES, [(b, a) for a, b in there[i]])  9.96 us
    ppermute x2, starting transfers between devices, local(): lax.ppermute(dx[i], AXES, [(b, a) for a, b in there[i]])  8.32 us
    ppermute x4, starting transfers between devices, local(): weights += [lax.ppermute(block, 'core', SWAP) for block in weights]  8.15 us
    ppermute x2, waiting for transfers between devices, local(): weights = [w, w_z] + [lax.ppermute(block, 'x0', SWAP) for block in (w, w_z)]  7.47 us
    ppermute x1, starting transfers between devices, local(): acts = spread(lax.ppermute(jnp.stack([inputs, out_grad]), AXES, there[0]))  6.88 us
  transfers between devices with their start and end apart: 18, of which 11 were waited for; matrix products, arithmetic and copies ran while one was open for 1% of the time, Pallas kernels for 2%

profile of v18, /device:TPU:4, one launch (start us, length us, event | category | flops | bytes accessed | tf_op | source)
XLA Modules:
  0.0 143.7 jit_solution(4874876162355738173)
XLA Ops:
  0.6 0.7 bitcast_convert_fusion
  1.3 0.0 copy-start.6
  1.3 0.0 copy-start.7
  1.3 1.1 multiply_convert_fusion.refs_0_
  2.4 4.3 %collective-permute-start.1 = (bf16[3,256,256]{2,1,0:T(8,128)(2,1)S(1)}, bf16[3,256,256]{2,1,0:T(8,128)(2,1)S(1)}, u32[]{:S(2)}, u32[]{:S(2)}) collective-permute-start(bf16[3,256,256]{2,1,0:T(8,128)(2,1)S(1)} %multiply_convert_fusion.refs_0_), channel_id=1, source_target_pairs={{0,1},{1,0},{2,3},{3,2},{4,5},{5,4},{6,7},{7,6},{8,9},{9,8},{10,11... | collective-permute-start | bytes 1179656 | tf_op jit(solution)/shard_map/ppermute | solution.py:210
  6.7 0.0 copy-done.6
  6.7 0.0 copy-done.7
  6.7 6.9 %collective-permute-start = (bf16[2,128,128]{2,1,0:T(8,128)(2,1)S(1)}, bf16[2,128,128]{2,1,0:T(8,128)(2,1)S(1)}, u32[]{:S(2)}, u32[]{:S(2)}) collective-permute-start(bf16[2,128,128]{2,1,0:T(8,128)(2,1)S(1)} %pad_maximum_fusion), channel_id=1, source_target_pairs={{0,0},{1,8},{2,2},{3,10},{4,4},{5,12},{6,6},{7,14},{8,128},{9,136}... | collective-permute-start | bytes 196616 | tf_op jit(solution)/shard_map/ppermute | solution.py:208
  13.6 4.2 %collective-permute-done.acts_ref = bf16[2,128,128]{2,1,0:T(8,128)(2,1)S(1)} collective-permute-done((bf16[2,128,128]{2,1,0:T(8,128)(2,1)S(1)}, bf16[2,128,128]{2,1,0:T(8,128)(2,1)S(1)}, u32[]{:S(2)}, u32[]{:S(2)}) %collective-permute-start) | collective-permute-done | bytes 65568 | tf_op jit(solution)/shard_map/ppermute | solution.py:208
  17.8 1.2 spread.1
  19.0 0.0 collective-permute-done.1.refs_1_
  19.0 14.6 %all-to-all-start = ((bf16[16,2,128,128]{3,2,1,0:T(8,128)(2,1)}), bf16[16,2,128,128]{3,2,1,0:T(8,128)(2,1)S(1)}, u32[]{:S(2)}, u32[]{:S(2)}) async-start(bf16[16,2,128,128]{3,2,1,0:T(8,128)(2,1)} %spread.1), calls=%async_computation | async-start | bytes 2097152 | tf_op jit(solution)/shard_map/all_to_all | solution.py:201
  33.6 3.2 %collective-permute-start.2 = (bf16[3,256,256]{2,1,0:T(8,128)(2,1)S(1)}, bf16[3,256,256]{2,1,0:T(8,128)(2,1)S(1)}, u32[]{:S(2)}, u32[]{:S(2)}) collective-permute-start(bf16[3,256,256]{2,1,0:T(8,128)(2,1)S(1)} %multiply_convert_fusion.refs_0_), channel_id=1, source_target_pairs={{0,64},{64,0},{1,65},{65,1},{2,66},{66,2},{3,67},{67,3},{4,68},{68... | collective-permute-start | bytes 1179656 | tf_op jit(solution)/shard_map/ppermute | solution.py:212
  36.8 2.7 %collective-permute-start.3 = (bf16[3,256,256]{2,1,0:T(8,128)(2,1)S(1)}, bf16[3,256,256]{2,1,0:T(8,128)(2,1)S(1)}, u32[]{:S(2)}, u32[]{:S(2)}) collective-permute-start(bf16[3,256,256]{2,1,0:T(8,128)(2,1)S(1)} %collective-permute-done.1.refs_1_), channel_id=1, source_target_pairs={{0,64},{64,0},{1,65},{65,1},{2,66},{66,2},{3,67},{67,3},{4,68},{68... | collective-permute-start | bytes 1179656 | tf_op jit(solution)/shard_map/ppermute | solution.py:212
  39.4 1.9 %collective-permute-start.4 = (bf16[3,256,256]{2,1,0:T(8,128)(2,1)S(1)}, bf16[3,256,256]{2,1,0:T(8,128)(2,1)S(1)}, u32[]{:S(2)}, u32[]{:S(2)}) collective-permute-start(bf16[3,256,256]{2,1,0:T(8,128)(2,1)S(1)} %multiply_convert_fusion.refs_0_), channel_id=1, source_target_pairs={{0,32},{32,0},{1,33},{33,1},{2,34},{34,2},{3,35},{35,3},{4,36},{36... | collective-permute-start | bytes 1179656 | tf_op jit(solution)/shard_map/ppermute | solution.py:213
  41.4 2.4 %collective-permute-start.5 = (bf16[3,256,256]{2,1,0:T(8,128)(2,1)S(1)}, bf16[3,256,256]{2,1,0:T(8,128)(2,1)S(1)}, u32[]{:S(2)}, u32[]{:S(2)}) collective-permute-start(bf16[3,256,256]{2,1,0:T(8,128)(2,1)S(1)} %collective-permute-done.1.refs_1_), channel_id=1, source_target_pairs={{0,32},{32,0},{1,33},{33,1},{2,34},{34,2},{3,35},{35,3},{4,36},{36... | collective-permute-start | bytes 1179656 | tf_op jit(solution)/shard_map/ppermute | solution.py:213
  43.8 3.7 %collective-permute-done.2.refs_2_ = bf16[3,256,256]{2,1,0:T(8,128)(2,1)S(1)} collective-permute-done((bf16[3,256,256]{2,1,0:T(8,128)(2,1)S(1)}, bf16[3,256,256]{2,1,0:T(8,128)(2,1)S(1)}, u32[]{:S(2)}, u32[]{:S(2)}) %collective-permute-start.2) | collective-permute-done | bytes 393248 | tf_op jit(solution)/shard_map/ppermute | solution.py:212
  47.5 1.9 %collective-permute-start.6 = (bf16[3,256,256]{2,1,0:T(8,128)(2,1)S(1)}, bf16[3,256,256]{2,1,0:T(8,128)(2,1)}, u32[]{:S(2)}, u32[]{:S(2)}) collective-permute-start(bf16[3,256,256]{2,1,0:T(8,128)(2,1)S(1)} %collective-permute-done.2.refs_2_), channel_id=1, source_target_pairs={{0,32},{32,0},{1,33},{33,1},{2,34},{34,2},{3,35},{35,3},{4,36},{36... | collective-permute-start | bytes 1179656 | tf_op jit(solution)/shard_map/ppermute | solution.py:213
  49.4 3.7 %collective-permute-done.3.refs_3_ = bf16[3,256,256]{2,1,0:T(8,128)(2,1)S(1)} collective-permute-done((bf16[3,256,256]{2,1,0:T(8,128)(2,1)S(1)}, bf16[3,256,256]{2,1,0:T(8,128)(2,1)S(1)}, u32[]{:S(2)}, u32[]{:S(2)}) %collective-permute-start.3) | collective-permute-done | bytes 393248 | tf_op jit(solution)/shard_map/ppermute | solution.py:212
  53.2 1.9 %collective-permute-start.7 = (bf16[3,256,256]{2,1,0:T(8,128)(2,1)S(1)}, bf16[3,256,256]{2,1,0:T(8,128)(2,1)}, u32[]{:S(2)}, u32[]{:S(2)}) collective-permute-start(bf16[3,256,256]{2,1,0:T(8,128)(2,1)S(1)} %collective-permute-done.3.refs_3_), channel_id=1, source_target_pairs={{0,32},{32,0},{1,33},{33,1},{2,34},{34,2},{3,35},{35,3},{4,36},{36... | collective-permute-start | bytes 1179656 | tf_op jit(solution)/shard_map/ppermute | solution.py:213
  55.1 0.1 pad_add_fusion.place_ref
  55.2 0.0 collective-permute-done.4.refs_4_
  55.2 0.0 copy-start
  55.2 0.0 collective-permute-done.6.refs_6_
  55.2 0.0 collective-permute-done.5.refs_5_
  55.2 0.0 copy-start.2
  55.2 1.7 %collective-permute-done.7.refs_7_ = bf16[3,256,256]{2,1,0:T(8,128)(2,1)} collective-permute-done((bf16[3,256,256]{2,1,0:T(8,128)(2,1)S(1)}, bf16[3,256,256]{2,1,0:T(8,128)(2,1)}, u32[]{:S(2)}, u32[]{:S(2)}) %collective-permute-start.7) | collective-permute-done | bytes 393248 | tf_op jit(solution)/shard_map/ppermute | solution.py:213
  56.9 5.7 %all-to-all-done = bf16[16,2,128,128]{3,2,1,0:T(8,128)(2,1)S(1)} async-done(((bf16[16,2,128,128]{3,2,1,0:T(8,128)(2,1)}), bf16[16,2,128,128]{3,2,1,0:T(8,128)(2,1)S(1)}, u32[]{:S(2)}, u32[]{:S(2)}) %all-to-all-start) | async-done | bytes 1048608 | tf_op jit(solution)/shard_map/all_to_all | solution.py:201
  62.6 3.0 %gates.1 = bf16[256,1536]{1,0:T(8,128)(2,1)} custom-call(s32[3]{0:T(128)S(1)} %pad_add_fusion.place_ref, bf16[2,8,2,128,128]{4,3,2,1,0:T(8,128)(2,1)S(1)} %bitcast.20, bf16[3,256,256]{2,1,0:T(8,128)(2,1)S(1)} %multiply_convert_fusion.refs_0_, bf16[3,256,256]{2,1,0:T(8,128)(2,1)S(1)} %collective-permute-done.1.refs_1_, ...), custom_call_target="tpu_custom_call" | custom-call | flops 800000000 | bytes 6000000 | tf_op jit(solution)/shard_map/gates/pallas_call | solution.py:96
  65.6 0.0 copy-done
  65.6 0.0 copy-done.2
  65.6 8.2 %all-to-all-start.1 = ((bf16[4,64,1536]{2,1,0:T(8,128)(2,1)}), bf16[4,64,1536]{2,1,0:T(8,128)(2,1)S(1)}, u32[]{:S(2)}, u32[]{:S(2)}) async-start(bf16[4,64,1536]{2,1,0:T(8,128)(2,1)} %bitcast.7), calls=%async_computation.1 | async-start | bytes 1572864 | tf_op jit(solution)/shard_map/all_to_all | solution.py:201
  73.9 1.9 %collective-permute-start.8 = (bf16[2,2,2,2,128,128]{5,4,3,2,1,0:T(8,128)(2,1)S(1)}, bf16[2,2,2,2,128,128]{5,4,3,2,1,0:T(8,128)(2,1)S(1)}, u32[]{:S(2)}, u32[]{:S(2)}) collective-permute-start(bf16[2,2,2,2,128,128]{5,4,3,2,1,0:T(8,128)(2,1)S(1)} %dynamic-slice_bitcast_fusion), channel_id=1, source_target_pairs={{0,32},{32,0},{1,33},{33,1},{2,34},{34,2},{3,35},{35,3},{4,36},{36... | collective-permute-start | bytes 1572872 | tf_op jit(solution)/shard_map/ppermute | solution.py:219
  75.8 1.9 %collective-permute-done.8.other_acts_ref = bf16[2,2,2,2,128,128]{5,4,3,2,1,0:T(8,128)(2,1)S(1)} collective-permute-done((bf16[2,2,2,2,128,128]{5,4,3,2,1,0:T(8,128)(2,1)S(1)}, bf16[2,2,2,2,128,128]{5,4,3,2,1,0:T(8,128)(2,1)S(1)}, u32[]{:S(2)}, u32[]{:S(2)}) %collective-permute-start.8) | collective-permute-done | bytes 524320 | tf_op jit(solution)/shard_map/ppermute | solution.py:219
  77.7 0.0 copy-start.4
  77.7 0.8 copy-done.4
  78.5 5.3 %all-to-all-done.1.parts_ref = bf16[4,64,1536]{2,1,0:T(8,128)(2,1)S(1)} async-done(((bf16[4,64,1536]{2,1,0:T(8,128)(2,1)}), bf16[4,64,1536]{2,1,0:T(8,128)(2,1)S(1)}, u32[]{:S(2)}, u32[]{:S(2)}) %all-to-all-start.1) | async-done | bytes 786464 | tf_op jit(solution)/shard_map/all_to_all | solution.py:201
  83.8 0.2 hidden_grads.1
  84.0 0.0 copy-start.1
  84.0 0.0 copy-start.3
  84.0 14.3 %all_to_all.20 = bf16[4,64,1536]{2,1,0:T(8,128)(2,1)S(1)} all-to-all(bf16[4,64,1536]{2,1,0:T(8,128)(2,1)S(1)} %hidden_grads.1), channel_id=1, replica_groups=mesh['yl'=2,'x1'=2,'x0'=2,'core'=2,'yh1'=2,'yh0'=2,'zh1'=2,'zh0'=2,'zl'=..., dimensions={0} | all-to-all | bytes 1572864 | tf_op jit(solution)/shard_map/all_to_all | solution.py:201
  98.3 0.0 copy-done.1
  98.3 0.0 copy-done.3
  98.3 2.7 %input_terms.1 = bf16[8,2,128,128]{3,2,1,0:T(8,128)(2,1)} custom-call(s32[3]{0:T(128)S(1)} %pad_add_fusion.place_ref, bf16[256,1536]{1,0:T(8,128)(2,1)S(1)} %bitcast.23, bf16[3,256,256]{2,1,0:T(8,128)(2,1)S(1)} %multiply_convert_fusion.refs_0_, bf16[3,256,256]{2,1,0:T(8,128)(2,1)S(1)} %collective-permute-done.1.refs_1_, ...), custom_call_target="tpu_custom_call" | custom-call | flops 540000000 | bytes 4000000 | tf_op jit(solution)/shard_map/input_terms/pallas_call | solution.py:151
  101.0 0.0 copy-start.5
  101.0 4.3 %all-to-all-start.3 = ((bf16[8,2,128,128]{3,2,1,0:T(8,128)(2,1)}), bf16[8,2,128,128]{3,2,1,0:T(8,128)(2,1)}, u32[]{:S(2)}, u32[]{:S(2)}) async-start(bf16[8,2,128,128]{3,2,1,0:T(8,128)(2,1)} %input_terms.1), calls=%async_computation.3 | async-start | bytes 1048576 | tf_op jit(solution)/shard_map/all_to_all | solution.py:201
  105.3 1.9 %collective-permute-start.11 = (bf16[256,1536]{1,0:T(8,128)(2,1)S(1)}, bf16[256,1536]{1,0:T(8,128)(2,1)S(1)}, u32[]{:S(2)}, u32[]{:S(2)}) collective-permute-start(bf16[256,1536]{1,0:T(8,128)(2,1)S(1)} %bitcast.24), channel_id=1, source_target_pairs={{0,32},{32,0},{1,33},{33,1},{2,34},{34,2},{3,35},{35,3},{4,36},{36... | collective-permute-start | bytes 2359304 | tf_op jit(solution)/shard_map/ppermute | solution.py:223
  107.2 2.3 %collective-permute-done.11.other_grads_ref = bf16[256,1536]{1,0:T(8,128)(2,1)S(1)} collective-permute-done((bf16[256,1536]{1,0:T(8,128)(2,1)S(1)}, bf16[256,1536]{1,0:T(8,128)(2,1)S(1)}, u32[]{:S(2)}, u32[]{:S(2)}) %collective-permute-start.11) | collective-permute-done | bytes 786464 | tf_op jit(solution)/shard_map/ppermute | solution.py:223
  109.5 0.0 copy-done.5
  109.5 2.4 %weight_terms.1 = (f32[3,256,256]{2,1,0:T(8,128)S(1)}, bf16[3,256,256]{2,1,0:T(8,128)(2,1)}, bf16[3,256,256]{2,1,0:T(8,128)(2,1)}, bf16[3,256,256]{2,1,0:T(8,128)(2,1)}) custom-call(s32[3]{0:T(128)S(1)} %pad_add_fusion.place_ref, bf16[2,8,2,128,128]{4,3,2,1,0:T(8,128)(2,1)S(1)} %bitcast.22, bf16[2,2,2,2,128,128]{5,4,3,2,1,0:T(8,128)(2,1)S(1)} %copy-done.5, ...), custom_call_target="tpu_custom_call" | custom-call | flops 800000000 | bytes 6000000 | tf_op jit(solution)/shard_map/weight_terms/pallas_call | solution.py:188
  111.8 2.2 %collective-permute-start.12 = (bf16[3,256,256]{2,1,0:T(8,128)(2,1)}, bf16[3,256,256]{2,1,0:T(8,128)(2,1)S(1)}, u32[]{:S(2)}, u32[]{:S(2)}) collective-permute-start(bf16[3,256,256]{2,1,0:T(8,128)(2,1)} %get-tuple-element.15), channel_id=1, source_target_pairs={{0,1},{1,0},{2,3},{3,2},{4,5},{5,4},{6,7},{7,6},{8,9},{9,8},{10,11... | collective-permute-start | bytes 1179656 | tf_op jit(solution)/shard_map/ppermute | solution.py:231
  114.1 4.0 %collective-permute-start.13 = (bf16[3,256,256]{2,1,0:T(8,128)(2,1)}, bf16[3,256,256]{2,1,0:T(8,128)(2,1)S(1)}, u32[]{:S(2)}, u32[]{:S(2)}) collective-permute-start(bf16[3,256,256]{2,1,0:T(8,128)(2,1)} %get-tuple-element.16), channel_id=1, source_target_pairs={{0,64},{64,0},{1,65},{65,1},{2,66},{66,2},{3,67},{67,3},{4,68},{68... | collective-permute-start | bytes 1179656 | tf_op jit(solution)/shard_map/ppermute | solution.py:232
  118.1 3.0 %collective-permute-start.14 = (bf16[3,256,256]{2,1,0:T(8,128)(2,1)}, bf16[3,256,256]{2,1,0:T(8,128)(2,1)S(1)}, u32[]{:S(2)}, u32[]{:S(2)}) collective-permute-start(bf16[3,256,256]{2,1,0:T(8,128)(2,1)} %get-tuple-element.17), channel_id=1, source_target_pairs={{0,65},{1,64},{64,1},{65,0},{2,67},{3,66},{66,3},{67,2},{4,69},{5,... | collective-permute-start | bytes 1179656 | tf_op jit(solution)/shard_map/ppermute | solution.py:233
  121.1 1.5 %all-to-all-done.3 = bf16[8,2,128,128]{3,2,1,0:T(8,128)(2,1)} async-done(((bf16[8,2,128,128]{3,2,1,0:T(8,128)(2,1)}), bf16[8,2,128,128]{3,2,1,0:T(8,128)(2,1)}, u32[]{:S(2)}, u32[]{:S(2)}) %all-to-all-start.3) | async-done | bytes 524320 | tf_op jit(solution)/shard_map/all_to_all | solution.py:201
  122.6 1.1 reduce_sum.12
  123.7 5.3 %collective-permute-start.9 = (bf16[128,128]{1,0:T(8,128)(2,1)S(1)}, bf16[128,128]{1,0:T(8,128)(2,1)S(1)}, u32[]{:S(2)}, u32[]{:S(2)}) collective-permute-start(bf16[128,128]{1,0:T(8,128)(2,1)S(1)} %get-tuple-element.18), channel_id=1, source_target_pairs={{0,0},{8,1},{2,2},{10,3},{4,4},{12,5},{6,6},{14,7},{128,8},{136,9}... | collective-permute-start | bytes 98312 | tf_op jit(solution)/shard_map/ppermute | solution.py:227
  129.0 3.0 %collective-permute-start.10 = (bf16[128,128]{1,0:T(8,128)(2,1)S(1)}, bf16[128,128]{1,0:T(8,128)(2,1)S(1)}, u32[]{:S(2)}, u32[]{:S(2)}) collective-permute-start(bf16[128,128]{1,0:T(8,128)(2,1)S(1)} %get-tuple-element.19), channel_id=1, source_target_pairs={{16,0},{24,1},{18,2},{26,3},{20,4},{28,5},{22,6},{30,7},{144,8},{1... | collective-permute-start | bytes 98312 | tf_op jit(solution)/shard_map/ppermute | solution.py:227
  132.0 4.9 %collective-permute-done.9 = bf16[128,128]{1,0:T(8,128)(2,1)S(1)} collective-permute-done((bf16[128,128]{1,0:T(8,128)(2,1)S(1)}, bf16[128,128]{1,0:T(8,128)(2,1)S(1)}, u32[]{:S(2)}, u32[]{:S(2)}) %collective-permute-start.9) | collective-permute-done | bytes 32800 | tf_op jit(solution)/shard_map/ppermute | solution.py:227
  136.9 5.1 %collective-permute-done.10 = bf16[128,128]{1,0:T(8,128)(2,1)S(1)} collective-permute-done((bf16[128,128]{1,0:T(8,128)(2,1)S(1)}, bf16[128,128]{1,0:T(8,128)(2,1)S(1)}, u32[]{:S(2)}, u32[]{:S(2)}) %collective-permute-start.10) | collective-permute-done | bytes 32800 | tf_op jit(solution)/shard_map/ppermute | solution.py:227
  142.0 0.6 add_convert_fusion
  142.6 0.0 collective-permute-done.12
  142.6 0.0 collective-permute-done.13
  142.6 0.0 collective-permute-done.14
  142.6 1.0 convert_add_fusion
  (3 shorter events, 0.1 us)
Async XLA Ops:
  1.3 5.4 %copy-start.6 = (bf16[128,128]{1,0:T(8,128)(2,1)S(1)}, bf16[128,128]{1,0:T(8,128)(2,1)}, u32[]{:S(2)}) copy-start(bf16[128,128]{1,0:T(8,128)(2,1)} %param.5) | copy-start | bytes 98308
  1.3 5.4 %copy-start.7 = (bf16[128,128]{1,0:T(8,128)(2,1)S(1)}, bf16[128,128]{1,0:T(8,128)(2,1)}, u32[]{:S(2)}) copy-start(bf16[128,128]{1,0:T(8,128)(2,1)} %param.4) | copy-start | bytes 98308
  2.4 16.6 %collective-permute-start.1 = (bf16[3,256,256]{2,1,0:T(8,128)(2,1)S(1)}, bf16[3,256,256]{2,1,0:T(8,128)(2,1)S(1)}, u32[]{:S(2)}, u32[]{:S(2)}) collective-permute-start(bf16[3,256,256]{2,1,0:T(8,128)(2,1)S(1)} %multiply_convert_fusion.refs_0_), channel_id=1, source_target_pairs={{0,1},{1,0},{2,3},{3,2},{4,5},{5,4},{6,7},{7,6},{8,9},{9,8},{10,11... | collective-permute-start | bytes 1179656 | tf_op jit(solution)/shard_map/ppermute | solution.py:210
  6.7 11.1 %collective-permute-start = (bf16[2,128,128]{2,1,0:T(8,128)(2,1)S(1)}, bf16[2,128,128]{2,1,0:T(8,128)(2,1)S(1)}, u32[]{:S(2)}, u32[]{:S(2)}) collective-permute-start(bf16[2,128,128]{2,1,0:T(8,128)(2,1)S(1)} %pad_maximum_fusion), channel_id=1, source_target_pairs={{0,0},{1,8},{2,2},{3,10},{4,4},{5,12},{6,6},{7,14},{8,128},{9,136}... | collective-permute-start | bytes 196616 | tf_op jit(solution)/shard_map/ppermute | solution.py:208
  19.0 43.6 %all-to-all-start = ((bf16[16,2,128,128]{3,2,1,0:T(8,128)(2,1)}), bf16[16,2,128,128]{3,2,1,0:T(8,128)(2,1)S(1)}, u32[]{:S(2)}, u32[]{:S(2)}) async-start(bf16[16,2,128,128]{3,2,1,0:T(8,128)(2,1)} %spread.1), calls=%async_computation | async-start | bytes 2097152 | tf_op jit(solution)/shard_map/all_to_all | solution.py:201
  33.6 13.9 %collective-permute-start.2 = (bf16[3,256,256]{2,1,0:T(8,128)(2,1)S(1)}, bf16[3,256,256]{2,1,0:T(8,128)(2,1)S(1)}, u32[]{:S(2)}, u32[]{:S(2)}) collective-permute-start(bf16[3,256,256]{2,1,0:T(8,128)(2,1)S(1)} %multiply_convert_fusion.refs_0_), channel_id=1, source_target_pairs={{0,64},{64,0},{1,65},{65,1},{2,66},{66,2},{3,67},{67,3},{4,68},{68... | collective-permute-start | bytes 1179656 | tf_op jit(solution)/shard_map/ppermute | solution.py:212
  36.8 16.4 %collective-permute-start.3 = (bf16[3,256,256]{2,1,0:T(8,128)(2,1)S(1)}, bf16[3,256,256]{2,1,0:T(8,128)(2,1)S(1)}, u32[]{:S(2)}, u32[]{:S(2)}) collective-permute-start(bf16[3,256,256]{2,1,0:T(8,128)(2,1)S(1)} %collective-permute-done.1.refs_1_), channel_id=1, source_target_pairs={{0,64},{64,0},{1,65},{65,1},{2,66},{66,2},{3,67},{67,3},{4,68},{68... | collective-permute-start | bytes 1179656 | tf_op jit(solution)/shard_map/ppermute | solution.py:212
  39.4 15.7 %collective-permute-start.4 = (bf16[3,256,256]{2,1,0:T(8,128)(2,1)S(1)}, bf16[3,256,256]{2,1,0:T(8,128)(2,1)S(1)}, u32[]{:S(2)}, u32[]{:S(2)}) collective-permute-start(bf16[3,256,256]{2,1,0:T(8,128)(2,1)S(1)} %multiply_convert_fusion.refs_0_), channel_id=1, source_target_pairs={{0,32},{32,0},{1,33},{33,1},{2,34},{34,2},{3,35},{35,3},{4,36},{36... | collective-permute-start | bytes 1179656 | tf_op jit(solution)/shard_map/ppermute | solution.py:213
  41.4 13.8 %collective-permute-start.5 = (bf16[3,256,256]{2,1,0:T(8,128)(2,1)S(1)}, bf16[3,256,256]{2,1,0:T(8,128)(2,1)S(1)}, u32[]{:S(2)}, u32[]{:S(2)}) collective-permute-start(bf16[3,256,256]{2,1,0:T(8,128)(2,1)S(1)} %collective-permute-done.1.refs_1_), channel_id=1, source_target_pairs={{0,32},{32,0},{1,33},{33,1},{2,34},{34,2},{3,35},{35,3},{4,36},{36... | collective-permute-start | bytes 1179656 | tf_op jit(solution)/shard_map/ppermute | solution.py:213
  47.5 7.7 %collective-permute-start.6 = (bf16[3,256,256]{2,1,0:T(8,128)(2,1)S(1)}, bf16[3,256,256]{2,1,0:T(8,128)(2,1)}, u32[]{:S(2)}, u32[]{:S(2)}) collective-permute-start(bf16[3,256,256]{2,1,0:T(8,128)(2,1)S(1)} %collective-permute-done.2.refs_2_), channel_id=1, source_target_pairs={{0,32},{32,0},{1,33},{33,1},{2,34},{34,2},{3,35},{35,3},{4,36},{36... | collective-permute-start | bytes 1179656 | tf_op jit(solution)/shard_map/ppermute | solution.py:213
  53.2 3.7 %collective-permute-start.7 = (bf16[3,256,256]{2,1,0:T(8,128)(2,1)S(1)}, bf16[3,256,256]{2,1,0:T(8,128)(2,1)}, u32[]{:S(2)}, u32[]{:S(2)}) collective-permute-start(bf16[3,256,256]{2,1,0:T(8,128)(2,1)S(1)} %collective-permute-done.3.refs_3_), channel_id=1, source_target_pairs={{0,32},{32,0},{1,33},{33,1},{2,34},{34,2},{3,35},{35,3},{4,36},{36... | collective-permute-start | bytes 1179656 | tf_op jit(solution)/shard_map/ppermute | solution.py:213
  55.2 10.4 %copy-start = (bf16[3,256,256]{2,1,0:T(8,128)(2,1)}, bf16[3,256,256]{2,1,0:T(8,128)(2,1)S(1)}, u32[]{:S(2)}) copy-start(bf16[3,256,256]{2,1,0:T(8,128)(2,1)S(1)} %collective-permute-done.4.refs_4_) | copy-start | bytes 1179652
  55.2 10.4 %copy-start.2 = (bf16[3,256,256]{2,1,0:T(8,128)(2,1)}, bf16[3,256,256]{2,1,0:T(8,128)(2,1)S(1)}, u32[]{:S(2)}) copy-start(bf16[3,256,256]{2,1,0:T(8,128)(2,1)S(1)} %collective-permute-done.5.refs_5_) | copy-start | bytes 1179652
  65.6 18.2 %all-to-all-start.1 = ((bf16[4,64,1536]{2,1,0:T(8,128)(2,1)}), bf16[4,64,1536]{2,1,0:T(8,128)(2,1)S(1)}, u32[]{:S(2)}, u32[]{:S(2)}) async-start(bf16[4,64,1536]{2,1,0:T(8,128)(2,1)} %bitcast.7), calls=%async_computation.1 | async-start | bytes 1572864 | tf_op jit(solution)/shard_map/all_to_all | solution.py:201
  73.9 3.8 %collective-permute-start.8 = (bf16[2,2,2,2,128,128]{5,4,3,2,1,0:T(8,128)(2,1)S(1)}, bf16[2,2,2,2,128,128]{5,4,3,2,1,0:T(8,128)(2,1)S(1)}, u32[]{:S(2)}, u32[]{:S(2)}) collective-permute-start(bf16[2,2,2,2,128,128]{5,4,3,2,1,0:T(8,128)(2,1)S(1)} %dynamic-slice_bitcast_fusion), channel_id=1, source_target_pairs={{0,32},{32,0},{1,33},{33,1},{2,34},{34,2},{3,35},{35,3},{4,36},{36... | collective-permute-start | bytes 1572872 | tf_op jit(solution)/shard_map/ppermute | solution.py:219
  77.7 0.8 copy-start.4
  84.0 14.3 %copy-start.1 = (bf16[3,256,256]{2,1,0:T(8,128)(2,1)S(1)}, bf16[3,256,256]{2,1,0:T(8,128)(2,1)}, u32[]{:S(2)}) copy-start(bf16[3,256,256]{2,1,0:T(8,128)(2,1)} %copy-done) | copy-start | bytes 1179652
  84.0 14.3 %copy-start.3 = (bf16[3,256,256]{2,1,0:T(8,128)(2,1)S(1)}, bf16[3,256,256]{2,1,0:T(8,128)(2,1)}, u32[]{:S(2)}) copy-start(bf16[3,256,256]{2,1,0:T(8,128)(2,1)} %copy-done.2) | copy-start | bytes 1179652
  101.0 8.5 %copy-start.5 = (bf16[2,2,2,2,128,128]{5,4,3,2,1,0:T(8,128)(2,1)S(1)}, bf16[2,2,2,2,128,128]{5,4,3,2,1,0:T(8,128)(2,1)}, u32[]{:S(2)}) copy-start(bf16[2,2,2,2,128,128]{5,4,3,2,1,0:T(8,128)(2,1)} %copy-done.4) | copy-start | bytes 1572868
  101.0 21.6 %all-to-all-start.3 = ((bf16[8,2,128,128]{3,2,1,0:T(8,128)(2,1)}), bf16[8,2,128,128]{3,2,1,0:T(8,128)(2,1)}, u32[]{:S(2)}, u32[]{:S(2)}) async-start(bf16[8,2,128,128]{3,2,1,0:T(8,128)(2,1)} %input_terms.1), calls=%async_computation.3 | async-start | bytes 1048576 | tf_op jit(solution)/shard_map/all_to_all | solution.py:201
  105.3 4.2 %collective-permute-start.11 = (bf16[256,1536]{1,0:T(8,128)(2,1)S(1)}, bf16[256,1536]{1,0:T(8,128)(2,1)S(1)}, u32[]{:S(2)}, u32[]{:S(2)}) collective-permute-start(bf16[256,1536]{1,0:T(8,128)(2,1)S(1)} %bitcast.24), channel_id=1, source_target_pairs={{0,32},{32,0},{1,33},{33,1},{2,34},{34,2},{3,35},{35,3},{4,36},{36... | collective-permute-start | bytes 2359304 | tf_op jit(solution)/shard_map/ppermute | solution.py:223
  111.8 30.8 %collective-permute-start.12 = (bf16[3,256,256]{2,1,0:T(8,128)(2,1)}, bf16[3,256,256]{2,1,0:T(8,128)(2,1)S(1)}, u32[]{:S(2)}, u32[]{:S(2)}) collective-permute-start(bf16[3,256,256]{2,1,0:T(8,128)(2,1)} %get-tuple-element.15), channel_id=1, source_target_pairs={{0,1},{1,0},{2,3},{3,2},{4,5},{5,4},{6,7},{7,6},{8,9},{9,8},{10,11... | collective-permute-start | bytes 1179656 | tf_op jit(solution)/shard_map/ppermute | solution.py:231
  114.1 28.5 %collective-permute-start.13 = (bf16[3,256,256]{2,1,0:T(8,128)(2,1)}, bf16[3,256,256]{2,1,0:T(8,128)(2,1)S(1)}, u32[]{:S(2)}, u32[]{:S(2)}) collective-permute-start(bf16[3,256,256]{2,1,0:T(8,128)(2,1)} %get-tuple-element.16), channel_id=1, source_target_pairs={{0,64},{64,0},{1,65},{65,1},{2,66},{66,2},{3,67},{67,3},{4,68},{68... | collective-permute-start | bytes 1179656 | tf_op jit(solution)/shard_map/ppermute | solution.py:232
  118.1 24.5 %collective-permute-start.14 = (bf16[3,256,256]{2,1,0:T(8,128)(2,1)}, bf16[3,256,256]{2,1,0:T(8,128)(2,1)S(1)}, u32[]{:S(2)}, u32[]{:S(2)}) collective-permute-start(bf16[3,256,256]{2,1,0:T(8,128)(2,1)} %get-tuple-element.17), channel_id=1, source_target_pairs={{0,65},{1,64},{64,1},{65,0},{2,67},{3,66},{66,3},{67,2},{4,69},{5,... | collective-permute-start | bytes 1179656 | tf_op jit(solution)/shard_map/ppermute | solution.py:233
  123.7 13.2 %collective-permute-start.9 = (bf16[128,128]{1,0:T(8,128)(2,1)S(1)}, bf16[128,128]{1,0:T(8,128)(2,1)S(1)}, u32[]{:S(2)}, u32[]{:S(2)}) collective-permute-start(bf16[128,128]{1,0:T(8,128)(2,1)S(1)} %get-tuple-element.18), channel_id=1, source_target_pairs={{0,0},{8,1},{2,2},{10,3},{4,4},{12,5},{6,6},{14,7},{128,8},{136,9}... | collective-permute-start | bytes 98312 | tf_op jit(solution)/shard_map/ppermute | solution.py:227
  129.0 13.0 %collective-permute-start.10 = (bf16[128,128]{1,0:T(8,128)(2,1)S(1)}, bf16[128,128]{1,0:T(8,128)(2,1)S(1)}, u32[]{:S(2)}, u32[]{:S(2)}) collective-permute-start(bf16[128,128]{1,0:T(8,128)(2,1)S(1)} %get-tuple-element.19), channel_id=1, source_target_pairs={{16,0},{24,1},{18,2},{26,3},{20,4},{28,5},{22,6},{30,7},{144,8},{1... | collective-permute-start | bytes 98312 | tf_op jit(solution)/shard_map/ppermute | solution.py:227

commit v19 on v15

--- a/solution.py
+++ b/solution.py
@@ -12,9 +12,9 @@
 ROW = ("yl", "x1", "x0", "core")
 COL = ("yh1", "yh0", "zh1", "zh0", "zl")
 AXES = ROW + COL
-SPREAD = ("zh1", "zh0", "yh0")
-GATHER = SPREAD + ("yh1",)
-REST = ("yl", "x1")
+SPREAD = ("yh0", "zh1", "zh0")
+GATHER = ("zh1", "zh0", "yh0", "yh1")
+REST = ("x1", "yl")
 SWAP = [(0, 1), (1, 0)]
 TOK = 128
 BLOCK = 256
@@ -45,11 +45,19 @@
     return pltpu.CompilerParams(vmem_limit_bytes=VMEM_LIMIT)
 
 
-def chunk(place_ref, f):
+def place_of(place_ref, f):
     core, x0 = place_ref[0], place_ref[1]
-    core = core if f < 4 else 1 - core
-    x0 = x0 if f % 4 < 2 else 1 - x0
-    return 4 * x0 + 2 * core + f % 2
+    return core if f < 4 else 1 - core, x0 if f % 4 < 2 else 1 - x0, f % 2
+
+
+def gathered(place_ref, f):
+    core, x0, b = place_of(place_ref, f)
+    return 4 * x0 + 2 * core + b
+
+
+def summed(place_ref, f):
+    core, x0, b = place_of(place_ref, f)
+    return 4 * b + 2 * x0 + core
 
 
 def half(place_ref, t):
@@ -82,7 +90,7 @@
     for p in range(2):
         for t in range(2):
             for f in range(8):
-                block = acts_ref[chunk(place_ref, f), half(place_ref, t), p]
+                block = acts_ref[gathered(place_ref, f), half(place_ref, t), p]
                 wide_ref[p, pl.ds(t * TOK, TOK), pl.ds(f * TOK, TOK)] = block
     for p in range(3):
         for j in range(2):
@@ -144,7 +152,7 @@
         for t in range(2):
             for f in range(2):
                 part = dx[t * TOK : (t + 1) * TOK, f * TOK : (f + 1) * TOK]
-                dx_ref[chunk(place_ref, 2 * s + f), t] = part
+                dx_ref[summed(place_ref, 2 * s + f), t] = part
 
 
 def input_terms(place, grads, *weights):
@@ -167,7 +175,7 @@
             for f in range(4):
                 x0 = place_ref[1] if f < 2 else 1 - place_ref[1]
                 cols = pl.ds(f * TOK, TOK)
-                mine = acts_ref[chunk(place_ref, f), half(place_ref, t), p]
+                mine = acts_ref[gathered(place_ref, f), half(place_ref, t), p]
                 wide_ref[p, pl.ds(t * TOK, TOK), cols] = mine
                 wide_ref[p, pl.ds(TOKENS + t * TOK, TOK), cols] = other_acts_ref[x0, f % 2, half(place_ref, t), p]
     for side in (1, 0):

time: 147 us -> 145 us (0.986)
  the two profiles are of different devices: /device:TPU:44 before, /device:TPU:4 now
where the time goes in v19:
time: 145 us; the launch traced here: 144 us
  starting transfers between devices  83 us (57%)
  waiting for transfers between devices  32.2 us (22%)
  blocking collectives  13.4 us (9%)
  Pallas kernels  9.39 us (6%)
  other arithmetic  4.63 us (3%)
    all_to_all x3, starting transfers between devices, exchange(): return lax.all_to_all(pieces, axes, split_axis=0, concat_axis=0, tiled=True)  29.3 us
    all_to_all x1, blocking collectives, exchange(): return lax.all_to_all(pieces, axes, split_axis=0, concat_axis=0, tiled=True)  13.4 us
    ppermute x2, starting transfers between devices, local(): lax.ppermute(dx[i], AXES, [(b, a) for a, b in there[i]])  12.8 us
    ppermute x4, starting transfers between devices, local(): weights += [lax.ppermute(block, 'core', SWAP) for block in weights]  8.15 us
    ppermute x2, waiting for transfers between devices, local(): weights = [w, w_z] + [lax.ppermute(block, 'x0', SWAP) for block in (w, w_z)]  7.47 us
    all_to_all x3, waiting for transfers between devices, exchange(): return lax.all_to_all(pieces, axes, split_axis=0, concat_axis=0, tiled=True)  7.37 us
    ppermute x2, waiting for transfers between devices, local(): lax.ppermute(dx[i], AXES, [(b, a) for a, b in there[i]])  7.27 us
    ppermute x1, starting transfers between devices, local(): acts = spread(lax.ppermute(jnp.stack([inputs, out_grad]), AXES, there[0]))  6.88 us
  transfers between devices with their start and end apart: 18, of which 10 were waited for; matrix products, arithmetic and copies ran while one was open for 1% of the time, Pallas kernels for 2%

profile of v19, /device:TPU:4, one launch (start us, length us, event | category | flops | bytes accessed | tf_op | source)
XLA Modules:
  0.0 144.4 jit_solution(14640283303258085626)
XLA Ops:
  0.6 0.7 bitcast_convert_fusion
  1.3 0.0 copy-start.6
  1.3 0.0 copy-start.7
  1.3 1.1 multiply_convert_fusion.refs_0_
  2.4 4.3 %collective-permute-start.1 = (bf16[3,256,256]{2,1,0:T(8,128)(2,1)S(1)}, bf16[3,256,256]{2,1,0:T(8,128)(2,1)S(1)}, u32[]{:S(2)}, u32[]{:S(2)}) collective-permute-start(bf16[3,256,256]{2,1,0:T(8,128)(2,1)S(1)} %multiply_convert_fusion.refs_0_), channel_id=1, source_target_pairs={{0,1},{1,0},{2,3},{3,2},{4,5},{5,4},{6,7},{7,6},{8,9},{9,8},{10,11... | collective-permute-start | bytes 1179656 | tf_op jit(solution)/shard_map/ppermute | solution.py:218
  6.7 0.0 copy-done.6
  6.7 0.0 copy-done.7
  6.7 6.9 %collective-permute-start = (bf16[2,128,128]{2,1,0:T(8,128)(2,1)S(1)}, bf16[2,128,128]{2,1,0:T(8,128)(2,1)S(1)}, u32[]{:S(2)}, u32[]{:S(2)}) collective-permute-start(bf16[2,128,128]{2,1,0:T(8,128)(2,1)S(1)} %pad_maximum_fusion), channel_id=1, source_target_pairs={{0,0},{1,8},{2,2},{3,10},{4,4},{5,12},{6,6},{7,14},{8,128},{9,136}... | collective-permute-start | bytes 196616 | tf_op jit(solution)/shard_map/ppermute | solution.py:216
  13.6 4.2 %collective-permute-done.acts_ref = bf16[2,128,128]{2,1,0:T(8,128)(2,1)S(1)} collective-permute-done((bf16[2,128,128]{2,1,0:T(8,128)(2,1)S(1)}, bf16[2,128,128]{2,1,0:T(8,128)(2,1)S(1)}, u32[]{:S(2)}, u32[]{:S(2)}) %collective-permute-start) | collective-permute-done | bytes 65568 | tf_op jit(solution)/shard_map/ppermute | solution.py:216
  17.8 1.2 spread.1
  19.0 0.0 collective-permute-done.1.refs_1_
  19.0 14.6 %all-to-all-start = ((bf16[16,2,128,128]{3,2,1,0:T(8,128)(2,1)}), bf16[16,2,128,128]{3,2,1,0:T(8,128)(2,1)S(1)}, u32[]{:S(2)}, u32[]{:S(2)}) async-start(bf16[16,2,128,128]{3,2,1,0:T(8,128)(2,1)} %spread.1), calls=%async_computation | async-start | bytes 2097152 | tf_op jit(solution)/shard_map/all_to_all | solution.py:209
  33.6 3.2 %collective-permute-start.2 = (bf16[3,256,256]{2,1,0:T(8,128)(2,1)S(1)}, bf16[3,256,256]{2,1,0:T(8,128)(2,1)S(1)}, u32[]{:S(2)}, u32[]{:S(2)}) collective-permute-start(bf16[3,256,256]{2,1,0:T(8,128)(2,1)S(1)} %multiply_convert_fusion.refs_0_), channel_id=1, source_target_pairs={{0,64},{64,0},{1,65},{65,1},{2,66},{66,2},{3,67},{67,3},{4,68},{68... | collective-permute-start | bytes 1179656 | tf_op jit(solution)/shard_map/ppermute | solution.py:220
  36.8 2.7 %collective-permute-start.3 = (bf16[3,256,256]{2,1,0:T(8,128)(2,1)S(1)}, bf16[3,256,256]{2,1,0:T(8,128)(2,1)S(1)}, u32[]{:S(2)}, u32[]{:S(2)}) collective-permute-start(bf16[3,256,256]{2,1,0:T(8,128)(2,1)S(1)} %collective-permute-done.1.refs_1_), channel_id=1, source_target_pairs={{0,64},{64,0},{1,65},{65,1},{2,66},{66,2},{3,67},{67,3},{4,68},{68... | collective-permute-start | bytes 1179656 | tf_op jit(solution)/shard_map/ppermute | solution.py:220
  39.4 1.9 %collective-permute-start.4 = (bf16[3,256,256]{2,1,0:T(8,128)(2,1)S(1)}, bf16[3,256,256]{2,1,0:T(8,128)(2,1)S(1)}, u32[]{:S(2)}, u32[]{:S(2)}) collective-permute-start(bf16[3,256,256]{2,1,0:T(8,128)(2,1)S(1)} %multiply_convert_fusion.refs_0_), channel_id=1, source_target_pairs={{0,32},{32,0},{1,33},{33,1},{2,34},{34,2},{3,35},{35,3},{4,36},{36... | collective-permute-start | bytes 1179656 | tf_op jit(solution)/shard_map/ppermute | solution.py:221
  41.4 2.4 %collective-permute-start.5 = (bf16[3,256,256]{2,1,0:T(8,128)(2,1)S(1)}, bf16[3,256,256]{2,1,0:T(8,128)(2,1)S(1)}, u32[]{:S(2)}, u32[]{:S(2)}) collective-permute-start(bf16[3,256,256]{2,1,0:T(8,128)(2,1)S(1)} %collective-permute-done.1.refs_1_), channel_id=1, source_target_pairs={{0,32},{32,0},{1,33},{33,1},{2,34},{34,2},{3,35},{35,3},{4,36},{36... | collective-permute-start | bytes 1179656 | tf_op jit(solution)/shard_map/ppermute | solution.py:221
  43.8 3.7 %collective-permute-done.2.refs_2_ = bf16[3,256,256]{2,1,0:T(8,128)(2,1)S(1)} collective-permute-done((bf16[3,256,256]{2,1,0:T(8,128)(2,1)S(1)}, bf16[3,256,256]{2,1,0:T(8,128)(2,1)S(1)}, u32[]{:S(2)}, u32[]{:S(2)}) %collective-permute-start.2) | collective-permute-done | bytes 393248 | tf_op jit(solution)/shard_map/ppermute | solution.py:220
  47.5 1.9 %collective-permute-start.6 = (bf16[3,256,256]{2,1,0:T(8,128)(2,1)S(1)}, bf16[3,256,256]{2,1,0:T(8,128)(2,1)}, u32[]{:S(2)}, u32[]{:S(2)}) collective-permute-start(bf16[3,256,256]{2,1,0:T(8,128)(2,1)S(1)} %collective-permute-done.2.refs_2_), channel_id=1, source_target_pairs={{0,32},{32,0},{1,33},{33,1},{2,34},{34,2},{3,35},{35,3},{4,36},{36... | collective-permute-start | bytes 1179656 | tf_op jit(solution)/shard_map/ppermute | solution.py:221
  49.4 3.7 %collective-permute-done.3.refs_3_ = bf16[3,256,256]{2,1,0:T(8,128)(2,1)S(1)} collective-permute-done((bf16[3,256,256]{2,1,0:T(8,128)(2,1)S(1)}, bf16[3,256,256]{2,1,0:T(8,128)(2,1)S(1)}, u32[]{:S(2)}, u32[]{:S(2)}) %collective-permute-start.3) | collective-permute-done | bytes 393248 | tf_op jit(solution)/shard_map/ppermute | solution.py:220
  53.2 1.9 %collective-permute-start.7 = (bf16[3,256,256]{2,1,0:T(8,128)(2,1)S(1)}, bf16[3,256,256]{2,1,0:T(8,128)(2,1)}, u32[]{:S(2)}, u32[]{:S(2)}) collective-permute-start(bf16[3,256,256]{2,1,0:T(8,128)(2,1)S(1)} %collective-permute-done.3.refs_3_), channel_id=1, source_target_pairs={{0,32},{32,0},{1,33},{33,1},{2,34},{34,2},{3,35},{35,3},{4,36},{36... | collective-permute-start | bytes 1179656 | tf_op jit(solution)/shard_map/ppermute | solution.py:221
  55.1 0.1 pad_add_fusion.place_ref
  55.2 0.0 collective-permute-done.4.refs_4_
  55.2 0.0 copy-start
  55.2 0.0 collective-permute-done.6.refs_6_
  55.2 0.0 collective-permute-done.5.refs_5_
  55.2 0.0 copy-start.2
  55.2 1.7 %collective-permute-done.7.refs_7_ = bf16[3,256,256]{2,1,0:T(8,128)(2,1)} collective-permute-done((bf16[3,256,256]{2,1,0:T(8,128)(2,1)S(1)}, bf16[3,256,256]{2,1,0:T(8,128)(2,1)}, u32[]{:S(2)}, u32[]{:S(2)}) %collective-permute-start.7) | collective-permute-done | bytes 393248 | tf_op jit(solution)/shard_map/ppermute | solution.py:221
  56.9 4.6 %all-to-all-done = bf16[16,2,128,128]{3,2,1,0:T(8,128)(2,1)S(1)} async-done(((bf16[16,2,128,128]{3,2,1,0:T(8,128)(2,1)}), bf16[16,2,128,128]{3,2,1,0:T(8,128)(2,1)S(1)}, u32[]{:S(2)}, u32[]{:S(2)}) %all-to-all-start) | async-done | bytes 1048608 | tf_op jit(solution)/shard_map/all_to_all | solution.py:209
  61.5 3.0 %gates.1 = bf16[256,1536]{1,0:T(8,128)(2,1)} custom-call(s32[3]{0:T(128)S(1)} %pad_add_fusion.place_ref, bf16[8,2,2,128,128]{4,3,2,1,0:T(8,128)(2,1)S(1)} %bitcast.20, bf16[3,256,256]{2,1,0:T(8,128)(2,1)S(1)} %multiply_convert_fusion.refs_0_, bf16[3,256,256]{2,1,0:T(8,128)(2,1)S(1)} %collective-permute-done.1.refs_1_, ...), custom_call_target="tpu_custom_call" | custom-call | flops 800000000 | bytes 6000000 | tf_op jit(solution)/shard_map/gates/pallas_call | solution.py:104
  64.5 0.0 copy-done
  64.5 0.0 copy-done.2
  64.5 9.3 %all-to-all-start.1 = ((bf16[4,64,1536]{2,1,0:T(8,128)(2,1)}), bf16[4,64,1536]{2,1,0:T(8,128)(2,1)S(1)}, u32[]{:S(2)}, u32[]{:S(2)}) async-start(bf16[4,64,1536]{2,1,0:T(8,128)(2,1)} %bitcast.7), calls=%async_computation.1 | async-start | bytes 1572864 | tf_op jit(solution)/shard_map/all_to_all | solution.py:209
  73.9 1.9 %collective-permute-start.8 = (bf16[2,2,2,2,128,128]{5,4,3,2,1,0:T(8,128)(2,1)S(1)}, bf16[2,2,2,2,128,128]{5,4,3,2,1,0:T(8,128)(2,1)S(1)}, u32[]{:S(2)}, u32[]{:S(2)}) collective-permute-start(bf16[2,2,2,2,128,128]{5,4,3,2,1,0:T(8,128)(2,1)S(1)} %dynamic-slice_bitcast_fusion), channel_id=1, source_target_pairs={{0,32},{32,0},{1,33},{33,1},{2,34},{34,2},{3,35},{35,3},{4,36},{36... | collective-permute-start | bytes 1572872 | tf_op jit(solution)/shard_map/ppermute | solution.py:227
  75.8 1.9 %collective-permute-done.8.other_acts_ref = bf16[2,2,2,2,128,128]{5,4,3,2,1,0:T(8,128)(2,1)S(1)} collective-permute-done((bf16[2,2,2,2,128,128]{5,4,3,2,1,0:T(8,128)(2,1)S(1)}, bf16[2,2,2,2,128,128]{5,4,3,2,1,0:T(8,128)(2,1)S(1)}, u32[]{:S(2)}, u32[]{:S(2)}) %collective-permute-start.8) | collective-permute-done | bytes 524320 | tf_op jit(solution)/shard_map/ppermute | solution.py:227
  77.7 0.0 copy-start.4
  77.7 0.8 copy-done.4
  78.5 2.8 %all-to-all-done.1.parts_ref = bf16[4,64,1536]{2,1,0:T(8,128)(2,1)S(1)} async-done(((bf16[4,64,1536]{2,1,0:T(8,128)(2,1)}), bf16[4,64,1536]{2,1,0:T(8,128)(2,1)S(1)}, u32[]{:S(2)}, u32[]{:S(2)}) %all-to-all-start.1) | async-done | bytes 786464 | tf_op jit(solution)/shard_map/all_to_all | solution.py:209
  81.3 0.2 hidden_grads.1
  81.5 0.0 copy-start.1
  81.5 0.0 copy-start.3
  81.5 13.4 %all_to_all.20 = bf16[4,64,1536]{2,1,0:T(8,128)(2,1)S(1)} all-to-all(bf16[4,64,1536]{2,1,0:T(8,128)(2,1)S(1)} %hidden_grads.1), channel_id=1, replica_groups=mesh['yl'=2,'x1'=2,'x0'=2,'core'=2,'yh1'=2,'yh0'=2,'zh1'=2,'zh0'=2,'zl'=..., dimensions={0} | all-to-all | bytes 1572864 | tf_op jit(solution)/shard_map/all_to_all | solution.py:209
  94.8 0.0 copy-done.1
  94.8 0.0 copy-done.3
  94.8 2.7 %input_terms.1 = bf16[8,2,128,128]{3,2,1,0:T(8,128)(2,1)} custom-call(s32[3]{0:T(128)S(1)} %pad_add_fusion.place_ref, bf16[256,1536]{1,0:T(8,128)(2,1)S(1)} %bitcast.23, bf16[3,256,256]{2,1,0:T(8,128)(2,1)S(1)} %multiply_convert_fusion.refs_0_, bf16[3,256,256]{2,1,0:T(8,128)(2,1)S(1)} %collective-permute-done.1.refs_1_, ...), custom_call_target="tpu_custom_call" | custom-call | flops 540000000 | bytes 4000000 | tf_op jit(solution)/shard_map/input_terms/pallas_call | solution.py:159
  97.5 0.0 copy-start.5
  97.5 5.4 %all-to-all-start.3 = ((bf16[8,2,128,128]{3,2,1,0:T(8,128)(2,1)}), bf16[8,2,128,128]{3,2,1,0:T(8,128)(2,1)}, u32[]{:S(2)}, u32[]{:S(2)}) async-start(bf16[8,2,128,128]{3,2,1,0:T(8,128)(2,1)} %input_terms.1), calls=%async_computation.3 | async-start | bytes 1048576 | tf_op jit(solution)/shard_map/all_to_all | solution.py:209
  102.9 1.9 %collective-permute-start.11 = (bf16[256,1536]{1,0:T(8,128)(2,1)S(1)}, bf16[256,1536]{1,0:T(8,128)(2,1)S(1)}, u32[]{:S(2)}, u32[]{:S(2)}) collective-permute-start(bf16[256,1536]{1,0:T(8,128)(2,1)S(1)} %bitcast.24), channel_id=1, source_target_pairs={{0,32},{32,0},{1,33},{33,1},{2,34},{34,2},{3,35},{35,3},{4,36},{36... | collective-permute-start | bytes 2359304 | tf_op jit(solution)/shard_map/ppermute | solution.py:231
  104.9 2.3 %collective-permute-done.11.other_grads_ref = bf16[256,1536]{1,0:T(8,128)(2,1)S(1)} collective-permute-done((bf16[256,1536]{1,0:T(8,128)(2,1)S(1)}, bf16[256,1536]{1,0:T(8,128)(2,1)S(1)}, u32[]{:S(2)}, u32[]{:S(2)}) %collective-permute-start.11) | collective-permute-done | bytes 786464 | tf_op jit(solution)/shard_map/ppermute | solution.py:231
  107.1 0.0 copy-done.5
  107.1 2.4 %weight_terms.1 = (f32[3,256,256]{2,1,0:T(8,128)S(1)}, bf16[3,256,256]{2,1,0:T(8,128)(2,1)}, bf16[3,256,256]{2,1,0:T(8,128)(2,1)}, bf16[3,256,256]{2,1,0:T(8,128)(2,1)}) custom-call(s32[3]{0:T(128)S(1)} %pad_add_fusion.place_ref, bf16[8,2,2,128,128]{4,3,2,1,0:T(8,128)(2,1)S(1)} %bitcast.22, bf16[2,2,2,2,128,128]{5,4,3,2,1,0:T(8,128)(2,1)S(1)} %copy-done.5, ...), custom_call_target="tpu_custom_call" | custom-call | flops 800000000 | bytes 6000000 | tf_op jit(solution)/shard_map/weight_terms/pallas_call | solution.py:196
  109.5 6.6 %collective-permute-start.12 = (bf16[3,256,256]{2,1,0:T(8,128)(2,1)}, bf16[3,256,256]{2,1,0:T(8,128)(2,1)S(1)}, u32[]{:S(2)}, u32[]{:S(2)}) collective-permute-start(bf16[3,256,256]{2,1,0:T(8,128)(2,1)} %get-tuple-element.15), channel_id=1, source_target_pairs={{0,1},{1,0},{2,3},{3,2},{4,5},{5,4},{6,7},{7,6},{8,9},{9,8},{10,11... | collective-permute-start | bytes 1179656 | tf_op jit(solution)/shard_map/ppermute | solution.py:239
  116.1 2.5 %collective-permute-start.13 = (bf16[3,256,256]{2,1,0:T(8,128)(2,1)}, bf16[3,256,256]{2,1,0:T(8,128)(2,1)S(1)}, u32[]{:S(2)}, u32[]{:S(2)}) collective-permute-start(bf16[3,256,256]{2,1,0:T(8,128)(2,1)} %get-tuple-element.16), channel_id=1, source_target_pairs={{0,64},{64,0},{1,65},{65,1},{2,66},{66,2},{3,67},{67,3},{4,68},{68... | collective-permute-start | bytes 1179656 | tf_op jit(solution)/shard_map/ppermute | solution.py:240
  118.6 2.8 %collective-permute-start.14 = (bf16[3,256,256]{2,1,0:T(8,128)(2,1)}, bf16[3,256,256]{2,1,0:T(8,128)(2,1)S(1)}, u32[]{:S(2)}, u32[]{:S(2)}) collective-permute-start(bf16[3,256,256]{2,1,0:T(8,128)(2,1)} %get-tuple-element.17), channel_id=1, source_target_pairs={{0,65},{1,64},{64,1},{65,0},{2,67},{3,66},{66,3},{67,2},{4,69},{5,... | collective-permute-start | bytes 1179656 | tf_op jit(solution)/shard_map/ppermute | solution.py:241
  121.4 0.0 all-to-all-done.3
  121.4 1.1 reduce_sum.12
  122.6 6.9 %collective-permute-start.9 = (bf16[128,128]{1,0:T(8,128)(2,1)S(1)}, bf16[128,128]{1,0:T(8,128)(2,1)S(1)}, u32[]{:S(2)}, u32[]{:S(2)}) collective-permute-start(bf16[128,128]{1,0:T(8,128)(2,1)S(1)} %get-tuple-element.18), channel_id=1, source_target_pairs={{0,0},{8,1},{2,2},{10,3},{4,4},{12,5},{6,6},{14,7},{128,8},{136,9}... | collective-permute-start | bytes 98312 | tf_op jit(solution)/shard_map/ppermute | solution.py:235
  129.4 5.9 %collective-permute-start.10 = (bf16[128,128]{1,0:T(8,128)(2,1)S(1)}, bf16[128,128]{1,0:T(8,128)(2,1)S(1)}, u32[]{:S(2)}, u32[]{:S(2)}) collective-permute-start(bf16[128,128]{1,0:T(8,128)(2,1)S(1)} %get-tuple-element.19), channel_id=1, source_target_pairs={{16,0},{24,1},{18,2},{26,3},{20,4},{28,5},{22,6},{30,7},{144,8},{1... | collective-permute-start | bytes 98312 | tf_op jit(solution)/shard_map/ppermute | solution.py:235
  135.4 2.5 %collective-permute-done.9 = bf16[128,128]{1,0:T(8,128)(2,1)S(1)} collective-permute-done((bf16[128,128]{1,0:T(8,128)(2,1)S(1)}, bf16[128,128]{1,0:T(8,128)(2,1)S(1)}, u32[]{:S(2)}, u32[]{:S(2)}) %collective-permute-start.9) | collective-permute-done | bytes 32800 | tf_op jit(solution)/shard_map/ppermute | solution.py:235
  138.0 4.7 %collective-permute-done.10 = bf16[128,128]{1,0:T(8,128)(2,1)S(1)} collective-permute-done((bf16[128,128]{1,0:T(8,128)(2,1)S(1)}, bf16[128,128]{1,0:T(8,128)(2,1)S(1)}, u32[]{:S(2)}, u32[]{:S(2)}) %collective-permute-start.10) | collective-permute-done | bytes 32800 | tf_op jit(solution)/shard_map/ppermute | solution.py:235
  142.7 0.6 add_convert_fusion
  143.3 0.0 collective-permute-done.12
  143.3 0.0 collective-permute-done.13
  143.3 0.0 collective-permute-done.14
  143.3 1.0 convert_add_fusion
  (3 shorter events, 0.1 us)
Async XLA Ops:
  1.3 5.4 %copy-start.6 = (bf16[128,128]{1,0:T(8,128)(2,1)S(1)}, bf16[128,128]{1,0:T(8,128)(2,1)}, u32[]{:S(2)}) copy-start(bf16[128,128]{1,0:T(8,128)(2,1)} %param.5) | copy-start | bytes 98308
  1.3 5.4 %copy-start.7 = (bf16[128,128]{1,0:T(8,128)(2,1)S(1)}, bf16[128,128]{1,0:T(8,128)(2,1)}, u32[]{:S(2)}) copy-start(bf16[128,128]{1,0:T(8,128)(2,1)} %param.4) | copy-start | bytes 98308
  2.4 16.6 %collective-permute-start.1 = (bf16[3,256,256]{2,1,0:T(8,128)(2,1)S(1)}, bf16[3,256,256]{2,1,0:T(8,128)(2,1)S(1)}, u32[]{:S(2)}, u32[]{:S(2)}) collective-permute-start(bf16[3,256,256]{2,1,0:T(8,128)(2,1)S(1)} %multiply_convert_fusion.refs_0_), channel_id=1, source_target_pairs={{0,1},{1,0},{2,3},{3,2},{4,5},{5,4},{6,7},{7,6},{8,9},{9,8},{10,11... | collective-permute-start | bytes 1179656 | tf_op jit(solution)/shard_map/ppermute | solution.py:218
  6.7 11.1 %collective-permute-start = (bf16[2,128,128]{2,1,0:T(8,128)(2,1)S(1)}, bf16[2,128,128]{2,1,0:T(8,128)(2,1)S(1)}, u32[]{:S(2)}, u32[]{:S(2)}) collective-permute-start(bf16[2,128,128]{2,1,0:T(8,128)(2,1)S(1)} %pad_maximum_fusion), channel_id=1, source_target_pairs={{0,0},{1,8},{2,2},{3,10},{4,4},{5,12},{6,6},{7,14},{8,128},{9,136}... | collective-permute-start | bytes 196616 | tf_op jit(solution)/shard_map/ppermute | solution.py:216
  19.0 42.5 %all-to-all-start = ((bf16[16,2,128,128]{3,2,1,0:T(8,128)(2,1)}), bf16[16,2,128,128]{3,2,1,0:T(8,128)(2,1)S(1)}, u32[]{:S(2)}, u32[]{:S(2)}) async-start(bf16[16,2,128,128]{3,2,1,0:T(8,128)(2,1)} %spread.1), calls=%async_computation | async-start | bytes 2097152 | tf_op jit(solution)/shard_map/all_to_all | solution.py:209
  33.6 13.9 %collective-permute-start.2 = (bf16[3,256,256]{2,1,0:T(8,128)(2,1)S(1)}, bf16[3,256,256]{2,1,0:T(8,128)(2,1)S(1)}, u32[]{:S(2)}, u32[]{:S(2)}) collective-permute-start(bf16[3,256,256]{2,1,0:T(8,128)(2,1)S(1)} %multiply_convert_fusion.refs_0_), channel_id=1, source_target_pairs={{0,64},{64,0},{1,65},{65,1},{2,66},{66,2},{3,67},{67,3},{4,68},{68... | collective-permute-start | bytes 1179656 | tf_op jit(solution)/shard_map/ppermute | solution.py:220
  36.8 16.4 %collective-permute-start.3 = (bf16[3,256,256]{2,1,0:T(8,128)(2,1)S(1)}, bf16[3,256,256]{2,1,0:T(8,128)(2,1)S(1)}, u32[]{:S(2)}, u32[]{:S(2)}) collective-permute-start(bf16[3,256,256]{2,1,0:T(8,128)(2,1)S(1)} %collective-permute-done.1.refs_1_), channel_id=1, source_target_pairs={{0,64},{64,0},{1,65},{65,1},{2,66},{66,2},{3,67},{67,3},{4,68},{68... | collective-permute-start | bytes 1179656 | tf_op jit(solution)/shard_map/ppermute | solution.py:220
  39.4 15.7 %collective-permute-start.4 = (bf16[3,256,256]{2,1,0:T(8,128)(2,1)S(1)}, bf16[3,256,256]{2,1,0:T(8,128)(2,1)S(1)}, u32[]{:S(2)}, u32[]{:S(2)}) collective-permute-start(bf16[3,256,256]{2,1,0:T(8,128)(2,1)S(1)} %multiply_convert_fusion.refs_0_), channel_id=1, source_target_pairs={{0,32},{32,0},{1,33},{33,1},{2,34},{34,2},{3,35},{35,3},{4,36},{36... | collective-permute-start | bytes 1179656 | tf_op jit(solution)/shard_map/ppermute | solution.py:221
  41.4 13.8 %collective-permute-start.5 = (bf16[3,256,256]{2,1,0:T(8,128)(2,1)S(1)}, bf16[3,256,256]{2,1,0:T(8,128)(2,1)S(1)}, u32[]{:S(2)}, u32[]{:S(2)}) collective-permute-start(bf16[3,256,256]{2,1,0:T(8,128)(2,1)S(1)} %collective-permute-done.1.refs_1_), channel_id=1, source_target_pairs={{0,32},{32,0},{1,33},{33,1},{2,34},{34,2},{3,35},{35,3},{4,36},{36... | collective-permute-start | bytes 1179656 | tf_op jit(solution)/shard_map/ppermute | solution.py:221
  47.5 7.7 %collective-permute-start.6 = (bf16[3,256,256]{2,1,0:T(8,128)(2,1)S(1)}, bf16[3,256,256]{2,1,0:T(8,128)(2,1)}, u32[]{:S(2)}, u32[]{:S(2)}) collective-permute-start(bf16[3,256,256]{2,1,0:T(8,128)(2,1)S(1)} %collective-permute-done.2.refs_2_), channel_id=1, source_target_pairs={{0,32},{32,0},{1,33},{33,1},{2,34},{34,2},{3,35},{35,3},{4,36},{36... | collective-permute-start | bytes 1179656 | tf_op jit(solution)/shard_map/ppermute | solution.py:221
  53.2 3.7 %collective-permute-start.7 = (bf16[3,256,256]{2,1,0:T(8,128)(2,1)S(1)}, bf16[3,256,256]{2,1,0:T(8,128)(2,1)}, u32[]{:S(2)}, u32[]{:S(2)}) collective-permute-start(bf16[3,256,256]{2,1,0:T(8,128)(2,1)S(1)} %collective-permute-done.3.refs_3_), channel_id=1, source_target_pairs={{0,32},{32,0},{1,33},{33,1},{2,34},{34,2},{3,35},{35,3},{4,36},{36... | collective-permute-start | bytes 1179656 | tf_op jit(solution)/shard_map/ppermute | solution.py:221
  55.2 9.3 %copy-start = (bf16[3,256,256]{2,1,0:T(8,128)(2,1)}, bf16[3,256,256]{2,1,0:T(8,128)(2,1)S(1)}, u32[]{:S(2)}) copy-start(bf16[3,256,256]{2,1,0:T(8,128)(2,1)S(1)} %collective-permute-done.4.refs_4_) | copy-start | bytes 1179652
  55.2 9.3 %copy-start.2 = (bf16[3,256,256]{2,1,0:T(8,128)(2,1)}, bf16[3,256,256]{2,1,0:T(8,128)(2,1)S(1)}, u32[]{:S(2)}) copy-start(bf16[3,256,256]{2,1,0:T(8,128)(2,1)S(1)} %collective-permute-done.5.refs_5_) | copy-start | bytes 1179652
  64.5 16.8 %all-to-all-start.1 = ((bf16[4,64,1536]{2,1,0:T(8,128)(2,1)}), bf16[4,64,1536]{2,1,0:T(8,128)(2,1)S(1)}, u32[]{:S(2)}, u32[]{:S(2)}) async-start(bf16[4,64,1536]{2,1,0:T(8,128)(2,1)} %bitcast.7), calls=%async_computation.1 | async-start | bytes 1572864 | tf_op jit(solution)/shard_map/all_to_all | solution.py:209
  73.9 3.8 %collective-permute-start.8 = (bf16[2,2,2,2,128,128]{5,4,3,2,1,0:T(8,128)(2,1)S(1)}, bf16[2,2,2,2,128,128]{5,4,3,2,1,0:T(8,128)(2,1)S(1)}, u32[]{:S(2)}, u32[]{:S(2)}) collective-permute-start(bf16[2,2,2,2,128,128]{5,4,3,2,1,0:T(8,128)(2,1)S(1)} %dynamic-slice_bitcast_fusion), channel_id=1, source_target_pairs={{0,32},{32,0},{1,33},{33,1},{2,34},{34,2},{3,35},{35,3},{4,36},{36... | collective-permute-start | bytes 1572872 | tf_op jit(solution)/shard_map/ppermute | solution.py:227
  77.7 0.8 copy-start.4
  81.5 13.4 %copy-start.1 = (bf16[3,256,256]{2,1,0:T(8,128)(2,1)S(1)}, bf16[3,256,256]{2,1,0:T(8,128)(2,1)}, u32[]{:S(2)}) copy-start(bf16[3,256,256]{2,1,0:T(8,128)(2,1)} %copy-done) | copy-start | bytes 1179652
  81.5 13.4 %copy-start.3 = (bf16[3,256,256]{2,1,0:T(8,128)(2,1)S(1)}, bf16[3,256,256]{2,1,0:T(8,128)(2,1)}, u32[]{:S(2)}) copy-start(bf16[3,256,256]{2,1,0:T(8,128)(2,1)} %copy-done.2) | copy-start | bytes 1179652
  97.5 9.6 %copy-start.5 = (bf16[2,2,2,2,128,128]{5,4,3,2,1,0:T(8,128)(2,1)S(1)}, bf16[2,2,2,2,128,128]{5,4,3,2,1,0:T(8,128)(2,1)}, u32[]{:S(2)}) copy-start(bf16[2,2,2,2,128,128]{5,4,3,2,1,0:T(8,128)(2,1)} %copy-done.4) | copy-start | bytes 1572868
  97.5 23.9 %all-to-all-start.3 = ((bf16[8,2,128,128]{3,2,1,0:T(8,128)(2,1)}), bf16[8,2,128,128]{3,2,1,0:T(8,128)(2,1)}, u32[]{:S(2)}, u32[]{:S(2)}) async-start(bf16[8,2,128,128]{3,2,1,0:T(8,128)(2,1)} %input_terms.1), calls=%async_computation.3 | async-start | bytes 1048576 | tf_op jit(solution)/shard_map/all_to_all | solution.py:209
  102.9 4.2 %collective-permute-start.11 = (bf16[256,1536]{1,0:T(8,128)(2,1)S(1)}, bf16[256,1536]{1,0:T(8,128)(2,1)S(1)}, u32[]{:S(2)}, u32[]{:S(2)}) collective-permute-start(bf16[256,1536]{1,0:T(8,128)(2,1)S(1)} %bitcast.24), channel_id=1, source_target_pairs={{0,32},{32,0},{1,33},{33,1},{2,34},{34,2},{3,35},{35,3},{4,36},{36... | collective-permute-start | bytes 2359304 | tf_op jit(solution)/shard_map/ppermute | solution.py:231
  109.5 33.8 %collective-permute-start.12 = (bf16[3,256,256]{2,1,0:T(8,128)(2,1)}, bf16[3,256,256]{2,1,0:T(8,128)(2,1)S(1)}, u32[]{:S(2)}, u32[]{:S(2)}) collective-permute-start(bf16[3,256,256]{2,1,0:T(8,128)(2,1)} %get-tuple-element.15), channel_id=1, source_target_pairs={{0,1},{1,0},{2,3},{3,2},{4,5},{5,4},{6,7},{7,6},{8,9},{9,8},{10,11... | collective-permute-start | bytes 1179656 | tf_op jit(solution)/shard_map/ppermute | solution.py:239
  116.1 27.2 %collective-permute-start.13 = (bf16[3,256,256]{2,1,0:T(8,128)(2,1)}, bf16[3,256,256]{2,1,0:T(8,128)(2,1)S(1)}, u32[]{:S(2)}, u32[]{:S(2)}) collective-permute-start(bf16[3,256,256]{2,1,0:T(8,128)(2,1)} %get-tuple-element.16), channel_id=1, source_target_pairs={{0,64},{64,0},{1,65},{65,1},{2,66},{66,2},{3,67},{67,3},{4,68},{68... | collective-permute-start | bytes 1179656 | tf_op jit(solution)/shard_map/ppermute | solution.py:240
  118.6 24.7 %collective-permute-start.14 = (bf16[3,256,256]{2,1,0:T(8,128)(2,1)}, bf16[3,256,256]{2,1,0:T(8,128)(2,1)S(1)}, u32[]{:S(2)}, u32[]{:S(2)}) collective-permute-start(bf16[3,256,256]{2,1,0:T(8,128)(2,1)} %get-tuple-element.17), channel_id=1, source_target_pairs={{0,65},{1,64},{64,1},{65,0},{2,67},{3,66},{66,3},{67,2},{4,69},{5,... | collective-permute-start | bytes 1179656 | tf_op jit(solution)/shard_map/ppermute | solution.py:241
  122.6 15.4 %collective-permute-start.9 = (bf16[128,128]{1,0:T(8,128)(2,1)S(1)}, bf16[128,128]{1,0:T(8,128)(2,1)S(1)}, u32[]{:S(2)}, u32[]{:S(2)}) collective-permute-start(bf16[128,128]{1,0:T(8,128)(2,1)S(1)} %get-tuple-element.18), channel_id=1, source_target_pairs={{0,0},{8,1},{2,2},{10,3},{4,4},{12,5},{6,6},{14,7},{128,8},{136,9}... | collective-permute-start | bytes 98312 | tf_op jit(solution)/shard_map/ppermute | solution.py:235
  129.4 13.2 %collective-permute-start.10 = (bf16[128,128]{1,0:T(8,128)(2,1)S(1)}, bf16[128,128]{1,0:T(8,128)(2,1)S(1)}, u32[]{:S(2)}, u32[]{:S(2)}) collective-permute-start(bf16[128,128]{1,0:T(8,128)(2,1)S(1)} %get-tuple-element.19), channel_id=1, source_target_pairs={{16,0},{24,1},{18,2},{26,3},{20,4},{28,5},{22,6},{30,7},{144,8},{1... | collective-permute-start | bytes 98312 | tf_op jit(solution)/shard_map/ppermute | solution.py:235

commit v20 on v19

--- a/solution.py
+++ b/solution.py
@@ -13,7 +13,7 @@
 COL = ("yh1", "yh0", "zh1", "zh0", "zl")
 AXES = ROW + COL
 SPREAD = ("yh0", "zh1", "zh0")
-GATHER = ("zh1", "zh0", "yh0", "yh1")
+GATHER = ("zh0", "zh1", "yh0", "yh1")
 REST = ("x1", "yl")
 SWAP = [(0, 1), (1, 0)]
 TOK = 128
@@ -52,7 +52,7 @@
 
 def gathered(place_ref, f):
     core, x0, b = place_of(place_ref, f)
-    return 4 * x0 + 2 * core + b
+    return 4 * core + 2 * x0 + b
 
 
 def summed(place_ref, f):
@@ -223,7 +223,7 @@
 
     parts = gates(place, acts, *weights)
     other_acts = acts.reshape(2, 2, 2, 2, 2, TOK, TOK)
-    other_acts = lax.dynamic_index_in_dim(other_acts, 1 - place[0], axis=1, keepdims=False)
+    other_acts = lax.dynamic_index_in_dim(other_acts, 1 - place[0], axis=0, keepdims=False)
     other_acts = lax.ppermute(other_acts, "core", SWAP)
     parts = exchange(parts.reshape(4, SHARE, GRADS), REST)
     parts, other_acts = lax.optimization_barrier((parts, other_acts))

time: 145 us -> 143 us (0.986)
  starting transfers between devices: 83 us -> 74.1 us
  waiting for transfers between devices: 32.2 us -> 37.5 us
    all_to_all x3, waiting for transfers between devices: 7.37 us -> 12 us  [exchange(): return lax.all_to_all(pieces, axes, split_axis=0, concat_axis=0, tiled=True)]
    all_to_all x3, starting transfers between devices: 29.3 us -> 25.7 us  [exchange(): return lax.all_to_all(pieces, axes, split_axis=0, concat_axis=0, tiled=True)]
    ppermute x1, starting transfers between devices: 6.61 us -> 3.01 us  [local(): weight_grad += lax.ppermute(z, 'zl', SWAP).astype(F32)]
    ppermute x2, starting transfers between devices: 12.8 us -> 10.3 us  [local(): lax.ppermute(dx[i], AXES, [(b, a) for a, b in there[i]])]
  transfers between devices with their start and end apart: 18 -> 18, of which waited for: 10 -> 11; matrix products, arithmetic and copies ran while one was open for 1% -> 1% of each run, Pallas kernels for 2% -> 2%
where the time goes in v20:
time: 143 us; the launch traced here: 142 us
  starting transfers between devices  74.1 us (52%)
  waiting for transfers between devices  37.5 us (26%)
  blocking collectives  14.3 us (10%)
  Pallas kernels  9.38 us (7%)
  other arithmetic  4.62 us (3%)
    all_to_all x3, starting transfers between devices, exchange(): return lax.all_to_all(pieces, axes, split_axis=0, concat_axis=0, tiled=True)  25.7 us
    all_to_all x1, blocking collectives, exchange(): return lax.all_to_all(pieces, axes, split_axis=0, concat_axis=0, tiled=True)  14.3 us
    all_to_all x3, waiting for transfers between devices, exchange(): return lax.all_to_all(pieces, axes, split_axis=0, concat_axis=0, tiled=True)  12 us
    ppermute x2, starting transfers between devices, local(): lax.ppermute(dx[i], AXES, [(b, a) for a, b in there[i]])  10.3 us
    ppermute x4, starting transfers between devices, local(): weights += [lax.ppermute(block, 'core', SWAP) for block in weights]  8.15 us
    ppermute x2, waiting for transfers between devices, local(): lax.ppermute(dx[i], AXES, [(b, a) for a, b in there[i]])  7.91 us
    ppermute x2, waiting for transfers between devices, local(): weights = [w, w_z] + [lax.ppermute(block, 'x0', SWAP) for block in (w, w_z)]  7.47 us
    ppermute x1, starting transfers between devices, local(): acts = spread(lax.ppermute(jnp.stack([inputs, out_grad]), AXES, there[0]))  6.88 us
  transfers between devices with their start and end apart: 18, of which 11 were waited for; matrix products, arithmetic and copies ran while one was open for 1% of the time, Pallas kernels for 2%

profile of v20, /device:TPU:4, one launch (start us, length us, event | category | flops | bytes accessed | tf_op | source)
XLA Modules:
  0.0 141.7 jit_solution(6608199658880562588)
XLA Ops:
  0.6 0.7 bitcast_convert_fusion
  1.3 0.0 copy-start.6
  1.3 0.0 copy-start.7
  1.3 1.1 multiply_convert_fusion.refs_0_
  2.4 4.3 %collective-permute-start.1 = (bf16[3,256,256]{2,1,0:T(8,128)(2,1)S(1)}, bf16[3,256,256]{2,1,0:T(8,128)(2,1)S(1)}, u32[]{:S(2)}, u32[]{:S(2)}) collective-permute-start(bf16[3,256,256]{2,1,0:T(8,128)(2,1)S(1)} %multiply_convert_fusion.refs_0_), channel_id=1, source_target_pairs={{0,1},{1,0},{2,3},{3,2},{4,5},{5,4},{6,7},{7,6},{8,9},{9,8},{10,11... | collective-permute-start | bytes 1179656 | tf_op jit(solution)/shard_map/ppermute | solution.py:218
  6.7 0.0 copy-done.6
  6.7 0.0 copy-done.7
  6.7 6.9 %collective-permute-start = (bf16[2,128,128]{2,1,0:T(8,128)(2,1)S(1)}, bf16[2,128,128]{2,1,0:T(8,128)(2,1)S(1)}, u32[]{:S(2)}, u32[]{:S(2)}) collective-permute-start(bf16[2,128,128]{2,1,0:T(8,128)(2,1)S(1)} %pad_maximum_fusion), channel_id=1, source_target_pairs={{0,0},{1,8},{2,2},{3,10},{4,4},{5,12},{6,6},{7,14},{8,128},{9,136}... | collective-permute-start | bytes 196616 | tf_op jit(solution)/shard_map/ppermute | solution.py:216
  13.6 4.2 %collective-permute-done.acts_ref = bf16[2,128,128]{2,1,0:T(8,128)(2,1)S(1)} collective-permute-done((bf16[2,128,128]{2,1,0:T(8,128)(2,1)S(1)}, bf16[2,128,128]{2,1,0:T(8,128)(2,1)S(1)}, u32[]{:S(2)}, u32[]{:S(2)}) %collective-permute-start) | collective-permute-done | bytes 65568 | tf_op jit(solution)/shard_map/ppermute | solution.py:216
  17.8 1.2 spread.1
  19.0 0.0 collective-permute-done.1.refs_1_
  19.0 14.6 %all-to-all-start = ((bf16[16,2,128,128]{3,2,1,0:T(8,128)(2,1)}), bf16[16,2,128,128]{3,2,1,0:T(8,128)(2,1)S(1)}, u32[]{:S(2)}, u32[]{:S(2)}) async-start(bf16[16,2,128,128]{3,2,1,0:T(8,128)(2,1)} %spread.1), calls=%async_computation | async-start | bytes 2097152 | tf_op jit(solution)/shard_map/all_to_all | solution.py:209
  33.6 3.2 %collective-permute-start.2 = (bf16[3,256,256]{2,1,0:T(8,128)(2,1)S(1)}, bf16[3,256,256]{2,1,0:T(8,128)(2,1)S(1)}, u32[]{:S(2)}, u32[]{:S(2)}) collective-permute-start(bf16[3,256,256]{2,1,0:T(8,128)(2,1)S(1)} %multiply_convert_fusion.refs_0_), channel_id=1, source_target_pairs={{0,64},{64,0},{1,65},{65,1},{2,66},{66,2},{3,67},{67,3},{4,68},{68... | collective-permute-start | bytes 1179656 | tf_op jit(solution)/shard_map/ppermute | solution.py:220
  36.8 2.7 %collective-permute-start.3 = (bf16[3,256,256]{2,1,0:T(8,128)(2,1)S(1)}, bf16[3,256,256]{2,1,0:T(8,128)(2,1)S(1)}, u32[]{:S(2)}, u32[]{:S(2)}) collective-permute-start(bf16[3,256,256]{2,1,0:T(8,128)(2,1)S(1)} %collective-permute-done.1.refs_1_), channel_id=1, source_target_pairs={{0,64},{64,0},{1,65},{65,1},{2,66},{66,2},{3,67},{67,3},{4,68},{68... | collective-permute-start | bytes 1179656 | tf_op jit(solution)/shard_map/ppermute | solution.py:220
  39.4 1.9 %collective-permute-start.4 = (bf16[3,256,256]{2,1,0:T(8,128)(2,1)S(1)}, bf16[3,256,256]{2,1,0:T(8,128)(2,1)S(1)}, u32[]{:S(2)}, u32[]{:S(2)}) collective-permute-start(bf16[3,256,256]{2,1,0:T(8,128)(2,1)S(1)} %multiply_convert_fusion.refs_0_), channel_id=1, source_target_pairs={{0,32},{32,0},{1,33},{33,1},{2,34},{34,2},{3,35},{35,3},{4,36},{36... | collective-permute-start | bytes 1179656 | tf_op jit(solution)/shard_map/ppermute | solution.py:221
  41.4 2.4 %collective-permute-start.5 = (bf16[3,256,256]{2,1,0:T(8,128)(2,1)S(1)}, bf16[3,256,256]{2,1,0:T(8,128)(2,1)S(1)}, u32[]{:S(2)}, u32[]{:S(2)}) collective-permute-start(bf16[3,256,256]{2,1,0:T(8,128)(2,1)S(1)} %collective-permute-done.1.refs_1_), channel_id=1, source_target_pairs={{0,32},{32,0},{1,33},{33,1},{2,34},{34,2},{3,35},{35,3},{4,36},{36... | collective-permute-start | bytes 1179656 | tf_op jit(solution)/shard_map/ppermute | solution.py:221
  43.8 3.7 %collective-permute-done.2.refs_2_ = bf16[3,256,256]{2,1,0:T(8,128)(2,1)S(1)} collective-permute-done((bf16[3,256,256]{2,1,0:T(8,128)(2,1)S(1)}, bf16[3,256,256]{2,1,0:T(8,128)(2,1)S(1)}, u32[]{:S(2)}, u32[]{:S(2)}) %collective-permute-start.2) | collective-permute-done | bytes 393248 | tf_op jit(solution)/shard_map/ppermute | solution.py:220
  47.5 1.9 %collective-permute-start.6 = (bf16[3,256,256]{2,1,0:T(8,128)(2,1)S(1)}, bf16[3,256,256]{2,1,0:T(8,128)(2,1)}, u32[]{:S(2)}, u32[]{:S(2)}) collective-permute-start(bf16[3,256,256]{2,1,0:T(8,128)(2,1)S(1)} %collective-permute-done.2.refs_2_), channel_id=1, source_target_pairs={{0,32},{32,0},{1,33},{33,1},{2,34},{34,2},{3,35},{35,3},{4,36},{36... | collective-permute-start | bytes 1179656 | tf_op jit(solution)/shard_map/ppermute | solution.py:221
  49.4 3.7 %collective-permute-done.3.refs_3_ = bf16[3,256,256]{2,1,0:T(8,128)(2,1)S(1)} collective-permute-done((bf16[3,256,256]{2,1,0:T(8,128)(2,1)S(1)}, bf16[3,256,256]{2,1,0:T(8,128)(2,1)S(1)}, u32[]{:S(2)}, u32[]{:S(2)}) %collective-permute-start.3) | collective-permute-done | bytes 393248 | tf_op jit(solution)/shard_map/ppermute | solution.py:220
  53.2 1.9 %collective-permute-start.7 = (bf16[3,256,256]{2,1,0:T(8,128)(2,1)S(1)}, bf16[3,256,256]{2,1,0:T(8,128)(2,1)}, u32[]{:S(2)}, u32[]{:S(2)}) collective-permute-start(bf16[3,256,256]{2,1,0:T(8,128)(2,1)S(1)} %collective-permute-done.3.refs_3_), channel_id=1, source_target_pairs={{0,32},{32,0},{1,33},{33,1},{2,34},{34,2},{3,35},{35,3},{4,36},{36... | collective-permute-start | bytes 1179656 | tf_op jit(solution)/shard_map/ppermute | solution.py:221
  55.1 0.1 pad_add_fusion.place_ref
  55.2 0.0 collective-permute-done.4.refs_4_
  55.2 0.0 copy-start
  55.2 0.0 collective-permute-done.6.refs_6_
  55.2 0.0 collective-permute-done.5.refs_5_
  55.2 0.0 copy-start.2
  55.2 1.7 %collective-permute-done.7.refs_7_ = bf16[3,256,256]{2,1,0:T(8,128)(2,1)} collective-permute-done((bf16[3,256,256]{2,1,0:T(8,128)(2,1)S(1)}, bf16[3,256,256]{2,1,0:T(8,128)(2,1)}, u32[]{:S(2)}, u32[]{:S(2)}) %collective-permute-start.7) | collective-permute-done | bytes 393248 | tf_op jit(solution)/shard_map/ppermute | solution.py:221
  56.9 5.0 %all-to-all-done = bf16[16,2,128,128]{3,2,1,0:T(8,128)(2,1)S(1)} async-done(((bf16[16,2,128,128]{3,2,1,0:T(8,128)(2,1)}), bf16[16,2,128,128]{3,2,1,0:T(8,128)(2,1)S(1)}, u32[]{:S(2)}, u32[]{:S(2)}) %all-to-all-start) | async-done | bytes 1048608 | tf_op jit(solution)/shard_map/all_to_all | solution.py:209
  61.9 3.0 %gates.1 = bf16[256,1536]{1,0:T(8,128)(2,1)} custom-call(s32[3]{0:T(128)S(1)} %pad_add_fusion.place_ref, bf16[8,2,2,128,128]{4,3,2,1,0:T(8,128)(2,1)S(1)} %bitcast.18, bf16[3,256,256]{2,1,0:T(8,128)(2,1)S(1)} %multiply_convert_fusion.refs_0_, bf16[3,256,256]{2,1,0:T(8,128)(2,1)S(1)} %collective-permute-done.1.refs_1_, ...), custom_call_target="tpu_custom_call" | custom-call | flops 800000000 | bytes 6000000 | tf_op jit(solution)/shard_map/gates/pallas_call | solution.py:104
  64.9 0.0 copy-done
  64.9 0.0 copy-done.2
  64.9 6.8 %all-to-all-start.1 = ((bf16[4,64,1536]{2,1,0:T(8,128)(2,1)}), bf16[4,64,1536]{2,1,0:T(8,128)(2,1)S(1)}, u32[]{:S(2)}, u32[]{:S(2)}) async-start(bf16[4,64,1536]{2,1,0:T(8,128)(2,1)} %bitcast.7), calls=%async_computation.1 | async-start | bytes 1572864 | tf_op jit(solution)/shard_map/all_to_all | solution.py:209
  71.8 1.9 %collective-permute-start.8 = (bf16[2,2,2,2,128,128]{5,4,3,2,1,0:T(8,128)(2,1)S(1)}, bf16[2,2,2,2,128,128]{5,4,3,2,1,0:T(8,128)(2,1)S(1)}, u32[]{:S(2)}, u32[]{:S(2)}) collective-permute-start(bf16[2,2,2,2,128,128]{5,4,3,2,1,0:T(8,128)(2,1)S(1)} %dynamic-slice_bitcast_fusion), channel_id=1, source_target_pairs={{0,32},{32,0},{1,33},{33,1},{2,34},{34,2},{3,35},{35,3},{4,36},{36... | collective-permute-start | bytes 1572872 | tf_op jit(solution)/shard_map/ppermute | solution.py:227
  73.7 1.9 %collective-permute-done.8.other_acts_ref = bf16[2,2,2,2,128,128]{5,4,3,2,1,0:T(8,128)(2,1)S(1)} collective-permute-done((bf16[2,2,2,2,128,128]{5,4,3,2,1,0:T(8,128)(2,1)S(1)}, bf16[2,2,2,2,128,128]{5,4,3,2,1,0:T(8,128)(2,1)S(1)}, u32[]{:S(2)}, u32[]{:S(2)}) %collective-permute-start.8) | collective-permute-done | bytes 524320 | tf_op jit(solution)/shard_map/ppermute | solution.py:227
  75.6 0.0 copy-start.4
  75.6 0.8 copy-done.4
  76.4 5.2 %all-to-all-done.1.parts_ref = bf16[4,64,1536]{2,1,0:T(8,128)(2,1)S(1)} async-done(((bf16[4,64,1536]{2,1,0:T(8,128)(2,1)}), bf16[4,64,1536]{2,1,0:T(8,128)(2,1)S(1)}, u32[]{:S(2)}, u32[]{:S(2)}) %all-to-all-start.1) | async-done | bytes 786464 | tf_op jit(solution)/shard_map/all_to_all | solution.py:209
  81.6 0.2 hidden_grads.1
  81.7 0.0 copy-start.1
  81.8 0.0 copy-start.3
  81.8 14.3 %all_to_all.20 = bf16[4,64,1536]{2,1,0:T(8,128)(2,1)S(1)} all-to-all(bf16[4,64,1536]{2,1,0:T(8,128)(2,1)S(1)} %hidden_grads.1), channel_id=1, replica_groups=mesh['yl'=2,'x1'=2,'x0'=2,'core'=2,'yh1'=2,'yh0'=2,'zh1'=2,'zh0'=2,'zl'=..., dimensions={0} | all-to-all | bytes 1572864 | tf_op jit(solution)/shard_map/all_to_all | solution.py:209
  96.0 0.0 copy-done.1
  96.0 0.0 copy-done.3
  96.1 2.7 %input_terms.1 = bf16[8,2,128,128]{3,2,1,0:T(8,128)(2,1)} custom-call(s32[3]{0:T(128)S(1)} %pad_add_fusion.place_ref, bf16[256,1536]{1,0:T(8,128)(2,1)S(1)} %bitcast.21, bf16[3,256,256]{2,1,0:T(8,128)(2,1)S(1)} %multiply_convert_fusion.refs_0_, bf16[3,256,256]{2,1,0:T(8,128)(2,1)S(1)} %collective-permute-done.1.refs_1_, ...), custom_call_target="tpu_custom_call" | custom-call | flops 540000000 | bytes 4000000 | tf_op jit(solution)/shard_map/input_terms/pallas_call | solution.py:159
  98.7 0.0 copy-start.5
  98.7 4.3 %all-to-all-start.3 = ((bf16[8,2,128,128]{3,2,1,0:T(8,128)(2,1)}), bf16[8,2,128,128]{3,2,1,0:T(8,128)(2,1)}, u32[]{:S(2)}, u32[]{:S(2)}) async-start(bf16[8,2,128,128]{3,2,1,0:T(8,128)(2,1)} %input_terms.1), calls=%async_computation.3 | async-start | bytes 1048576 | tf_op jit(solution)/shard_map/all_to_all | solution.py:209
  103.0 1.9 %collective-permute-start.11 = (bf16[256,1536]{1,0:T(8,128)(2,1)S(1)}, bf16[256,1536]{1,0:T(8,128)(2,1)S(1)}, u32[]{:S(2)}, u32[]{:S(2)}) collective-permute-start(bf16[256,1536]{1,0:T(8,128)(2,1)S(1)} %bitcast.22), channel_id=1, source_target_pairs={{0,32},{32,0},{1,33},{33,1},{2,34},{34,2},{3,35},{35,3},{4,36},{36... | collective-permute-start | bytes 2359304 | tf_op jit(solution)/shard_map/ppermute | solution.py:231
  105.0 2.3 %collective-permute-done.11.other_grads_ref = bf16[256,1536]{1,0:T(8,128)(2,1)S(1)} collective-permute-done((bf16[256,1536]{1,0:T(8,128)(2,1)S(1)}, bf16[256,1536]{1,0:T(8,128)(2,1)S(1)}, u32[]{:S(2)}, u32[]{:S(2)}) %collective-permute-start.11) | collective-permute-done | bytes 786464 | tf_op jit(solution)/shard_map/ppermute | solution.py:231
  107.2 0.0 copy-done.5
  107.2 2.4 %weight_terms.1 = (f32[3,256,256]{2,1,0:T(8,128)S(1)}, bf16[3,256,256]{2,1,0:T(8,128)(2,1)}, bf16[3,256,256]{2,1,0:T(8,128)(2,1)}, bf16[3,256,256]{2,1,0:T(8,128)(2,1)}) custom-call(s32[3]{0:T(128)S(1)} %pad_add_fusion.place_ref, bf16[8,2,2,128,128]{4,3,2,1,0:T(8,128)(2,1)S(1)} %bitcast.20, bf16[2,2,2,2,128,128]{5,4,3,2,1,0:T(8,128)(2,1)S(1)} %copy-done.5, ...), custom_call_target="tpu_custom_call" | custom-call | flops 800000000 | bytes 6000000 | tf_op jit(solution)/shard_map/weight_terms/pallas_call | solution.py:196
  109.6 3.0 %collective-permute-start.12 = (bf16[3,256,256]{2,1,0:T(8,128)(2,1)}, bf16[3,256,256]{2,1,0:T(8,128)(2,1)S(1)}, u32[]{:S(2)}, u32[]{:S(2)}) collective-permute-start(bf16[3,256,256]{2,1,0:T(8,128)(2,1)} %get-tuple-element.15), channel_id=1, source_target_pairs={{0,1},{1,0},{2,3},{3,2},{4,5},{5,4},{6,7},{7,6},{8,9},{9,8},{10,11... | collective-permute-start | bytes 1179656 | tf_op jit(solution)/shard_map/ppermute | solution.py:239
  112.6 3.7 %collective-permute-start.13 = (bf16[3,256,256]{2,1,0:T(8,128)(2,1)}, bf16[3,256,256]{2,1,0:T(8,128)(2,1)S(1)}, u32[]{:S(2)}, u32[]{:S(2)}) collective-permute-start(bf16[3,256,256]{2,1,0:T(8,128)(2,1)} %get-tuple-element.16), channel_id=1, source_target_pairs={{0,64},{64,0},{1,65},{65,1},{2,66},{66,2},{3,67},{67,3},{4,68},{68... | collective-permute-start | bytes 1179656 | tf_op jit(solution)/shard_map/ppermute | solution.py:240
  116.3 2.5 %collective-permute-start.14 = (bf16[3,256,256]{2,1,0:T(8,128)(2,1)}, bf16[3,256,256]{2,1,0:T(8,128)(2,1)S(1)}, u32[]{:S(2)}, u32[]{:S(2)}) collective-permute-start(bf16[3,256,256]{2,1,0:T(8,128)(2,1)} %get-tuple-element.17), channel_id=1, source_target_pairs={{0,65},{1,64},{64,1},{65,0},{2,67},{3,66},{66,3},{67,2},{4,69},{5,... | collective-permute-start | bytes 1179656 | tf_op jit(solution)/shard_map/ppermute | solution.py:241
  118.8 1.8 %all-to-all-done.3 = bf16[8,2,128,128]{3,2,1,0:T(8,128)(2,1)} async-done(((bf16[8,2,128,128]{3,2,1,0:T(8,128)(2,1)}), bf16[8,2,128,128]{3,2,1,0:T(8,128)(2,1)}, u32[]{:S(2)}, u32[]{:S(2)}) %all-to-all-start.3) | async-done | bytes 524320 | tf_op jit(solution)/shard_map/all_to_all | solution.py:209
  120.7 1.1 reduce_sum.12
  121.8 4.9 %collective-permute-start.9 = (bf16[128,128]{1,0:T(8,128)(2,1)S(1)}, bf16[128,128]{1,0:T(8,128)(2,1)S(1)}, u32[]{:S(2)}, u32[]{:S(2)}) collective-permute-start(bf16[128,128]{1,0:T(8,128)(2,1)S(1)} %get-tuple-element.18), channel_id=1, source_target_pairs={{0,0},{8,1},{2,2},{10,3},{4,4},{12,5},{6,6},{14,7},{128,8},{136,9}... | collective-permute-start | bytes 98312 | tf_op jit(solution)/shard_map/ppermute | solution.py:235
  126.7 5.3 %collective-permute-start.10 = (bf16[128,128]{1,0:T(8,128)(2,1)S(1)}, bf16[128,128]{1,0:T(8,128)(2,1)S(1)}, u32[]{:S(2)}, u32[]{:S(2)}) collective-permute-start(bf16[128,128]{1,0:T(8,128)(2,1)S(1)} %get-tuple-element.19), channel_id=1, source_target_pairs={{16,0},{24,1},{18,2},{26,3},{20,4},{28,5},{22,6},{30,7},{144,8},{1... | collective-permute-start | bytes 98312 | tf_op jit(solution)/shard_map/ppermute | solution.py:235
  132.1 2.9 %collective-permute-done.9 = bf16[128,128]{1,0:T(8,128)(2,1)S(1)} collective-permute-done((bf16[128,128]{1,0:T(8,128)(2,1)S(1)}, bf16[128,128]{1,0:T(8,128)(2,1)S(1)}, u32[]{:S(2)}, u32[]{:S(2)}) %collective-permute-start.9) | collective-permute-done | bytes 32800 | tf_op jit(solution)/shard_map/ppermute | solution.py:235
  135.0 5.0 %collective-permute-done.10 = bf16[128,128]{1,0:T(8,128)(2,1)S(1)} collective-permute-done((bf16[128,128]{1,0:T(8,128)(2,1)S(1)}, bf16[128,128]{1,0:T(8,128)(2,1)S(1)}, u32[]{:S(2)}, u32[]{:S(2)}) %collective-permute-start.10) | collective-permute-done | bytes 32800 | tf_op jit(solution)/shard_map/ppermute | solution.py:235
  140.0 0.6 add_convert_fusion
  140.6 0.0 collective-permute-done.12
  140.6 0.0 collective-permute-done.13
  140.6 0.0 collective-permute-done.14
  140.6 1.0 convert_add_fusion
  (3 shorter events, 0.1 us)
Async XLA Ops:
  1.3 5.4 %copy-start.6 = (bf16[128,128]{1,0:T(8,128)(2,1)S(1)}, bf16[128,128]{1,0:T(8,128)(2,1)}, u32[]{:S(2)}) copy-start(bf16[128,128]{1,0:T(8,128)(2,1)} %param.5) | copy-start | bytes 98308
  1.3 5.4 %copy-start.7 = (bf16[128,128]{1,0:T(8,128)(2,1)S(1)}, bf16[128,128]{1,0:T(8,128)(2,1)}, u32[]{:S(2)}) copy-start(bf16[128,128]{1,0:T(8,128)(2,1)} %param.4) | copy-start | bytes 98308
  2.4 16.6 %collective-permute-start.1 = (bf16[3,256,256]{2,1,0:T(8,128)(2,1)S(1)}, bf16[3,256,256]{2,1,0:T(8,128)(2,1)S(1)}, u32[]{:S(2)}, u32[]{:S(2)}) collective-permute-start(bf16[3,256,256]{2,1,0:T(8,128)(2,1)S(1)} %multiply_convert_fusion.refs_0_), channel_id=1, source_target_pairs={{0,1},{1,0},{2,3},{3,2},{4,5},{5,4},{6,7},{7,6},{8,9},{9,8},{10,11... | collective-permute-start | bytes 1179656 | tf_op jit(solution)/shard_map/ppermute | solution.py:218
  6.7 11.1 %collective-permute-start = (bf16[2,128,128]{2,1,0:T(8,128)(2,1)S(1)}, bf16[2,128,128]{2,1,0:T(8,128)(2,1)S(1)}, u32[]{:S(2)}, u32[]{:S(2)}) collective-permute-start(bf16[2,128,128]{2,1,0:T(8,128)(2,1)S(1)} %pad_maximum_fusion), channel_id=1, source_target_pairs={{0,0},{1,8},{2,2},{3,10},{4,4},{5,12},{6,6},{7,14},{8,128},{9,136}... | collective-permute-start | bytes 196616 | tf_op jit(solution)/shard_map/ppermute | solution.py:216
  19.0 42.9 %all-to-all-start = ((bf16[16,2,128,128]{3,2,1,0:T(8,128)(2,1)}), bf16[16,2,128,128]{3,2,1,0:T(8,128)(2,1)S(1)}, u32[]{:S(2)}, u32[]{:S(2)}) async-start(bf16[16,2,128,128]{3,2,1,0:T(8,128)(2,1)} %spread.1), calls=%async_computation | async-start | bytes 2097152 | tf_op jit(solution)/shard_map/all_to_all | solution.py:209
  33.6 13.9 %collective-permute-start.2 = (bf16[3,256,256]{2,1,0:T(8,128)(2,1)S(1)}, bf16[3,256,256]{2,1,0:T(8,128)(2,1)S(1)}, u32[]{:S(2)}, u32[]{:S(2)}) collective-permute-start(bf16[3,256,256]{2,1,0:T(8,128)(2,1)S(1)} %multiply_convert_fusion.refs_0_), channel_id=1, source_target_pairs={{0,64},{64,0},{1,65},{65,1},{2,66},{66,2},{3,67},{67,3},{4,68},{68... | collective-permute-start | bytes 1179656 | tf_op jit(solution)/shard_map/ppermute | solution.py:220
  36.8 16.4 %collective-permute-start.3 = (bf16[3,256,256]{2,1,0:T(8,128)(2,1)S(1)}, bf16[3,256,256]{2,1,0:T(8,128)(2,1)S(1)}, u32[]{:S(2)}, u32[]{:S(2)}) collective-permute-start(bf16[3,256,256]{2,1,0:T(8,128)(2,1)S(1)} %collective-permute-done.1.refs_1_), channel_id=1, source_target_pairs={{0,64},{64,0},{1,65},{65,1},{2,66},{66,2},{3,67},{67,3},{4,68},{68... | collective-permute-start | bytes 1179656 | tf_op jit(solution)/shard_map/ppermute | solution.py:220
  39.4 15.7 %collective-permute-start.4 = (bf16[3,256,256]{2,1,0:T(8,128)(2,1)S(1)}, bf16[3,256,256]{2,1,0:T(8,128)(2,1)S(1)}, u32[]{:S(2)}, u32[]{:S(2)}) collective-permute-start(bf16[3,256,256]{2,1,0:T(8,128)(2,1)S(1)} %multiply_convert_fusion.refs_0_), channel_id=1, source_target_pairs={{0,32},{32,0},{1,33},{33,1},{2,34},{34,2},{3,35},{35,3},{4,36},{36... | collective-permute-start | bytes 1179656 | tf_op jit(solution)/shard_map/ppermute | solution.py:221
  41.4 13.8 %collective-permute-start.5 = (bf16[3,256,256]{2,1,0:T(8,128)(2,1)S(1)}, bf16[3,256,256]{2,1,0:T(8,128)(2,1)S(1)}, u32[]{:S(2)}, u32[]{:S(2)}) collective-permute-start(bf16[3,256,256]{2,1,0:T(8,128)(2,1)S(1)} %collective-permute-done.1.refs_1_), channel_id=1, source_target_pairs={{0,32},{32,0},{1,33},{33,1},{2,34},{34,2},{3,35},{35,3},{4,36},{36... | collective-permute-start | bytes 1179656 | tf_op jit(solution)/shard_map/ppermute | solution.py:221
  47.5 7.7 %collective-permute-start.6 = (bf16[3,256,256]{2,1,0:T(8,128)(2,1)S(1)}, bf16[3,256,256]{2,1,0:T(8,128)(2,1)}, u32[]{:S(2)}, u32[]{:S(2)}) collective-permute-start(bf16[3,256,256]{2,1,0:T(8,128)(2,1)S(1)} %collective-permute-done.2.refs_2_), channel_id=1, source_target_pairs={{0,32},{32,0},{1,33},{33,1},{2,34},{34,2},{3,35},{35,3},{4,36},{36... | collective-permute-start | bytes 1179656 | tf_op jit(solution)/shard_map/ppermute | solution.py:221
  53.2 3.7 %collective-permute-start.7 = (bf16[3,256,256]{2,1,0:T(8,128)(2,1)S(1)}, bf16[3,256,256]{2,1,0:T(8,128)(2,1)}, u32[]{:S(2)}, u32[]{:S(2)}) collective-permute-start(bf16[3,256,256]{2,1,0:T(8,128)(2,1)S(1)} %collective-permute-done.3.refs_3_), channel_id=1, source_target_pairs={{0,32},{32,0},{1,33},{33,1},{2,34},{34,2},{3,35},{35,3},{4,36},{36... | collective-permute-start | bytes 1179656 | tf_op jit(solution)/shard_map/ppermute | solution.py:221
  55.2 9.7 %copy-start = (bf16[3,256,256]{2,1,0:T(8,128)(2,1)}, bf16[3,256,256]{2,1,0:T(8,128)(2,1)S(1)}, u32[]{:S(2)}) copy-start(bf16[3,256,256]{2,1,0:T(8,128)(2,1)S(1)} %collective-permute-done.4.refs_4_) | copy-start | bytes 1179652
  55.2 9.7 %copy-start.2 = (bf16[3,256,256]{2,1,0:T(8,128)(2,1)}, bf16[3,256,256]{2,1,0:T(8,128)(2,1)S(1)}, u32[]{:S(2)}) copy-start(bf16[3,256,256]{2,1,0:T(8,128)(2,1)S(1)} %collective-permute-done.5.refs_5_) | copy-start | bytes 1179652
  64.9 16.6 %all-to-all-start.1 = ((bf16[4,64,1536]{2,1,0:T(8,128)(2,1)}), bf16[4,64,1536]{2,1,0:T(8,128)(2,1)S(1)}, u32[]{:S(2)}, u32[]{:S(2)}) async-start(bf16[4,64,1536]{2,1,0:T(8,128)(2,1)} %bitcast.7), calls=%async_computation.1 | async-start | bytes 1572864 | tf_op jit(solution)/shard_map/all_to_all | solution.py:209
  71.8 3.8 %collective-permute-start.8 = (bf16[2,2,2,2,128,128]{5,4,3,2,1,0:T(8,128)(2,1)S(1)}, bf16[2,2,2,2,128,128]{5,4,3,2,1,0:T(8,128)(2,1)S(1)}, u32[]{:S(2)}, u32[]{:S(2)}) collective-permute-start(bf16[2,2,2,2,128,128]{5,4,3,2,1,0:T(8,128)(2,1)S(1)} %dynamic-slice_bitcast_fusion), channel_id=1, source_target_pairs={{0,32},{32,0},{1,33},{33,1},{2,34},{34,2},{3,35},{35,3},{4,36},{36... | collective-permute-start | bytes 1572872 | tf_op jit(solution)/shard_map/ppermute | solution.py:227
  75.6 0.8 copy-start.4
  81.7 14.3 %copy-start.1 = (bf16[3,256,256]{2,1,0:T(8,128)(2,1)S(1)}, bf16[3,256,256]{2,1,0:T(8,128)(2,1)}, u32[]{:S(2)}) copy-start(bf16[3,256,256]{2,1,0:T(8,128)(2,1)} %copy-done) | copy-start | bytes 1179652
  81.8 14.3 %copy-start.3 = (bf16[3,256,256]{2,1,0:T(8,128)(2,1)S(1)}, bf16[3,256,256]{2,1,0:T(8,128)(2,1)}, u32[]{:S(2)}) copy-start(bf16[3,256,256]{2,1,0:T(8,128)(2,1)} %copy-done.2) | copy-start | bytes 1179652
  98.7 8.5 %copy-start.5 = (bf16[2,2,2,2,128,128]{5,4,3,2,1,0:T(8,128)(2,1)S(1)}, bf16[2,2,2,2,128,128]{5,4,3,2,1,0:T(8,128)(2,1)}, u32[]{:S(2)}) copy-start(bf16[2,2,2,2,128,128]{5,4,3,2,1,0:T(8,128)(2,1)} %copy-done.4) | copy-start | bytes 1572868
  98.7 21.9 %all-to-all-start.3 = ((bf16[8,2,128,128]{3,2,1,0:T(8,128)(2,1)}), bf16[8,2,128,128]{3,2,1,0:T(8,128)(2,1)}, u32[]{:S(2)}, u32[]{:S(2)}) async-start(bf16[8,2,128,128]{3,2,1,0:T(8,128)(2,1)} %input_terms.1), calls=%async_computation.3 | async-start | bytes 1048576 | tf_op jit(solution)/shard_map/all_to_all | solution.py:209
  103.0 4.2 %collective-permute-start.11 = (bf16[256,1536]{1,0:T(8,128)(2,1)S(1)}, bf16[256,1536]{1,0:T(8,128)(2,1)S(1)}, u32[]{:S(2)}, u32[]{:S(2)}) collective-permute-start(bf16[256,1536]{1,0:T(8,128)(2,1)S(1)} %bitcast.22), channel_id=1, source_target_pairs={{0,32},{32,0},{1,33},{33,1},{2,34},{34,2},{3,35},{35,3},{4,36},{36... | collective-permute-start | bytes 2359304 | tf_op jit(solution)/shard_map/ppermute | solution.py:231
  109.6 31.0 %collective-permute-start.12 = (bf16[3,256,256]{2,1,0:T(8,128)(2,1)}, bf16[3,256,256]{2,1,0:T(8,128)(2,1)S(1)}, u32[]{:S(2)}, u32[]{:S(2)}) collective-permute-start(bf16[3,256,256]{2,1,0:T(8,128)(2,1)} %get-tuple-element.15), channel_id=1, source_target_pairs={{0,1},{1,0},{2,3},{3,2},{4,5},{5,4},{6,7},{7,6},{8,9},{9,8},{10,11... | collective-permute-start | bytes 1179656 | tf_op jit(solution)/shard_map/ppermute | solution.py:239
  112.6 28.0 %collective-permute-start.13 = (bf16[3,256,256]{2,1,0:T(8,128)(2,1)}, bf16[3,256,256]{2,1,0:T(8,128)(2,1)S(1)}, u32[]{:S(2)}, u32[]{:S(2)}) collective-permute-start(bf16[3,256,256]{2,1,0:T(8,128)(2,1)} %get-tuple-element.16), channel_id=1, source_target_pairs={{0,64},{64,0},{1,65},{65,1},{2,66},{66,2},{3,67},{67,3},{4,68},{68... | collective-permute-start | bytes 1179656 | tf_op jit(solution)/shard_map/ppermute | solution.py:240
  116.3 24.3 %collective-permute-start.14 = (bf16[3,256,256]{2,1,0:T(8,128)(2,1)}, bf16[3,256,256]{2,1,0:T(8,128)(2,1)S(1)}, u32[]{:S(2)}, u32[]{:S(2)}) collective-permute-start(bf16[3,256,256]{2,1,0:T(8,128)(2,1)} %get-tuple-element.17), channel_id=1, source_target_pairs={{0,65},{1,64},{64,1},{65,0},{2,67},{3,66},{66,3},{67,2},{4,69},{5,... | collective-permute-start | bytes 1179656 | tf_op jit(solution)/shard_map/ppermute | solution.py:241
  121.8 13.2 %collective-permute-start.9 = (bf16[128,128]{1,0:T(8,128)(2,1)S(1)}, bf16[128,128]{1,0:T(8,128)(2,1)S(1)}, u32[]{:S(2)}, u32[]{:S(2)}) collective-permute-start(bf16[128,128]{1,0:T(8,128)(2,1)S(1)} %get-tuple-element.18), channel_id=1, source_target_pairs={{0,0},{8,1},{2,2},{10,3},{4,4},{12,5},{6,6},{14,7},{128,8},{136,9}... | collective-permute-start | bytes 98312 | tf_op jit(solution)/shard_map/ppermute | solution.py:235
  126.7 13.2 %collective-permute-start.10 = (bf16[128,128]{1,0:T(8,128)(2,1)S(1)}, bf16[128,128]{1,0:T(8,128)(2,1)S(1)}, u32[]{:S(2)}, u32[]{:S(2)}) collective-permute-start(bf16[128,128]{1,0:T(8,128)(2,1)S(1)} %get-tuple-element.19), channel_id=1, source_target_pairs={{16,0},{24,1},{18,2},{26,3},{20,4},{28,5},{22,6},{30,7},{144,8},{1... | collective-permute-start | bytes 98312 | tf_op jit(solution)/shard_map/ppermute | solution.py:235

commit v21 on v20

--- a/solution.py
+++ b/solution.py
@@ -12,8 +12,8 @@
 ROW = ("yl", "x1", "x0", "core")
 COL = ("yh1", "yh0", "zh1", "zh0", "zl")
 AXES = ROW + COL
-SPREAD = ("yh0", "zh1", "zh0")
-GATHER = ("zh0", "zh1", "yh0", "yh1")
+SPREAD = ("yh0", "zh0", "zh1")
+GATHER = ("zh0", "zh1", "yh1", "yh0")
 REST = ("x1", "yl")
 SWAP = [(0, 1), (1, 0)]
 TOK = 128
@@ -51,13 +51,13 @@
 
 
 def gathered(place_ref, f):
-    core, x0, b = place_of(place_ref, f)
-    return 4 * core + 2 * x0 + b
+    core, x0, unused = place_of(place_ref, f)
+    return 2 * core + x0
 
 
 def summed(place_ref, f):
     core, x0, b = place_of(place_ref, f)
-    return 4 * b + 2 * x0 + core
+    return 4 * b + 2 * core + x0
 
 
 def half(place_ref, t):
@@ -90,7 +90,7 @@
     for p in range(2):
         for t in range(2):
             for f in range(8):
-                block = acts_ref[gathered(place_ref, f), half(place_ref, t), p]
+                block = acts_ref[gathered(place_ref, f), half(place_ref, t), f % 2, p]
                 wide_ref[p, pl.ds(t * TOK, TOK), pl.ds(f * TOK, TOK)] = block
     for p in range(3):
         for j in range(2):
@@ -175,9 +175,9 @@
             for f in range(4):
                 x0 = place_ref[1] if f < 2 else 1 - place_ref[1]
                 cols = pl.ds(f * TOK, TOK)
-                mine = acts_ref[gathered(place_ref, f), half(place_ref, t), p]
+                mine = acts_ref[gathered(place_ref, f), half(place_ref, t), f % 2, p]
                 wide_ref[p, pl.ds(t * TOK, TOK), cols] = mine
-                wide_ref[p, pl.ds(TOKENS + t * TOK, TOK), cols] = other_acts_ref[x0, f % 2, half(place_ref, t), p]
+                wide_ref[p, pl.ds(TOKENS + t * TOK, TOK), cols] = other_acts_ref[x0, half(place_ref, t), f % 2, p]
     for side in (1, 0):
         for p in range(3):
             for j in range(2):
@@ -219,7 +219,7 @@
     acts, w_z = lax.optimization_barrier((acts, w_z))
     weights = [w, w_z] + [lax.ppermute(block, "x0", SWAP) for block in (w, w_z)]
     weights += [lax.ppermute(block, "core", SWAP) for block in weights]
-    acts = exchange(acts, GATHER).reshape(8, 2, 2, TOK, TOK)
+    acts = exchange(acts, GATHER).reshape(4, 2, 2, 2, TOK, TOK)
 
     parts = gates(place, acts, *weights)
     other_acts = acts.reshape(2, 2, 2, 2, 2, TOK, TOK)

time: 143 us -> 144 us (level)
  waiting for transfers between devices: 37.5 us -> 40.2 us
    ppermute x2, waiting for transfers between devices: 7.91 us -> 10.2 us  [local(): lax.ppermute(dx[i], AXES, [(b, a) for a, b in there[i]])]
  transfers between devices with their start and end apart: 18 -> 18, of which waited for: 11 -> 10; matrix products, arithmetic and copies ran while one was open for 1% -> 1% of each run, Pallas kernels for 2% -> 2%
where the time goes in v21:
time: 144 us
  starting transfers between devices  73.8 us (51%)
  waiting for transfers between devices  40.2 us (28%)
  blocking collectives  13.7 us (10%)
  Pallas kernels  9.36 us (6%)
  other arithmetic  4.63 us (3%)
    all_to_all x3, starting transfers between devices, exchange(): return lax.all_to_all(pieces, axes, split_axis=0, concat_axis=0, tiled=True)  26 us
    all_to_all x1, blocking collectives, exchange(): return lax.all_to_all(pieces, axes, split_axis=0, concat_axis=0, tiled=True)  13.7 us
    all_to_all x3, waiting for transfers between devices, exchange(): return lax.all_to_all(pieces, axes, split_axis=0, concat_axis=0, tiled=True)  12.5 us
    ppermute x2, waiting for transfers between devices, local(): lax.ppermute(dx[i], AXES, [(b, a) for a, b in there[i]])  10.2 us
    ppermute x2, starting transfers between devices, local(): lax.ppermute(dx[i], AXES, [(b, a) for a, b in there[i]])  9.72 us
    ppermute x4, starting transfers between devices, local(): weights += [lax.ppermute(block, 'core', SWAP) for block in weights]  8.15 us
    ppermute x2, waiting for transfers between devices, local(): weights = [w, w_z] + [lax.ppermute(block, 'x0', SWAP) for block in (w, w_z)]  7.47 us
    ppermute x1, starting transfers between devices, local(): acts = spread(lax.ppermute(jnp.stack([inputs, out_grad]), AXES, there[0]))  6.88 us
  transfers between devices with their start and end apart: 18, of which 10 were waited for; matrix products, arithmetic and copies ran while one was open for 1% of the time, Pallas kernels for 2%

profile of v21, /device:TPU:4, one launch (start us, length us, event | category | flops | bytes accessed | tf_op | source)
XLA Modules:
  0.0 143.5 jit_solution(6491027671847401689)
XLA Ops:
  0.6 0.7 bitcast_convert_fusion
  1.3 0.0 copy-start.6
  1.3 0.0 copy-start.7
  1.3 1.1 multiply_convert_fusion.refs_0_
  2.4 4.3 %collective-permute-start.1 = (bf16[3,256,256]{2,1,0:T(8,128)(2,1)S(1)}, bf16[3,256,256]{2,1,0:T(8,128)(2,1)S(1)}, u32[]{:S(2)}, u32[]{:S(2)}) collective-permute-start(bf16[3,256,256]{2,1,0:T(8,128)(2,1)S(1)} %multiply_convert_fusion.refs_0_), channel_id=1, source_target_pairs={{0,1},{1,0},{2,3},{3,2},{4,5},{5,4},{6,7},{7,6},{8,9},{9,8},{10,11... | collective-permute-start | bytes 1179656 | tf_op jit(solution)/shard_map/ppermute | solution.py:218
  6.7 0.0 copy-done.6
  6.7 0.0 copy-done.7
  6.7 6.9 %collective-permute-start = (bf16[2,128,128]{2,1,0:T(8,128)(2,1)S(1)}, bf16[2,128,128]{2,1,0:T(8,128)(2,1)S(1)}, u32[]{:S(2)}, u32[]{:S(2)}) collective-permute-start(bf16[2,128,128]{2,1,0:T(8,128)(2,1)S(1)} %pad_maximum_fusion), channel_id=1, source_target_pairs={{0,0},{1,8},{2,2},{3,10},{4,4},{5,12},{6,6},{7,14},{8,128},{9,136}... | collective-permute-start | bytes 196616 | tf_op jit(solution)/shard_map/ppermute | solution.py:216
  13.6 4.2 %collective-permute-done.acts_ref = bf16[2,128,128]{2,1,0:T(8,128)(2,1)S(1)} collective-permute-done((bf16[2,128,128]{2,1,0:T(8,128)(2,1)S(1)}, bf16[2,128,128]{2,1,0:T(8,128)(2,1)S(1)}, u32[]{:S(2)}, u32[]{:S(2)}) %collective-permute-start) | collective-permute-done | bytes 65568 | tf_op jit(solution)/shard_map/ppermute | solution.py:216
  17.8 1.2 spread.1
  19.0 0.0 collective-permute-done.1.refs_1_
  19.0 14.6 %all-to-all-start = ((bf16[16,2,128,128]{3,2,1,0:T(8,128)(2,1)}), bf16[16,2,128,128]{3,2,1,0:T(8,128)(2,1)S(1)}, u32[]{:S(2)}, u32[]{:S(2)}) async-start(bf16[16,2,128,128]{3,2,1,0:T(8,128)(2,1)} %spread.1), calls=%async_computation | async-start | bytes 2097152 | tf_op jit(solution)/shard_map/all_to_all | solution.py:209
  33.6 3.2 %collective-permute-start.2 = (bf16[3,256,256]{2,1,0:T(8,128)(2,1)S(1)}, bf16[3,256,256]{2,1,0:T(8,128)(2,1)S(1)}, u32[]{:S(2)}, u32[]{:S(2)}) collective-permute-start(bf16[3,256,256]{2,1,0:T(8,128)(2,1)S(1)} %multiply_convert_fusion.refs_0_), channel_id=1, source_target_pairs={{0,64},{64,0},{1,65},{65,1},{2,66},{66,2},{3,67},{67,3},{4,68},{68... | collective-permute-start | bytes 1179656 | tf_op jit(solution)/shard_map/ppermute | solution.py:220
  36.8 2.7 %collective-permute-start.3 = (bf16[3,256,256]{2,1,0:T(8,128)(2,1)S(1)}, bf16[3,256,256]{2,1,0:T(8,128)(2,1)S(1)}, u32[]{:S(2)}, u32[]{:S(2)}) collective-permute-start(bf16[3,256,256]{2,1,0:T(8,128)(2,1)S(1)} %collective-permute-done.1.refs_1_), channel_id=1, source_target_pairs={{0,64},{64,0},{1,65},{65,1},{2,66},{66,2},{3,67},{67,3},{4,68},{68... | collective-permute-start | bytes 1179656 | tf_op jit(solution)/shard_map/ppermute | solution.py:220
  39.4 1.9 %collective-permute-start.4 = (bf16[3,256,256]{2,1,0:T(8,128)(2,1)S(1)}, bf16[3,256,256]{2,1,0:T(8,128)(2,1)S(1)}, u32[]{:S(2)}, u32[]{:S(2)}) collective-permute-start(bf16[3,256,256]{2,1,0:T(8,128)(2,1)S(1)} %multiply_convert_fusion.refs_0_), channel_id=1, source_target_pairs={{0,32},{32,0},{1,33},{33,1},{2,34},{34,2},{3,35},{35,3},{4,36},{36... | collective-permute-start | bytes 1179656 | tf_op jit(solution)/shard_map/ppermute | solution.py:221
  41.4 2.4 %collective-permute-start.5 = (bf16[3,256,256]{2,1,0:T(8,128)(2,1)S(1)}, bf16[3,256,256]{2,1,0:T(8,128)(2,1)S(1)}, u32[]{:S(2)}, u32[]{:S(2)}) collective-permute-start(bf16[3,256,256]{2,1,0:T(8,128)(2,1)S(1)} %collective-permute-done.1.refs_1_), channel_id=1, source_target_pairs={{0,32},{32,0},{1,33},{33,1},{2,34},{34,2},{3,35},{35,3},{4,36},{36... | collective-permute-start | bytes 1179656 | tf_op jit(solution)/shard_map/ppermute | solution.py:221
  43.8 3.7 %collective-permute-done.2.refs_2_ = bf16[3,256,256]{2,1,0:T(8,128)(2,1)S(1)} collective-permute-done((bf16[3,256,256]{2,1,0:T(8,128)(2,1)S(1)}, bf16[3,256,256]{2,1,0:T(8,128)(2,1)S(1)}, u32[]{:S(2)}, u32[]{:S(2)}) %collective-permute-start.2) | collective-permute-done | bytes 393248 | tf_op jit(solution)/shard_map/ppermute | solution.py:220
  47.5 1.9 %collective-permute-start.6 = (bf16[3,256,256]{2,1,0:T(8,128)(2,1)S(1)}, bf16[3,256,256]{2,1,0:T(8,128)(2,1)}, u32[]{:S(2)}, u32[]{:S(2)}) collective-permute-start(bf16[3,256,256]{2,1,0:T(8,128)(2,1)S(1)} %collective-permute-done.2.refs_2_), channel_id=1, source_target_pairs={{0,32},{32,0},{1,33},{33,1},{2,34},{34,2},{3,35},{35,3},{4,36},{36... | collective-permute-start | bytes 1179656 | tf_op jit(solution)/shard_map/ppermute | solution.py:221
  49.4 3.7 %collective-permute-done.3.refs_3_ = bf16[3,256,256]{2,1,0:T(8,128)(2,1)S(1)} collective-permute-done((bf16[3,256,256]{2,1,0:T(8,128)(2,1)S(1)}, bf16[3,256,256]{2,1,0:T(8,128)(2,1)S(1)}, u32[]{:S(2)}, u32[]{:S(2)}) %collective-permute-start.3) | collective-permute-done | bytes 393248 | tf_op jit(solution)/shard_map/ppermute | solution.py:220
  53.2 1.9 %collective-permute-start.7 = (bf16[3,256,256]{2,1,0:T(8,128)(2,1)S(1)}, bf16[3,256,256]{2,1,0:T(8,128)(2,1)}, u32[]{:S(2)}, u32[]{:S(2)}) collective-permute-start(bf16[3,256,256]{2,1,0:T(8,128)(2,1)S(1)} %collective-permute-done.3.refs_3_), channel_id=1, source_target_pairs={{0,32},{32,0},{1,33},{33,1},{2,34},{34,2},{3,35},{35,3},{4,36},{36... | collective-permute-start | bytes 1179656 | tf_op jit(solution)/shard_map/ppermute | solution.py:221
  55.1 0.1 pad_add_fusion.place_ref
  55.2 0.0 collective-permute-done.4.refs_4_
  55.2 0.0 copy-start
  55.2 0.0 collective-permute-done.6.refs_6_
  55.2 0.0 collective-permute-done.5.refs_5_
  55.2 0.0 copy-start.2
  55.2 1.7 %collective-permute-done.7.refs_7_ = bf16[3,256,256]{2,1,0:T(8,128)(2,1)} collective-permute-done((bf16[3,256,256]{2,1,0:T(8,128)(2,1)S(1)}, bf16[3,256,256]{2,1,0:T(8,128)(2,1)}, u32[]{:S(2)}, u32[]{:S(2)}) %collective-permute-start.7) | collective-permute-done | bytes 393248 | tf_op jit(solution)/shard_map/ppermute | solution.py:221
  56.9 8.2 %all-to-all-done = bf16[16,2,128,128]{3,2,1,0:T(8,128)(2,1)S(1)} async-done(((bf16[16,2,128,128]{3,2,1,0:T(8,128)(2,1)}), bf16[16,2,128,128]{3,2,1,0:T(8,128)(2,1)S(1)}, u32[]{:S(2)}, u32[]{:S(2)}) %all-to-all-start) | async-done | bytes 1048608 | tf_op jit(solution)/shard_map/all_to_all | solution.py:209
  65.1 3.0 %gates.1 = bf16[256,1536]{1,0:T(8,128)(2,1)} custom-call(s32[3]{0:T(128)S(1)} %pad_add_fusion.place_ref, bf16[4,2,2,2,128,128]{5,4,3,2,1,0:T(8,128)(2,1)S(1)} %bitcast.18, bf16[3,256,256]{2,1,0:T(8,128)(2,1)S(1)} %multiply_convert_fusion.refs_0_, bf16[3,256,256]{2,1,0:T(8,128)(2,1)S(1)} %collective-permute-done.1.refs_1_, ...), custom_call_target="tpu_custom_call" | custom-call | flops 800000000 | bytes 6000000 | tf_op jit(solution)/shard_map/gates/pallas_call | solution.py:104
  68.1 0.0 copy-done
  68.1 0.0 copy-done.2
  68.1 4.8 %all-to-all-start.1 = ((bf16[4,64,1536]{2,1,0:T(8,128)(2,1)}), bf16[4,64,1536]{2,1,0:T(8,128)(2,1)S(1)}, u32[]{:S(2)}, u32[]{:S(2)}) async-start(bf16[4,64,1536]{2,1,0:T(8,128)(2,1)} %bitcast.7), calls=%async_computation.1 | async-start | bytes 1572864 | tf_op jit(solution)/shard_map/all_to_all | solution.py:209
  72.9 1.9 %collective-permute-start.8 = (bf16[2,2,2,2,128,128]{5,4,3,2,1,0:T(8,128)(2,1)S(1)}, bf16[2,2,2,2,128,128]{5,4,3,2,1,0:T(8,128)(2,1)S(1)}, u32[]{:S(2)}, u32[]{:S(2)}) collective-permute-start(bf16[2,2,2,2,128,128]{5,4,3,2,1,0:T(8,128)(2,1)S(1)} %dynamic-slice_bitcast_fusion), channel_id=1, source_target_pairs={{0,32},{32,0},{1,33},{33,1},{2,34},{34,2},{3,35},{35,3},{4,36},{36... | collective-permute-start | bytes 1572872 | tf_op jit(solution)/shard_map/ppermute | solution.py:227
  74.9 1.9 %collective-permute-done.8.other_acts_ref = bf16[2,2,2,2,128,128]{5,4,3,2,1,0:T(8,128)(2,1)S(1)} collective-permute-done((bf16[2,2,2,2,128,128]{5,4,3,2,1,0:T(8,128)(2,1)S(1)}, bf16[2,2,2,2,128,128]{5,4,3,2,1,0:T(8,128)(2,1)S(1)}, u32[]{:S(2)}, u32[]{:S(2)}) %collective-permute-start.8) | collective-permute-done | bytes 524320 | tf_op jit(solution)/shard_map/ppermute | solution.py:227
  76.7 0.0 copy-start.4
  76.7 0.8 copy-done.4
  77.5 4.3 %all-to-all-done.1.parts_ref = bf16[4,64,1536]{2,1,0:T(8,128)(2,1)S(1)} async-done(((bf16[4,64,1536]{2,1,0:T(8,128)(2,1)}), bf16[4,64,1536]{2,1,0:T(8,128)(2,1)S(1)}, u32[]{:S(2)}, u32[]{:S(2)}) %all-to-all-start.1) | async-done | bytes 786464 | tf_op jit(solution)/shard_map/all_to_all | solution.py:209
  81.9 0.2 hidden_grads.1
  82.1 0.0 copy-start.1
  82.1 0.0 copy-start.3
  82.1 13.7 %all_to_all.20 = bf16[4,64,1536]{2,1,0:T(8,128)(2,1)S(1)} all-to-all(bf16[4,64,1536]{2,1,0:T(8,128)(2,1)S(1)} %hidden_grads.1), channel_id=1, replica_groups=mesh['yl'=2,'x1'=2,'x0'=2,'core'=2,'yh1'=2,'yh0'=2,'zh1'=2,'zh0'=2,'zl'=..., dimensions={0} | all-to-all | bytes 1572864 | tf_op jit(solution)/shard_map/all_to_all | solution.py:209
  95.8 0.0 copy-done.1
  95.8 0.0 copy-done.3
  95.8 2.7 %input_terms.1 = bf16[8,2,128,128]{3,2,1,0:T(8,128)(2,1)} custom-call(s32[3]{0:T(128)S(1)} %pad_add_fusion.place_ref, bf16[256,1536]{1,0:T(8,128)(2,1)S(1)} %bitcast.21, bf16[3,256,256]{2,1,0:T(8,128)(2,1)S(1)} %multiply_convert_fusion.refs_0_, bf16[3,256,256]{2,1,0:T(8,128)(2,1)S(1)} %collective-permute-done.1.refs_1_, ...), custom_call_target="tpu_custom_call" | custom-call | flops 540000000 | bytes 4000000 | tf_op jit(solution)/shard_map/input_terms/pallas_call | solution.py:159
  98.4 0.0 copy-start.5
  98.4 6.6 %all-to-all-start.3 = ((bf16[8,2,128,128]{3,2,1,0:T(8,128)(2,1)}), bf16[8,2,128,128]{3,2,1,0:T(8,128)(2,1)}, u32[]{:S(2)}, u32[]{:S(2)}) async-start(bf16[8,2,128,128]{3,2,1,0:T(8,128)(2,1)} %input_terms.1), calls=%async_computation.3 | async-start | bytes 1048576 | tf_op jit(solution)/shard_map/all_to_all | solution.py:209
  105.0 1.9 %collective-permute-start.11 = (bf16[256,1536]{1,0:T(8,128)(2,1)S(1)}, bf16[256,1536]{1,0:T(8,128)(2,1)S(1)}, u32[]{:S(2)}, u32[]{:S(2)}) collective-permute-start(bf16[256,1536]{1,0:T(8,128)(2,1)S(1)} %bitcast.22), channel_id=1, source_target_pairs={{0,32},{32,0},{1,33},{33,1},{2,34},{34,2},{3,35},{35,3},{4,36},{36... | collective-permute-start | bytes 2359304 | tf_op jit(solution)/shard_map/ppermute | solution.py:231
  107.0 2.3 %collective-permute-done.11.other_grads_ref = bf16[256,1536]{1,0:T(8,128)(2,1)S(1)} collective-permute-done((bf16[256,1536]{1,0:T(8,128)(2,1)S(1)}, bf16[256,1536]{1,0:T(8,128)(2,1)S(1)}, u32[]{:S(2)}, u32[]{:S(2)}) %collective-permute-start.11) | collective-permute-done | bytes 786464 | tf_op jit(solution)/shard_map/ppermute | solution.py:231
  109.2 0.0 copy-done.5
  109.2 2.4 %weight_terms.1 = (f32[3,256,256]{2,1,0:T(8,128)S(1)}, bf16[3,256,256]{2,1,0:T(8,128)(2,1)}, bf16[3,256,256]{2,1,0:T(8,128)(2,1)}, bf16[3,256,256]{2,1,0:T(8,128)(2,1)}) custom-call(s32[3]{0:T(128)S(1)} %pad_add_fusion.place_ref, bf16[4,2,2,2,128,128]{5,4,3,2,1,0:T(8,128)(2,1)S(1)} %bitcast.20, bf16[2,2,2,2,128,128]{5,4,3,2,1,0:T(8,128)(2,1)S(1)} %copy-done.5, ...), custom_call_target="tpu_custom_call" | custom-call | flops 800000000 | bytes 6000000 | tf_op jit(solution)/shard_map/weight_terms/pallas_call | solution.py:196
  111.6 3.3 %collective-permute-start.12 = (bf16[3,256,256]{2,1,0:T(8,128)(2,1)}, bf16[3,256,256]{2,1,0:T(8,128)(2,1)S(1)}, u32[]{:S(2)}, u32[]{:S(2)}) collective-permute-start(bf16[3,256,256]{2,1,0:T(8,128)(2,1)} %get-tuple-element.15), channel_id=1, source_target_pairs={{0,1},{1,0},{2,3},{3,2},{4,5},{5,4},{6,7},{7,6},{8,9},{9,8},{10,11... | collective-permute-start | bytes 1179656 | tf_op jit(solution)/shard_map/ppermute | solution.py:239
  114.9 2.9 %collective-permute-start.13 = (bf16[3,256,256]{2,1,0:T(8,128)(2,1)}, bf16[3,256,256]{2,1,0:T(8,128)(2,1)S(1)}, u32[]{:S(2)}, u32[]{:S(2)}) collective-permute-start(bf16[3,256,256]{2,1,0:T(8,128)(2,1)} %get-tuple-element.16), channel_id=1, source_target_pairs={{0,64},{64,0},{1,65},{65,1},{2,66},{66,2},{3,67},{67,3},{4,68},{68... | collective-permute-start | bytes 1179656 | tf_op jit(solution)/shard_map/ppermute | solution.py:240
  117.8 3.0 %collective-permute-start.14 = (bf16[3,256,256]{2,1,0:T(8,128)(2,1)}, bf16[3,256,256]{2,1,0:T(8,128)(2,1)S(1)}, u32[]{:S(2)}, u32[]{:S(2)}) collective-permute-start(bf16[3,256,256]{2,1,0:T(8,128)(2,1)} %get-tuple-element.17), channel_id=1, source_target_pairs={{0,65},{1,64},{64,1},{65,0},{2,67},{3,66},{66,3},{67,2},{4,69},{5,... | collective-permute-start | bytes 1179656 | tf_op jit(solution)/shard_map/ppermute | solution.py:241
  120.8 0.0 all-to-all-done.3
  120.8 1.1 reduce_sum.12
  122.0 6.9 %collective-permute-start.9 = (bf16[128,128]{1,0:T(8,128)(2,1)S(1)}, bf16[128,128]{1,0:T(8,128)(2,1)S(1)}, u32[]{:S(2)}, u32[]{:S(2)}) collective-permute-start(bf16[128,128]{1,0:T(8,128)(2,1)S(1)} %get-tuple-element.18), channel_id=1, source_target_pairs={{0,0},{8,1},{2,2},{10,3},{4,4},{12,5},{6,6},{14,7},{128,8},{136,9}... | collective-permute-start | bytes 98312 | tf_op jit(solution)/shard_map/ppermute | solution.py:235
  128.8 2.8 %collective-permute-start.10 = (bf16[128,128]{1,0:T(8,128)(2,1)S(1)}, bf16[128,128]{1,0:T(8,128)(2,1)S(1)}, u32[]{:S(2)}, u32[]{:S(2)}) collective-permute-start(bf16[128,128]{1,0:T(8,128)(2,1)S(1)} %get-tuple-element.19), channel_id=1, source_target_pairs={{16,0},{24,1},{18,2},{26,3},{20,4},{28,5},{22,6},{30,7},{144,8},{1... | collective-permute-start | bytes 98312 | tf_op jit(solution)/shard_map/ppermute | solution.py:235
  131.7 6.5 %collective-permute-done.9 = bf16[128,128]{1,0:T(8,128)(2,1)S(1)} collective-permute-done((bf16[128,128]{1,0:T(8,128)(2,1)S(1)}, bf16[128,128]{1,0:T(8,128)(2,1)S(1)}, u32[]{:S(2)}, u32[]{:S(2)}) %collective-permute-start.9) | collective-permute-done | bytes 32800 | tf_op jit(solution)/shard_map/ppermute | solution.py:235
  138.2 3.6 %collective-permute-done.10 = bf16[128,128]{1,0:T(8,128)(2,1)S(1)} collective-permute-done((bf16[128,128]{1,0:T(8,128)(2,1)S(1)}, bf16[128,128]{1,0:T(8,128)(2,1)S(1)}, u32[]{:S(2)}, u32[]{:S(2)}) %collective-permute-start.10) | collective-permute-done | bytes 32800 | tf_op jit(solution)/shard_map/ppermute | solution.py:235
  141.9 0.6 add_convert_fusion
  142.5 0.0 collective-permute-done.12
  142.5 0.0 collective-permute-done.13
  142.5 0.0 collective-permute-done.14
  142.5 1.0 convert_add_fusion
  (3 shorter events, 0.1 us)
Async XLA Ops:
  1.3 5.4 %copy-start.6 = (bf16[128,128]{1,0:T(8,128)(2,1)S(1)}, bf16[128,128]{1,0:T(8,128)(2,1)}, u32[]{:S(2)}) copy-start(bf16[128,128]{1,0:T(8,128)(2,1)} %param.5) | copy-start | bytes 98308
  1.3 5.4 %copy-start.7 = (bf16[128,128]{1,0:T(8,128)(2,1)S(1)}, bf16[128,128]{1,0:T(8,128)(2,1)}, u32[]{:S(2)}) copy-start(bf16[128,128]{1,0:T(8,128)(2,1)} %param.4) | copy-start | bytes 98308
  2.4 16.6 %collective-permute-start.1 = (bf16[3,256,256]{2,1,0:T(8,128)(2,1)S(1)}, bf16[3,256,256]{2,1,0:T(8,128)(2,1)S(1)}, u32[]{:S(2)}, u32[]{:S(2)}) collective-permute-start(bf16[3,256,256]{2,1,0:T(8,128)(2,1)S(1)} %multiply_convert_fusion.refs_0_), channel_id=1, source_target_pairs={{0,1},{1,0},{2,3},{3,2},{4,5},{5,4},{6,7},{7,6},{8,9},{9,8},{10,11... | collective-permute-start | bytes 1179656 | tf_op jit(solution)/shard_map/ppermute | solution.py:218
  6.7 11.1 %collective-permute-start = (bf16[2,128,128]{2,1,0:T(8,128)(2,1)S(1)}, bf16[2,128,128]{2,1,0:T(8,128)(2,1)S(1)}, u32[]{:S(2)}, u32[]{:S(2)}) collective-permute-start(bf16[2,128,128]{2,1,0:T(8,128)(2,1)S(1)} %pad_maximum_fusion), channel_id=1, source_target_pairs={{0,0},{1,8},{2,2},{3,10},{4,4},{5,12},{6,6},{7,14},{8,128},{9,136}... | collective-permute-start | bytes 196616 | tf_op jit(solution)/shard_map/ppermute | solution.py:216
  19.0 46.1 %all-to-all-start = ((bf16[16,2,128,128]{3,2,1,0:T(8,128)(2,1)}), bf16[16,2,128,128]{3,2,1,0:T(8,128)(2,1)S(1)}, u32[]{:S(2)}, u32[]{:S(2)}) async-start(bf16[16,2,128,128]{3,2,1,0:T(8,128)(2,1)} %spread.1), calls=%async_computation | async-start | bytes 2097152 | tf_op jit(solution)/shard_map/all_to_all | solution.py:209
  33.6 13.9 %collective-permute-start.2 = (bf16[3,256,256]{2,1,0:T(8,128)(2,1)S(1)}, bf16[3,256,256]{2,1,0:T(8,128)(2,1)S(1)}, u32[]{:S(2)}, u32[]{:S(2)}) collective-permute-start(bf16[3,256,256]{2,1,0:T(8,128)(2,1)S(1)} %multiply_convert_fusion.refs_0_), channel_id=1, source_target_pairs={{0,64},{64,0},{1,65},{65,1},{2,66},{66,2},{3,67},{67,3},{4,68},{68... | collective-permute-start | bytes 1179656 | tf_op jit(solution)/shard_map/ppermute | solution.py:220
  36.8 16.4 %collective-permute-start.3 = (bf16[3,256,256]{2,1,0:T(8,128)(2,1)S(1)}, bf16[3,256,256]{2,1,0:T(8,128)(2,1)S(1)}, u32[]{:S(2)}, u32[]{:S(2)}) collective-permute-start(bf16[3,256,256]{2,1,0:T(8,128)(2,1)S(1)} %collective-permute-done.1.refs_1_), channel_id=1, source_target_pairs={{0,64},{64,0},{1,65},{65,1},{2,66},{66,2},{3,67},{67,3},{4,68},{68... | collective-permute-start | bytes 1179656 | tf_op jit(solution)/shard_map/ppermute | solution.py:220
  39.4 15.7 %collective-permute-start.4 = (bf16[3,256,256]{2,1,0:T(8,128)(2,1)S(1)}, bf16[3,256,256]{2,1,0:T(8,128)(2,1)S(1)}, u32[]{:S(2)}, u32[]{:S(2)}) collective-permute-start(bf16[3,256,256]{2,1,0:T(8,128)(2,1)S(1)} %multiply_convert_fusion.refs_0_), channel_id=1, source_target_pairs={{0,32},{32,0},{1,33},{33,1},{2,34},{34,2},{3,35},{35,3},{4,36},{36... | collective-permute-start | bytes 1179656 | tf_op jit(solution)/shard_map/ppermute | solution.py:221
  41.4 13.8 %collective-permute-start.5 = (bf16[3,256,256]{2,1,0:T(8,128)(2,1)S(1)}, bf16[3,256,256]{2,1,0:T(8,128)(2,1)S(1)}, u32[]{:S(2)}, u32[]{:S(2)}) collective-permute-start(bf16[3,256,256]{2,1,0:T(8,128)(2,1)S(1)} %collective-permute-done.1.refs_1_), channel_id=1, source_target_pairs={{0,32},{32,0},{1,33},{33,1},{2,34},{34,2},{3,35},{35,3},{4,36},{36... | collective-permute-start | bytes 1179656 | tf_op jit(solution)/shard_map/ppermute | solution.py:221
  47.5 7.7 %collective-permute-start.6 = (bf16[3,256,256]{2,1,0:T(8,128)(2,1)S(1)}, bf16[3,256,256]{2,1,0:T(8,128)(2,1)}, u32[]{:S(2)}, u32[]{:S(2)}) collective-permute-start(bf16[3,256,256]{2,1,0:T(8,128)(2,1)S(1)} %collective-permute-done.2.refs_2_), channel_id=1, source_target_pairs={{0,32},{32,0},{1,33},{33,1},{2,34},{34,2},{3,35},{35,3},{4,36},{36... | collective-permute-start | bytes 1179656 | tf_op jit(solution)/shard_map/ppermute | solution.py:221
  53.2 3.7 %collective-permute-start.7 = (bf16[3,256,256]{2,1,0:T(8,128)(2,1)S(1)}, bf16[3,256,256]{2,1,0:T(8,128)(2,1)}, u32[]{:S(2)}, u32[]{:S(2)}) collective-permute-start(bf16[3,256,256]{2,1,0:T(8,128)(2,1)S(1)} %collective-permute-done.3.refs_3_), channel_id=1, source_target_pairs={{0,32},{32,0},{1,33},{33,1},{2,34},{34,2},{3,35},{35,3},{4,36},{36... | collective-permute-start | bytes 1179656 | tf_op jit(solution)/shard_map/ppermute | solution.py:221
  55.2 12.9 %copy-start = (bf16[3,256,256]{2,1,0:T(8,128)(2,1)}, bf16[3,256,256]{2,1,0:T(8,128)(2,1)S(1)}, u32[]{:S(2)}) copy-start(bf16[3,256,256]{2,1,0:T(8,128)(2,1)S(1)} %collective-permute-done.4.refs_4_) | copy-start | bytes 1179652
  55.2 12.9 %copy-start.2 = (bf16[3,256,256]{2,1,0:T(8,128)(2,1)}, bf16[3,256,256]{2,1,0:T(8,128)(2,1)S(1)}, u32[]{:S(2)}) copy-start(bf16[3,256,256]{2,1,0:T(8,128)(2,1)S(1)} %collective-permute-done.5.refs_5_) | copy-start | bytes 1179652
  68.1 13.8 %all-to-all-start.1 = ((bf16[4,64,1536]{2,1,0:T(8,128)(2,1)}), bf16[4,64,1536]{2,1,0:T(8,128)(2,1)S(1)}, u32[]{:S(2)}, u32[]{:S(2)}) async-start(bf16[4,64,1536]{2,1,0:T(8,128)(2,1)} %bitcast.7), calls=%async_computation.1 | async-start | bytes 1572864 | tf_op jit(solution)/shard_map/all_to_all | solution.py:209
  72.9 3.8 %collective-permute-start.8 = (bf16[2,2,2,2,128,128]{5,4,3,2,1,0:T(8,128)(2,1)S(1)}, bf16[2,2,2,2,128,128]{5,4,3,2,1,0:T(8,128)(2,1)S(1)}, u32[]{:S(2)}, u32[]{:S(2)}) collective-permute-start(bf16[2,2,2,2,128,128]{5,4,3,2,1,0:T(8,128)(2,1)S(1)} %dynamic-slice_bitcast_fusion), channel_id=1, source_target_pairs={{0,32},{32,0},{1,33},{33,1},{2,34},{34,2},{3,35},{35,3},{4,36},{36... | collective-permute-start | bytes 1572872 | tf_op jit(solution)/shard_map/ppermute | solution.py:227
  76.7 0.8 copy-start.4
  82.1 13.7 %copy-start.1 = (bf16[3,256,256]{2,1,0:T(8,128)(2,1)S(1)}, bf16[3,256,256]{2,1,0:T(8,128)(2,1)}, u32[]{:S(2)}) copy-start(bf16[3,256,256]{2,1,0:T(8,128)(2,1)} %copy-done) | copy-start | bytes 1179652
  82.1 13.7 %copy-start.3 = (bf16[3,256,256]{2,1,0:T(8,128)(2,1)S(1)}, bf16[3,256,256]{2,1,0:T(8,128)(2,1)}, u32[]{:S(2)}) copy-start(bf16[3,256,256]{2,1,0:T(8,128)(2,1)} %copy-done.2) | copy-start | bytes 1179652
  98.4 10.8 %copy-start.5 = (bf16[2,2,2,2,128,128]{5,4,3,2,1,0:T(8,128)(2,1)S(1)}, bf16[2,2,2,2,128,128]{5,4,3,2,1,0:T(8,128)(2,1)}, u32[]{:S(2)}) copy-start(bf16[2,2,2,2,128,128]{5,4,3,2,1,0:T(8,128)(2,1)} %copy-done.4) | copy-start | bytes 1572868
  98.4 22.4 %all-to-all-start.3 = ((bf16[8,2,128,128]{3,2,1,0:T(8,128)(2,1)}), bf16[8,2,128,128]{3,2,1,0:T(8,128)(2,1)}, u32[]{:S(2)}, u32[]{:S(2)}) async-start(bf16[8,2,128,128]{3,2,1,0:T(8,128)(2,1)} %input_terms.1), calls=%async_computation.3 | async-start | bytes 1048576 | tf_op jit(solution)/shard_map/all_to_all | solution.py:209
  105.0 4.2 %collective-permute-start.11 = (bf16[256,1536]{1,0:T(8,128)(2,1)S(1)}, bf16[256,1536]{1,0:T(8,128)(2,1)S(1)}, u32[]{:S(2)}, u32[]{:S(2)}) collective-permute-start(bf16[256,1536]{1,0:T(8,128)(2,1)S(1)} %bitcast.22), channel_id=1, source_target_pairs={{0,32},{32,0},{1,33},{33,1},{2,34},{34,2},{3,35},{35,3},{4,36},{36... | collective-permute-start | bytes 2359304 | tf_op jit(solution)/shard_map/ppermute | solution.py:231
  111.6 30.9 %collective-permute-start.12 = (bf16[3,256,256]{2,1,0:T(8,128)(2,1)}, bf16[3,256,256]{2,1,0:T(8,128)(2,1)S(1)}, u32[]{:S(2)}, u32[]{:S(2)}) collective-permute-start(bf16[3,256,256]{2,1,0:T(8,128)(2,1)} %get-tuple-element.15), channel_id=1, source_target_pairs={{0,1},{1,0},{2,3},{3,2},{4,5},{5,4},{6,7},{7,6},{8,9},{9,8},{10,11... | collective-permute-start | bytes 1179656 | tf_op jit(solution)/shard_map/ppermute | solution.py:239
  114.9 27.6 %collective-permute-start.13 = (bf16[3,256,256]{2,1,0:T(8,128)(2,1)}, bf16[3,256,256]{2,1,0:T(8,128)(2,1)S(1)}, u32[]{:S(2)}, u32[]{:S(2)}) collective-permute-start(bf16[3,256,256]{2,1,0:T(8,128)(2,1)} %get-tuple-element.16), channel_id=1, source_target_pairs={{0,64},{64,0},{1,65},{65,1},{2,66},{66,2},{3,67},{67,3},{4,68},{68... | collective-permute-start | bytes 1179656 | tf_op jit(solution)/shard_map/ppermute | solution.py:240
  117.8 24.7 %collective-permute-start.14 = (bf16[3,256,256]{2,1,0:T(8,128)(2,1)}, bf16[3,256,256]{2,1,0:T(8,128)(2,1)S(1)}, u32[]{:S(2)}, u32[]{:S(2)}) collective-permute-start(bf16[3,256,256]{2,1,0:T(8,128)(2,1)} %get-tuple-element.17), channel_id=1, source_target_pairs={{0,65},{1,64},{64,1},{65,0},{2,67},{3,66},{66,3},{67,2},{4,69},{5,... | collective-permute-start | bytes 1179656 | tf_op jit(solution)/shard_map/ppermute | solution.py:241
  122.0 16.3 %collective-permute-start.9 = (bf16[128,128]{1,0:T(8,128)(2,1)S(1)}, bf16[128,128]{1,0:T(8,128)(2,1)S(1)}, u32[]{:S(2)}, u32[]{:S(2)}) collective-permute-start(bf16[128,128]{1,0:T(8,128)(2,1)S(1)} %get-tuple-element.18), channel_id=1, source_target_pairs={{0,0},{8,1},{2,2},{10,3},{4,4},{12,5},{6,6},{14,7},{128,8},{136,9}... | collective-permute-start | bytes 98312 | tf_op jit(solution)/shard_map/ppermute | solution.py:235
  128.8 13.0 %collective-permute-start.10 = (bf16[128,128]{1,0:T(8,128)(2,1)S(1)}, bf16[128,128]{1,0:T(8,128)(2,1)S(1)}, u32[]{:S(2)}, u32[]{:S(2)}) collective-permute-start(bf16[128,128]{1,0:T(8,128)(2,1)S(1)} %get-tuple-element.19), channel_id=1, source_target_pairs={{16,0},{24,1},{18,2},{26,3},{20,4},{28,5},{22,6},{30,7},{144,8},{1... | collective-permute-start | bytes 98312 | tf_op jit(solution)/shard_map/ppermute | solution.py:235
